TPU v7x, 1024 devices: a whole 4x8x16 slice. The times are simulated.
1024 devices in a mesh: row: 16 (over z_hi, x, core), col: 64 (over y, z_lo).
Axes of the slice: x: 4, y: 8, z: 16 (z_hi: 2, z_lo: 8; z = z_hi * 8 + z_lo), core: 2. Of those that a mesh axis runs over, the one named last changes fastest.
Arguments:
- features: bfloat16 [131072, 256], P(('row', 'col')), may hold values from -6 to 6
- tile_values: int32 [16, 64, 10, 128, 128], P('row', 'col'), may hold values 0 or 1
- tile_block_row: int32 [16, 64, 10], P('row', 'col'), may hold values from 0 to 63
- tile_block_col: int32 [16, 64, 10], P('row', 'col'), may hold values from 0 to 15
- tile_count: int32 [16, 64], P('row', 'col'), may hold values from 8 to 10, as said below
- in_degree: int32 [131072], P(('row', 'col')), may hold values from 1 to 8
- w_self: bfloat16 [256, 256], replicated, may hold values from -0.375 to 0.375
- w_neigh: bfloat16 [256, 256], replicated, may hold values from -0.375 to 0.375
- bias: float32 [256], replicated, may hold values from -4 to 4
- grad_out: bfloat16 [131072, 256], P(('row', 'col')), may hold values from -6 to 6
Outputs:
- hidden: bfloat16 [131072, 256], P(('row', 'col'))
- grad_features: bfloat16 [131072, 256], P(('row', 'col'))
- grad_w_self: float32 [256, 256], replicated
- grad_w_neigh: float32 [256, 256], replicated
- grad_bias: float32 [256], replicated
Inputs may be any that keep to these rules, and one draw needn't show every extreme that they name: `tile_count`: at least one grid block holds exactly 10 live slots.
All inputs are finite; a program needn't handle non-finite values. No bound on the sum of `tile_values` on one device may be relied on, other than what follows from the above.
Results may differ from a plain program's by a relative error of at most 0.007.
Values may be sent and summed in bfloat16 or wider, within the bound.
No kernel may reach another device: no remote copies, remote signals or barrier semaphores. Data moves between devices by JAX's collectives and lax.ppermute only.
A program may use at most 32 MiB of HBM per device.

v0:
```python
import jax
import jax.numpy as jnp
from jax import lax
from jax.sharding import PartitionSpec as P


def activate(values):
    return jax.nn.gelu(values, approximate=True)


def weight_totals(features, aggregate, grad_pre):
    contract = (((0,), (0,)), ((), ()))
    self_term = lax.dot_general(features, grad_pre, contract, preferred_element_type=jnp.float32)
    neigh_term = lax.dot_general(aggregate, grad_pre, contract, preferred_element_type=jnp.float32)
    bias_term = jnp.sum(grad_pre.astype(jnp.float32), axis=0)
    return lax.psum((self_term, neigh_term, bias_term), ("row", "col"))


def body(
    features,
    tile_values,
    tile_block_row,
    tile_block_col,
    tile_count,
    in_degree,
    w_self,
    w_neigh,
    bias,
    grad_out,
):
    highest = lax.Precision.HIGHEST
    node_rows, width = features.shape
    tile_side = tile_values.shape[3]
    slot_count = tile_values.shape[2]
    dest_tiles = node_rows * lax.axis_size("col") // tile_side
    source_tiles = node_rows * lax.axis_size("row") // tile_side
    tiles = tile_values[0, 0].astype(jnp.bfloat16)
    dest_pos = tile_block_row[0, 0]
    source_pos = tile_block_col[0, 0]
    live = jnp.arange(slot_count, dtype=jnp.int32) < tile_count[0, 0]
    dest_onehot = (
        (jnp.arange(dest_tiles, dtype=jnp.int32)[:, None] == dest_pos[None, :]) & live[None, :]
    ).astype(jnp.float32)
    source_onehot = (
        (jnp.arange(source_tiles, dtype=jnp.int32)[:, None] == source_pos[None, :]) & live[None, :]
    ).astype(jnp.float32)
    row_edges = jnp.sum(tile_values[0, 0], axis=2).astype(jnp.float32)
    edge_partial = jnp.dot(dest_onehot, row_edges, precision=highest).reshape(
        dest_tiles * tile_side
    )
    panel = lax.all_gather(features, "row", axis=0, tiled=True)
    picked = panel.reshape(source_tiles, tile_side, width)[source_pos]
    contrib = jnp.einsum("sij,sjf->sif", tiles, picked, preferred_element_type=jnp.float32)
    partial_value = jnp.einsum("ds,sif->dif", dest_onehot, contrib, precision=highest).reshape(
        dest_tiles * tile_side, width
    )
    neigh_sum, edge_counts = (
        lax.psum_scatter(partial_value, "col", scatter_dimension=0, tiled=True),
        lax.psum_scatter(edge_partial, "col", scatter_dimension=0, tiled=True),
    )
    degree = (edge_counts + in_degree.astype(jnp.float32))[:, None]
    aggregate = (neigh_sum / degree).astype(jnp.bfloat16)
    preact = (
        jnp.dot(features, w_self, preferred_element_type=jnp.float32)
        + jnp.dot(aggregate, w_neigh, preferred_element_type=jnp.float32)
        + bias
    )
    hidden, pullback = jax.vjp(activate, preact)
    grad_pre = pullback(grad_out.astype(jnp.float32))[0].astype(jnp.bfloat16)
    transpose_dims = (((1,), (1,)), ((), ()))
    neigh_back = lax.dot_general(
        grad_pre, w_neigh, transpose_dims, preferred_element_type=jnp.float32
    )
    scaled_grad = (neigh_back / degree).astype(jnp.bfloat16)
    dest_block = lax.all_gather(scaled_grad, "col", axis=0, tiled=True)
    dest_picked = dest_block.reshape(dest_tiles, tile_side, width)[dest_pos]
    back = jnp.einsum("sij,sif->sjf", tiles, dest_picked, preferred_element_type=jnp.float32)
    back_partial = jnp.einsum("ds,sif->dif", source_onehot, back, precision=highest).reshape(
        source_tiles * tile_side, width
    )
    back_sum = lax.psum_scatter(
        back_partial.astype(jnp.bfloat16), "row", scatter_dimension=0, tiled=True
    ).astype(jnp.float32)
    self_back = lax.dot_general(
        grad_pre, w_self, transpose_dims, preferred_element_type=jnp.float32
    )
    grad_features = (self_back + back_sum).astype(jnp.bfloat16)
    grad_w_self, grad_w_neigh, grad_bias = weight_totals(features, aggregate, grad_pre)
    return (hidden.astype(jnp.bfloat16), grad_features, grad_w_self, grad_w_neigh, grad_bias)


def solution(mesh):
    in_specs = (
        P(("row", "col"), None),
        P("row", "col", None, None, None),
        P("row", "col", None),
        P("row", "col", None),
        P("row", "col"),
        P(("row", "col")),
        P(),
        P(),
        P(),
        P(("row", "col"), None),
    )
    out_specs = (P(("row", "col"), None), P(("row", "col"), None), P(), P(), P())
    return jax.shard_map(body, mesh=mesh, in_specs=in_specs, out_specs=out_specs, check_vma=False)
```

profile of v0, /device:TPU:1, one launch (start us, length us, event | category | flops | bytes accessed | tf_op | source)
XLA Modules:
  0.0 1661.8 jit_solution(2882695766893193417)
XLA Ops:
  7.2 0.0 copy-start
  7.2 0.0 all-gather.3.cloned.1.call-start
  7.2 0.7 all-gather.3.cloned.1.call-update
  7.9 0.0 reduce-scatter.3.cloned.1.call-start
  8.6 0.7 fusion.32
  9.3 97.2 %all-gather.3.cloned.1.call-done = bf16[2048,256]{1,0:T(8,128)(2,1)} async-done(((bf16[128,256]{1,0:T(8,128)(2,1)}), bf16[2048,256]{1,0:T(8,128)(2,1)}) %all-gather.3.cloned.1.call-update) | async-done | bytes 1048592 | tf_op jit(solution)/shard_map/all_gather | solution.py:51
  106.5 1.8 gather_fusion
  108.3 1.5 convolution_bitcast_fusion.1
  109.8 0.0 copy-start.7
  109.8 1.2 copy.26
  111.0 0.0 copy-done.7
  111.0 3.6 fusion.21
  114.6 8.1 copy.27
  122.7 0.0 copy-start.1
  122.7 0.0 copy-start.9
  122.7 0.0 copy-start.2
  122.7 0.0 copy-start.3
  122.7 0.0 copy-start.11
  122.7 0.0 copy-start.12
  122.7 0.0 reduce-scatter.3.cloned.1.call-update
  122.7 0.0 all-gather.5.cloned.1.call-start
  122.8 1.0 copy-done.1
  123.8 0.2 reduce_sum.18
  124.0 1.3 dynamic-slice
  125.9 0.3 convolution_bitcast_fusion.3
  126.2 402.3 %all-reduce = f32[8192]{0:T(1024)S(1)} all-reduce(f32[8192]{0:T(1024)S(1)} %convolution_bitcast_fusion.3), channel_id=3, replica_groups=mesh['row'=16,'col'=64] {'col'}, use_global_device_ids=true, to_apply=%region_2.0.clone | all-reduce | flops 8192 | bytes 65536
  528.5 0.0 copy-done.9
  528.5 0.1 dynamic-slice_add_fusion
  528.6 0.0 copy-done.2
  528.6 0.0 copy-done.3
  528.6 0.2 fusion.36
  528.8 31.7 %reduce-scatter.3.cloned.1.call-done = f32[128,256]{1,0:T(8,128)} async-done(((f32[8192,256]{1,0:T(8,128)}), f32[128,256]{1,0:T(8,128)}) %reduce-scatter.3.cloned.1.call-update) | async-done | bytes 131088 | tf_op jit(solution)/shard_map/reduce_scatter | solution.py:58
  560.4 0.0 copy-done
  560.4 0.0 copy-done.11
  560.4 0.0 copy-done.12
  560.4 1.9 convert_reduce_fusion
  562.4 0.8 fusion.2
  563.2 0.0 all-gather.5.cloned.1.call-update
  563.2 0.0 all-reduce.4.cloned.1.call-start
  563.3 0.9 convolution_bitcast_fusion.2
  564.2 0.0 copy-done.10
  564.2 1.0 fusion.34
  565.2 0.0 all-reduce.4.cloned.1.call-update
  565.2 0.2 reduce-scatter.5.cloned.1.call-start
  565.5 441.6 %all-gather.5.cloned.1.call-done = bf16[8192,256]{1,0:T(8,128)(2,1)} async-done(((bf16[128,256]{1,0:T(8,128)(2,1)}), bf16[8192,256]{1,0:T(8,128)(2,1)}) %all-gather.5.cloned.1.call-update) | async-done | bytes 4194320 | tf_op jit(solution)/shard_map/all_gather | solution.py:75
  1007.0 0.0 copy-done.5
  1007.0 2.8 gather_fusion.1
  1009.8 0.4 convolution_bitcast_fusion
  1010.2 0.0 copy-start.8
  1010.2 1.2 copy.29
  1011.4 0.0 copy-done.8
  1011.4 1.1 convolution_convert_fusion
  1012.5 0.0 copy-start.4
  1012.5 0.0 copy-start.6
  1012.6 1.3 copy.30
  1013.9 0.0 reduce-scatter.5.cloned.1.call-update
  1013.9 162.7 %psum.23 = f32[256]{0:T(256)} all-reduce(f32[256]{0:T(256)S(1)} %get-tuple-element.27), channel_id=1, replica_groups=mesh['row'=16,'col'=64] {'row','col'}, use_global_device_ids=true, to_apply=%region_7.0 | all-reduce | flops 256 | bytes 2048 | tf_op jit(solution)/shard_map/psum | solution.py:16
  1176.6 356.9 %all-reduce.4.cloned.1.call-done = (f32[256,256]{0,1:T(8,128)}, f32[256,256]{1,0:T(8,128)}) async-done(((f32[256,256]{0,1:T(8,128)}, f32[256,256]{1,0:T(8,128)}), (f32[256,256]{0,1:T(8,128)}, f32[256,256]{1,0:T(8,128)})) %all-reduce.4.cloned.1.call-update) | async-done | bytes 524304 | tf_op jit(solution)/shard_map/psum | solution.py:16
  1533.5 1.8 copy.31
  1535.3 116.6 %reduce-scatter.5.cloned.1.call-done = bf16[128,256]{1,0:T(8,128)(2,1)} async-done(((bf16[2048,256]{1,0:T(8,128)(2,1)}), bf16[128,256]{1,0:T(8,128)(2,1)}) %reduce-scatter.5.cloned.1.call-update) | async-done | bytes 65552 | tf_op jit(solution)/shard_map/reduce_scatter | solution.py:81
  1652.0 0.0 copy-done.4
  1652.0 0.0 copy-done.6
  1652.0 1.7 fusion.1
  1653.6 1.7 copy.37
  (6 shorter events, 0.0 us)
Async XLA Ops:
  7.2 553.3 %copy-start = (bf16[256,256]{1,0:T(8,128)(2,1)S(1)}, bf16[256,256]{1,0:T(8,128)(2,1)}, u32[]{:S(2)}) copy-start(bf16[256,256]{1,0:T(8,128)(2,1)} %param.17) | copy-start | bytes 393220
  7.2 99.3 %all-gather.3.cloned.1.call-start = ((), (), s32[]{:S(2)}) async-start(), calls=%async_computation.2 | async-start | bytes 1114112 | tf_op jit(solution)/shard_map/all_gather | solution.py:51
  7.9 552.5 %reduce-scatter.3.cloned.1.call-start = ((), (), s32[]{:S(2)}) async-start(), calls=%async_computation.3 | async-start | bytes 8519680 | tf_op jit(solution)/shard_map/reduce_scatter | solution.py:58
  109.8 1.2 copy-start.7
  122.7 1.1 copy-start.1
  122.7 405.8 %copy-start.9 = (s32[128]{0:T(128)S(1)}, s32[128]{0:T(128)}, u32[]{:S(2)}) copy-start(s32[128]{0:T(128)} %param.15) | copy-start | bytes 1540
  122.7 405.9 %copy-start.2 = (bf16[128,256]{1,0:T(8,128)(2,1)S(1)}, bf16[128,256]{1,0:T(8,128)(2,1)}, u32[]{:S(2)}) copy-start(bf16[128,256]{1,0:T(8,128)(2,1)} %param.10) | copy-start | bytes 196612
  122.7 405.9 %copy-start.3 = (bf16[256,256]{1,0:T(8,128)(2,1)S(1)}, bf16[256,256]{1,0:T(8,128)(2,1)}, u32[]{:S(2)}) copy-start(bf16[256,256]{1,0:T(8,128)(2,1)} %param.16) | copy-start | bytes 393220
  122.7 437.7 %copy-start.11 = (bf16[128,256]{1,0:T(8,128)(2,1)S(1)}, bf16[128,256]{1,0:T(8,128)(2,1)}, u32[]{:S(2)}) copy-start(bf16[128,256]{1,0:T(8,128)(2,1)} %param.19) | copy-start | bytes 196612
  122.7 437.7 %copy-start.12 = (f32[256]{0:T(256)S(1)}, f32[256]{0:T(256)}, u32[]{:S(2)}) copy-start(f32[256]{0:T(256)} %param.18) | copy-start | bytes 3076
  122.7 884.3 %all-gather.5.cloned.1.call-start = ((), (), s32[]{:S(2)}) async-start(), calls=%async_computation.4 | async-start | bytes 4259840 | tf_op jit(solution)/shard_map/all_gather | solution.py:75
  560.4 3.8 copy-start.10
  562.4 444.7 %copy-start.5 = (bf16[128,256]{1,0:T(8,128)(2,1)}, bf16[128,256]{1,0:T(8,128)(2,1)S(1)}, u32[]{:S(2)}) copy-start(bf16[128,256]{1,0:T(8,128)(2,1)S(1)} %get-tuple-element.28) | copy-start | bytes 196612
  563.2 970.3 %all-reduce.4.cloned.1.call-start = ((), (), s32[]{:S(2)}) async-start(), calls=%async_computation.6 | async-start | bytes 1048576 | tf_op jit(solution)/shard_map/psum | solution.py:16
  565.2 1086.7 %reduce-scatter.5.cloned.1.call-start = ((), (), s32[]{:S(2)}) async-start(), calls=%async_computation.5 | async-start | bytes 1114112 | tf_op jit(solution)/shard_map/reduce_scatter | solution.py:81
  1010.2 1.2 copy-start.8
  1012.5 639.4 %copy-start.4 = (bf16[256,256]{1,0:T(8,128)(2,1)S(1)}, bf16[256,256]{1,0:T(8,128)(2,1)}, u32[]{:S(2)}) copy-start(bf16[256,256]{1,0:T(8,128)(2,1)} %param.16) | copy-start | bytes 393220
  1012.5 639.4 %copy-start.6 = (bf16[128,256]{1,0:T(8,128)(2,1)S(1)}, bf16[128,256]{1,0:T(8,128)(2,1)}, u32[]{:S(2)}) copy-start(bf16[128,256]{1,0:T(8,128)(2,1)} %copy-done.5) | copy-start | bytes 196612
Sparse Core Ops, SparseCore 0:
  12.5 93.9 all-gather.2
  122.9 437.5 reduce-scatter.2
  563.3 443.6 all-gather.4
  1013.1 520.4 all-reduce.3
  1539.3 112.6 reduce-scatter.4
where the time goes:
time: 1660 us
  waiting for transfers between devices  1040 us (63%)
  blocking collectives  565 us (34%)
  local copies, waits for them, and re-layouts  22.1 us (1%)
    all_gather x1, waiting for transfers between devices, body(): dest_block = lax.all_gather(scaled_grad, 'col', axis=0, tiled=True)  442 us
    unnamed x1, blocking collectives  402 us
    psum x1, waiting for transfers between devices, weight_totals(): return lax.psum((self_term, neigh_term, bias_term), ('row', 'col'))  357 us
    psum x1, blocking collectives, weight_totals(): return lax.psum((self_term, neigh_term, bias_term), ('row', 'col'))  163 us
    reduce_scatter x1, waiting for transfers between devices, body(): lax.psum_scatter(back_partial.astype(jnp.bfloat16), 'row', scatter_dimens...  117 us
    all_gather x1, waiting for transfers between devices, body(): panel = lax.all_gather(features, 'row', axis=0, tiled=True)  97.2 us
  transfers between devices with their start and end apart: 5, of which 5 were waited for; matrix products, arithmetic and copies ran while one was open for 1% of the time, Pallas kernels for 0%

commit v1 on v0

v1 whole, which is shorter than its diff:
```python
import functools

import jax
import jax.numpy as jnp
from jax import lax
from jax.experimental import pallas as pl
from jax.experimental.pallas import tpu as pltpu
from jax.sharding import Mesh, PartitionSpec as P

BF = jnp.bfloat16
F32 = jnp.float32
TILE = 128
HID = 256
QUAD = 4
CNT = 16
CHUNK = QUAD * TILE + CNT
VMEM = pl.BlockSpec(memory_space=pltpu.VMEM)
SMEM = pl.BlockSpec(memory_space=pltpu.SMEM)


def call(kernel, out, in_specs, *args, scratch=(), flops=0):
    shapes = [jax.ShapeDtypeStruct(s, t) for s, t in out]
    moved = sum(a.size * a.dtype.itemsize for a in args)
    moved += sum(s.size * s.dtype.itemsize for s in shapes)
    return pl.pallas_call(
        kernel,
        out_shape=shapes,
        in_specs=in_specs,
        out_specs=[VMEM] * len(shapes),
        scratch_shapes=list(scratch),
        compiler_params=pltpu.CompilerParams(vmem_limit_bytes=48 * 1024 * 1024),
        cost_estimate=pl.CostEstimate(flops=flops, bytes_accessed=moved, transcendentals=0),
    )(*args)


def split_counts(n):
    hi = n.astype(BF)
    lo = (n - hi.astype(F32)).astype(BF)
    return jnp.concatenate([hi, lo], axis=1)


def joined(block):
    return block[:, :TILE].astype(F32) + block[:, TILE:].astype(F32)


def row_counts(tile):
    ones = jnp.ones((8, TILE), BF)
    return lax.dot_general(ones, tile, (((1,), (1,)), ((), ())), preferred_element_type=F32)[0:1]


def add_counts(acc, chunk, lay, row):
    at = pl.multiple_of(chunk * CHUNK + QUAD * TILE, 16)
    mine = lax.broadcasted_iota(jnp.int32, (8, TILE), 0) == lay
    acc[pl.ds(at, 8), 0:TILE] += jnp.where(mine, jnp.broadcast_to(row, (8, TILE)), 0.0)


def contrib_kernel(slots, src, tiles, panel, msg, tiles_bf):
    msg[slots * TILE :, :] = jnp.zeros((CNT, HID), BF)
    rows = []
    for s in range(slots):
        tile = tiles[s].astype(F32).astype(BF)
        tiles_bf[s] = tile
        at = pl.multiple_of(src[s] * TILE, TILE)
        got = jnp.dot(tile, panel[pl.ds(at, TILE), :], preferred_element_type=F32)
        msg[s * TILE : (s + 1) * TILE, :] = got.astype(BF)
        rows.append(row_counts(tile))
    rows.append(jnp.zeros((CNT - slots, TILE), F32))
    counts = jnp.concatenate(rows, axis=0)
    msg[slots * TILE :, :] = jnp.concatenate([counts, jnp.zeros_like(counts)], axis=1).astype(BF)


def own_kernel(slots, src, idx, tiles, panel, acc):
    acc[...] = jnp.zeros_like(acc)
    for s in range(slots):

        @pl.when(idx[s] >= 0)
        def _():
            at = pl.multiple_of(src[s] * TILE, TILE)
            got = jnp.dot(tiles[s], panel[pl.ds(at, TILE), :], preferred_element_type=F32)
            chunk = idx[s] // QUAD
            lay = idx[s] % QUAD
            to = pl.multiple_of(chunk * CHUNK + lay * TILE, 16)
            acc[pl.ds(to, TILE), :] += got
            add_counts(acc, chunk, lay, row_counts(tiles[s]))


def merge_kernel(slots, chunks, idx, acc_in, recv, *refs):
    outs, acc = refs[:-1], refs[-1]
    acc[...] = acc_in[...]
    counts = recv[slots * TILE :, 0:TILE].astype(F32)
    for s in range(slots):

        @pl.when(idx[s] >= 0)
        def _():
            chunk = idx[s] // QUAD
            lay = idx[s] % QUAD
            to = pl.multiple_of(chunk * CHUNK + lay * TILE, 16)
            acc[pl.ds(to, TILE), :] += recv[s * TILE : (s + 1) * TILE, :].astype(F32)
            add_counts(acc, chunk, lay, counts[s : s + 1])

    for o in range(chunks):
        at = o * CHUNK
        outs[o][0 : QUAD * TILE, :] = acc[at : at + QUAD * TILE, :].astype(BF)
        outs[o][QUAD * TILE :, :] = split_counts(acc[at + QUAD * TILE : at + CHUNK, 0:TILE])


def add_kernel(recv, own, out):
    n = QUAD * TILE
    out[0:n, :] = (recv[0:n, :].astype(F32) + own[0:n, :].astype(F32)).astype(BF)
    out[n:, :] = split_counts(joined(recv[n:, :]) + joined(own[n:, :]))


def ring_end_kernel(*refs):
    parts, keep, send = refs[:-2], refs[-2], refs[-1]
    half, n = 2 * TILE, QUAD * TILE
    first = sum(p[0:half, :].astype(F32) for p in parts)
    second = sum(p[half:n, :].astype(F32) for p in parts)
    counts = sum(joined(p[n:, :]) for p in parts)
    keep[0:half, :] = first
    keep[half:, :] = jnp.concatenate([counts, counts], axis=1)
    send[0:half, :] = second.astype(BF)
    send[half:, :] = split_counts(counts)


def half_kernel(keep_in, recv, keep, send):
    half = 2 * TILE
    counts = keep_in[half : half + 8, 0:TILE] + joined(recv[half:, :])[2:10]
    counts = jnp.concatenate([counts, counts], axis=0)
    keep[0:TILE, :] = keep_in[0:TILE, :] + recv[0:TILE, :].astype(F32)
    keep[TILE:, :] = jnp.concatenate([counts, counts], axis=1)
    send[0:TILE, :] = (keep_in[TILE:half, :] + recv[TILE:half, :].astype(F32)).astype(BF)
    send[TILE:, :] = split_counts(counts)


def degree_column(row):
    eye = lax.broadcasted_iota(jnp.int32, (TILE, TILE), 0) == lax.broadcasted_iota(
        jnp.int32, (TILE, TILE), 1
    )
    wide = jnp.broadcast_to(row, (TILE, TILE))
    return jnp.sum(jnp.where(eye, wide, 0.0), axis=1, keepdims=True)


def node_kernel(
    keep, recv, in_degree, features, w_self, w_neigh, bias, grad_out, hidden, aggregate, grad_pre, scaled
):
    neigh = keep[0:TILE, :] + recv[0:TILE, :].astype(F32)
    edges = keep[TILE : TILE + 1, 0:TILE] + joined(recv[TILE:, :])[1:2]
    degree = degree_column(edges + in_degree[...].astype(F32))
    mean = (neigh / degree).astype(BF)
    aggregate[...] = mean
    v = (
        jnp.dot(features[...], w_self[...], preferred_element_type=F32)
        + jnp.dot(mean, w_neigh[...], preferred_element_type=F32)
        + bias[...]
    )
    c = 0.7978845608028654
    t = jnp.tanh(c * (v + 0.044715 * v * v * v))
    hidden[...] = (0.5 * v * (1.0 + t)).astype(BF)
    slope = 0.5 * (1.0 + t) + 0.5 * v * (1.0 - t * t) * (c * (1.0 + 3.0 * 0.044715 * v * v))
    g = (grad_out[...].astype(F32) * slope).astype(BF)
    grad_pre[...] = g
    back = lax.dot_general(g, w_neigh[...], (((1,), (1,)), ((), ())), preferred_element_type=F32)
    scaled[...] = (back / degree).astype(BF)


def weight_kernel(place, features, aggregate, grad_pre, w_self, keep, send, self_back):
    g = grad_pre[...]
    contract = (((0,), (0,)), ((), ()))
    first = lax.dot_general(features[...], g, contract, preferred_element_type=F32)
    second = lax.dot_general(aggregate[...], g, contract, preferred_element_type=F32)
    bias = jnp.broadcast_to(jnp.sum(g.astype(F32), axis=0, keepdims=True), (8, HID))
    mine = place[0] == 0
    keep[0:HID, :] = jnp.where(mine, first, second)
    send[0:HID, :] = jnp.where(mine, second, first)
    keep[HID:, :] = bias
    send[HID:, :] = bias
    self_back[...] = lax.dot_general(
        g, w_self[...], (((1,), (1,)), ((), ())), preferred_element_type=F32
    )


def weight_cut_kernel(size, place, keep_in, recv, *outs):
    rows = HID // size
    bias = keep_in[HID:, :] + recv[HID:, :]
    for d in range(size):
        at = pl.multiple_of(lax.rem(place[1] + d, size) * rows, 8)
        outs[d][0:rows, :] = keep_in[pl.ds(at, rows), :] + recv[pl.ds(at, rows), :]
        outs[d][rows:, :] = bias


def sum_kernel(*refs):
    refs[-1][...] = functools.reduce(lambda a, b: a + b, [r[...] for r in refs[:-1]])


def pick_kernel(slots, idx, local, msg):
    for s in range(slots):
        at = pl.multiple_of(jnp.maximum(idx[s], 0) * TILE, TILE)
        msg[s * TILE : (s + 1) * TILE, :] = local[pl.ds(at, TILE), :]


def back_kernel(slots, src, idx, live, tiles, local, recv, keep, send, acc, held):
    acc[...] = jnp.zeros_like(acc)
    for s in range(slots):

        @pl.when(live[s] > 0)
        def _():
            @pl.when(idx[s] >= 0)
            def _():
                at = pl.multiple_of(idx[s] * TILE, TILE)
                held[...] = local[pl.ds(at, TILE), :]

            @pl.when(idx[s] < 0)
            def _():
                held[...] = recv[s * TILE : (s + 1) * TILE, :]

            got = lax.dot_general(
                tiles[s], held[...], (((0,), (0,)), ((), ())), preferred_element_type=F32
            )
            to = pl.multiple_of(src[s] * TILE, TILE)
            acc[pl.ds(to, TILE), :] += got

    half = keep.shape[0]
    keep[...] = acc[0:half, :]
    send[...] = acc[half:, :].astype(BF)


def back_cut_kernel(keep_in, recv, keep, *sends):
    rows = keep.shape[0]
    for d, ref in enumerate((keep,) + sends):
        at = d * rows
        got = keep_in[at : at + rows, :] + recv[at : at + rows, :].astype(F32)
        ref[...] = got.astype(ref.dtype)


def back_gather_kernel(pieces, *refs):
    ins, outs = refs[: len(refs) - pieces], refs[len(refs) - pieces :]
    for d, ref in enumerate(outs):
        at = slice(d * TILE, (d + 1) * TILE)
        ref[...] = sum(r[at, :].astype(F32) for r in ins).astype(ref.dtype)


def body(
    features,
    tile_values,
    tile_block_row,
    tile_block_col,
    tile_count,
    in_degree,
    w_self,
    w_neigh,
    bias,
    grad_out,
):
    nh, nx, nk, ny, nl = (lax.axis_size(a) for a in ("h", "x", "k", "y", "l"))
    h, x, k, y, l = (lax.axis_index(a) for a in ("h", "x", "k", "y", "l"))
    slots = tile_values.shape[2]
    sources = nh * nx * nk

    def flip(value, axis, bit):
        n = lax.axis_size(axis)
        return lax.ppermute(value, axis, [(i, i ^ bit) for i in range(n)])

    def shift(value, axis, by):
        n = lax.axis_size(axis)
        return lax.ppermute(value, axis, [(i, (i + by) % n) for i in range(n)])

    slot = jnp.arange(slots, dtype=jnp.int32)
    live = (slot < tile_count[0, 0]).astype(jnp.int32)
    dest = jnp.where(live > 0, tile_block_row[0, 0], -1)
    source = tile_block_col[0, 0]
    sh, sx, sk = source // (nx * nk), (source // nk) % nx, source % nk
    src = (sk ^ k) * (nx * nh) + ((sx - x) % nx) * nh + (sh ^ h)

    def place(d):
        dl = d % nl
        far = (dl >> 1) ^ (l >> 1)
        lay = ((far & 1) << 1) | (far >> 1)
        at = ((d // nl - y) % ny) * QUAD + lay
        return jnp.where((d >= 0) & ((dl & 1) == (l & 1)), at, -1)

    meta = jnp.zeros((8, TILE), jnp.int32).at[0, :slots].set(dest)
    other = flip(meta, "l", 1)[0, :slots]
    own_idx, other_idx = place(dest), place(other)

    panel = features
    if nh > 1:
        panel = jnp.concatenate([panel, flip(panel, "h", 1)], axis=0)
    panel = jnp.concatenate([panel] + [shift(panel, "x", -d) for d in range(1, nx)], axis=0)
    panel = jnp.concatenate([panel, flip(panel, "k", 1)], axis=0)

    tile_flops = 2 * slots * TILE * TILE * HID
    msg, tiles = call(
        functools.partial(contrib_kernel, slots),
        [((slots * TILE + CNT, HID), BF), ((slots, TILE, TILE), BF)],
        [SMEM, VMEM, VMEM],
        src,
        tile_values[0, 0],
        panel,
        flops=tile_flops,
    )
    got = flip(msg, "l", 1)
    (acc,) = call(
        functools.partial(own_kernel, slots),
        [((ny * CHUNK, HID), F32)],
        [SMEM, SMEM, VMEM, VMEM],
        src,
        own_idx,
        tiles,
        panel,
        flops=tile_flops,
    )
    chunks = call(
        functools.partial(merge_kernel, slots, ny),
        [((CHUNK, HID), BF)] * ny,
        [SMEM, VMEM, VMEM],
        other_idx,
        acc,
        got,
        scratch=[pltpu.VMEM((ny * CHUNK, HID), F32)],
    )

    ups, downs = ny // 2, ny - 1 - ny // 2
    up, down = chunks[ups], chunks[(-downs) % ny]
    parts = [chunks[0]]
    for step in range(1, ups + 1):
        up = shift(up, "y", 1)
        if step <= downs:
            down = shift(down, "y", -1)
        if step < ups:
            (up,) = call(add_kernel, [((CHUNK, HID), BF)], [VMEM] * 2, up, chunks[ups - step])
        if step < downs:
            (down,) = call(
                add_kernel, [((CHUNK, HID), BF)], [VMEM] * 2, down, chunks[ny - downs + step]
            )
    parts.append(up)
    if downs:
        parts.append(down)
    half_rows, last_rows = 2 * TILE + CNT, TILE + CNT
    keep, send = call(
        ring_end_kernel,
        [((half_rows, HID), F32), ((half_rows, HID), BF)],
        [VMEM] * len(parts),
        *parts,
    )
    keep, send = call(
        half_kernel,
        [((last_rows, HID), F32), ((last_rows, HID), BF)],
        [VMEM] * 2,
        keep,
        flip(send, "l", 2),
    )
    node = ((TILE, HID), BF)
    hidden, aggregate, grad_pre, scaled = call(
        node_kernel,
        [node] * 4,
        [VMEM] * 8,
        keep,
        flip(send, "l", 4),
        in_degree.reshape(1, TILE),
        features,
        w_self,
        w_neigh,
        bias.reshape(1, HID),
        grad_out,
        flops=6 * TILE * HID * HID,
    )

    local = jnp.concatenate([scaled, flip(scaled, "l", 4)], axis=0)
    local = jnp.concatenate([local, flip(local, "l", 2)], axis=0)
    blocks = {0: local}
    up = down = local
    for step in range(1, ups + 1):
        up = shift(up, "y", 1)
        blocks[(-step) % ny] = up
        if step <= downs:
            down = shift(down, "y", -1)
            blocks[step] = down

    where = jnp.stack([k, x]).astype(jnp.int32)
    wide = ((HID + 8, HID), F32)
    w_keep, w_send, self_back = call(
        weight_kernel,
        [wide, wide, ((TILE, HID), F32)],
        [SMEM] + [VMEM] * 4,
        where,
        features,
        aggregate,
        grad_pre,
        w_self,
        flops=6 * TILE * HID * HID,
    )
    w_rows = HID // nx
    cut = ((w_rows + 8, HID), F32)
    cuts = call(
        functools.partial(weight_cut_kernel, nx),
        [cut] * nx,
        [SMEM, VMEM, VMEM],
        where,
        w_keep,
        flip(w_send, "k", 1),
    )
    got = [cuts[0]] + [shift(cuts[d], "x", d) for d in range(1, nx)]
    (total,) = call(sum_kernel, [cut], [VMEM] * nx, *got)
    for axis in ("y", "l", "h"):
        bit = 1
        while bit < lax.axis_size(axis):
            total = total + flip(total, axis, bit)
            bit *= 2
    grad_bias = total[w_rows]
    piece = total[:w_rows]
    whole = jnp.zeros((HID, HID), F32)
    for d in range(nx):
        part = piece if d == 0 else shift(piece, "x", -d)
        whole = lax.dynamic_update_slice(whole, part, (((x + d) % nx) * w_rows, 0))
    across = flip(whole, "k", 1)
    grad_w_self = jnp.where(k == 0, whole, across)
    grad_w_neigh = jnp.where(k == 0, across, whole)

    local = jnp.concatenate([blocks[o] for o in range(ny)], axis=0)
    (msg,) = call(
        functools.partial(pick_kernel, slots),
        [((slots * TILE, HID), BF)],
        [SMEM, VMEM],
        other_idx,
        local,
    )
    half = sources // 2 * TILE
    keep, send = call(
        functools.partial(back_kernel, slots),
        [((half, HID), F32), ((half, HID), BF)],
        [SMEM, SMEM, SMEM, VMEM, VMEM, VMEM],
        src,
        own_idx,
        live,
        tiles,
        local,
        flip(msg, "l", 1),
        scratch=[pltpu.VMEM((sources * TILE, HID), F32), pltpu.VMEM((TILE, HID), BF)],
        flops=tile_flops,
    )
    group = nh * TILE
    pieces = call(
        back_cut_kernel,
        [((group, HID), F32)] + [((group, HID), BF)] * (nx - 1),
        [VMEM] * 2,
        keep,
        flip(send, "k", 1),
    )
    got = [pieces[0]] + [shift(pieces[d], "x", d) for d in range(1, nx)]
    last = call(
        functools.partial(back_gather_kernel, nh),
        [((TILE, HID), F32)] + [((TILE, HID), BF)] * (nh - 1),
        [VMEM] * nx,
        *got,
    )
    back_sum = last[0]
    if nh > 1:
        back_sum = back_sum + flip(last[1], "h", 1).astype(F32)
    grad_features = (self_back + back_sum).astype(BF)
    return hidden, grad_features, grad_w_self, grad_w_neigh, grad_bias


def on_mesh(mesh):
    row, col = ("h", "x", "k"), ("y", "l")
    nodes = P(row + col, None)
    in_specs = (
        nodes,
        P(row, col, None, None, None),
        P(row, col, None),
        P(row, col, None),
        P(row, col),
        P(row + col),
        P(),
        P(),
        P(),
        nodes,
    )
    out_specs = (nodes, nodes, P(), P(), P())
    return jax.shard_map(body, mesh=mesh, in_specs=in_specs, out_specs=out_specs, check_vma=False)


def solution(mesh):
    devices = mesh.devices.reshape(2, 4, 2, 8, 8)
    return on_mesh(Mesh(devices, ("h", "x", "k", "y", "l")))
```

time: 1660 us -> 327 us (0.20)
  waiting for transfers between devices: 1040 us -> 82.9 us
  blocking collectives: 565 us -> 0 us
  starting transfers between devices: 0.38 us -> 211 us
    all_gather x2 -> x0, waiting for transfers between devices: 539 us -> none  [the longest x1 442 us: body(): dest_block = lax.all_gather(scaled_grad, 'col', axis=0, tiled=True)]
    unnamed x1 -> x0, blocking collectives: 402 us -> none
    psum x1 -> x0, waiting for transfers between devices: 357 us -> none  [weight_totals(): return lax.psum((self_term, neigh_term, bias_term), ('row', 'col'))]
    ppermute x0 -> x46, starting transfers between devices: none -> 211 us  [the longest x20 129 us: flip(): return lax.ppermute(value, axis, [(i, i ^ bit) for i in range(n)])]
    psum x1 -> x0, blocking collectives: 163 us -> none  [weight_totals(): return lax.psum((self_term, neigh_term, bias_term), ('row', 'col'))]
    reduce_scatter x2 -> x0, waiting for transfers between devices: 148 us -> none  [the longest x1 117 us: body(): lax.psum_scatter(back_partial.astype(jnp.bfloat16), 'row', scatter_dimens...]
    ppermute x0 -> x46, waiting for transfers between devices: none -> 82.9 us  [the longest x20 54.1 us: flip(): return lax.ppermute(value, axis, [(i, i ^ bit) for i in range(n)])]
  transfers between devices with their start and end apart: 5 -> 46, of which waited for: 5 -> 27; matrix products, arithmetic and copies ran while one was open for 1% -> 2% of each run, Pallas kernels for 0% -> 3%
where the time goes in v1:
time: 327 us; the launch traced here: 323 us
  starting transfers between devices  211 us (65%)
  waiting for transfers between devices  82.9 us (25%)
  Pallas kernels  13.8 us (4%)
  local copies, waits for them, and re-layouts  9.84 us (3%)
    ppermute x20, starting transfers between devices, flip(): return lax.ppermute(value, axis, [(i, i ^ bit) for i in range(n)])  129 us
    ppermute x26, starting transfers between devices, shift(): return lax.ppermute(value, axis, [(i, (i + by) % n) for i in range(n)])  82.8 us
    ppermute x20, waiting for transfers between devices, flip(): return lax.ppermute(value, axis, [(i, i ^ bit) for i in range(n)])  54.1 us
    ppermute x26, waiting for transfers between devices, shift(): return lax.ppermute(value, axis, [(i, (i + by) % n) for i in range(n)])  28.8 us
    pallas_call x18, Pallas kernels, call(): pl.pallas_call(kernel, out_shape=shapes, in_specs=in_specs, out_specs=[VM...  13.8 us
  transfers between devices with their start and end apart: 46, of which 27 were waited for; matrix products, arithmetic and copies ran while one was open for 2% of the time, Pallas kernels for 3%

profile of v1, /device:TPU:1, one launch (start us, length us, event | category | flops | bytes accessed | tf_op | source)
XLA Modules:
  0.0 322.6 jit_solution(3540551836054605667)
XLA Ops:
  0.6 20.0 %collective-permute-start.1 = (bf16[128,256]{1,0:T(8,128)(2,1)}, bf16[128,256]{1,0:T(8,128)(2,1)S(1)}, u32[]{:S(2)}, u32[]{:S(2)}) collective-permute-start(bf16[128,256]{1,0:T(8,128)(2,1)} %features.3), channel_id=1, source_target_pairs={{0,512},{512,0},{1,513},{513,1},{2,514},{514,2},{3,515},{515,3},{4... | collective-permute-start | bytes 196616 | tf_op jit(solution)/shard_map/ppermute | solution.py:261
  22.7 4.4 %collective-permute-start.2 = (bf16[256,256]{1,0:T(8,128)(2,1)S(1)}, bf16[256,256]{1,0:T(8,128)(2,1)S(1)}, u32[]{:S(2)}, u32[]{:S(2)}) collective-permute-start(bf16[256,256]{1,0:T(8,128)(2,1)S(1)} %get-tuple-element.101), channel_id=1, source_target_pairs={{0,384},{128,0},{256,128},{384,256},{1,385},{129,1},{257,129},{385... | collective-permute-start | bytes 393224 | tf_op jit(solution)/shard_map/ppermute | solution.py:265
  27.1 2.4 collective-permute-start.3
  29.6 2.5 collective-permute-start.4
  32.1 2.2 collective-permute-done.3
  34.4 2.1 collective-permute-done.4
  36.5 8.8 %collective-permute-start.5 = (bf16[1024,256]{1,0:T(8,128)(2,1)S(1)}, bf16[1024,256]{1,0:T(8,128)(2,1)S(1)}, u32[]{:S(2)}, u32[]{:S(2)}) collective-permute-start(bf16[1024,256]{1,0:T(8,128)(2,1)S(1)} %get-tuple-element.87), channel_id=1, source_target_pairs={{0,64},{64,0},{1,65},{65,1},{2,66},{66,2},{3,67},{67,3},{4,68},{68... | collective-permute-start | bytes 1572872 | tf_op jit(solution)/shard_map/ppermute | solution.py:261
  47.9 1.9 collective-permute-start.6
  49.9 3.4 %collective-permute-start = (s32[8,128]{1,0:T(8,128)S(1)}, s32[8,128]{1,0:T(8,128)S(1)}, u32[]{:S(2)}, u32[]{:S(2)}) collective-permute-start(s32[8,128]{1,0:T(8,128)S(1)} %scatter.4), channel_id=1, source_target_pairs={{0,1},{1,0},{2,3},{3,2},{4,5},{5,4},{6,7},{7,6},{8,9},{9,8},{10,11... | collective-permute-start | bytes 12296 | tf_op jit(solution)/shard_map/ppermute | solution.py:261
  53.3 12.7 %collective-permute-done = s32[8,128]{1,0:T(8,128)S(1)} collective-permute-done((s32[8,128]{1,0:T(8,128)S(1)}, s32[8,128]{1,0:T(8,128)S(1)}, u32[]{:S(2)}, u32[]{:S(2)}) %collective-permute-start) | collective-permute-done | bytes 4128 | tf_op jit(solution)/shard_map/ppermute | solution.py:261
  68.0 2.1 copy-done
  70.0 3.0 shard_map.139
  73.0 1.9 collective-permute-start.7
  74.9 4.6 %collective-permute-start.11 = (bf16[528,256]{1,0:T(8,128)(2,1)S(1)}, bf16[528,256]{1,0:T(8,128)(2,1)S(1)}, u32[]{:S(2)}, u32[]{:S(2)}) collective-permute-start(bf16[528,256]{1,0:T(8,128)(2,1)S(1)} %get-tuple-element.57), channel_id=1, source_target_pairs={{0,56},{8,0},{16,8},{24,16},{32,24},{40,32},{48,40},{56,48},{1,57}... | collective-permute-start | bytes 811016 | tf_op jit(solution)/shard_map/ppermute | solution.py:265
  79.5 3.7 %collective-permute-done.7.recv = bf16[528,256]{1,0:T(8,128)(2,1)S(1)} collective-permute-done((bf16[528,256]{1,0:T(8,128)(2,1)S(1)}, bf16[528,256]{1,0:T(8,128)(2,1)S(1)}, u32[]{:S(2)}, u32[]{:S(2)}) %collective-permute-start.7) | collective-permute-done | bytes 270368 | tf_op jit(solution)/shard_map/ppermute | solution.py:265
  83.3 1.9 collective-permute-start.8
  85.4 4.7 %collective-permute-start.12 = (bf16[528,256]{1,0:T(8,128)(2,1)S(1)}, bf16[528,256]{1,0:T(8,128)(2,1)S(1)}, u32[]{:S(2)}, u32[]{:S(2)}) collective-permute-start(bf16[528,256]{1,0:T(8,128)(2,1)S(1)} %shard_map.143), channel_id=1, source_target_pairs={{0,56},{8,0},{16,8},{24,16},{32,24},{40,32},{48,40},{56,48},{1,57}... | collective-permute-start | bytes 811016 | tf_op jit(solution)/shard_map/ppermute | solution.py:265
  90.1 2.5 collective-permute-done.8.recv
  92.7 1.9 collective-permute-start.9
  94.8 4.6 %collective-permute-start.13 = (bf16[528,256]{1,0:T(8,128)(2,1)S(1)}, bf16[528,256]{1,0:T(8,128)(2,1)S(1)}, u32[]{:S(2)}, u32[]{:S(2)}) collective-permute-start(bf16[528,256]{1,0:T(8,128)(2,1)S(1)} %shard_map.144), channel_id=1, source_target_pairs={{0,56},{8,0},{16,8},{24,16},{32,24},{40,32},{48,40},{56,48},{1,57}... | collective-permute-start | bytes 811016 | tf_op jit(solution)/shard_map/ppermute | solution.py:265
  101.2 1.9 collective-permute-start.10
  103.2 6.5 %collective-permute-done.10.refs_1_ = bf16[528,256]{1,0:T(8,128)(2,1)S(1)} collective-permute-done((bf16[528,256]{1,0:T(8,128)(2,1)S(1)}, bf16[528,256]{1,0:T(8,128)(2,1)S(1)}, u32[]{:S(2)}, u32[]{:S(2)}) %collective-permute-start.10) | collective-permute-done | bytes 270368 | tf_op jit(solution)/shard_map/ppermute | solution.py:265
  109.7 2.0 collective-permute-start.14
  111.8 5.3 %collective-permute-done.14.recv = bf16[272,256]{1,0:T(8,128)(2,1)S(1)} collective-permute-done((bf16[272,256]{1,0:T(8,128)(2,1)S(1)}, bf16[272,256]{1,0:T(8,128)(2,1)S(1)}, u32[]{:S(2)}, u32[]{:S(2)}) %collective-permute-start.14) | collective-permute-done | bytes 139296 | tf_op jit(solution)/shard_map/ppermute | solution.py:261
  117.1 6.1 %collective-permute-start.15 = (bf16[144,256]{1,0:T(8,128)(2,1)S(1)}, bf16[144,256]{1,0:T(8,128)(2,1)S(1)}, u32[]{:S(2)}, u32[]{:S(2)}) collective-permute-start(bf16[144,256]{1,0:T(8,128)(2,1)S(1)} %get-tuple-element.63), channel_id=1, source_target_pairs={{0,4},{1,5},{2,6},{3,7},{4,0},{5,1},{6,2},{7,3},{8,12},{9,13},{10,... | collective-permute-start | bytes 221192 | tf_op jit(solution)/shard_map/ppermute | solution.py:261
  123.2 3.7 %collective-permute-done.15.recv = bf16[144,256]{1,0:T(8,128)(2,1)S(1)} collective-permute-done((bf16[144,256]{1,0:T(8,128)(2,1)S(1)}, bf16[144,256]{1,0:T(8,128)(2,1)S(1)}, u32[]{:S(2)}, u32[]{:S(2)}) %collective-permute-start.15) | collective-permute-done | bytes 73760 | tf_op jit(solution)/shard_map/ppermute | solution.py:261
  127.9 5.3 %collective-permute-start.16 = (bf16[128,256]{1,0:T(8,128)(2,1)S(1)}, bf16[128,256]{1,0:T(8,128)(2,1)S(1)}, u32[]{:S(2)}, u32[]{:S(2)}) collective-permute-start(bf16[128,256]{1,0:T(8,128)(2,1)S(1)} %get-tuple-element.68), channel_id=1, source_target_pairs={{0,4},{1,5},{2,6},{3,7},{4,0},{5,1},{6,2},{7,3},{8,12},{9,13},{10,... | collective-permute-start | bytes 196616 | tf_op jit(solution)/shard_map/ppermute | solution.py:261
  133.2 4.3 %collective-permute-done.16 = bf16[128,256]{1,0:T(8,128)(2,1)S(1)} collective-permute-done((bf16[128,256]{1,0:T(8,128)(2,1)S(1)}, bf16[128,256]{1,0:T(8,128)(2,1)S(1)}, u32[]{:S(2)}, u32[]{:S(2)}) %collective-permute-start.16) | collective-permute-done | bytes 65568 | tf_op jit(solution)/shard_map/ppermute | solution.py:261
  137.5 3.7 %collective-permute-start.17 = (bf16[256,256]{1,0:T(8,128)(2,1)S(1)}, bf16[256,256]{1,0:T(8,128)(2,1)S(1)}, u32[]{:S(2)}, u32[]{:S(2)}) collective-permute-start(bf16[256,256]{1,0:T(8,128)(2,1)S(1)} %pad_maximum_fusion), channel_id=1, source_target_pairs={{0,2},{1,3},{2,0},{3,1},{4,6},{5,7},{6,4},{7,5},{8,10},{9,11},{10,... | collective-permute-start | bytes 393224 | tf_op jit(solution)/shard_map/ppermute | solution.py:261
  141.3 5.4 %collective-permute-done.17 = bf16[256,256]{1,0:T(8,128)(2,1)S(1)} collective-permute-done((bf16[256,256]{1,0:T(8,128)(2,1)S(1)}, bf16[256,256]{1,0:T(8,128)(2,1)S(1)}, u32[]{:S(2)}, u32[]{:S(2)}) %collective-permute-start.17) | collective-permute-done | bytes 131104 | tf_op jit(solution)/shard_map/ppermute | solution.py:261
  146.8 1.9 collective-permute-start.21
  148.7 4.6 %collective-permute-start.18 = (bf16[512,256]{1,0:T(8,128)(2,1)S(1)}, bf16[512,256]{1,0:T(8,128)(2,1)S(1)}, u32[]{:S(2)}, u32[]{:S(2)}) collective-permute-start(bf16[512,256]{1,0:T(8,128)(2,1)S(1)} %get-tuple-element.85), channel_id=1, source_target_pairs={{0,56},{8,0},{16,8},{24,16},{32,24},{40,32},{48,40},{56,48},{1,57}... | collective-permute-start | bytes 786440 | tf_op jit(solution)/shard_map/ppermute | solution.py:265
  155.1 1.9 collective-permute-start.22
  158.5 13.7 %collective-permute-start.31 = (f32[264,256]{1,0:T(8,128)S(1)}, f32[264,256]{1,0:T(8,128)S(1)}, u32[]{:S(2)}, u32[]{:S(2)}) collective-permute-start(f32[264,256]{1,0:T(8,128)S(1)} %get-tuple-element.78), channel_id=1, source_target_pairs={{0,64},{64,0},{1,65},{65,1},{2,66},{66,2},{3,67},{67,3},{4,68},{68... | collective-permute-start | bytes 811016 | tf_op jit(solution)/shard_map/ppermute | solution.py:261
  172.3 4.9 %collective-permute-start.19 = (bf16[512,256]{1,0:T(8,128)(2,1)S(1)}, bf16[512,256]{1,0:T(8,128)(2,1)S(1)}, u32[]{:S(2)}, u32[]{:S(2)}) collective-permute-start(bf16[512,256]{1,0:T(8,128)(2,1)S(1)} %collective-permute-done.18), channel_id=1, source_target_pairs={{0,56},{8,0},{16,8},{24,16},{32,24},{40,32},{48,40},{56,48},{1,57}... | collective-permute-start | bytes 786440 | tf_op jit(solution)/shard_map/ppermute | solution.py:265
  177.1 1.9 collective-permute-start.23
  179.7 1.9 collective-permute-start.32
  181.6 3.2 collective-permute-start.33
  184.8 3.3 %collective-permute-start.34 = (f32[72,256]{1,0:T(8,128)S(1)}, f32[72,256]{1,0:T(8,128)S(1)}, u32[]{:S(2)}, u32[]{:S(2)}) collective-permute-start(f32[72,256]{1,0:T(8,128)S(1)} %get-tuple-element.82), channel_id=1, source_target_pairs={{0,384},{128,0},{256,128},{384,256},{1,385},{129,1},{257,129},{385... | collective-permute-start | bytes 221192 | tf_op jit(solution)/shard_map/ppermute | solution.py:265
  190.4 1.9 collective-permute-start.35
  192.4 4.7 %collective-permute-start.20 = (bf16[512,256]{1,0:T(8,128)(2,1)S(1)}, bf16[512,256]{1,0:T(8,128)(2,1)S(1)}, u32[]{:S(2)}, u32[]{:S(2)}) collective-permute-start(bf16[512,256]{1,0:T(8,128)(2,1)S(1)} %collective-permute-done.19), channel_id=1, source_target_pairs={{0,56},{8,0},{16,8},{24,16},{32,24},{40,32},{48,40},{56,48},{1,57}... | collective-permute-start | bytes 786440 | tf_op jit(solution)/shard_map/ppermute | solution.py:265
  197.1 4.4 %collective-permute-start.36 = (f32[72,256]{1,0:T(8,128)S(1)}, f32[72,256]{1,0:T(8,128)S(1)}, u32[]{:S(2)}, u32[]{:S(2)}) collective-permute-start(f32[72,256]{1,0:T(8,128)S(1)} %add.124), channel_id=1, source_target_pairs={{0,16},{8,24},{16,0},{24,8},{32,48},{40,56},{48,32},{56,40},{1,17}... | collective-permute-start | bytes 221192 | tf_op jit(solution)/shard_map/ppermute | solution.py:261
  201.6 3.4 %collective-permute-start.24 = (bf16[512,256]{1,0:T(8,128)(2,1)S(1)}, bf16[512,256]{1,0:T(8,128)(2,1)S(1)}, u32[]{:S(2)}, u32[]{:S(2)}) collective-permute-start(bf16[512,256]{1,0:T(8,128)(2,1)S(1)} %collective-permute-done.23), channel_id=1, source_target_pairs={{0,8},{8,16},{16,24},{24,32},{32,40},{40,48},{48,56},{56,0},{1,9},... | collective-permute-start | bytes 786440 | tf_op jit(solution)/shard_map/ppermute | solution.py:265
  206.1 4.5 %collective-permute-start.37 = (f32[72,256]{1,0:T(8,128)S(1)}, f32[72,256]{1,0:T(8,128)S(1)}, u32[]{:S(2)}, u32[]{:S(2)}) collective-permute-start(f32[72,256]{1,0:T(8,128)S(1)} %add.125), channel_id=1, source_target_pairs={{0,32},{8,40},{16,48},{24,56},{32,0},{40,8},{48,16},{56,24},{1,33}... | collective-permute-start | bytes 221192 | tf_op jit(solution)/shard_map/ppermute | solution.py:261
  212.2 1.9 collective-permute-start.25
  215.8 1.9 collective-permute-start.38
  217.7 10.4 %collective-permute-done.38 = f32[72,256]{1,0:T(8,128)S(1)} collective-permute-done((f32[72,256]{1,0:T(8,128)S(1)}, f32[72,256]{1,0:T(8,128)S(1)}, u32[]{:S(2)}, u32[]{:S(2)}) %collective-permute-start.38) | collective-permute-done | bytes 73760 | tf_op jit(solution)/shard_map/ppermute | solution.py:261
  228.2 3.9 %collective-permute-start.39 = (f32[72,256]{1,0:T(8,128)S(1)}, f32[72,256]{1,0:T(8,128)S(1)}, u32[]{:S(2)}, u32[]{:S(2)}) collective-permute-start(f32[72,256]{1,0:T(8,128)S(1)} %add.127), channel_id=1, source_target_pairs={{0,2},{1,3},{2,0},{3,1},{4,6},{5,7},{6,4},{7,5},{8,10},{9,11},{10,... | collective-permute-start | bytes 221192 | tf_op jit(solution)/shard_map/ppermute | solution.py:261
  232.1 2.1 collective-permute-done.39
  234.2 8.1 %collective-permute-start.40 = (f32[72,256]{1,0:T(8,128)S(1)}, f32[72,256]{1,0:T(8,128)S(1)}, u32[]{:S(2)}, u32[]{:S(2)}) collective-permute-start(f32[72,256]{1,0:T(8,128)S(1)} %add.128), channel_id=1, source_target_pairs={{0,4},{1,5},{2,6},{3,7},{4,0},{5,1},{6,2},{7,3},{8,12},{9,13},{10,... | collective-permute-start | bytes 221192 | tf_op jit(solution)/shard_map/ppermute | solution.py:261
  242.3 2.5 collective-permute-done.40
  244.8 12.2 %collective-permute-start.41 = (f32[72,256]{1,0:T(8,128)S(1)}, f32[72,256]{1,0:T(8,128)S(1)}, u32[]{:S(2)}, u32[]{:S(2)}) collective-permute-start(f32[72,256]{1,0:T(8,128)S(1)} %add.129), channel_id=1, source_target_pairs={{0,512},{512,0},{1,513},{513,1},{2,514},{514,2},{3,515},{515,3},{4... | collective-permute-start | bytes 221192 | tf_op jit(solution)/shard_map/ppermute | solution.py:261
  257.1 2.0 collective-permute-done.41
  259.8 6.5 %collective-permute-start.42 = (f32[64,256]{1,0:T(8,128)}, f32[64,256]{1,0:T(8,128)}, u32[]{:S(2)}, u32[]{:S(2)}) collective-permute-start(f32[64,256]{1,0:T(8,128)} %get-tuple-element.93), channel_id=1, source_target_pairs={{0,384},{128,0},{256,128},{384,256},{1,385},{129,1},{257,129},{385... | collective-permute-start | bytes 196616 | tf_op jit(solution)/shard_map/ppermute | solution.py:265
  268.3 3.5 %shard_map.150 = (f32[1024,256]{1,0:T(8,128)S(1)}, bf16[1024,256]{1,0:T(8,128)(2,1)}) custom-call(s32[10]{0:T(128)S(1)} %fusion.5.src, s32[10]{0:T(128)S(1)} %and_select_fusion.2.idx, s32[10]{0:T(128)S(1)} %compare_convert_fusion.live, bf16[10,128,128]{2,1,0:T(8,128)(2,1)S(1)} %get-tuple-element.50.tiles, ...), custom_call_target="tpu_custom_call" | custom-call | flops 83886080 | bytes 4653176 | tf_op jit(solution)/shard_map/pallas_call | solution.py:25
  271.7 10.6 %collective-permute-start.26 = (bf16[1024,256]{1,0:T(8,128)(2,1)}, bf16[1024,256]{1,0:T(8,128)(2,1)S(1)}, u32[]{:S(2)}, u32[]{:S(2)}) collective-permute-start(bf16[1024,256]{1,0:T(8,128)(2,1)} %get-tuple-element.70), channel_id=1, source_target_pairs={{0,64},{64,0},{1,65},{65,1},{2,66},{66,2},{3,67},{67,3},{4,68},{68... | collective-permute-start | bytes 1572872 | tf_op jit(solution)/shard_map/ppermute | solution.py:261
  282.3 1.9 collective-permute-start.43
  284.3 2.2 collective-permute-start.44
  291.9 2.8 collective-permute-start.45
  294.9 1.9 collective-permute-start.27
  296.8 3.7 %collective-permute-start.28 = (bf16[256,256]{1,0:T(8,128)(2,1)S(1)}, bf16[256,256]{1,0:T(8,128)(2,1)S(1)}, u32[]{:S(2)}, u32[]{:S(2)}) collective-permute-start(bf16[256,256]{1,0:T(8,128)(2,1)S(1)} %get-tuple-element.73), channel_id=1, source_target_pairs={{0,256},{128,384},{256,0},{384,128},{1,257},{129,385},{257,1},{385... | collective-permute-start | bytes 393224 | tf_op jit(solution)/shard_map/ppermute | solution.py:265
  300.5 4.0 %collective-permute-start.29 = (bf16[256,256]{1,0:T(8,128)(2,1)S(1)}, bf16[256,256]{1,0:T(8,128)(2,1)S(1)}, u32[]{:S(2)}, u32[]{:S(2)}) collective-permute-start(bf16[256,256]{1,0:T(8,128)(2,1)S(1)} %get-tuple-element.74), channel_id=1, source_target_pairs={{0,384},{128,0},{256,128},{384,256},{1,385},{129,1},{257,129},{385... | collective-permute-start | bytes 393224 | tf_op jit(solution)/shard_map/ppermute | solution.py:265
  305.9 2.2 collective-permute-done.29.refs_3_
  308.2 11.5 %collective-permute-start.30 = (bf16[128,256]{1,0:T(8,128)(2,1)S(1)}, bf16[128,256]{1,0:T(8,128)(2,1)S(1)}, u32[]{:S(2)}, u32[]{:S(2)}) collective-permute-start(bf16[128,256]{1,0:T(8,128)(2,1)S(1)} %get-tuple-element.76), channel_id=1, source_target_pairs={{0,512},{512,0},{1,513},{513,1},{2,514},{514,2},{3,515},{515,3},{4... | collective-permute-start | bytes 196616 | tf_op jit(solution)/shard_map/ppermute | solution.py:261
  (115 shorter events, 32.6 us)
Async XLA Ops:
  0.6 46.3 %copy-start.1 = (s32[1,1,10,128,128]{4,3,2,1,0:T(8,128)S(1)}, s32[1,1,10,128,128]{4,3,2,1,0:T(8,128)}, u32[]{:S(2)}) copy-start(s32[1,1,10,128,128]{4,3,2,1,0:T(8,128)} %param.13) | copy-start | bytes 1966084
  0.6 22.1 %collective-permute-start.1 = (bf16[128,256]{1,0:T(8,128)(2,1)}, bf16[128,256]{1,0:T(8,128)(2,1)S(1)}, u32[]{:S(2)}, u32[]{:S(2)}) collective-permute-start(bf16[128,256]{1,0:T(8,128)(2,1)} %features.3), channel_id=1, source_target_pairs={{0,512},{512,0},{1,513},{513,1},{2,514},{514,2},{3,515},{515,3},{4... | collective-permute-start | bytes 196616 | tf_op jit(solution)/shard_map/ppermute | solution.py:261
  22.7 27.1 %copy-start.14 = (s32[1,1,10]{2,1,0:T(1,128)S(1)}, s32[1,1,10]{2,1,0:T(1,128)}, u32[]{:S(2)}) copy-start(s32[1,1,10]{2,1,0:T(1,128)} %param.14) | copy-start | bytes 124
  22.7 9.4 %collective-permute-start.2 = (bf16[256,256]{1,0:T(8,128)(2,1)S(1)}, bf16[256,256]{1,0:T(8,128)(2,1)S(1)}, u32[]{:S(2)}, u32[]{:S(2)}) collective-permute-start(bf16[256,256]{1,0:T(8,128)(2,1)S(1)} %get-tuple-element.101), channel_id=1, source_target_pairs={{0,384},{128,0},{256,128},{384,256},{1,385},{129,1},{257,129},{385... | collective-permute-start | bytes 393224 | tf_op jit(solution)/shard_map/ppermute | solution.py:265
  27.1 7.2 %collective-permute-start.3 = (bf16[256,256]{1,0:T(8,128)(2,1)S(1)}, bf16[256,256]{1,0:T(8,128)(2,1)S(1)}, u32[]{:S(2)}, u32[]{:S(2)}) collective-permute-start(bf16[256,256]{1,0:T(8,128)(2,1)S(1)} %get-tuple-element.101), channel_id=1, source_target_pairs={{0,256},{128,384},{256,0},{384,128},{1,257},{129,385},{257,1},{385... | collective-permute-start | bytes 393224 | tf_op jit(solution)/shard_map/ppermute | solution.py:265
  29.6 6.9 %collective-permute-start.4 = (bf16[256,256]{1,0:T(8,128)(2,1)S(1)}, bf16[256,256]{1,0:T(8,128)(2,1)S(1)}, u32[]{:S(2)}, u32[]{:S(2)}) collective-permute-start(bf16[256,256]{1,0:T(8,128)(2,1)S(1)} %get-tuple-element.101), channel_id=1, source_target_pairs={{0,128},{128,256},{256,384},{384,0},{1,129},{129,257},{257,385},{3... | collective-permute-start | bytes 393224 | tf_op jit(solution)/shard_map/ppermute | solution.py:265
  36.5 10.4 %collective-permute-start.5 = (bf16[1024,256]{1,0:T(8,128)(2,1)S(1)}, bf16[1024,256]{1,0:T(8,128)(2,1)S(1)}, u32[]{:S(2)}, u32[]{:S(2)}) collective-permute-start(bf16[1024,256]{1,0:T(8,128)(2,1)S(1)} %get-tuple-element.87), channel_id=1, source_target_pairs={{0,64},{64,0},{1,65},{65,1},{2,66},{66,2},{3,67},{67,3},{4,68},{68... | collective-permute-start | bytes 1572872 | tf_op jit(solution)/shard_map/ppermute | solution.py:261
  47.9 22.1 %collective-permute-start.6 = (bf16[1296,256]{1,0:T(8,128)(2,1)S(1)}, bf16[1296,256]{1,0:T(8,128)(2,1)S(1)}, u32[]{:S(2)}, u32[]{:S(2)}) collective-permute-start(bf16[1296,256]{1,0:T(8,128)(2,1)S(1)} %get-tuple-element.51), channel_id=1, source_target_pairs={{0,1},{1,0},{2,3},{3,2},{4,5},{5,4},{6,7},{7,6},{8,9},{9,8},{10,11... | collective-permute-start | bytes 1990664 | tf_op jit(solution)/shard_map/ppermute | solution.py:261
  49.9 16.1 %collective-permute-start = (s32[8,128]{1,0:T(8,128)S(1)}, s32[8,128]{1,0:T(8,128)S(1)}, u32[]{:S(2)}, u32[]{:S(2)}) collective-permute-start(s32[8,128]{1,0:T(8,128)S(1)} %scatter.4), channel_id=1, source_target_pairs={{0,1},{1,0},{2,3},{3,2},{4,5},{5,4},{6,7},{7,6},{8,9},{9,8},{10,11... | collective-permute-start | bytes 12296 | tf_op jit(solution)/shard_map/ppermute | solution.py:261
  68.0 2.1 copy-start
  73.0 10.3 %collective-permute-start.7 = (bf16[528,256]{1,0:T(8,128)(2,1)S(1)}, bf16[528,256]{1,0:T(8,128)(2,1)S(1)}, u32[]{:S(2)}, u32[]{:S(2)}) collective-permute-start(bf16[528,256]{1,0:T(8,128)(2,1)S(1)} %get-tuple-element.53), channel_id=1, source_target_pairs={{0,8},{8,16},{16,24},{24,32},{32,40},{40,48},{48,56},{56,0},{1,9},... | collective-permute-start | bytes 811016 | tf_op jit(solution)/shard_map/ppermute | solution.py:265
  74.9 10.3 %collective-permute-start.11 = (bf16[528,256]{1,0:T(8,128)(2,1)S(1)}, bf16[528,256]{1,0:T(8,128)(2,1)S(1)}, u32[]{:S(2)}, u32[]{:S(2)}) collective-permute-start(bf16[528,256]{1,0:T(8,128)(2,1)S(1)} %get-tuple-element.57), channel_id=1, source_target_pairs={{0,56},{8,0},{16,8},{24,16},{32,24},{40,32},{48,40},{56,48},{1,57}... | collective-permute-start | bytes 811016 | tf_op jit(solution)/shard_map/ppermute | solution.py:265
  83.3 9.3 %collective-permute-start.8 = (bf16[528,256]{1,0:T(8,128)(2,1)S(1)}, bf16[528,256]{1,0:T(8,128)(2,1)S(1)}, u32[]{:S(2)}, u32[]{:S(2)}) collective-permute-start(bf16[528,256]{1,0:T(8,128)(2,1)S(1)} %shard_map.140), channel_id=1, source_target_pairs={{0,8},{8,16},{16,24},{24,32},{32,40},{40,48},{48,56},{56,0},{1,9},... | collective-permute-start | bytes 811016 | tf_op jit(solution)/shard_map/ppermute | solution.py:265
  85.3 41.6 %copy-start.4 = (bf16[128,256]{1,0:T(8,128)(2,1)S(1)}, bf16[128,256]{1,0:T(8,128)(2,1)}, u32[]{:S(2)}) copy-start(bf16[128,256]{1,0:T(8,128)(2,1)} %features.3) | copy-start | bytes 196612
  85.3 41.6 %copy-start.5 = (bf16[256,256]{1,0:T(8,128)(2,1)S(1)}, bf16[256,256]{1,0:T(8,128)(2,1)}, u32[]{:S(2)}) copy-start(bf16[256,256]{1,0:T(8,128)(2,1)} %w_self.3) | copy-start | bytes 393220
  85.3 41.6 %copy-start.8 = (bf16[256,256]{1,0:T(8,128)(2,1)S(1)}, bf16[256,256]{1,0:T(8,128)(2,1)}, u32[]{:S(2)}) copy-start(bf16[256,256]{1,0:T(8,128)(2,1)} %w_neigh.1) | copy-start | bytes 393220
  85.3 41.6 %copy-start.9 = (bf16[128,256]{1,0:T(8,128)(2,1)S(1)}, bf16[128,256]{1,0:T(8,128)(2,1)}, u32[]{:S(2)}) copy-start(bf16[128,256]{1,0:T(8,128)(2,1)} %grad_out.1) | copy-start | bytes 196612
  85.3 41.6 %copy-start.10 = (f32[256]{0:T(256)S(1)}, f32[256]{0:T(256)}, u32[]{:S(2)}) copy-start(f32[256]{0:T(256)} %param.20) | copy-start | bytes 3076
  85.3 41.6 %copy-start.11 = (s32[128]{0:T(128)S(1)}, s32[128]{0:T(128)}, u32[]{:S(2)}) copy-start(s32[128]{0:T(128)} %param.17) | copy-start | bytes 1540
  85.4 9.2 %collective-permute-start.12 = (bf16[528,256]{1,0:T(8,128)(2,1)S(1)}, bf16[528,256]{1,0:T(8,128)(2,1)S(1)}, u32[]{:S(2)}, u32[]{:S(2)}) collective-permute-start(bf16[528,256]{1,0:T(8,128)(2,1)S(1)} %shard_map.143), channel_id=1, source_target_pairs={{0,56},{8,0},{16,8},{24,16},{32,24},{40,32},{48,40},{56,48},{1,57}... | collective-permute-start | bytes 811016 | tf_op jit(solution)/shard_map/ppermute | solution.py:265
  92.7 8.4 %collective-permute-start.9 = (bf16[528,256]{1,0:T(8,128)(2,1)S(1)}, bf16[528,256]{1,0:T(8,128)(2,1)S(1)}, u32[]{:S(2)}, u32[]{:S(2)}) collective-permute-start(bf16[528,256]{1,0:T(8,128)(2,1)S(1)} %shard_map.141), channel_id=1, source_target_pairs={{0,8},{8,16},{16,24},{24,32},{32,40},{40,48},{48,56},{56,0},{1,9},... | collective-permute-start | bytes 811016 | tf_op jit(solution)/shard_map/ppermute | solution.py:265
  94.8 8.4 %collective-permute-start.13 = (bf16[528,256]{1,0:T(8,128)(2,1)S(1)}, bf16[528,256]{1,0:T(8,128)(2,1)S(1)}, u32[]{:S(2)}, u32[]{:S(2)}) collective-permute-start(bf16[528,256]{1,0:T(8,128)(2,1)S(1)} %shard_map.144), channel_id=1, source_target_pairs={{0,56},{8,0},{16,8},{24,16},{32,24},{40,32},{48,40},{56,48},{1,57}... | collective-permute-start | bytes 811016 | tf_op jit(solution)/shard_map/ppermute | solution.py:265
  101.2 8.4 %collective-permute-start.10 = (bf16[528,256]{1,0:T(8,128)(2,1)S(1)}, bf16[528,256]{1,0:T(8,128)(2,1)S(1)}, u32[]{:S(2)}, u32[]{:S(2)}) collective-permute-start(bf16[528,256]{1,0:T(8,128)(2,1)S(1)} %shard_map.142), channel_id=1, source_target_pairs={{0,8},{8,16},{16,24},{24,32},{32,40},{40,48},{48,56},{56,0},{1,9},... | collective-permute-start | bytes 811016 | tf_op jit(solution)/shard_map/ppermute | solution.py:265
  109.7 7.3 %collective-permute-start.14 = (bf16[272,256]{1,0:T(8,128)(2,1)S(1)}, bf16[272,256]{1,0:T(8,128)(2,1)S(1)}, u32[]{:S(2)}, u32[]{:S(2)}) collective-permute-start(bf16[272,256]{1,0:T(8,128)(2,1)S(1)} %get-tuple-element.61), channel_id=1, source_target_pairs={{0,2},{1,3},{2,0},{3,1},{4,6},{5,7},{6,4},{7,5},{8,10},{9,11},{10,... | collective-permute-start | bytes 417800 | tf_op jit(solution)/shard_map/ppermute | solution.py:261
  117.1 9.8 %collective-permute-start.15 = (bf16[144,256]{1,0:T(8,128)(2,1)S(1)}, bf16[144,256]{1,0:T(8,128)(2,1)S(1)}, u32[]{:S(2)}, u32[]{:S(2)}) collective-permute-start(bf16[144,256]{1,0:T(8,128)(2,1)S(1)} %get-tuple-element.63), channel_id=1, source_target_pairs={{0,4},{1,5},{2,6},{3,7},{4,0},{5,1},{6,2},{7,3},{8,12},{9,13},{10,... | collective-permute-start | bytes 221192 | tf_op jit(solution)/shard_map/ppermute | solution.py:261
  127.9 9.6 %collective-permute-start.16 = (bf16[128,256]{1,0:T(8,128)(2,1)S(1)}, bf16[128,256]{1,0:T(8,128)(2,1)S(1)}, u32[]{:S(2)}, u32[]{:S(2)}) collective-permute-start(bf16[128,256]{1,0:T(8,128)(2,1)S(1)} %get-tuple-element.68), channel_id=1, source_target_pairs={{0,4},{1,5},{2,6},{3,7},{4,0},{5,1},{6,2},{7,3},{8,12},{9,13},{10,... | collective-permute-start | bytes 196616 | tf_op jit(solution)/shard_map/ppermute | solution.py:261
  137.5 9.2 %collective-permute-start.17 = (bf16[256,256]{1,0:T(8,128)(2,1)S(1)}, bf16[256,256]{1,0:T(8,128)(2,1)S(1)}, u32[]{:S(2)}, u32[]{:S(2)}) collective-permute-start(bf16[256,256]{1,0:T(8,128)(2,1)S(1)} %pad_maximum_fusion), channel_id=1, source_target_pairs={{0,2},{1,3},{2,0},{3,1},{4,6},{5,7},{6,4},{7,5},{8,10},{9,11},{10,... | collective-permute-start | bytes 393224 | tf_op jit(solution)/shard_map/ppermute | solution.py:261
  146.8 8.3 %collective-permute-start.21 = (bf16[512,256]{1,0:T(8,128)(2,1)S(1)}, bf16[512,256]{1,0:T(8,128)(2,1)S(1)}, u32[]{:S(2)}, u32[]{:S(2)}) collective-permute-start(bf16[512,256]{1,0:T(8,128)(2,1)S(1)} %get-tuple-element.85), channel_id=1, source_target_pairs={{0,8},{8,16},{16,24},{24,32},{32,40},{40,48},{48,56},{56,0},{1,9},... | collective-permute-start | bytes 786440 | tf_op jit(solution)/shard_map/ppermute | solution.py:265
  148.7 23.6 %collective-permute-start.18 = (bf16[512,256]{1,0:T(8,128)(2,1)S(1)}, bf16[512,256]{1,0:T(8,128)(2,1)S(1)}, u32[]{:S(2)}, u32[]{:S(2)}) collective-permute-start(bf16[512,256]{1,0:T(8,128)(2,1)S(1)} %get-tuple-element.85), channel_id=1, source_target_pairs={{0,56},{8,0},{16,8},{24,16},{32,24},{40,32},{48,40},{56,48},{1,57}... | collective-permute-start | bytes 786440 | tf_op jit(solution)/shard_map/ppermute | solution.py:265
  155.1 22.1 %collective-permute-start.22 = (bf16[512,256]{1,0:T(8,128)(2,1)S(1)}, bf16[512,256]{1,0:T(8,128)(2,1)S(1)}, u32[]{:S(2)}, u32[]{:S(2)}) collective-permute-start(bf16[512,256]{1,0:T(8,128)(2,1)S(1)} %collective-permute-done.21), channel_id=1, source_target_pairs={{0,8},{8,16},{16,24},{24,32},{32,40},{40,48},{48,56},{56,0},{1,9},... | collective-permute-start | bytes 786440 | tf_op jit(solution)/shard_map/ppermute | solution.py:265
  157.9 0.7 copy-start.6
  158.5 20.5 %collective-permute-start.31 = (f32[264,256]{1,0:T(8,128)S(1)}, f32[264,256]{1,0:T(8,128)S(1)}, u32[]{:S(2)}, u32[]{:S(2)}) collective-permute-start(f32[264,256]{1,0:T(8,128)S(1)} %get-tuple-element.78), channel_id=1, source_target_pairs={{0,64},{64,0},{1,65},{65,1},{2,66},{66,2},{3,67},{67,3},{4,68},{68... | collective-permute-start | bytes 811016 | tf_op jit(solution)/shard_map/ppermute | solution.py:261
  172.3 20.1 %collective-permute-start.19 = (bf16[512,256]{1,0:T(8,128)(2,1)S(1)}, bf16[512,256]{1,0:T(8,128)(2,1)S(1)}, u32[]{:S(2)}, u32[]{:S(2)}) collective-permute-start(bf16[512,256]{1,0:T(8,128)(2,1)S(1)} %collective-permute-done.18), channel_id=1, source_target_pairs={{0,56},{8,0},{16,8},{24,16},{32,24},{40,32},{48,40},{56,48},{1,57}... | collective-permute-start | bytes 786440 | tf_op jit(solution)/shard_map/ppermute | solution.py:265
  177.1 24.4 %collective-permute-start.23 = (bf16[512,256]{1,0:T(8,128)(2,1)S(1)}, bf16[512,256]{1,0:T(8,128)(2,1)S(1)}, u32[]{:S(2)}, u32[]{:S(2)}) collective-permute-start(bf16[512,256]{1,0:T(8,128)(2,1)S(1)} %collective-permute-done.22), channel_id=1, source_target_pairs={{0,8},{8,16},{16,24},{24,32},{32,40},{40,48},{48,56},{56,0},{1,9},... | collective-permute-start | bytes 786440 | tf_op jit(solution)/shard_map/ppermute | solution.py:265
  179.7 8.4 %collective-permute-start.32 = (f32[72,256]{1,0:T(8,128)S(1)}, f32[72,256]{1,0:T(8,128)S(1)}, u32[]{:S(2)}, u32[]{:S(2)}) collective-permute-start(f32[72,256]{1,0:T(8,128)S(1)} %get-tuple-element.80), channel_id=1, source_target_pairs={{0,128},{128,256},{256,384},{384,0},{1,129},{129,257},{257,385},{3... | collective-permute-start | bytes 221192 | tf_op jit(solution)/shard_map/ppermute | solution.py:265
  181.6 7.0 %collective-permute-start.33 = (f32[72,256]{1,0:T(8,128)S(1)}, f32[72,256]{1,0:T(8,128)S(1)}, u32[]{:S(2)}, u32[]{:S(2)}) collective-permute-start(f32[72,256]{1,0:T(8,128)S(1)} %get-tuple-element.81), channel_id=1, source_target_pairs={{0,256},{128,384},{256,0},{384,128},{1,257},{129,385},{257,1},{385... | collective-permute-start | bytes 221192 | tf_op jit(solution)/shard_map/ppermute | solution.py:265
  184.8 5.6 %collective-permute-start.34 = (f32[72,256]{1,0:T(8,128)S(1)}, f32[72,256]{1,0:T(8,128)S(1)}, u32[]{:S(2)}, u32[]{:S(2)}) collective-permute-start(f32[72,256]{1,0:T(8,128)S(1)} %get-tuple-element.82), channel_id=1, source_target_pairs={{0,384},{128,0},{256,128},{384,256},{1,385},{129,1},{257,129},{385... | collective-permute-start | bytes 221192 | tf_op jit(solution)/shard_map/ppermute | solution.py:265
  190.4 6.7 %collective-permute-start.35 = (f32[72,256]{1,0:T(8,128)S(1)}, f32[72,256]{1,0:T(8,128)S(1)}, u32[]{:S(2)}, u32[]{:S(2)}) collective-permute-start(f32[72,256]{1,0:T(8,128)S(1)} %shard_map.154), channel_id=1, source_target_pairs={{0,8},{8,0},{16,24},{24,16},{32,40},{40,32},{48,56},{56,48},{1,9},... | collective-permute-start | bytes 221192 | tf_op jit(solution)/shard_map/ppermute | solution.py:261
  192.4 18.2 %collective-permute-start.20 = (bf16[512,256]{1,0:T(8,128)(2,1)S(1)}, bf16[512,256]{1,0:T(8,128)(2,1)S(1)}, u32[]{:S(2)}, u32[]{:S(2)}) collective-permute-start(bf16[512,256]{1,0:T(8,128)(2,1)S(1)} %collective-permute-done.19), channel_id=1, source_target_pairs={{0,56},{8,0},{16,8},{24,16},{32,24},{40,32},{48,40},{56,48},{1,57}... | collective-permute-start | bytes 786440 | tf_op jit(solution)/shard_map/ppermute | solution.py:265
  197.1 8.9 %collective-permute-start.36 = (f32[72,256]{1,0:T(8,128)S(1)}, f32[72,256]{1,0:T(8,128)S(1)}, u32[]{:S(2)}, u32[]{:S(2)}) collective-permute-start(f32[72,256]{1,0:T(8,128)S(1)} %add.124), channel_id=1, source_target_pairs={{0,16},{8,24},{16,0},{24,8},{32,48},{40,56},{48,32},{56,40},{1,17}... | collective-permute-start | bytes 221192 | tf_op jit(solution)/shard_map/ppermute | solution.py:261
  201.6 9.1 %collective-permute-start.24 = (bf16[512,256]{1,0:T(8,128)(2,1)S(1)}, bf16[512,256]{1,0:T(8,128)(2,1)S(1)}, u32[]{:S(2)}, u32[]{:S(2)}) collective-permute-start(bf16[512,256]{1,0:T(8,128)(2,1)S(1)} %collective-permute-done.23), channel_id=1, source_target_pairs={{0,8},{8,16},{16,24},{24,32},{32,40},{40,48},{48,56},{56,0},{1,9},... | collective-permute-start | bytes 786440 | tf_op jit(solution)/shard_map/ppermute | solution.py:265
  206.1 9.7 %collective-permute-start.37 = (f32[72,256]{1,0:T(8,128)S(1)}, f32[72,256]{1,0:T(8,128)S(1)}, u32[]{:S(2)}, u32[]{:S(2)}) collective-permute-start(f32[72,256]{1,0:T(8,128)S(1)} %add.125), channel_id=1, source_target_pairs={{0,32},{8,40},{16,48},{24,56},{32,0},{40,8},{48,16},{56,24},{1,33}... | collective-permute-start | bytes 221192 | tf_op jit(solution)/shard_map/ppermute | solution.py:261
  212.2 54.1 %collective-permute-start.25 = (bf16[1280,256]{1,0:T(8,128)(2,1)}, bf16[1280,256]{1,0:T(8,128)(2,1)S(1)}, u32[]{:S(2)}, u32[]{:S(2)}) collective-permute-start(bf16[1280,256]{1,0:T(8,128)(2,1)} %shard_map.149), channel_id=1, source_target_pairs={{0,1},{1,0},{2,3},{3,2},{4,5},{5,4},{6,7},{7,6},{8,9},{9,8},{10,11... | collective-permute-start | bytes 1966088 | tf_op jit(solution)/shard_map/ppermute | solution.py:261
  215.8 12.4 %collective-permute-start.38 = (f32[72,256]{1,0:T(8,128)S(1)}, f32[72,256]{1,0:T(8,128)S(1)}, u32[]{:S(2)}, u32[]{:S(2)}) collective-permute-start(f32[72,256]{1,0:T(8,128)S(1)} %add.126), channel_id=1, source_target_pairs={{0,1},{1,0},{2,3},{3,2},{4,5},{5,4},{6,7},{7,6},{8,9},{9,8},{10,11... | collective-permute-start | bytes 221192 | tf_op jit(solution)/shard_map/ppermute | solution.py:261
  228.2 6.0 %collective-permute-start.39 = (f32[72,256]{1,0:T(8,128)S(1)}, f32[72,256]{1,0:T(8,128)S(1)}, u32[]{:S(2)}, u32[]{:S(2)}) collective-permute-start(f32[72,256]{1,0:T(8,128)S(1)} %add.127), channel_id=1, source_target_pairs={{0,2},{1,3},{2,0},{3,1},{4,6},{5,7},{6,4},{7,5},{8,10},{9,11},{10,... | collective-permute-start | bytes 221192 | tf_op jit(solution)/shard_map/ppermute | solution.py:261
  234.2 10.6 %collective-permute-start.40 = (f32[72,256]{1,0:T(8,128)S(1)}, f32[72,256]{1,0:T(8,128)S(1)}, u32[]{:S(2)}, u32[]{:S(2)}) collective-permute-start(f32[72,256]{1,0:T(8,128)S(1)} %add.128), channel_id=1, source_target_pairs={{0,4},{1,5},{2,6},{3,7},{4,0},{5,1},{6,2},{7,3},{8,12},{9,13},{10,... | collective-permute-start | bytes 221192 | tf_op jit(solution)/shard_map/ppermute | solution.py:261
  244.8 14.3 %collective-permute-start.41 = (f32[72,256]{1,0:T(8,128)S(1)}, f32[72,256]{1,0:T(8,128)S(1)}, u32[]{:S(2)}, u32[]{:S(2)}) collective-permute-start(f32[72,256]{1,0:T(8,128)S(1)} %add.129), channel_id=1, source_target_pairs={{0,512},{512,0},{1,513},{513,1},{2,514},{514,2},{3,515},{515,3},{4... | collective-permute-start | bytes 221192 | tf_op jit(solution)/shard_map/ppermute | solution.py:261
  259.8 6.5 %copy-start.12 = (f32[256,256]{1,0:T(8,128)}, f32[256,256]{1,0:T(8,128)S(1)}, u32[]{:S(2)}) copy-start(f32[256,256]{1,0:T(8,128)S(1)} %get-tuple-element.94) | copy-start | bytes 786436
  259.8 26.7 %collective-permute-start.42 = (f32[64,256]{1,0:T(8,128)}, f32[64,256]{1,0:T(8,128)}, u32[]{:S(2)}, u32[]{:S(2)}) collective-permute-start(f32[64,256]{1,0:T(8,128)} %get-tuple-element.93), channel_id=1, source_target_pairs={{0,384},{128,0},{256,128},{384,256},{1,385},{129,1},{257,129},{385... | collective-permute-start | bytes 196616 | tf_op jit(solution)/shard_map/ppermute | solution.py:265
  266.3 0.9 copy-start.2
  267.2 1.1 copy-start.3
  271.7 50.3 %copy-start.7 = (f32[128,256]{1,0:T(8,128)S(1)}, f32[128,256]{1,0:T(8,128)}, u32[]{:S(2)}) copy-start(f32[128,256]{1,0:T(8,128)} %copy-done.6) | copy-start | bytes 393220
  271.7 23.0 %collective-permute-start.26 = (bf16[1024,256]{1,0:T(8,128)(2,1)}, bf16[1024,256]{1,0:T(8,128)(2,1)S(1)}, u32[]{:S(2)}, u32[]{:S(2)}) collective-permute-start(bf16[1024,256]{1,0:T(8,128)(2,1)} %get-tuple-element.70), channel_id=1, source_target_pairs={{0,64},{64,0},{1,65},{65,1},{2,66},{66,2},{3,67},{67,3},{4,68},{68... | collective-permute-start | bytes 1572872 | tf_op jit(solution)/shard_map/ppermute | solution.py:261
  282.3 7.3 %collective-permute-start.43 = (f32[64,256]{1,0:T(8,128)}, f32[64,256]{1,0:T(8,128)S(1)}, u32[]{:S(2)}, u32[]{:S(2)}) collective-permute-start(f32[64,256]{1,0:T(8,128)} %get-tuple-element.93), channel_id=1, source_target_pairs={{0,256},{128,384},{256,0},{384,128},{1,257},{129,385},{257,1},{385... | collective-permute-start | bytes 196616 | tf_op jit(solution)/shard_map/ppermute | solution.py:265
  284.3 7.0 %collective-permute-start.44 = (f32[64,256]{1,0:T(8,128)}, f32[64,256]{1,0:T(8,128)S(1)}, u32[]{:S(2)}, u32[]{:S(2)}) collective-permute-start(f32[64,256]{1,0:T(8,128)} %get-tuple-element.93), channel_id=1, source_target_pairs={{0,128},{128,256},{256,384},{384,0},{1,129},{129,257},{257,385},{3... | collective-permute-start | bytes 196616 | tf_op jit(solution)/shard_map/ppermute | solution.py:265
  291.9 27.8 %copy-start.13 = (f32[256,256]{1,0:T(8,128)S(1)}, f32[256,256]{1,0:T(8,128)}, u32[]{:S(2)}) copy-start(f32[256,256]{1,0:T(8,128)} %constant_dynamic-update-slice_fusion.26) | copy-start | bytes 786436
  291.9 27.8 %collective-permute-start.45 = (f32[256,256]{1,0:T(8,128)}, f32[256,256]{1,0:T(8,128)S(1)}, u32[]{:S(2)}, u32[]{:S(2)}) collective-permute-start(f32[256,256]{1,0:T(8,128)} %constant_dynamic-update-slice_fusion.26), channel_id=1, source_target_pairs={{0,64},{64,0},{1,65},{65,1},{2,66},{66,2},{3,67},{67,3},{4,68},{68... | collective-permute-start | bytes 786440 | tf_op jit(solution)/shard_map/ppermute | solution.py:261
  294.9 11.0 %collective-permute-start.27 = (bf16[256,256]{1,0:T(8,128)(2,1)S(1)}, bf16[256,256]{1,0:T(8,128)(2,1)S(1)}, u32[]{:S(2)}, u32[]{:S(2)}) collective-permute-start(bf16[256,256]{1,0:T(8,128)(2,1)S(1)} %get-tuple-element.72), channel_id=1, source_target_pairs={{0,128},{128,256},{256,384},{384,0},{1,129},{129,257},{257,385},{3... | collective-permute-start | bytes 393224 | tf_op jit(solution)/shard_map/ppermute | solution.py:265
  296.8 9.1 %collective-permute-start.28 = (bf16[256,256]{1,0:T(8,128)(2,1)S(1)}, bf16[256,256]{1,0:T(8,128)(2,1)S(1)}, u32[]{:S(2)}, u32[]{:S(2)}) collective-permute-start(bf16[256,256]{1,0:T(8,128)(2,1)S(1)} %get-tuple-element.73), channel_id=1, source_target_pairs={{0,256},{128,384},{256,0},{384,128},{1,257},{129,385},{257,1},{385... | collective-permute-start | bytes 393224 | tf_op jit(solution)/shard_map/ppermute | solution.py:265
  300.5 7.6 %collective-permute-start.29 = (bf16[256,256]{1,0:T(8,128)(2,1)S(1)}, bf16[256,256]{1,0:T(8,128)(2,1)S(1)}, u32[]{:S(2)}, u32[]{:S(2)}) collective-permute-start(bf16[256,256]{1,0:T(8,128)(2,1)S(1)} %get-tuple-element.74), channel_id=1, source_target_pairs={{0,384},{128,0},{256,128},{384,256},{1,385},{129,1},{257,129},{385... | collective-permute-start | bytes 393224 | tf_op jit(solution)/shard_map/ppermute | solution.py:265
  308.2 13.8 %collective-permute-start.30 = (bf16[128,256]{1,0:T(8,128)(2,1)S(1)}, bf16[128,256]{1,0:T(8,128)(2,1)S(1)}, u32[]{:S(2)}, u32[]{:S(2)}) collective-permute-start(bf16[128,256]{1,0:T(8,128)(2,1)S(1)} %get-tuple-element.76), channel_id=1, source_target_pairs={{0,512},{512,0},{1,513},{513,1},{2,514},{514,2},{3,515},{515,3},{4... | collective-permute-start | bytes 196616 | tf_op jit(solution)/shard_map/ppermute | solution.py:261

commit v2 on v1

--- a/solution.py
+++ b/solution.py
@@ -16,6 +16,7 @@
 CHUNK = QUAD * TILE + CNT
 VMEM = pl.BlockSpec(memory_space=pltpu.VMEM)
 SMEM = pl.BlockSpec(memory_space=pltpu.SMEM)
+AFTER = pl.BlockSpec(memory_space=pl.ANY)
 
 
 def call(kernel, out, in_specs, *args, scratch=(), flops=0):
@@ -55,7 +56,6 @@
 
 
 def contrib_kernel(slots, src, tiles, panel, msg, tiles_bf):
-    msg[slots * TILE :, :] = jnp.zeros((CNT, HID), BF)
     rows = []
     for s in range(slots):
         tile = tiles[s].astype(F32).astype(BF)
@@ -69,34 +69,31 @@
     msg[slots * TILE :, :] = jnp.concatenate([counts, jnp.zeros_like(counts)], axis=1).astype(BF)
 
 
-def own_kernel(slots, src, idx, tiles, panel, acc):
+def merge_kernel(slots, chunks, src, idx, other_idx, tiles, panel, recv, *refs):
+    outs, acc = refs[:-1], refs[-1]
     acc[...] = jnp.zeros_like(acc)
+    counts = recv[slots * TILE :, 0:TILE].astype(F32)
+
+    def put(at, tile, row):
+        chunk = at // QUAD
+        lay = at % QUAD
+        to = pl.multiple_of(chunk * CHUNK + lay * TILE, 16)
+        acc[pl.ds(to, TILE), :] += tile
+        add_counts(acc, chunk, lay, row)
+
     for s in range(slots):
 
         @pl.when(idx[s] >= 0)
         def _():
             at = pl.multiple_of(src[s] * TILE, TILE)
             got = jnp.dot(tiles[s], panel[pl.ds(at, TILE), :], preferred_element_type=F32)
-            chunk = idx[s] // QUAD
-            lay = idx[s] % QUAD
-            to = pl.multiple_of(chunk * CHUNK + lay * TILE, 16)
-            acc[pl.ds(to, TILE), :] += got
-            add_counts(acc, chunk, lay, row_counts(tiles[s]))
-
-
-def merge_kernel(slots, chunks, idx, acc_in, recv, *refs):
-    outs, acc = refs[:-1], refs[-1]
-    acc[...] = acc_in[...]
-    counts = recv[slots * TILE :, 0:TILE].astype(F32)
-    for s in range(slots):
-
-        @pl.when(idx[s] >= 0)
+            put(idx[s], got, row_counts(tiles[s]))
+
+        @pl.when(other_idx[s] >= 0)
         def _():
-            chunk = idx[s] // QUAD
-            lay = idx[s] % QUAD
-            to = pl.multiple_of(chunk * CHUNK + lay * TILE, 16)
-            acc[pl.ds(to, TILE), :] += recv[s * TILE : (s + 1) * TILE, :].astype(F32)
-            add_counts(acc, chunk, lay, counts[s : s + 1])
+            put(
+                other_idx[s], recv[s * TILE : (s + 1) * TILE, :].astype(F32), counts[s : s + 1]
+            )
 
     for o in range(chunks):
         at = o * CHUNK
@@ -141,7 +138,8 @@
 
 
 def node_kernel(
-    keep, recv, in_degree, features, w_self, w_neigh, bias, grad_out, hidden, aggregate, grad_pre, scaled
+    keep, recv, in_degree, features, w_self, w_neigh, bias, grad_out,
+    hidden, aggregate, grad_pre, scaled,
 ):
     neigh = keep[0:TILE, :] + recv[0:TILE, :].astype(F32)
     edges = keep[TILE : TILE + 1, 0:TILE] + joined(recv[TILE:, :])[1:2]
@@ -192,13 +190,26 @@
     refs[-1][...] = functools.reduce(lambda a, b: a + b, [r[...] for r in refs[:-1]])
 
 
-def pick_kernel(slots, idx, local, msg):
+def whole_kernel(rows, place, own, *refs):
+    recvs, whole = refs[:-1], refs[-1]
+    size = len(recvs) + 1
+    for d in range(size):
+        at = lax.rem(place[1] + size - d, size)
+        block = own if d == 0 else recvs[d - 1]
+        whole[pl.ds(pl.multiple_of(at * rows, 8), rows), :] = block[0:rows, :]
+
+        @pl.when(at == 0)
+        def _():
+            whole[HID:, :] = block[rows:, :]
+
+
+def pick_kernel(slots, idx, local, after, msg):
     for s in range(slots):
         at = pl.multiple_of(jnp.maximum(idx[s], 0) * TILE, TILE)
         msg[s * TILE : (s + 1) * TILE, :] = local[pl.ds(at, TILE), :]
 
 
-def back_kernel(slots, src, idx, live, tiles, local, recv, keep, send, acc, held):
+def back_kernel(slots, src, idx, live, tiles, recv, local, after, keep, send, acc, got):
     acc[...] = jnp.zeros_like(acc)
     for s in range(slots):
 
@@ -207,24 +218,25 @@
             @pl.when(idx[s] >= 0)
             def _():
                 at = pl.multiple_of(idx[s] * TILE, TILE)
-                held[...] = local[pl.ds(at, TILE), :]
+                got[...] = local[pl.ds(at, TILE), :]
 
             @pl.when(idx[s] < 0)
             def _():
-                held[...] = recv[s * TILE : (s + 1) * TILE, :]
-
-            got = lax.dot_general(
-                tiles[s], held[...], (((0,), (0,)), ((), ())), preferred_element_type=F32
+                got[...] = recv[s * TILE : (s + 1) * TILE, :]
+
+            term = lax.dot_general(
+                tiles[s], got[...], (((0,), (0,)), ((), ())), preferred_element_type=F32
             )
             to = pl.multiple_of(src[s] * TILE, TILE)
-            acc[pl.ds(to, TILE), :] += got
+            acc[pl.ds(to, TILE), :] += term
 
     half = keep.shape[0]
     keep[...] = acc[0:half, :]
     send[...] = acc[half:, :].astype(BF)
 
 
-def back_cut_kernel(keep_in, recv, keep, *sends):
+def back_cut_kernel(keep_in, recv, total, passed, keep, *sends):
+    passed[...] = total[...]
     rows = keep.shape[0]
     for d, ref in enumerate((keep,) + sends):
         at = d * rows
@@ -232,8 +244,9 @@
         ref[...] = got.astype(ref.dtype)
 
 
-def back_gather_kernel(pieces, *refs):
-    ins, outs = refs[: len(refs) - pieces], refs[len(refs) - pieces :]
+def back_gather_kernel(count, total, *refs):
+    ins, passed, outs = refs[:count], refs[count], refs[count + 1 :]
+    passed[...] = total[...]
     for d, ref in enumerate(outs):
         at = slice(d * TILE, (d + 1) * TILE)
         ref[...] = sum(r[at, :].astype(F32) for r in ins).astype(ref.dtype)
@@ -269,18 +282,21 @@
     dest = jnp.where(live > 0, tile_block_row[0, 0], -1)
     source = tile_block_col[0, 0]
     sh, sx, sk = source // (nx * nk), (source // nk) % nx, source % nk
-    src = (sk ^ k) * (nx * nh) + ((sx - x) % nx) * nh + (sh ^ h)
+    src = ((sk ^ k) * nx + (sx - x) % nx) * nh + (sh ^ h)
 
     def place(d):
         dl = d % nl
         far = (dl >> 1) ^ (l >> 1)
         lay = ((far & 1) << 1) | (far >> 1)
-        at = ((d // nl - y) % ny) * QUAD + lay
-        return jnp.where((d >= 0) & ((dl & 1) == (l & 1)), at, -1)
+        mine = (d >= 0) & ((dl & 1) == (l & 1))
+        ring = jnp.where(mine, ((d // nl - y) % ny) * QUAD + lay, -1)
+        return ring, jnp.where(mine, (d // nl) * QUAD + lay, -1)
 
     meta = jnp.zeros((8, TILE), jnp.int32).at[0, :slots].set(dest)
     other = flip(meta, "l", 1)[0, :slots]
-    own_idx, other_idx = place(dest), place(other)
+    own_ring, own_idx = place(dest)
+    other_ring, other_idx = place(other)
+    where = jnp.stack([k, x, y]).astype(jnp.int32)
 
     panel = features
     if nh > 1:
@@ -298,25 +314,18 @@
         panel,
         flops=tile_flops,
     )
-    got = flip(msg, "l", 1)
-    (acc,) = call(
-        functools.partial(own_kernel, slots),
-        [((ny * CHUNK, HID), F32)],
-        [SMEM, SMEM, VMEM, VMEM],
-        src,
-        own_idx,
-        tiles,
-        panel,
-        flops=tile_flops,
-    )
     chunks = call(
         functools.partial(merge_kernel, slots, ny),
         [((CHUNK, HID), BF)] * ny,
-        [SMEM, VMEM, VMEM],
-        other_idx,
-        acc,
-        got,
+        [SMEM, SMEM, SMEM, VMEM, VMEM, VMEM],
+        src,
+        own_ring,
+        other_ring,
+        tiles,
+        panel,
+        flip(msg, "l", 1),
         scratch=[pltpu.VMEM((ny * CHUNK, HID), F32)],
+        flops=tile_flops,
     )
 
     ups, downs = ny // 2, ny - 1 - ny // 2
@@ -367,16 +376,8 @@
 
     local = jnp.concatenate([scaled, flip(scaled, "l", 4)], axis=0)
     local = jnp.concatenate([local, flip(local, "l", 2)], axis=0)
-    blocks = {0: local}
-    up = down = local
-    for step in range(1, ups + 1):
-        up = shift(up, "y", 1)
-        blocks[(-step) % ny] = up
-        if step <= downs:
-            down = shift(down, "y", -1)
-            blocks[step] = down
-
-    where = jnp.stack([k, x]).astype(jnp.int32)
+    local = lax.all_gather(local, "y", axis=0, tiled=True)
+
     wide = ((HID + 8, HID), F32)
     w_keep, w_send, self_back = call(
         weight_kernel,
@@ -399,65 +400,73 @@
         w_keep,
         flip(w_send, "k", 1),
     )
-    got = [cuts[0]] + [shift(cuts[d], "x", d) for d in range(1, nx)]
-    (total,) = call(sum_kernel, [cut], [VMEM] * nx, *got)
-    for axis in ("y", "l", "h"):
-        bit = 1
-        while bit < lax.axis_size(axis):
-            total = total + flip(total, axis, bit)
-            bit *= 2
-    grad_bias = total[w_rows]
-    piece = total[:w_rows]
-    whole = jnp.zeros((HID, HID), F32)
-    for d in range(nx):
-        part = piece if d == 0 else shift(piece, "x", -d)
-        whole = lax.dynamic_update_slice(whole, part, (((x + d) % nx) * w_rows, 0))
-    across = flip(whole, "k", 1)
-    grad_w_self = jnp.where(k == 0, whole, across)
-    grad_w_neigh = jnp.where(k == 0, across, whole)
-
-    local = jnp.concatenate([blocks[o] for o in range(ny)], axis=0)
+    cuts = [cuts[0]] + [shift(cuts[d], "x", d) for d in range(1, nx)]
+    (total,) = call(sum_kernel, [cut], [VMEM] * nx, *cuts)
+
+    def add_over(value, axis, bit):
+        return value + flip(value, axis, bit) if bit < lax.axis_size(axis) else value
+
+    for bit in (1, 2, 4):
+        total = add_over(total, "l", bit)
+
     (msg,) = call(
         functools.partial(pick_kernel, slots),
         [((slots * TILE, HID), BF)],
-        [SMEM, VMEM],
+        [SMEM, VMEM, AFTER],
         other_idx,
         local,
-    )
+        total,
+    )
+    total = add_over(add_over(total, "y", 1), "y", 2)
     half = sources // 2 * TILE
     keep, send = call(
         functools.partial(back_kernel, slots),
         [((half, HID), F32), ((half, HID), BF)],
-        [SMEM, SMEM, SMEM, VMEM, VMEM, VMEM],
+        [SMEM, SMEM, SMEM, VMEM, VMEM, VMEM, AFTER],
         src,
         own_idx,
         live,
         tiles,
+        flip(msg, "l", 1),
         local,
-        flip(msg, "l", 1),
+        total,
         scratch=[pltpu.VMEM((sources * TILE, HID), F32), pltpu.VMEM((TILE, HID), BF)],
         flops=tile_flops,
     )
     group = nh * TILE
-    pieces = call(
+    total, *pieces = call(
         back_cut_kernel,
-        [((group, HID), F32)] + [((group, HID), BF)] * (nx - 1),
-        [VMEM] * 2,
+        [cut, ((group, HID), F32)] + [((group, HID), BF)] * (nx - 1),
+        [VMEM] * 3,
         keep,
         flip(send, "k", 1),
+        add_over(total, "y", 4),
     )
     got = [pieces[0]] + [shift(pieces[d], "x", d) for d in range(1, nx)]
-    last = call(
-        functools.partial(back_gather_kernel, nh),
-        [((TILE, HID), F32)] + [((TILE, HID), BF)] * (nh - 1),
-        [VMEM] * nx,
+    total, *last = call(
+        functools.partial(back_gather_kernel, nx),
+        [cut, ((TILE, HID), F32)] + [node] * (nh - 1),
+        [VMEM] * (nx + 1),
+        add_over(total, "h", 1),
         *got,
     )
-    back_sum = last[0]
+    back = self_back + last[0]
     if nh > 1:
-        back_sum = back_sum + flip(last[1], "h", 1).astype(F32)
-    grad_features = (self_back + back_sum).astype(BF)
-    return hidden, grad_features, grad_w_self, grad_w_neigh, grad_bias
+        back = back + flip(last[1], "h", 1).astype(F32)
+    grad_features = back.astype(BF)
+
+    (whole,) = call(
+        functools.partial(whole_kernel, w_rows),
+        [wide],
+        [SMEM] + [VMEM] * nx,
+        where,
+        total,
+        *[shift(total, "x", d) for d in range(1, nx)],
+    )
+    across = flip(whole, "k", 1)
+    first = jnp.where(k == 0, whole, across)
+    second = jnp.where(k == 0, across, whole)[:HID]
+    return hidden, grad_features, first[:HID], second, first[HID]
 
 
 def on_mesh(mesh):

time: 327 us -> 310 us (0.948); the launches traced: 323 us -> 309 us
  starting transfers between devices: 211 us -> 197 us
  between operations: 2.23 us -> 15.4 us
  local copies, waits for them, and re-layouts: 9.84 us -> 3.9 us
  Pallas kernels: 13.8 us -> 9.94 us
  waiting for transfers between devices: 82.9 us -> 79.3 us
    ppermute x26 -> x19, starting transfers between devices: 82.8 us -> 59.4 us  [shift(): return lax.ppermute(value, axis, [(i, (i + by) % n) for i in range(n)])]
    ppermute x20, starting transfers between devices: 129 us -> 137 us  [flip(): return lax.ppermute(value, axis, [(i, i ^ bit) for i in range(n)])]
    ppermute x26 -> x19, waiting for transfers between devices: 28.8 us -> 21.1 us  [shift(): return lax.ppermute(value, axis, [(i, (i + by) % n) for i in range(n)])]
    all_gather x0 -> x1, waiting for transfers between devices: none -> 6.96 us  [body(): local = lax.all_gather(local, 'y', axis=0, tiled=True)]
    pallas_call x18, Pallas kernels: 13.8 us -> 9.94 us  [call(): pl.pallas_call(kernel, out_shape=shapes, in_specs=in_specs, out_specs=[VM...]
  transfers between devices with their start and end apart: 46 -> 40, of which waited for: 27 -> 23; matrix products, arithmetic and copies ran while one was open for 2% -> 1% of each run, Pallas kernels for 3% -> 1%
where the time goes in v2:
time: 310 us; the launch traced here: 309 us
  starting transfers between devices  197 us (64%)
  waiting for transfers between devices  79.3 us (26%)
  between operations  15.4 us (5%)
  Pallas kernels  9.94 us (3%)
  local copies, waits for them, and re-layouts  3.9 us (1%)
  other arithmetic  3.72 us (1%)
    ppermute x20, starting transfers between devices, flip(): return lax.ppermute(value, axis, [(i, i ^ bit) for i in range(n)])  137 us
    ppermute x19, starting transfers between devices, shift(): return lax.ppermute(value, axis, [(i, (i + by) % n) for i in range(n)])  59.4 us
    ppermute x20, waiting for transfers between devices, flip(): return lax.ppermute(value, axis, [(i, i ^ bit) for i in range(n)])  51.2 us
    ppermute x19, waiting for transfers between devices, shift(): return lax.ppermute(value, axis, [(i, (i + by) % n) for i in range(n)])  21.1 us
    pallas_call x18, Pallas kernels, call(): pl.pallas_call(kernel, out_shape=shapes, in_specs=in_specs, out_specs=[VM...  9.94 us
    all_gather x1, waiting for transfers between devices, body(): local = lax.all_gather(local, 'y', axis=0, tiled=True)  6.96 us
  transfers between devices with their start and end apart: 40, of which 23 were waited for; matrix products, arithmetic and copies ran while one was open for 1% of the time, Pallas kernels for 1%

profile of v2, /device:TPU:1, one launch (start us, length us, event | category | flops | bytes accessed | tf_op | source)
XLA Modules:
  0.0 309.0 jit_solution(13044065369958234486)
XLA Ops:
  7.2 20.0 %collective-permute-start.1 = (bf16[128,256]{1,0:T(8,128)(2,1)}, bf16[128,256]{1,0:T(8,128)(2,1)S(1)}, u32[]{:S(2)}, u32[]{:S(2)}) collective-permute-start(bf16[128,256]{1,0:T(8,128)(2,1)} %features.3), channel_id=1, source_target_pairs={{0,512},{512,0},{1,513},{513,1},{2,514},{514,2},{3,515},{515,3},{4... | collective-permute-start | bytes 196616 | tf_op jit(solution)/shard_map/ppermute | solution.py:274
  28.1 1.2 collective-permute-done.1
  29.3 4.4 %collective-permute-start.2 = (bf16[256,256]{1,0:T(8,128)(2,1)S(1)}, bf16[256,256]{1,0:T(8,128)(2,1)S(1)}, u32[]{:S(2)}, u32[]{:S(2)}) collective-permute-start(bf16[256,256]{1,0:T(8,128)(2,1)S(1)} %get-tuple-element.103), channel_id=1, source_target_pairs={{0,384},{128,0},{256,128},{384,256},{1,385},{129,1},{257,129},{385... | collective-permute-start | bytes 393224 | tf_op jit(solution)/shard_map/ppermute | solution.py:278
  33.7 2.4 collective-permute-start.3
  36.1 2.5 collective-permute-start.4
  38.7 2.2 collective-permute-done.3
  41.0 2.1 collective-permute-done.4
  43.1 8.8 %collective-permute-start.5 = (bf16[1024,256]{1,0:T(8,128)(2,1)S(1)}, bf16[1024,256]{1,0:T(8,128)(2,1)S(1)}, u32[]{:S(2)}, u32[]{:S(2)}) collective-permute-start(bf16[1024,256]{1,0:T(8,128)(2,1)S(1)} %get-tuple-element.95), channel_id=1, source_target_pairs={{0,64},{64,0},{1,65},{65,1},{2,66},{66,2},{3,67},{67,3},{4,68},{68... | collective-permute-start | bytes 1572872 | tf_op jit(solution)/shard_map/ppermute | solution.py:274
  53.2 1.9 collective-permute-start
  56.9 3.4 %collective-permute-start.6 = (bf16[1296,256]{1,0:T(8,128)(2,1)S(1)}, bf16[1296,256]{1,0:T(8,128)(2,1)S(1)}, u32[]{:S(2)}, u32[]{:S(2)}) collective-permute-start(bf16[1296,256]{1,0:T(8,128)(2,1)S(1)} %get-tuple-element.53), channel_id=1, source_target_pairs={{0,1},{1,0},{2,3},{3,2},{4,5},{5,4},{6,7},{7,6},{8,9},{9,8},{10,11... | collective-permute-start | bytes 1990664 | tf_op jit(solution)/shard_map/ppermute | solution.py:274
  60.4 15.0 %collective-permute-done.6.recv = bf16[1296,256]{1,0:T(8,128)(2,1)S(1)} collective-permute-done((bf16[1296,256]{1,0:T(8,128)(2,1)S(1)}, bf16[1296,256]{1,0:T(8,128)(2,1)S(1)}, u32[]{:S(2)}, u32[]{:S(2)}) %collective-permute-start.6) | collective-permute-done | bytes 663584 | tf_op jit(solution)/shard_map/ppermute | solution.py:274
  75.4 2.2 shard_map.138
  77.5 1.9 collective-permute-start.7
  79.5 4.6 %collective-permute-start.11 = (bf16[528,256]{1,0:T(8,128)(2,1)S(1)}, bf16[528,256]{1,0:T(8,128)(2,1)S(1)}, u32[]{:S(2)}, u32[]{:S(2)}) collective-permute-start(bf16[528,256]{1,0:T(8,128)(2,1)S(1)} %get-tuple-element.59), channel_id=1, source_target_pairs={{0,56},{8,0},{16,8},{24,16},{32,24},{40,32},{48,40},{56,48},{1,57}... | collective-permute-start | bytes 811016 | tf_op jit(solution)/shard_map/ppermute | solution.py:278
  84.0 3.9 %collective-permute-done.7.recv = bf16[528,256]{1,0:T(8,128)(2,1)S(1)} collective-permute-done((bf16[528,256]{1,0:T(8,128)(2,1)S(1)}, bf16[528,256]{1,0:T(8,128)(2,1)S(1)}, u32[]{:S(2)}, u32[]{:S(2)}) %collective-permute-start.7) | collective-permute-done | bytes 270368 | tf_op jit(solution)/shard_map/ppermute | solution.py:278
  88.0 1.9 collective-permute-start.8
  90.1 4.7 %collective-permute-start.12 = (bf16[528,256]{1,0:T(8,128)(2,1)S(1)}, bf16[528,256]{1,0:T(8,128)(2,1)S(1)}, u32[]{:S(2)}, u32[]{:S(2)}) collective-permute-start(bf16[528,256]{1,0:T(8,128)(2,1)S(1)} %shard_map.142), channel_id=1, source_target_pairs={{0,56},{8,0},{16,8},{24,16},{32,24},{40,32},{48,40},{56,48},{1,57}... | collective-permute-start | bytes 811016 | tf_op jit(solution)/shard_map/ppermute | solution.py:278
  94.8 2.7 collective-permute-done.8.recv
  97.6 1.9 collective-permute-start.9
  99.6 4.6 %collective-permute-start.13 = (bf16[528,256]{1,0:T(8,128)(2,1)S(1)}, bf16[528,256]{1,0:T(8,128)(2,1)S(1)}, u32[]{:S(2)}, u32[]{:S(2)}) collective-permute-start(bf16[528,256]{1,0:T(8,128)(2,1)S(1)} %shard_map.143), channel_id=1, source_target_pairs={{0,56},{8,0},{16,8},{24,16},{32,24},{40,32},{48,40},{56,48},{1,57}... | collective-permute-start | bytes 811016 | tf_op jit(solution)/shard_map/ppermute | solution.py:278
  104.2 1.8 collective-permute-done.9.recv
  106.1 1.9 collective-permute-start.10
  108.0 6.5 %collective-permute-done.10.refs_1_ = bf16[528,256]{1,0:T(8,128)(2,1)S(1)} collective-permute-done((bf16[528,256]{1,0:T(8,128)(2,1)S(1)}, bf16[528,256]{1,0:T(8,128)(2,1)S(1)}, u32[]{:S(2)}, u32[]{:S(2)}) %collective-permute-start.10) | collective-permute-done | bytes 270368 | tf_op jit(solution)/shard_map/ppermute | solution.py:278
  114.6 3.0 collective-permute-start.14
  117.6 5.2 %collective-permute-done.14.recv = bf16[272,256]{1,0:T(8,128)(2,1)S(1)} collective-permute-done((bf16[272,256]{1,0:T(8,128)(2,1)S(1)}, bf16[272,256]{1,0:T(8,128)(2,1)S(1)}, u32[]{:S(2)}, u32[]{:S(2)}) %collective-permute-start.14) | collective-permute-done | bytes 139296 | tf_op jit(solution)/shard_map/ppermute | solution.py:274
  122.8 6.7 %collective-permute-start.15 = (bf16[144,256]{1,0:T(8,128)(2,1)S(1)}, bf16[144,256]{1,0:T(8,128)(2,1)S(1)}, u32[]{:S(2)}, u32[]{:S(2)}) collective-permute-start(bf16[144,256]{1,0:T(8,128)(2,1)S(1)} %get-tuple-element.65), channel_id=1, source_target_pairs={{0,4},{1,5},{2,6},{3,7},{4,0},{5,1},{6,2},{7,3},{8,12},{9,13},{10,... | collective-permute-start | bytes 221192 | tf_op jit(solution)/shard_map/ppermute | solution.py:274
  129.6 2.3 collective-permute-done.15.recv
  132.9 6.7 %collective-permute-start.16 = (bf16[128,256]{1,0:T(8,128)(2,1)S(1)}, bf16[128,256]{1,0:T(8,128)(2,1)S(1)}, u32[]{:S(2)}, u32[]{:S(2)}) collective-permute-start(bf16[128,256]{1,0:T(8,128)(2,1)S(1)} %get-tuple-element.70), channel_id=1, source_target_pairs={{0,4},{1,5},{2,6},{3,7},{4,0},{5,1},{6,2},{7,3},{8,12},{9,13},{10,... | collective-permute-start | bytes 196616 | tf_op jit(solution)/shard_map/ppermute | solution.py:274
  139.7 2.2 collective-permute-done.16
  141.8 4.7 %collective-permute-start.17 = (bf16[256,256]{1,0:T(8,128)(2,1)S(1)}, bf16[256,256]{1,0:T(8,128)(2,1)S(1)}, u32[]{:S(2)}, u32[]{:S(2)}) collective-permute-start(bf16[256,256]{1,0:T(8,128)(2,1)S(1)} %pad_maximum_fusion.1), channel_id=1, source_target_pairs={{0,2},{1,3},{2,0},{3,1},{4,6},{5,7},{6,4},{7,5},{8,10},{9,11},{10,... | collective-permute-start | bytes 393224 | tf_op jit(solution)/shard_map/ppermute | solution.py:274
  146.5 3.8 %collective-permute-done.17 = bf16[256,256]{1,0:T(8,128)(2,1)S(1)} collective-permute-done((bf16[256,256]{1,0:T(8,128)(2,1)S(1)}, bf16[256,256]{1,0:T(8,128)(2,1)S(1)}, u32[]{:S(2)}, u32[]{:S(2)}) %collective-permute-start.17) | collective-permute-done | bytes 131104 | tf_op jit(solution)/shard_map/ppermute | solution.py:274
  151.9 12.2 %collective-permute-start.18 = (f32[264,256]{1,0:T(8,128)S(1)}, f32[264,256]{1,0:T(8,128)S(1)}, u32[]{:S(2)}, u32[]{:S(2)}) collective-permute-start(f32[264,256]{1,0:T(8,128)S(1)} %get-tuple-element.72), channel_id=1, source_target_pairs={{0,64},{64,0},{1,65},{65,1},{2,66},{66,2},{3,67},{67,3},{4,68},{68... | collective-permute-start | bytes 811016 | tf_op jit(solution)/shard_map/ppermute | solution.py:274
  164.1 1.2 collective-permute-done.18.recv
  165.9 1.9 collective-permute-start.19
  167.8 3.8 %collective-permute-start.20 = (f32[72,256]{1,0:T(8,128)S(1)}, f32[72,256]{1,0:T(8,128)S(1)}, u32[]{:S(2)}, u32[]{:S(2)}) collective-permute-start(f32[72,256]{1,0:T(8,128)S(1)} %get-tuple-element.75), channel_id=1, source_target_pairs={{0,256},{128,384},{256,0},{384,128},{1,257},{129,385},{257,1},{385... | collective-permute-start | bytes 221192 | tf_op jit(solution)/shard_map/ppermute | solution.py:278
  171.6 3.2 %collective-permute-start.21 = (f32[72,256]{1,0:T(8,128)S(1)}, f32[72,256]{1,0:T(8,128)S(1)}, u32[]{:S(2)}, u32[]{:S(2)}) collective-permute-start(f32[72,256]{1,0:T(8,128)S(1)} %get-tuple-element.76), channel_id=1, source_target_pairs={{0,384},{128,0},{256,128},{384,256},{1,385},{129,1},{257,129},{385... | collective-permute-start | bytes 221192 | tf_op jit(solution)/shard_map/ppermute | solution.py:278
  174.9 1.9 collective-permute-done.21.refs_3_
  176.7 1.9 collective-permute-start.22
  178.7 3.6 %collective-permute-done.22 = f32[72,256]{1,0:T(8,128)S(1)} collective-permute-done((f32[72,256]{1,0:T(8,128)S(1)}, f32[72,256]{1,0:T(8,128)S(1)}, u32[]{:S(2)}, u32[]{:S(2)}) %collective-permute-start.22) | collective-permute-done | bytes 73760 | tf_op jit(solution)/shard_map/ppermute | solution.py:274
  182.3 4.0 %collective-permute-start.23 = (f32[72,256]{1,0:T(8,128)S(1)}, f32[72,256]{1,0:T(8,128)S(1)}, u32[]{:S(2)}, u32[]{:S(2)}) collective-permute-start(f32[72,256]{1,0:T(8,128)S(1)} %add.96), channel_id=1, source_target_pairs={{0,2},{1,3},{2,0},{3,1},{4,6},{5,7},{6,4},{7,5},{8,10},{9,11},{10,... | collective-permute-start | bytes 221192 | tf_op jit(solution)/shard_map/ppermute | solution.py:274
  186.3 2.5 collective-permute-done.23
  188.8 6.6 %collective-permute-start.24 = (f32[72,256]{1,0:T(8,128)S(1)}, f32[72,256]{1,0:T(8,128)S(1)}, u32[]{:S(2)}, u32[]{:S(2)}) collective-permute-start(f32[72,256]{1,0:T(8,128)S(1)} %add.97), channel_id=1, source_target_pairs={{0,4},{1,5},{2,6},{3,7},{4,0},{5,1},{6,2},{7,3},{8,12},{9,13},{10,... | collective-permute-start | bytes 221192 | tf_op jit(solution)/shard_map/ppermute | solution.py:274
  195.4 2.4 collective-permute-done.24
  197.8 7.0 %all-gather.2.cloned.1.call-done.local = bf16[4096,256]{1,0:T(8,128)(2,1)} async-done(((bf16[512,256]{1,0:T(8,128)(2,1)}), bf16[4096,256]{1,0:T(8,128)(2,1)}) %all-gather.2.cloned.1.call-update) | async-done | bytes 2097168 | tf_op jit(solution)/shard_map/all_gather | solution.py:379
  204.8 1.6 copy-done
  207.0 3.4 %collective-permute-start.25 = (bf16[1280,256]{1,0:T(8,128)(2,1)S(1)}, bf16[1280,256]{1,0:T(8,128)(2,1)S(1)}, u32[]{:S(2)}, u32[]{:S(2)}) collective-permute-start(bf16[1280,256]{1,0:T(8,128)(2,1)S(1)} %shard_map.150), channel_id=1, source_target_pairs={{0,1},{1,0},{2,3},{3,2},{4,5},{5,4},{6,7},{7,6},{8,9},{9,8},{10,11... | collective-permute-start | bytes 1966088 | tf_op jit(solution)/shard_map/ppermute | solution.py:274
  210.3 2.5 collective-permute-start.26
  212.9 2.6 collective-permute-done.26
  215.5 3.7 %collective-permute-start.27 = (f32[72,256]{1,0:T(8,128)S(1)}, f32[72,256]{1,0:T(8,128)S(1)}, u32[]{:S(2)}, u32[]{:S(2)}) collective-permute-start(f32[72,256]{1,0:T(8,128)S(1)} %add.99), channel_id=1, source_target_pairs={{0,16},{8,24},{16,0},{24,8},{32,48},{40,56},{48,32},{56,40},{1,17}... | collective-permute-start | bytes 221192 | tf_op jit(solution)/shard_map/ppermute | solution.py:274
  219.1 2.8 collective-permute-done.27
  222.0 2.5 shard_map.151
  224.5 8.7 %collective-permute-start.28 = (bf16[1024,256]{1,0:T(8,128)(2,1)S(1)}, bf16[1024,256]{1,0:T(8,128)(2,1)S(1)}, u32[]{:S(2)}, u32[]{:S(2)}) collective-permute-start(bf16[1024,256]{1,0:T(8,128)(2,1)S(1)} %get-tuple-element.78), channel_id=1, source_target_pairs={{0,64},{64,0},{1,65},{65,1},{2,66},{66,2},{3,67},{67,3},{4,68},{68... | collective-permute-start | bytes 1572872 | tf_op jit(solution)/shard_map/ppermute | solution.py:274
  233.2 5.8 %collective-permute-start.29 = (f32[72,256]{1,0:T(8,128)S(1)}, f32[72,256]{1,0:T(8,128)S(1)}, u32[]{:S(2)}, u32[]{:S(2)}) collective-permute-start(f32[72,256]{1,0:T(8,128)S(1)} %add.100.after), channel_id=1, source_target_pairs={{0,32},{8,40},{16,48},{24,56},{32,0},{40,8},{48,16},{56,24},{1,33}... | collective-permute-start | bytes 221192 | tf_op jit(solution)/shard_map/ppermute | solution.py:274
  239.0 3.9 %collective-permute-done.29 = f32[72,256]{1,0:T(8,128)S(1)} collective-permute-done((f32[72,256]{1,0:T(8,128)S(1)}, f32[72,256]{1,0:T(8,128)S(1)}, u32[]{:S(2)}, u32[]{:S(2)}) %collective-permute-start.29) | collective-permute-done | bytes 73760 | tf_op jit(solution)/shard_map/ppermute | solution.py:274
  243.0 2.7 collective-permute-start.31
  245.7 4.5 %collective-permute-start.32 = (bf16[256,256]{1,0:T(8,128)(2,1)S(1)}, bf16[256,256]{1,0:T(8,128)(2,1)S(1)}, u32[]{:S(2)}, u32[]{:S(2)}) collective-permute-start(bf16[256,256]{1,0:T(8,128)(2,1)S(1)} %get-tuple-element.82), channel_id=1, source_target_pairs={{0,256},{128,384},{256,0},{384,128},{1,257},{129,385},{257,1},{385... | collective-permute-start | bytes 393224 | tf_op jit(solution)/shard_map/ppermute | solution.py:278
  250.2 4.0 %collective-permute-start.33 = (bf16[256,256]{1,0:T(8,128)(2,1)S(1)}, bf16[256,256]{1,0:T(8,128)(2,1)S(1)}, u32[]{:S(2)}, u32[]{:S(2)}) collective-permute-start(bf16[256,256]{1,0:T(8,128)(2,1)S(1)} %get-tuple-element.83), channel_id=1, source_target_pairs={{0,384},{128,0},{256,128},{384,256},{1,385},{129,1},{257,129},{385... | collective-permute-start | bytes 393224 | tf_op jit(solution)/shard_map/ppermute | solution.py:278
  254.2 14.1 %collective-permute-start.30 = (f32[72,256]{1,0:T(8,128)S(1)}, f32[72,256]{1,0:T(8,128)S(1)}, u32[]{:S(2)}, u32[]{:S(2)}) collective-permute-start(f32[72,256]{1,0:T(8,128)S(1)} %get-tuple-element.79), channel_id=1, source_target_pairs={{0,512},{512,0},{1,513},{513,1},{2,514},{514,2},{3,515},{515,3},{4... | collective-permute-start | bytes 221192 | tf_op jit(solution)/shard_map/ppermute | solution.py:274
  268.4 2.4 collective-permute-done.30
  270.9 1.9 collective-permute-start.35
  272.8 2.7 collective-permute-start.36
  275.5 3.8 %collective-permute-start.37 = (f32[72,256]{1,0:T(8,128)S(1)}, f32[72,256]{1,0:T(8,128)S(1)}, u32[]{:S(2)}, u32[]{:S(2)}) collective-permute-start(f32[72,256]{1,0:T(8,128)S(1)} %get-tuple-element.86.own), channel_id=1, source_target_pairs={{0,384},{128,0},{256,128},{384,256},{1,385},{129,1},{257,129},{385... | collective-permute-start | bytes 221192 | tf_op jit(solution)/shard_map/ppermute | solution.py:278
  279.3 12.5 %collective-permute-start.34 = (bf16[128,256]{1,0:T(8,128)(2,1)S(1)}, bf16[128,256]{1,0:T(8,128)(2,1)S(1)}, u32[]{:S(2)}, u32[]{:S(2)}) collective-permute-start(bf16[128,256]{1,0:T(8,128)(2,1)S(1)} %get-tuple-element.85), channel_id=1, source_target_pairs={{0,512},{512,0},{1,513},{513,1},{2,514},{514,2},{3,515},{515,3},{4... | collective-permute-start | bytes 196616 | tf_op jit(solution)/shard_map/ppermute | solution.py:274
  292.5 6.5 %collective-permute-start.38 = (f32[264,256]{1,0:T(8,128)S(1)}, f32[264,256]{1,0:T(8,128)S(1)}, u32[]{:S(2)}, u32[]{:S(2)}) collective-permute-start(f32[264,256]{1,0:T(8,128)S(1)} %shard_map.154), channel_id=1, source_target_pairs={{0,64},{64,0},{1,65},{65,1},{2,66},{66,2},{3,67},{67,3},{4,68},{68... | collective-permute-start | bytes 811016 | tf_op jit(solution)/shard_map/ppermute | solution.py:274
  (83 shorter events, 11.9 us)
Async XLA Ops:
  7.2 48.7 %copy-start.2 = (s32[1,1,10,128,128]{4,3,2,1,0:T(8,128)S(1)}, s32[1,1,10,128,128]{4,3,2,1,0:T(8,128)}, u32[]{:S(2)}) copy-start(s32[1,1,10,128,128]{4,3,2,1,0:T(8,128)} %param.13) | copy-start | bytes 1966084
  7.2 197.6 %all-gather.2.cloned.1.call-start = ((), (), s32[]{:S(2)}) async-start(), calls=%async_computation | async-start | bytes 2359296 | tf_op jit(solution)/shard_map/all_gather | solution.py:379
  7.2 22.1 %collective-permute-start.1 = (bf16[128,256]{1,0:T(8,128)(2,1)}, bf16[128,256]{1,0:T(8,128)(2,1)S(1)}, u32[]{:S(2)}, u32[]{:S(2)}) collective-permute-start(bf16[128,256]{1,0:T(8,128)(2,1)} %features.3), channel_id=1, source_target_pairs={{0,512},{512,0},{1,513},{513,1},{2,514},{514,2},{3,515},{515,3},{4... | collective-permute-start | bytes 196616 | tf_op jit(solution)/shard_map/ppermute | solution.py:274
  29.3 31.0 %copy-start.9 = (s32[1,1,10]{2,1,0:T(1,128)S(1)}, s32[1,1,10]{2,1,0:T(1,128)}, u32[]{:S(2)}) copy-start(s32[1,1,10]{2,1,0:T(1,128)} %param.14) | copy-start | bytes 124
  29.3 9.4 %collective-permute-start.2 = (bf16[256,256]{1,0:T(8,128)(2,1)S(1)}, bf16[256,256]{1,0:T(8,128)(2,1)S(1)}, u32[]{:S(2)}, u32[]{:S(2)}) collective-permute-start(bf16[256,256]{1,0:T(8,128)(2,1)S(1)} %get-tuple-element.103), channel_id=1, source_target_pairs={{0,384},{128,0},{256,128},{384,256},{1,385},{129,1},{257,129},{385... | collective-permute-start | bytes 393224 | tf_op jit(solution)/shard_map/ppermute | solution.py:278
  33.7 7.2 %collective-permute-start.3 = (bf16[256,256]{1,0:T(8,128)(2,1)S(1)}, bf16[256,256]{1,0:T(8,128)(2,1)S(1)}, u32[]{:S(2)}, u32[]{:S(2)}) collective-permute-start(bf16[256,256]{1,0:T(8,128)(2,1)S(1)} %get-tuple-element.103), channel_id=1, source_target_pairs={{0,256},{128,384},{256,0},{384,128},{1,257},{129,385},{257,1},{385... | collective-permute-start | bytes 393224 | tf_op jit(solution)/shard_map/ppermute | solution.py:278
  36.1 6.9 %collective-permute-start.4 = (bf16[256,256]{1,0:T(8,128)(2,1)S(1)}, bf16[256,256]{1,0:T(8,128)(2,1)S(1)}, u32[]{:S(2)}, u32[]{:S(2)}) collective-permute-start(bf16[256,256]{1,0:T(8,128)(2,1)S(1)} %get-tuple-element.103), channel_id=1, source_target_pairs={{0,128},{128,256},{256,384},{384,0},{1,129},{129,257},{257,385},{3... | collective-permute-start | bytes 393224 | tf_op jit(solution)/shard_map/ppermute | solution.py:278
  43.1 12.8 %collective-permute-start.5 = (bf16[1024,256]{1,0:T(8,128)(2,1)S(1)}, bf16[1024,256]{1,0:T(8,128)(2,1)S(1)}, u32[]{:S(2)}, u32[]{:S(2)}) collective-permute-start(bf16[1024,256]{1,0:T(8,128)(2,1)S(1)} %get-tuple-element.95), channel_id=1, source_target_pairs={{0,64},{64,0},{1,65},{65,1},{2,66},{66,2},{3,67},{67,3},{4,68},{68... | collective-permute-start | bytes 1572872 | tf_op jit(solution)/shard_map/ppermute | solution.py:274
  53.2 7.1 %collective-permute-start = (s32[8,128]{1,0:T(8,128)S(1)}, s32[8,128]{1,0:T(8,128)S(1)}, u32[]{:S(2)}, u32[]{:S(2)}) collective-permute-start(s32[8,128]{1,0:T(8,128)S(1)} %scatter.4), channel_id=1, source_target_pairs={{0,1},{1,0},{2,3},{3,2},{4,5},{5,4},{6,7},{7,6},{8,9},{9,8},{10,11... | collective-permute-start | bytes 12296 | tf_op jit(solution)/shard_map/ppermute | solution.py:274
  56.9 18.4 %collective-permute-start.6 = (bf16[1296,256]{1,0:T(8,128)(2,1)S(1)}, bf16[1296,256]{1,0:T(8,128)(2,1)S(1)}, u32[]{:S(2)}, u32[]{:S(2)}) collective-permute-start(bf16[1296,256]{1,0:T(8,128)(2,1)S(1)} %get-tuple-element.53), channel_id=1, source_target_pairs={{0,1},{1,0},{2,3},{3,2},{4,5},{5,4},{6,7},{7,6},{8,9},{9,8},{10,11... | collective-permute-start | bytes 1990664 | tf_op jit(solution)/shard_map/ppermute | solution.py:274
  77.5 10.4 %collective-permute-start.7 = (bf16[528,256]{1,0:T(8,128)(2,1)S(1)}, bf16[528,256]{1,0:T(8,128)(2,1)S(1)}, u32[]{:S(2)}, u32[]{:S(2)}) collective-permute-start(bf16[528,256]{1,0:T(8,128)(2,1)S(1)} %get-tuple-element.55), channel_id=1, source_target_pairs={{0,8},{8,16},{16,24},{24,32},{32,40},{40,48},{48,56},{56,0},{1,9},... | collective-permute-start | bytes 811016 | tf_op jit(solution)/shard_map/ppermute | solution.py:278
  79.5 10.5 %collective-permute-start.11 = (bf16[528,256]{1,0:T(8,128)(2,1)S(1)}, bf16[528,256]{1,0:T(8,128)(2,1)S(1)}, u32[]{:S(2)}, u32[]{:S(2)}) collective-permute-start(bf16[528,256]{1,0:T(8,128)(2,1)S(1)} %get-tuple-element.59), channel_id=1, source_target_pairs={{0,56},{8,0},{16,8},{24,16},{32,24},{40,32},{48,40},{56,48},{1,57}... | collective-permute-start | bytes 811016 | tf_op jit(solution)/shard_map/ppermute | solution.py:278
  88.0 9.5 %collective-permute-start.8 = (bf16[528,256]{1,0:T(8,128)(2,1)S(1)}, bf16[528,256]{1,0:T(8,128)(2,1)S(1)}, u32[]{:S(2)}, u32[]{:S(2)}) collective-permute-start(bf16[528,256]{1,0:T(8,128)(2,1)S(1)} %shard_map.139), channel_id=1, source_target_pairs={{0,8},{8,16},{16,24},{24,32},{32,40},{40,48},{48,56},{56,0},{1,9},... | collective-permute-start | bytes 811016 | tf_op jit(solution)/shard_map/ppermute | solution.py:278
  90.0 41.9 %copy-start.3 = (bf16[128,256]{1,0:T(8,128)(2,1)S(1)}, bf16[128,256]{1,0:T(8,128)(2,1)}, u32[]{:S(2)}) copy-start(bf16[128,256]{1,0:T(8,128)(2,1)} %features.3) | copy-start | bytes 196612
  90.0 41.9 %copy-start.4 = (bf16[256,256]{1,0:T(8,128)(2,1)S(1)}, bf16[256,256]{1,0:T(8,128)(2,1)}, u32[]{:S(2)}) copy-start(bf16[256,256]{1,0:T(8,128)(2,1)} %w_self.3) | copy-start | bytes 393220
  90.0 41.9 %copy-start.5 = (bf16[256,256]{1,0:T(8,128)(2,1)S(1)}, bf16[256,256]{1,0:T(8,128)(2,1)}, u32[]{:S(2)}) copy-start(bf16[256,256]{1,0:T(8,128)(2,1)} %w_neigh.1) | copy-start | bytes 393220
  90.0 41.9 %copy-start.6 = (bf16[128,256]{1,0:T(8,128)(2,1)S(1)}, bf16[128,256]{1,0:T(8,128)(2,1)}, u32[]{:S(2)}) copy-start(bf16[128,256]{1,0:T(8,128)(2,1)} %grad_out.1) | copy-start | bytes 196612
  90.0 41.9 %copy-start.7 = (f32[256]{0:T(256)S(1)}, f32[256]{0:T(256)}, u32[]{:S(2)}) copy-start(f32[256]{0:T(256)} %param.20) | copy-start | bytes 3076
  90.0 41.9 %copy-start.8 = (s32[128]{0:T(128)S(1)}, s32[128]{0:T(128)}, u32[]{:S(2)}) copy-start(s32[128]{0:T(128)} %param.17) | copy-start | bytes 1540
  90.1 9.4 %collective-permute-start.12 = (bf16[528,256]{1,0:T(8,128)(2,1)S(1)}, bf16[528,256]{1,0:T(8,128)(2,1)S(1)}, u32[]{:S(2)}, u32[]{:S(2)}) collective-permute-start(bf16[528,256]{1,0:T(8,128)(2,1)S(1)} %shard_map.142), channel_id=1, source_target_pairs={{0,56},{8,0},{16,8},{24,16},{32,24},{40,32},{48,40},{56,48},{1,57}... | collective-permute-start | bytes 811016 | tf_op jit(solution)/shard_map/ppermute | solution.py:278
  97.6 8.4 %collective-permute-start.9 = (bf16[528,256]{1,0:T(8,128)(2,1)S(1)}, bf16[528,256]{1,0:T(8,128)(2,1)S(1)}, u32[]{:S(2)}, u32[]{:S(2)}) collective-permute-start(bf16[528,256]{1,0:T(8,128)(2,1)S(1)} %shard_map.140), channel_id=1, source_target_pairs={{0,8},{8,16},{16,24},{24,32},{32,40},{40,48},{48,56},{56,0},{1,9},... | collective-permute-start | bytes 811016 | tf_op jit(solution)/shard_map/ppermute | solution.py:278
  99.6 8.4 %collective-permute-start.13 = (bf16[528,256]{1,0:T(8,128)(2,1)S(1)}, bf16[528,256]{1,0:T(8,128)(2,1)S(1)}, u32[]{:S(2)}, u32[]{:S(2)}) collective-permute-start(bf16[528,256]{1,0:T(8,128)(2,1)S(1)} %shard_map.143), channel_id=1, source_target_pairs={{0,56},{8,0},{16,8},{24,16},{32,24},{40,32},{48,40},{56,48},{1,57}... | collective-permute-start | bytes 811016 | tf_op jit(solution)/shard_map/ppermute | solution.py:278
  106.1 8.4 %collective-permute-start.10 = (bf16[528,256]{1,0:T(8,128)(2,1)S(1)}, bf16[528,256]{1,0:T(8,128)(2,1)S(1)}, u32[]{:S(2)}, u32[]{:S(2)}) collective-permute-start(bf16[528,256]{1,0:T(8,128)(2,1)S(1)} %shard_map.141), channel_id=1, source_target_pairs={{0,8},{8,16},{16,24},{24,32},{32,40},{40,48},{48,56},{56,0},{1,9},... | collective-permute-start | bytes 811016 | tf_op jit(solution)/shard_map/ppermute | solution.py:278
  114.6 8.2 %collective-permute-start.14 = (bf16[272,256]{1,0:T(8,128)(2,1)S(1)}, bf16[272,256]{1,0:T(8,128)(2,1)S(1)}, u32[]{:S(2)}, u32[]{:S(2)}) collective-permute-start(bf16[272,256]{1,0:T(8,128)(2,1)S(1)} %get-tuple-element.63), channel_id=1, source_target_pairs={{0,2},{1,3},{2,0},{3,1},{4,6},{5,7},{6,4},{7,5},{8,10},{9,11},{10,... | collective-permute-start | bytes 417800 | tf_op jit(solution)/shard_map/ppermute | solution.py:274
  122.8 9.1 %collective-permute-start.15 = (bf16[144,256]{1,0:T(8,128)(2,1)S(1)}, bf16[144,256]{1,0:T(8,128)(2,1)S(1)}, u32[]{:S(2)}, u32[]{:S(2)}) collective-permute-start(bf16[144,256]{1,0:T(8,128)(2,1)S(1)} %get-tuple-element.65), channel_id=1, source_target_pairs={{0,4},{1,5},{2,6},{3,7},{4,0},{5,1},{6,2},{7,3},{8,12},{9,13},{10,... | collective-permute-start | bytes 221192 | tf_op jit(solution)/shard_map/ppermute | solution.py:274
  132.9 8.9 %collective-permute-start.16 = (bf16[128,256]{1,0:T(8,128)(2,1)S(1)}, bf16[128,256]{1,0:T(8,128)(2,1)S(1)}, u32[]{:S(2)}, u32[]{:S(2)}) collective-permute-start(bf16[128,256]{1,0:T(8,128)(2,1)S(1)} %get-tuple-element.70), channel_id=1, source_target_pairs={{0,4},{1,5},{2,6},{3,7},{4,0},{5,1},{6,2},{7,3},{8,12},{9,13},{10,... | collective-permute-start | bytes 196616 | tf_op jit(solution)/shard_map/ppermute | solution.py:274
  141.8 8.4 %collective-permute-start.17 = (bf16[256,256]{1,0:T(8,128)(2,1)S(1)}, bf16[256,256]{1,0:T(8,128)(2,1)S(1)}, u32[]{:S(2)}, u32[]{:S(2)}) collective-permute-start(bf16[256,256]{1,0:T(8,128)(2,1)S(1)} %pad_maximum_fusion.1), channel_id=1, source_target_pairs={{0,2},{1,3},{2,0},{3,1},{4,6},{5,7},{6,4},{7,5},{8,10},{9,11},{10,... | collective-permute-start | bytes 393224 | tf_op jit(solution)/shard_map/ppermute | solution.py:274
  151.9 13.4 %collective-permute-start.18 = (f32[264,256]{1,0:T(8,128)S(1)}, f32[264,256]{1,0:T(8,128)S(1)}, u32[]{:S(2)}, u32[]{:S(2)}) collective-permute-start(f32[264,256]{1,0:T(8,128)S(1)} %get-tuple-element.72), channel_id=1, source_target_pairs={{0,64},{64,0},{1,65},{65,1},{2,66},{66,2},{3,67},{67,3},{4,68},{68... | collective-permute-start | bytes 811016 | tf_op jit(solution)/shard_map/ppermute | solution.py:274
  165.9 9.0 %collective-permute-start.19 = (f32[72,256]{1,0:T(8,128)S(1)}, f32[72,256]{1,0:T(8,128)S(1)}, u32[]{:S(2)}, u32[]{:S(2)}) collective-permute-start(f32[72,256]{1,0:T(8,128)S(1)} %get-tuple-element.74), channel_id=1, source_target_pairs={{0,128},{128,256},{256,384},{384,0},{1,129},{129,257},{257,385},{3... | collective-permute-start | bytes 221192 | tf_op jit(solution)/shard_map/ppermute | solution.py:278
  167.8 7.1 %collective-permute-start.20 = (f32[72,256]{1,0:T(8,128)S(1)}, f32[72,256]{1,0:T(8,128)S(1)}, u32[]{:S(2)}, u32[]{:S(2)}) collective-permute-start(f32[72,256]{1,0:T(8,128)S(1)} %get-tuple-element.75), channel_id=1, source_target_pairs={{0,256},{128,384},{256,0},{384,128},{1,257},{129,385},{257,1},{385... | collective-permute-start | bytes 221192 | tf_op jit(solution)/shard_map/ppermute | solution.py:278
  171.6 5.1 %collective-permute-start.21 = (f32[72,256]{1,0:T(8,128)S(1)}, f32[72,256]{1,0:T(8,128)S(1)}, u32[]{:S(2)}, u32[]{:S(2)}) collective-permute-start(f32[72,256]{1,0:T(8,128)S(1)} %get-tuple-element.76), channel_id=1, source_target_pairs={{0,384},{128,0},{256,128},{384,256},{1,385},{129,1},{257,129},{385... | collective-permute-start | bytes 221192 | tf_op jit(solution)/shard_map/ppermute | solution.py:278
  176.7 5.5 %collective-permute-start.22 = (f32[72,256]{1,0:T(8,128)S(1)}, f32[72,256]{1,0:T(8,128)S(1)}, u32[]{:S(2)}, u32[]{:S(2)}) collective-permute-start(f32[72,256]{1,0:T(8,128)S(1)} %shard_map.149), channel_id=1, source_target_pairs={{0,1},{1,0},{2,3},{3,2},{4,5},{5,4},{6,7},{7,6},{8,9},{9,8},{10,11... | collective-permute-start | bytes 221192 | tf_op jit(solution)/shard_map/ppermute | solution.py:274
  182.3 6.5 %collective-permute-start.23 = (f32[72,256]{1,0:T(8,128)S(1)}, f32[72,256]{1,0:T(8,128)S(1)}, u32[]{:S(2)}, u32[]{:S(2)}) collective-permute-start(f32[72,256]{1,0:T(8,128)S(1)} %add.96), channel_id=1, source_target_pairs={{0,2},{1,3},{2,0},{3,1},{4,6},{5,7},{6,4},{7,5},{8,10},{9,11},{10,... | collective-permute-start | bytes 221192 | tf_op jit(solution)/shard_map/ppermute | solution.py:274
  188.8 9.0 %collective-permute-start.24 = (f32[72,256]{1,0:T(8,128)S(1)}, f32[72,256]{1,0:T(8,128)S(1)}, u32[]{:S(2)}, u32[]{:S(2)}) collective-permute-start(f32[72,256]{1,0:T(8,128)S(1)} %add.97), channel_id=1, source_target_pairs={{0,4},{1,5},{2,6},{3,7},{4,0},{5,1},{6,2},{7,3},{8,12},{9,13},{10,... | collective-permute-start | bytes 221192 | tf_op jit(solution)/shard_map/ppermute | solution.py:274
  204.8 1.6 copy-start
  206.4 15.6 %copy-start.1 = (bf16[4096,256]{1,0:T(8,128)(2,1)S(1)}, bf16[4096,256]{1,0:T(8,128)(2,1)}, u32[]{:S(2)}) copy-start(bf16[4096,256]{1,0:T(8,128)(2,1)} %all-gather.2.cloned.1.call-done.local) | copy-start | bytes 6291460
  207.0 15.0 %collective-permute-start.25 = (bf16[1280,256]{1,0:T(8,128)(2,1)S(1)}, bf16[1280,256]{1,0:T(8,128)(2,1)S(1)}, u32[]{:S(2)}, u32[]{:S(2)}) collective-permute-start(bf16[1280,256]{1,0:T(8,128)(2,1)S(1)} %shard_map.150), channel_id=1, source_target_pairs={{0,1},{1,0},{2,3},{3,2},{4,5},{5,4},{6,7},{7,6},{8,9},{9,8},{10,11... | collective-permute-start | bytes 1966088 | tf_op jit(solution)/shard_map/ppermute | solution.py:274
  210.3 5.1 %collective-permute-start.26 = (f32[72,256]{1,0:T(8,128)S(1)}, f32[72,256]{1,0:T(8,128)S(1)}, u32[]{:S(2)}, u32[]{:S(2)}) collective-permute-start(f32[72,256]{1,0:T(8,128)S(1)} %add.98.after), channel_id=1, source_target_pairs={{0,8},{8,0},{16,24},{24,16},{32,40},{40,32},{48,56},{56,48},{1,9},... | collective-permute-start | bytes 221192 | tf_op jit(solution)/shard_map/ppermute | solution.py:274
  215.5 6.5 %collective-permute-start.27 = (f32[72,256]{1,0:T(8,128)S(1)}, f32[72,256]{1,0:T(8,128)S(1)}, u32[]{:S(2)}, u32[]{:S(2)}) collective-permute-start(f32[72,256]{1,0:T(8,128)S(1)} %add.99), channel_id=1, source_target_pairs={{0,16},{8,24},{16,0},{24,8},{32,48},{40,56},{48,32},{56,40},{1,17}... | collective-permute-start | bytes 221192 | tf_op jit(solution)/shard_map/ppermute | solution.py:274
  224.5 18.4 %collective-permute-start.28 = (bf16[1024,256]{1,0:T(8,128)(2,1)S(1)}, bf16[1024,256]{1,0:T(8,128)(2,1)S(1)}, u32[]{:S(2)}, u32[]{:S(2)}) collective-permute-start(bf16[1024,256]{1,0:T(8,128)(2,1)S(1)} %get-tuple-element.78), channel_id=1, source_target_pairs={{0,64},{64,0},{1,65},{65,1},{2,66},{66,2},{3,67},{67,3},{4,68},{68... | collective-permute-start | bytes 1572872 | tf_op jit(solution)/shard_map/ppermute | solution.py:274
  233.2 9.7 %collective-permute-start.29 = (f32[72,256]{1,0:T(8,128)S(1)}, f32[72,256]{1,0:T(8,128)S(1)}, u32[]{:S(2)}, u32[]{:S(2)}) collective-permute-start(f32[72,256]{1,0:T(8,128)S(1)} %add.100.after), channel_id=1, source_target_pairs={{0,32},{8,40},{16,48},{24,56},{32,0},{40,8},{48,16},{56,24},{1,33}... | collective-permute-start | bytes 221192 | tf_op jit(solution)/shard_map/ppermute | solution.py:274
  243.0 27.7 %collective-permute-start.31 = (bf16[256,256]{1,0:T(8,128)(2,1)S(1)}, bf16[256,256]{1,0:T(8,128)(2,1)S(1)}, u32[]{:S(2)}, u32[]{:S(2)}) collective-permute-start(bf16[256,256]{1,0:T(8,128)(2,1)S(1)} %get-tuple-element.81), channel_id=1, source_target_pairs={{0,128},{128,256},{256,384},{384,0},{1,129},{129,257},{257,385},{3... | collective-permute-start | bytes 393224 | tf_op jit(solution)/shard_map/ppermute | solution.py:278
  245.7 25.0 %collective-permute-start.32 = (bf16[256,256]{1,0:T(8,128)(2,1)S(1)}, bf16[256,256]{1,0:T(8,128)(2,1)S(1)}, u32[]{:S(2)}, u32[]{:S(2)}) collective-permute-start(bf16[256,256]{1,0:T(8,128)(2,1)S(1)} %get-tuple-element.82), channel_id=1, source_target_pairs={{0,256},{128,384},{256,0},{384,128},{1,257},{129,385},{257,1},{385... | collective-permute-start | bytes 393224 | tf_op jit(solution)/shard_map/ppermute | solution.py:278
  250.2 20.5 %collective-permute-start.33 = (bf16[256,256]{1,0:T(8,128)(2,1)S(1)}, bf16[256,256]{1,0:T(8,128)(2,1)S(1)}, u32[]{:S(2)}, u32[]{:S(2)}) collective-permute-start(bf16[256,256]{1,0:T(8,128)(2,1)S(1)} %get-tuple-element.83), channel_id=1, source_target_pairs={{0,384},{128,0},{256,128},{384,256},{1,385},{129,1},{257,129},{385... | collective-permute-start | bytes 393224 | tf_op jit(solution)/shard_map/ppermute | solution.py:278
  254.2 16.5 %collective-permute-start.30 = (f32[72,256]{1,0:T(8,128)S(1)}, f32[72,256]{1,0:T(8,128)S(1)}, u32[]{:S(2)}, u32[]{:S(2)}) collective-permute-start(f32[72,256]{1,0:T(8,128)S(1)} %get-tuple-element.79), channel_id=1, source_target_pairs={{0,512},{512,0},{1,513},{513,1},{2,514},{514,2},{3,515},{515,3},{4... | collective-permute-start | bytes 221192 | tf_op jit(solution)/shard_map/ppermute | solution.py:274
  270.9 21.0 %collective-permute-start.35 = (f32[72,256]{1,0:T(8,128)S(1)}, f32[72,256]{1,0:T(8,128)S(1)}, u32[]{:S(2)}, u32[]{:S(2)}) collective-permute-start(f32[72,256]{1,0:T(8,128)S(1)} %get-tuple-element.86.own), channel_id=1, source_target_pairs={{0,128},{128,256},{256,384},{384,0},{1,129},{129,257},{257,385},{3... | collective-permute-start | bytes 221192 | tf_op jit(solution)/shard_map/ppermute | solution.py:278
  272.8 19.1 %collective-permute-start.36 = (f32[72,256]{1,0:T(8,128)S(1)}, f32[72,256]{1,0:T(8,128)S(1)}, u32[]{:S(2)}, u32[]{:S(2)}) collective-permute-start(f32[72,256]{1,0:T(8,128)S(1)} %get-tuple-element.86.own), channel_id=1, source_target_pairs={{0,256},{128,384},{256,0},{384,128},{1,257},{129,385},{257,1},{385... | collective-permute-start | bytes 221192 | tf_op jit(solution)/shard_map/ppermute | solution.py:278
  275.5 16.4 %collective-permute-start.37 = (f32[72,256]{1,0:T(8,128)S(1)}, f32[72,256]{1,0:T(8,128)S(1)}, u32[]{:S(2)}, u32[]{:S(2)}) collective-permute-start(f32[72,256]{1,0:T(8,128)S(1)} %get-tuple-element.86.own), channel_id=1, source_target_pairs={{0,384},{128,0},{256,128},{384,256},{1,385},{129,1},{257,129},{385... | collective-permute-start | bytes 221192 | tf_op jit(solution)/shard_map/ppermute | solution.py:278
  279.3 19.6 %collective-permute-start.34 = (bf16[128,256]{1,0:T(8,128)(2,1)S(1)}, bf16[128,256]{1,0:T(8,128)(2,1)S(1)}, u32[]{:S(2)}, u32[]{:S(2)}) collective-permute-start(bf16[128,256]{1,0:T(8,128)(2,1)S(1)} %get-tuple-element.85), channel_id=1, source_target_pairs={{0,512},{512,0},{1,513},{513,1},{2,514},{514,2},{3,515},{515,3},{4... | collective-permute-start | bytes 196616 | tf_op jit(solution)/shard_map/ppermute | solution.py:274
  292.5 7.6 %collective-permute-start.38 = (f32[264,256]{1,0:T(8,128)S(1)}, f32[264,256]{1,0:T(8,128)S(1)}, u32[]{:S(2)}, u32[]{:S(2)}) collective-permute-start(f32[264,256]{1,0:T(8,128)S(1)} %shard_map.154), channel_id=1, source_target_pairs={{0,64},{64,0},{1,65},{65,1},{2,66},{66,2},{3,67},{67,3},{4,68},{68... | collective-permute-start | bytes 811016 | tf_op jit(solution)/shard_map/ppermute | solution.py:274
Sparse Core Ops, SparseCore 0:
  151.1 53.6 all-gather.1

commit v3 on v2

--- a/solution.py
+++ b/solution.py
@@ -16,7 +16,7 @@
 CHUNK = QUAD * TILE + CNT
 VMEM = pl.BlockSpec(memory_space=pltpu.VMEM)
 SMEM = pl.BlockSpec(memory_space=pltpu.SMEM)
-AFTER = pl.BlockSpec(memory_space=pl.ANY)
+PIECE = 80
 
 
 def call(kernel, out, in_specs, *args, scratch=(), flops=0):
@@ -180,45 +180,72 @@
 def weight_cut_kernel(size, place, keep_in, recv, *outs):
     rows = HID // size
     bias = keep_in[HID:, :] + recv[HID:, :]
-    for d in range(size):
+    for d, ref in enumerate(outs):
         at = pl.multiple_of(lax.rem(place[1] + d, size) * rows, 8)
-        outs[d][0:rows, :] = keep_in[pl.ds(at, rows), :] + recv[pl.ds(at, rows), :]
-        outs[d][rows:, :] = bias
-
-
-def sum_kernel(*refs):
-    refs[-1][...] = functools.reduce(lambda a, b: a + b, [r[...] for r in refs[:-1]])
-
-
-def whole_kernel(rows, place, own, *refs):
-    recvs, whole = refs[:-1], refs[-1]
-    size = len(recvs) + 1
-    for d in range(size):
-        at = lax.rem(place[1] + size - d, size)
-        block = own if d == 0 else recvs[d - 1]
-        whole[pl.ds(pl.multiple_of(at * rows, 8), rows), :] = block[0:rows, :]
-
-        @pl.when(at == 0)
+        block = keep_in[pl.ds(at, rows), :] + recv[pl.ds(at, rows), :]
+        ref[...] = jnp.concatenate([block, bias, jnp.zeros_like(bias)], axis=0).astype(ref.dtype)
+
+
+def pack_kernel(scaled, *refs):
+    cuts, out = refs[:-1], refs[-1]
+    out[0:TILE, :] = scaled[...]
+    out[TILE:, :] = sum(c[...].astype(F32) for c in cuts).astype(BF)
+
+
+def two_terms(value):
+    hi = value.astype(BF)
+    return jnp.concatenate([hi, (value - hi.astype(F32)).astype(BF)], axis=0)
+
+
+def one_value(terms):
+    return terms[0:PIECE].astype(F32) + terms[PIECE:].astype(F32)
+
+
+def join_kernel(own, recv, out):
+    n = own.shape[0] - PIECE
+    out[0:n, :] = own[0:n, :]
+    out[n : 2 * n, :] = recv[0:n, :]
+    total = own[n:, :].astype(F32) + recv[n:, :].astype(F32)
+    out[2 * n :, :] = two_terms(total) if n == 2 * TILE else total.astype(BF)
+
+
+def piece_kernel(own, recv, out):
+    n = own.shape[0] - 2 * PIECE
+    out[...] = (one_value(own[n:, :]) + one_value(recv[n:, :])).astype(BF)
+
+
+def pick_kernel(slots, chunks, idx, place, *refs):
+    blocks, msg, held = refs[:chunks], refs[chunks], refs[chunks + 1]
+    for s in range(slots):
+        for o in range(chunks):
+
+            @pl.when((idx[s] >= 0) & (idx[s] // QUAD == o))
+            def _():
+                at = pl.multiple_of((idx[s] % QUAD) * TILE, TILE)
+                msg[s * TILE : (s + 1) * TILE, :] = blocks[o][pl.ds(at, TILE), :]
+
+        @pl.when(idx[s] < 0)
         def _():
-            whole[HID:, :] = block[rows:, :]
-
-
-def pick_kernel(slots, idx, local, after, msg):
-    for s in range(slots):
-        at = pl.multiple_of(jnp.maximum(idx[s], 0) * TILE, TILE)
-        msg[s * TILE : (s + 1) * TILE, :] = local[pl.ds(at, TILE), :]
-
-
-def back_kernel(slots, src, idx, live, tiles, recv, local, after, keep, send, acc, got):
+            msg[s * TILE : (s + 1) * TILE, :] = jnp.zeros((TILE, HID), BF)
+
+    for o in range(chunks):
+        held[lax.rem(place[2] + o, chunks)] = one_value(blocks[o][QUAD * TILE :, :])
+    msg[slots * TILE :, :] = two_terms(sum(held[o] for o in range(chunks)))
+
+
+def back_kernel(slots, chunks, src, idx, live, tiles, recv, *refs):
+    blocks, (keep, send, acc, got) = refs[:chunks], refs[chunks:]
     acc[...] = jnp.zeros_like(acc)
     for s in range(slots):
 
         @pl.when(live[s] > 0)
         def _():
-            @pl.when(idx[s] >= 0)
-            def _():
-                at = pl.multiple_of(idx[s] * TILE, TILE)
-                got[...] = local[pl.ds(at, TILE), :]
+            for o in range(chunks):
+
+                @pl.when((idx[s] >= 0) & (idx[s] // QUAD == o))
+                def _():
+                    at = pl.multiple_of((idx[s] % QUAD) * TILE, TILE)
+                    got[...] = blocks[o][pl.ds(at, TILE), :]
 
             @pl.when(idx[s] < 0)
             def _():
@@ -235,21 +262,31 @@
     send[...] = acc[half:, :].astype(BF)
 
 
-def back_cut_kernel(keep_in, recv, total, passed, keep, *sends):
-    passed[...] = total[...]
+def back_cut_kernel(keep_in, recv, piece_in, far_piece, keep, piece, *sends):
+    piece[...] = (piece_in[...].astype(F32) + far_piece[...].astype(F32)).astype(BF)
     rows = keep.shape[0]
     for d, ref in enumerate((keep,) + sends):
         at = d * rows
         got = keep_in[at : at + rows, :] + recv[at : at + rows, :].astype(F32)
-        ref[...] = got.astype(ref.dtype)
-
-
-def back_gather_kernel(count, total, *refs):
-    ins, passed, outs = refs[:count], refs[count], refs[count + 1 :]
-    passed[...] = total[...]
+        ref[0:rows, :] = got.astype(ref.dtype)
+        if d:
+            ref[rows:, :] = piece[...]
+
+
+def back_gather_kernel(size, place, near, piece, *refs):
+    recvs, (whole, *outs) = refs[: size - 1], refs[size - 1 :]
+    rows, n = HID // size, near.shape[0]
     for d, ref in enumerate(outs):
         at = slice(d * TILE, (d + 1) * TILE)
-        ref[...] = sum(r[at, :].astype(F32) for r in ins).astype(ref.dtype)
+        ref[...] = (near[at, :] + sum(r[at, :].astype(F32) for r in recvs)).astype(ref.dtype)
+    for d in range(size):
+        at = lax.rem(place[1] + size - d, size)
+        block = piece[...] if d == 0 else recvs[d - 1][n:, :]
+        whole[pl.ds(pl.multiple_of(at * rows, 16), rows), :] = block[0:rows, :]
+
+        @pl.when(at == 0)
+        def _():
+            whole[HID:, :] = block[rows:, :]
 
 
 def body(
@@ -289,13 +326,11 @@
         far = (dl >> 1) ^ (l >> 1)
         lay = ((far & 1) << 1) | (far >> 1)
         mine = (d >= 0) & ((dl & 1) == (l & 1))
-        ring = jnp.where(mine, ((d // nl - y) % ny) * QUAD + lay, -1)
-        return ring, jnp.where(mine, (d // nl) * QUAD + lay, -1)
+        return jnp.where(mine, ((d // nl - y) % ny) * QUAD + lay, -1)
 
     meta = jnp.zeros((8, TILE), jnp.int32).at[0, :slots].set(dest)
     other = flip(meta, "l", 1)[0, :slots]
-    own_ring, own_idx = place(dest)
-    other_ring, other_idx = place(other)
+    own_idx, other_idx = place(dest), place(other)
     where = jnp.stack([k, x, y]).astype(jnp.int32)
 
     panel = features
@@ -319,8 +354,8 @@
         [((CHUNK, HID), BF)] * ny,
         [SMEM, SMEM, SMEM, VMEM, VMEM, VMEM],
         src,
-        own_ring,
-        other_ring,
+        own_idx,
+        other_idx,
         tiles,
         panel,
         flip(msg, "l", 1),
@@ -374,10 +409,6 @@
         flops=6 * TILE * HID * HID,
     )
 
-    local = jnp.concatenate([scaled, flip(scaled, "l", 4)], axis=0)
-    local = jnp.concatenate([local, flip(local, "l", 2)], axis=0)
-    local = lax.all_gather(local, "y", axis=0, tiled=True)
-
     wide = ((HID + 8, HID), F32)
     w_keep, w_send, self_back = call(
         weight_kernel,
@@ -390,82 +421,88 @@
         w_self,
         flops=6 * TILE * HID * HID,
     )
-    w_rows = HID // nx
-    cut = ((w_rows + 8, HID), F32)
     cuts = call(
         functools.partial(weight_cut_kernel, nx),
-        [cut] * nx,
+        [((PIECE, HID), F32)] + [((PIECE, HID), BF)] * (nx - 1),
         [SMEM, VMEM, VMEM],
         where,
         w_keep,
         flip(w_send, "k", 1),
     )
     cuts = [cuts[0]] + [shift(cuts[d], "x", d) for d in range(1, nx)]
-    (total,) = call(sum_kernel, [cut], [VMEM] * nx, *cuts)
-
-    def add_over(value, axis, bit):
-        return value + flip(value, axis, bit) if bit < lax.axis_size(axis) else value
-
-    for bit in (1, 2, 4):
-        total = add_over(total, "l", bit)
-
+
+    (packed,) = call(
+        pack_kernel, [((TILE + PIECE, HID), BF)], [VMEM] * (nx + 1), scaled, *cuts
+    )
+    for bit, rows in ((4, 2 * TILE + PIECE), (2, 4 * TILE + 2 * PIECE)):
+        (packed,) = call(
+            join_kernel,
+            [((rows, HID), BF)],
+            [VMEM] * 2,
+            packed,
+            flip(packed, "l", bit),
+        )
+    blocks = [packed] * ny
+    up = down = packed
+    for step in range(1, ups + 1):
+        up = shift(up, "y", 1)
+        blocks[(-step) % ny] = up
+        if step <= downs:
+            down = shift(down, "y", -1)
+            blocks[step] = down
     (msg,) = call(
-        functools.partial(pick_kernel, slots),
-        [((slots * TILE, HID), BF)],
-        [SMEM, VMEM, AFTER],
+        functools.partial(pick_kernel, slots, ny),
+        [((slots * TILE + 2 * PIECE, HID), BF)],
+        [SMEM, SMEM] + [VMEM] * ny,
         other_idx,
-        local,
-        total,
-    )
-    total = add_over(add_over(total, "y", 1), "y", 2)
+        where,
+        *blocks,
+        scratch=[pltpu.VMEM((ny, PIECE, HID), F32)],
+    )
+    got = flip(msg, "l", 1)
+    (piece,) = call(piece_kernel, [((PIECE, HID), BF)], [VMEM] * 2, msg, got)
+    far_piece = flip(piece, "h", 1) if nh > 1 else jnp.zeros_like(piece)
+
     half = sources // 2 * TILE
     keep, send = call(
-        functools.partial(back_kernel, slots),
+        functools.partial(back_kernel, slots, ny),
         [((half, HID), F32), ((half, HID), BF)],
-        [SMEM, SMEM, SMEM, VMEM, VMEM, VMEM, AFTER],
+        [SMEM, SMEM, SMEM, VMEM, VMEM] + [VMEM] * ny,
         src,
         own_idx,
         live,
         tiles,
-        flip(msg, "l", 1),
-        local,
-        total,
+        got,
+        *blocks,
         scratch=[pltpu.VMEM((sources * TILE, HID), F32), pltpu.VMEM((TILE, HID), BF)],
         flops=tile_flops,
     )
     group = nh * TILE
-    total, *pieces = call(
+    near, piece, *sends = call(
         back_cut_kernel,
-        [cut, ((group, HID), F32)] + [((group, HID), BF)] * (nx - 1),
-        [VMEM] * 3,
+        [((group, HID), F32), ((PIECE, HID), BF)] + [((group + PIECE, HID), BF)] * (nx - 1),
+        [VMEM] * 4,
         keep,
         flip(send, "k", 1),
-        add_over(total, "y", 4),
-    )
-    got = [pieces[0]] + [shift(pieces[d], "x", d) for d in range(1, nx)]
-    total, *last = call(
+        piece,
+        far_piece,
+    )
+    whole, *last = call(
         functools.partial(back_gather_kernel, nx),
-        [cut, ((TILE, HID), F32)] + [node] * (nh - 1),
-        [VMEM] * (nx + 1),
-        add_over(total, "h", 1),
-        *got,
+        [((HID + 16, HID), BF), ((TILE, HID), F32)] + [node] * (nh - 1),
+        [SMEM] + [VMEM] * (nx + 1),
+        where,
+        near,
+        piece,
+        *[shift(sends[d - 1], "x", d) for d in range(1, nx)],
     )
     back = self_back + last[0]
     if nh > 1:
         back = back + flip(last[1], "h", 1).astype(F32)
     grad_features = back.astype(BF)
-
-    (whole,) = call(
-        functools.partial(whole_kernel, w_rows),
-        [wide],
-        [SMEM] + [VMEM] * nx,
-        where,
-        total,
-        *[shift(total, "x", d) for d in range(1, nx)],
-    )
     across = flip(whole, "k", 1)
-    first = jnp.where(k == 0, whole, across)
-    second = jnp.where(k == 0, across, whole)[:HID]
+    first = jnp.where(k == 0, whole, across).astype(F32)
+    second = jnp.where(k == 0, across, whole)[:HID].astype(F32)
     return hidden, grad_features, first[:HID], second, first[HID]
 
 

time: 310 us -> 296 us (0.955)
  starting transfers between devices: 197 us -> 172 us
  waiting for transfers between devices: 79.3 us -> 104 us
  between operations: 15.4 us -> 1.9 us
    ppermute x20 -> x14, starting transfers between devices: 137 us -> 102 us  [flip(): return lax.ppermute(value, axis, [(i, i ^ bit) for i in range(n)])]
    ppermute x19 -> x23, waiting for transfers between devices: 21.1 us -> 47.2 us  [shift(): return lax.ppermute(value, axis, [(i, (i + by) % n) for i in range(n)])]
    ppermute x19 -> x23, starting transfers between devices: 59.4 us -> 69.9 us  [shift(): return lax.ppermute(value, axis, [(i, (i + by) % n) for i in range(n)])]
    all_gather x1 -> x0, waiting for transfers between devices: 6.96 us -> none  [body(): local = lax.all_gather(local, 'y', axis=0, tiled=True)]
    ppermute x20 -> x14, waiting for transfers between devices: 51.2 us -> 56.8 us  [flip(): return lax.ppermute(value, axis, [(i, i ^ bit) for i in range(n)])]
    pallas_call x18 -> x20, Pallas kernels: 9.94 us -> 12.6 us  [call(): pl.pallas_call(kernel, out_shape=shapes, in_specs=in_specs, out_specs=[VM...]
  transfers between devices with their start and end apart: 40 -> 37, of which waited for: 23 -> 24; matrix products, arithmetic and copies ran while one was open for 1% -> 1% of each run, Pallas kernels for 1% -> 0%
where the time goes in v3:
time: 296 us; the launch traced here: 295 us
  starting transfers between devices  172 us (58%)
  waiting for transfers between devices  104 us (35%)
  Pallas kernels  12.6 us (4%)
    ppermute x14, starting transfers between devices, flip(): return lax.ppermute(value, axis, [(i, i ^ bit) for i in range(n)])  102 us
    ppermute x23, starting transfers between devices, shift(): return lax.ppermute(value, axis, [(i, (i + by) % n) for i in range(n)])  69.9 us
    ppermute x14, waiting for transfers between devices, flip(): return lax.ppermute(value, axis, [(i, i ^ bit) for i in range(n)])  56.8 us
    ppermute x23, waiting for transfers between devices, shift(): return lax.ppermute(value, axis, [(i, (i + by) % n) for i in range(n)])  47.2 us
    pallas_call x20, Pallas kernels, call(): pl.pallas_call(kernel, out_shape=shapes, in_specs=in_specs, out_specs=[VM...  12.6 us
  transfers between devices with their start and end apart: 37, of which 24 were waited for; matrix products, arithmetic and copies ran while one was open for 1% of the time, Pallas kernels for 0%

profile of v3, /device:TPU:1, one launch (start us, length us, event | category | flops | bytes accessed | tf_op | source)
XLA Modules:
  0.0 294.8 jit_solution(6607908686518277669)
XLA Ops:
  0.6 19.9 %collective-permute-start.1 = (bf16[128,256]{1,0:T(8,128)(2,1)}, bf16[128,256]{1,0:T(8,128)(2,1)S(1)}, u32[]{:S(2)}, u32[]{:S(2)}) collective-permute-start(bf16[128,256]{1,0:T(8,128)(2,1)} %features.3), channel_id=1, source_target_pairs={{0,512},{512,0},{1,513},{513,1},{2,514},{514,2},{3,515},{515,3},{4... | collective-permute-start | bytes 196616 | tf_op jit(solution)/shard_map/ppermute | solution.py:311
  21.4 1.2 collective-permute-done.1
  22.6 4.4 %collective-permute-start.2 = (bf16[256,256]{1,0:T(8,128)(2,1)S(1)}, bf16[256,256]{1,0:T(8,128)(2,1)S(1)}, u32[]{:S(2)}, u32[]{:S(2)}) collective-permute-start(bf16[256,256]{1,0:T(8,128)(2,1)S(1)} %get-tuple-element.95), channel_id=1, source_target_pairs={{0,384},{128,0},{256,128},{384,256},{1,385},{129,1},{257,129},{385... | collective-permute-start | bytes 393224 | tf_op jit(solution)/shard_map/ppermute | solution.py:315
  27.0 2.4 collective-permute-start.3
  29.4 2.5 collective-permute-start.4
  32.0 2.2 collective-permute-done.3
  34.2 2.1 collective-permute-done.4
  36.4 9.0 %collective-permute-start.5 = (bf16[1024,256]{1,0:T(8,128)(2,1)S(1)}, bf16[1024,256]{1,0:T(8,128)(2,1)S(1)}, u32[]{:S(2)}, u32[]{:S(2)}) collective-permute-start(bf16[1024,256]{1,0:T(8,128)(2,1)S(1)} %get-tuple-element.87), channel_id=1, source_target_pairs={{0,64},{64,0},{1,65},{65,1},{2,66},{66,2},{3,67},{67,3},{4,68},{68... | collective-permute-start | bytes 1572872 | tf_op jit(solution)/shard_map/ppermute | solution.py:311
  46.9 1.0 shard_map.137
  47.9 1.9 collective-permute-start.6
  49.9 3.4 %collective-permute-start = (s32[8,128]{1,0:T(8,128)S(1)}, s32[8,128]{1,0:T(8,128)S(1)}, u32[]{:S(2)}, u32[]{:S(2)}) collective-permute-start(s32[8,128]{1,0:T(8,128)S(1)} %scatter.4), channel_id=1, source_target_pairs={{0,1},{1,0},{2,3},{3,2},{4,5},{5,4},{6,7},{7,6},{8,9},{9,8},{10,11... | collective-permute-start | bytes 12296 | tf_op jit(solution)/shard_map/ppermute | solution.py:311
  53.3 12.7 %collective-permute-done = s32[8,128]{1,0:T(8,128)S(1)} collective-permute-done((s32[8,128]{1,0:T(8,128)S(1)}, s32[8,128]{1,0:T(8,128)S(1)}, u32[]{:S(2)}, u32[]{:S(2)}) %collective-permute-start) | collective-permute-done | bytes 4128 | tf_op jit(solution)/shard_map/ppermute | solution.py:311
  66.1 1.9 shard_map.138
  68.0 2.3 collective-permute-start.7
  70.3 4.2 %collective-permute-start.11 = (bf16[528,256]{1,0:T(8,128)(2,1)S(1)}, bf16[528,256]{1,0:T(8,128)(2,1)S(1)}, u32[]{:S(2)}, u32[]{:S(2)}) collective-permute-start(bf16[528,256]{1,0:T(8,128)(2,1)S(1)} %get-tuple-element.59), channel_id=1, source_target_pairs={{0,56},{8,0},{16,8},{24,16},{32,24},{40,32},{48,40},{56,48},{1,57}... | collective-permute-start | bytes 811016 | tf_op jit(solution)/shard_map/ppermute | solution.py:315
  74.5 3.3 %collective-permute-done.7.recv = bf16[528,256]{1,0:T(8,128)(2,1)S(1)} collective-permute-done((bf16[528,256]{1,0:T(8,128)(2,1)S(1)}, bf16[528,256]{1,0:T(8,128)(2,1)S(1)}, u32[]{:S(2)}, u32[]{:S(2)}) %collective-permute-start.7) | collective-permute-done | bytes 270368 | tf_op jit(solution)/shard_map/ppermute | solution.py:315
  77.9 1.9 collective-permute-start.8
  79.9 4.6 %collective-permute-start.12 = (bf16[528,256]{1,0:T(8,128)(2,1)S(1)}, bf16[528,256]{1,0:T(8,128)(2,1)S(1)}, u32[]{:S(2)}, u32[]{:S(2)}) collective-permute-start(bf16[528,256]{1,0:T(8,128)(2,1)S(1)} %shard_map.142), channel_id=1, source_target_pairs={{0,56},{8,0},{16,8},{24,16},{32,24},{40,32},{48,40},{56,48},{1,57}... | collective-permute-start | bytes 811016 | tf_op jit(solution)/shard_map/ppermute | solution.py:315
  84.5 2.3 collective-permute-done.8.recv
  86.9 1.9 collective-permute-start.9
  88.9 4.6 %collective-permute-start.13 = (bf16[528,256]{1,0:T(8,128)(2,1)S(1)}, bf16[528,256]{1,0:T(8,128)(2,1)S(1)}, u32[]{:S(2)}, u32[]{:S(2)}) collective-permute-start(bf16[528,256]{1,0:T(8,128)(2,1)S(1)} %shard_map.143), channel_id=1, source_target_pairs={{0,56},{8,0},{16,8},{24,16},{32,24},{40,32},{48,40},{56,48},{1,57}... | collective-permute-start | bytes 811016 | tf_op jit(solution)/shard_map/ppermute | solution.py:315
  93.5 1.8 collective-permute-done.9.recv
  95.3 1.9 collective-permute-start.10
  97.3 6.5 %collective-permute-done.10.refs_1_ = bf16[528,256]{1,0:T(8,128)(2,1)S(1)} collective-permute-done((bf16[528,256]{1,0:T(8,128)(2,1)S(1)}, bf16[528,256]{1,0:T(8,128)(2,1)S(1)}, u32[]{:S(2)}, u32[]{:S(2)}) %collective-permute-start.10) | collective-permute-done | bytes 270368 | tf_op jit(solution)/shard_map/ppermute | solution.py:315
  103.9 3.8 %collective-permute-start.14 = (bf16[272,256]{1,0:T(8,128)(2,1)S(1)}, bf16[272,256]{1,0:T(8,128)(2,1)S(1)}, u32[]{:S(2)}, u32[]{:S(2)}) collective-permute-start(bf16[272,256]{1,0:T(8,128)(2,1)S(1)} %get-tuple-element.63), channel_id=1, source_target_pairs={{0,2},{1,3},{2,0},{3,1},{4,6},{5,7},{6,4},{7,5},{8,10},{9,11},{10,... | collective-permute-start | bytes 417800 | tf_op jit(solution)/shard_map/ppermute | solution.py:311
  107.7 2.9 collective-permute-done.14.recv
  110.6 8.4 %collective-permute-start.15 = (bf16[144,256]{1,0:T(8,128)(2,1)S(1)}, bf16[144,256]{1,0:T(8,128)(2,1)S(1)}, u32[]{:S(2)}, u32[]{:S(2)}) collective-permute-start(bf16[144,256]{1,0:T(8,128)(2,1)S(1)} %get-tuple-element.65), channel_id=1, source_target_pairs={{0,4},{1,5},{2,6},{3,7},{4,0},{5,1},{6,2},{7,3},{8,12},{9,13},{10,... | collective-permute-start | bytes 221192 | tf_op jit(solution)/shard_map/ppermute | solution.py:311
  119.1 1.6 collective-permute-done.15.recv
  121.4 1.0 shard_map.146
  123.2 12.3 %collective-permute-start.16 = (f32[264,256]{1,0:T(8,128)S(1)}, f32[264,256]{1,0:T(8,128)S(1)}, u32[]{:S(2)}, u32[]{:S(2)}) collective-permute-start(f32[264,256]{1,0:T(8,128)S(1)} %get-tuple-element.72), channel_id=1, source_target_pairs={{0,64},{64,0},{1,65},{65,1},{2,66},{66,2},{3,67},{67,3},{4,68},{68... | collective-permute-start | bytes 811016 | tf_op jit(solution)/shard_map/ppermute | solution.py:311
  135.5 1.2 collective-permute-done.16.recv
  137.3 1.9 collective-permute-start.17
  139.2 4.3 %collective-permute-start.18 = (bf16[80,256]{1,0:T(8,128)(2,1)S(1)}, bf16[80,256]{1,0:T(8,128)(2,1)S(1)}, u32[]{:S(2)}, u32[]{:S(2)}) collective-permute-start(bf16[80,256]{1,0:T(8,128)(2,1)S(1)} %get-tuple-element.75), channel_id=1, source_target_pairs={{0,256},{128,384},{256,0},{384,128},{1,257},{129,385},{257,1},{385... | collective-permute-start | bytes 122888 | tf_op jit(solution)/shard_map/ppermute | solution.py:315
  143.5 2.1 collective-permute-start.19
  145.7 2.6 collective-permute-done.19.refs_3_
  148.3 4.6 %collective-permute-start.20 = (bf16[208,256]{1,0:T(8,128)(2,1)S(1)}, bf16[208,256]{1,0:T(8,128)(2,1)S(1)}, u32[]{:S(2)}, u32[]{:S(2)}) collective-permute-start(bf16[208,256]{1,0:T(8,128)(2,1)S(1)} %shard_map.149.own), channel_id=1, source_target_pairs={{0,4},{1,5},{2,6},{3,7},{4,0},{5,1},{6,2},{7,3},{8,12},{9,13},{10,... | collective-permute-start | bytes 319496 | tf_op jit(solution)/shard_map/ppermute | solution.py:311
  152.9 11.3 %collective-permute-done.20.recv = bf16[208,256]{1,0:T(8,128)(2,1)S(1)} collective-permute-done((bf16[208,256]{1,0:T(8,128)(2,1)S(1)}, bf16[208,256]{1,0:T(8,128)(2,1)S(1)}, u32[]{:S(2)}, u32[]{:S(2)}) %collective-permute-start.20) | collective-permute-done | bytes 106528 | tf_op jit(solution)/shard_map/ppermute | solution.py:311
  164.2 1.9 collective-permute-start.21
  166.1 9.7 %collective-permute-done.21.recv = bf16[336,256]{1,0:T(8,128)(2,1)S(1)} collective-permute-done((bf16[336,256]{1,0:T(8,128)(2,1)S(1)}, bf16[336,256]{1,0:T(8,128)(2,1)S(1)}, u32[]{:S(2)}, u32[]{:S(2)}) %collective-permute-start.21) | collective-permute-done | bytes 172064 | tf_op jit(solution)/shard_map/ppermute | solution.py:311
  175.9 1.9 collective-permute-start.25
  177.8 4.6 %collective-permute-start.22 = (bf16[672,256]{1,0:T(8,128)(2,1)S(1)}, bf16[672,256]{1,0:T(8,128)(2,1)S(1)}, u32[]{:S(2)}, u32[]{:S(2)}) collective-permute-start(bf16[672,256]{1,0:T(8,128)(2,1)S(1)} %shard_map.151.refs_0_), channel_id=1, source_target_pairs={{0,56},{8,0},{16,8},{24,16},{32,24},{40,32},{48,40},{56,48},{1,57}... | collective-permute-start | bytes 1032200 | tf_op jit(solution)/shard_map/ppermute | solution.py:315
  182.4 5.7 %collective-permute-done.25.refs_7_ = bf16[672,256]{1,0:T(8,128)(2,1)S(1)} collective-permute-done((bf16[672,256]{1,0:T(8,128)(2,1)S(1)}, bf16[672,256]{1,0:T(8,128)(2,1)S(1)}, u32[]{:S(2)}, u32[]{:S(2)}) %collective-permute-start.25) | collective-permute-done | bytes 344096 | tf_op jit(solution)/shard_map/ppermute | solution.py:315
  188.1 1.9 collective-permute-start.26
  190.1 4.6 %collective-permute-start.23 = (bf16[672,256]{1,0:T(8,128)(2,1)S(1)}, bf16[672,256]{1,0:T(8,128)(2,1)S(1)}, u32[]{:S(2)}, u32[]{:S(2)}) collective-permute-start(bf16[672,256]{1,0:T(8,128)(2,1)S(1)} %collective-permute-done.22.refs_1_), channel_id=1, source_target_pairs={{0,56},{8,0},{16,8},{24,16},{32,24},{40,32},{48,40},{56,48},{1,57}... | collective-permute-start | bytes 1032200 | tf_op jit(solution)/shard_map/ppermute | solution.py:315
  194.6 4.8 %collective-permute-done.26.refs_6_ = bf16[672,256]{1,0:T(8,128)(2,1)S(1)} collective-permute-done((bf16[672,256]{1,0:T(8,128)(2,1)S(1)}, bf16[672,256]{1,0:T(8,128)(2,1)S(1)}, u32[]{:S(2)}, u32[]{:S(2)}) %collective-permute-start.26) | collective-permute-done | bytes 344096 | tf_op jit(solution)/shard_map/ppermute | solution.py:315
  199.4 1.9 collective-permute-start.27
  201.4 4.6 %collective-permute-start.24 = (bf16[672,256]{1,0:T(8,128)(2,1)S(1)}, bf16[672,256]{1,0:T(8,128)(2,1)S(1)}, u32[]{:S(2)}, u32[]{:S(2)}) collective-permute-start(bf16[672,256]{1,0:T(8,128)(2,1)S(1)} %collective-permute-done.23.refs_2_), channel_id=1, source_target_pairs={{0,56},{8,0},{16,8},{24,16},{32,24},{40,32},{48,40},{56,48},{1,57}... | collective-permute-start | bytes 1032200 | tf_op jit(solution)/shard_map/ppermute | solution.py:315
  206.0 3.9 %collective-permute-done.27.refs_5_ = bf16[672,256]{1,0:T(8,128)(2,1)S(1)} collective-permute-done((bf16[672,256]{1,0:T(8,128)(2,1)S(1)}, bf16[672,256]{1,0:T(8,128)(2,1)S(1)}, u32[]{:S(2)}, u32[]{:S(2)}) %collective-permute-start.27) | collective-permute-done | bytes 344096 | tf_op jit(solution)/shard_map/ppermute | solution.py:315
  209.8 1.9 collective-permute-start.28
  211.8 7.3 %collective-permute-done.28.refs_4_ = bf16[672,256]{1,0:T(8,128)(2,1)S(1)} collective-permute-done((bf16[672,256]{1,0:T(8,128)(2,1)S(1)}, bf16[672,256]{1,0:T(8,128)(2,1)S(1)}, u32[]{:S(2)}, u32[]{:S(2)}) %collective-permute-start.28) | collective-permute-done | bytes 344096 | tf_op jit(solution)/shard_map/ppermute | solution.py:315
  219.0 1.9 shard_map.152.own
  221.0 1.9 collective-permute-start.29
  222.9 13.5 %collective-permute-done.29.recv = bf16[1440,256]{1,0:T(8,128)(2,1)S(1)} collective-permute-done((bf16[1440,256]{1,0:T(8,128)(2,1)S(1)}, bf16[1440,256]{1,0:T(8,128)(2,1)S(1)}, u32[]{:S(2)}, u32[]{:S(2)}) %collective-permute-start.29) | collective-permute-done | bytes 737312 | tf_op jit(solution)/shard_map/ppermute | solution.py:311
  236.5 4.0 %shard_map.153 = (f32[1024,256]{1,0:T(8,128)S(1)}, bf16[1024,256]{1,0:T(8,128)(2,1)S(1)}) custom-call(s32[10]{0:T(128)S(1)} %xor_add_fusion.src, s32[10]{0:T(128)S(1)} %and_select_fusion.6.idx, s32[10]{0:T(128)S(1)} %compare_convert_fusion.1.live, bf16[10,128,128]{2,1,0:T(8,128)(2,1)S(1)} %get-tuple-element.52.tiles, ...), custom_call_target="tpu_custom_call" | custom-call | flops 83886080 | bytes 5390456 | tf_op jit(solution)/shard_map/pallas_call | solution.py:26
  240.5 6.6 %collective-permute-start.30 = (bf16[1024,256]{1,0:T(8,128)(2,1)S(1)}, bf16[1024,256]{1,0:T(8,128)(2,1)S(1)}, u32[]{:S(2)}, u32[]{:S(2)}) collective-permute-start(bf16[1024,256]{1,0:T(8,128)(2,1)S(1)} %get-tuple-element.78), channel_id=1, source_target_pairs={{0,64},{64,0},{1,65},{65,1},{2,66},{66,2},{3,67},{67,3},{4,68},{68... | collective-permute-start | bytes 1572872 | tf_op jit(solution)/shard_map/ppermute | solution.py:311
  247.1 11.9 %collective-permute-start.31 = (bf16[80,256]{1,0:T(8,128)(2,1)S(1)}, bf16[80,256]{1,0:T(8,128)(2,1)S(1)}, u32[]{:S(2)}, u32[]{:S(2)}) collective-permute-start(bf16[80,256]{1,0:T(8,128)(2,1)S(1)} %shard_map.154.piece_in), channel_id=1, source_target_pairs={{0,512},{512,0},{1,513},{513,1},{2,514},{514,2},{3,515},{515,3},{4... | collective-permute-start | bytes 122888 | tf_op jit(solution)/shard_map/ppermute | solution.py:311
  259.1 1.5 collective-permute-done.31.far_piece
  260.7 2.6 collective-permute-start.32
  263.3 4.5 %collective-permute-start.33 = (bf16[336,256]{1,0:T(8,128)(2,1)S(1)}, bf16[336,256]{1,0:T(8,128)(2,1)S(1)}, u32[]{:S(2)}, u32[]{:S(2)}) collective-permute-start(bf16[336,256]{1,0:T(8,128)(2,1)S(1)} %get-tuple-element.82), channel_id=1, source_target_pairs={{0,256},{128,384},{256,0},{384,128},{1,257},{129,385},{257,1},{385... | collective-permute-start | bytes 516104 | tf_op jit(solution)/shard_map/ppermute | solution.py:315
  267.8 2.3 collective-permute-start.34
  270.2 2.9 collective-permute-done.33.refs_1_
  273.1 1.8 collective-permute-done.34.refs_2_
  275.5 12.0 %collective-permute-start.35 = (bf16[128,256]{1,0:T(8,128)(2,1)S(1)}, bf16[128,256]{1,0:T(8,128)(2,1)S(1)}, u32[]{:S(2)}, u32[]{:S(2)}) collective-permute-start(bf16[128,256]{1,0:T(8,128)(2,1)S(1)} %get-tuple-element.85), channel_id=1, source_target_pairs={{0,512},{512,0},{1,513},{513,1},{2,514},{514,2},{3,515},{515,3},{4... | collective-permute-start | bytes 196616 | tf_op jit(solution)/shard_map/ppermute | solution.py:311
  287.6 4.2 %collective-permute-start.36 = (bf16[272,256]{1,0:T(8,128)(2,1)S(1)}, bf16[272,256]{1,0:T(8,128)(2,1)S(1)}, u32[]{:S(2)}, u32[]{:S(2)}) collective-permute-start(bf16[272,256]{1,0:T(8,128)(2,1)S(1)} %get-tuple-element.86), channel_id=1, source_target_pairs={{0,64},{64,0},{1,65},{65,1},{2,66},{66,2},{3,67},{67,3},{4,68},{68... | collective-permute-start | bytes 417800 | tf_op jit(solution)/shard_map/ppermute | solution.py:311
  (66 shorter events, 8.4 us)
Async XLA Ops:
  0.6 21.9 %collective-permute-start.1 = (bf16[128,256]{1,0:T(8,128)(2,1)}, bf16[128,256]{1,0:T(8,128)(2,1)S(1)}, u32[]{:S(2)}, u32[]{:S(2)}) collective-permute-start(bf16[128,256]{1,0:T(8,128)(2,1)} %features.3), channel_id=1, source_target_pairs={{0,512},{512,0},{1,513},{513,1},{2,514},{514,2},{3,515},{515,3},{4... | collective-permute-start | bytes 196616 | tf_op jit(solution)/shard_map/ppermute | solution.py:311
  22.6 9.4 %collective-permute-start.2 = (bf16[256,256]{1,0:T(8,128)(2,1)S(1)}, bf16[256,256]{1,0:T(8,128)(2,1)S(1)}, u32[]{:S(2)}, u32[]{:S(2)}) collective-permute-start(bf16[256,256]{1,0:T(8,128)(2,1)S(1)} %get-tuple-element.95), channel_id=1, source_target_pairs={{0,384},{128,0},{256,128},{384,256},{1,385},{129,1},{257,129},{385... | collective-permute-start | bytes 393224 | tf_op jit(solution)/shard_map/ppermute | solution.py:315
  27.0 7.2 %collective-permute-start.3 = (bf16[256,256]{1,0:T(8,128)(2,1)S(1)}, bf16[256,256]{1,0:T(8,128)(2,1)S(1)}, u32[]{:S(2)}, u32[]{:S(2)}) collective-permute-start(bf16[256,256]{1,0:T(8,128)(2,1)S(1)} %get-tuple-element.95), channel_id=1, source_target_pairs={{0,256},{128,384},{256,0},{384,128},{1,257},{129,385},{257,1},{385... | collective-permute-start | bytes 393224 | tf_op jit(solution)/shard_map/ppermute | solution.py:315
  29.4 6.9 %collective-permute-start.4 = (bf16[256,256]{1,0:T(8,128)(2,1)S(1)}, bf16[256,256]{1,0:T(8,128)(2,1)S(1)}, u32[]{:S(2)}, u32[]{:S(2)}) collective-permute-start(bf16[256,256]{1,0:T(8,128)(2,1)S(1)} %get-tuple-element.95), channel_id=1, source_target_pairs={{0,128},{128,256},{256,384},{384,0},{1,129},{129,257},{257,385},{3... | collective-permute-start | bytes 393224 | tf_op jit(solution)/shard_map/ppermute | solution.py:315
  34.2 11.8 %copy-start.7 = (s32[1,1,10]{2,1,0:T(1,128)S(1)}, s32[1,1,10]{2,1,0:T(1,128)}, u32[]{:S(2)}) copy-start(s32[1,1,10]{2,1,0:T(1,128)} %param.15) | copy-start | bytes 124
  36.3 10.5 %copy-start = (s32[1,1,10,128,128]{4,3,2,1,0:T(8,128)S(1)}, s32[1,1,10,128,128]{4,3,2,1,0:T(8,128)}, u32[]{:S(2)}) copy-start(s32[1,1,10,128,128]{4,3,2,1,0:T(8,128)} %param.13) | copy-start | bytes 1966084
  36.4 10.5 %collective-permute-start.5 = (bf16[1024,256]{1,0:T(8,128)(2,1)S(1)}, bf16[1024,256]{1,0:T(8,128)(2,1)S(1)}, u32[]{:S(2)}, u32[]{:S(2)}) collective-permute-start(bf16[1024,256]{1,0:T(8,128)(2,1)S(1)} %get-tuple-element.87), channel_id=1, source_target_pairs={{0,64},{64,0},{1,65},{65,1},{2,66},{66,2},{3,67},{67,3},{4,68},{68... | collective-permute-start | bytes 1572872 | tf_op jit(solution)/shard_map/ppermute | solution.py:311
  47.9 1.9 copy-start.8
  47.9 18.1 %collective-permute-start.6 = (bf16[1296,256]{1,0:T(8,128)(2,1)S(1)}, bf16[1296,256]{1,0:T(8,128)(2,1)S(1)}, u32[]{:S(2)}, u32[]{:S(2)}) collective-permute-start(bf16[1296,256]{1,0:T(8,128)(2,1)S(1)} %get-tuple-element.53), channel_id=1, source_target_pairs={{0,1},{1,0},{2,3},{3,2},{4,5},{5,4},{6,7},{7,6},{8,9},{9,8},{10,11... | collective-permute-start | bytes 1990664 | tf_op jit(solution)/shard_map/ppermute | solution.py:311
  49.9 16.1 %collective-permute-start = (s32[8,128]{1,0:T(8,128)S(1)}, s32[8,128]{1,0:T(8,128)S(1)}, u32[]{:S(2)}, u32[]{:S(2)}) collective-permute-start(s32[8,128]{1,0:T(8,128)S(1)} %scatter.4), channel_id=1, source_target_pairs={{0,1},{1,0},{2,3},{3,2},{4,5},{5,4},{6,7},{7,6},{8,9},{9,8},{10,11... | collective-permute-start | bytes 12296 | tf_op jit(solution)/shard_map/ppermute | solution.py:311
  68.0 9.8 %collective-permute-start.7 = (bf16[528,256]{1,0:T(8,128)(2,1)S(1)}, bf16[528,256]{1,0:T(8,128)(2,1)S(1)}, u32[]{:S(2)}, u32[]{:S(2)}) collective-permute-start(bf16[528,256]{1,0:T(8,128)(2,1)S(1)} %get-tuple-element.55), channel_id=1, source_target_pairs={{0,8},{8,16},{16,24},{24,32},{32,40},{40,48},{48,56},{56,0},{1,9},... | collective-permute-start | bytes 811016 | tf_op jit(solution)/shard_map/ppermute | solution.py:315
  70.3 9.5 %collective-permute-start.11 = (bf16[528,256]{1,0:T(8,128)(2,1)S(1)}, bf16[528,256]{1,0:T(8,128)(2,1)S(1)}, u32[]{:S(2)}, u32[]{:S(2)}) collective-permute-start(bf16[528,256]{1,0:T(8,128)(2,1)S(1)} %get-tuple-element.59), channel_id=1, source_target_pairs={{0,56},{8,0},{16,8},{24,16},{32,24},{40,32},{48,40},{56,48},{1,57}... | collective-permute-start | bytes 811016 | tf_op jit(solution)/shard_map/ppermute | solution.py:315
  77.9 8.9 %collective-permute-start.8 = (bf16[528,256]{1,0:T(8,128)(2,1)S(1)}, bf16[528,256]{1,0:T(8,128)(2,1)S(1)}, u32[]{:S(2)}, u32[]{:S(2)}) collective-permute-start(bf16[528,256]{1,0:T(8,128)(2,1)S(1)} %shard_map.139), channel_id=1, source_target_pairs={{0,8},{8,16},{16,24},{24,32},{32,40},{40,48},{48,56},{56,0},{1,9},... | collective-permute-start | bytes 811016 | tf_op jit(solution)/shard_map/ppermute | solution.py:315
  79.9 8.9 %collective-permute-start.12 = (bf16[528,256]{1,0:T(8,128)(2,1)S(1)}, bf16[528,256]{1,0:T(8,128)(2,1)S(1)}, u32[]{:S(2)}, u32[]{:S(2)}) collective-permute-start(bf16[528,256]{1,0:T(8,128)(2,1)S(1)} %shard_map.142), channel_id=1, source_target_pairs={{0,56},{8,0},{16,8},{24,16},{32,24},{40,32},{48,40},{56,48},{1,57}... | collective-permute-start | bytes 811016 | tf_op jit(solution)/shard_map/ppermute | solution.py:315
  86.9 8.4 %collective-permute-start.9 = (bf16[528,256]{1,0:T(8,128)(2,1)S(1)}, bf16[528,256]{1,0:T(8,128)(2,1)S(1)}, u32[]{:S(2)}, u32[]{:S(2)}) collective-permute-start(bf16[528,256]{1,0:T(8,128)(2,1)S(1)} %shard_map.140), channel_id=1, source_target_pairs={{0,8},{8,16},{16,24},{24,32},{32,40},{40,48},{48,56},{56,0},{1,9},... | collective-permute-start | bytes 811016 | tf_op jit(solution)/shard_map/ppermute | solution.py:315
  88.9 8.4 %collective-permute-start.13 = (bf16[528,256]{1,0:T(8,128)(2,1)S(1)}, bf16[528,256]{1,0:T(8,128)(2,1)S(1)}, u32[]{:S(2)}, u32[]{:S(2)}) collective-permute-start(bf16[528,256]{1,0:T(8,128)(2,1)S(1)} %shard_map.143), channel_id=1, source_target_pairs={{0,56},{8,0},{16,8},{24,16},{32,24},{40,32},{48,40},{56,48},{1,57}... | collective-permute-start | bytes 811016 | tf_op jit(solution)/shard_map/ppermute | solution.py:315
  95.3 8.4 %collective-permute-start.10 = (bf16[528,256]{1,0:T(8,128)(2,1)S(1)}, bf16[528,256]{1,0:T(8,128)(2,1)S(1)}, u32[]{:S(2)}, u32[]{:S(2)}) collective-permute-start(bf16[528,256]{1,0:T(8,128)(2,1)S(1)} %shard_map.141), channel_id=1, source_target_pairs={{0,8},{8,16},{16,24},{24,32},{32,40},{40,48},{48,56},{56,0},{1,9},... | collective-permute-start | bytes 811016 | tf_op jit(solution)/shard_map/ppermute | solution.py:315
  103.9 6.7 %collective-permute-start.14 = (bf16[272,256]{1,0:T(8,128)(2,1)S(1)}, bf16[272,256]{1,0:T(8,128)(2,1)S(1)}, u32[]{:S(2)}, u32[]{:S(2)}) collective-permute-start(bf16[272,256]{1,0:T(8,128)(2,1)S(1)} %get-tuple-element.63), channel_id=1, source_target_pairs={{0,2},{1,3},{2,0},{3,1},{4,6},{5,7},{6,4},{7,5},{8,10},{9,11},{10,... | collective-permute-start | bytes 417800 | tf_op jit(solution)/shard_map/ppermute | solution.py:311
  110.6 10.2 %copy-start.1 = (bf16[128,256]{1,0:T(8,128)(2,1)S(1)}, bf16[128,256]{1,0:T(8,128)(2,1)}, u32[]{:S(2)}) copy-start(bf16[128,256]{1,0:T(8,128)(2,1)} %features.3) | copy-start | bytes 196612
  110.6 10.2 %copy-start.2 = (bf16[256,256]{1,0:T(8,128)(2,1)S(1)}, bf16[256,256]{1,0:T(8,128)(2,1)}, u32[]{:S(2)}) copy-start(bf16[256,256]{1,0:T(8,128)(2,1)} %w_self.3) | copy-start | bytes 393220
  110.6 10.2 %copy-start.3 = (bf16[256,256]{1,0:T(8,128)(2,1)S(1)}, bf16[256,256]{1,0:T(8,128)(2,1)}, u32[]{:S(2)}) copy-start(bf16[256,256]{1,0:T(8,128)(2,1)} %w_neigh.1) | copy-start | bytes 393220
  110.6 10.2 %copy-start.4 = (bf16[128,256]{1,0:T(8,128)(2,1)S(1)}, bf16[128,256]{1,0:T(8,128)(2,1)}, u32[]{:S(2)}) copy-start(bf16[128,256]{1,0:T(8,128)(2,1)} %grad_out.1) | copy-start | bytes 196612
  110.6 10.1 %collective-permute-start.15 = (bf16[144,256]{1,0:T(8,128)(2,1)S(1)}, bf16[144,256]{1,0:T(8,128)(2,1)S(1)}, u32[]{:S(2)}, u32[]{:S(2)}) collective-permute-start(bf16[144,256]{1,0:T(8,128)(2,1)S(1)} %get-tuple-element.65), channel_id=1, source_target_pairs={{0,4},{1,5},{2,6},{3,7},{4,0},{5,1},{6,2},{7,3},{8,12},{9,13},{10,... | collective-permute-start | bytes 221192 | tf_op jit(solution)/shard_map/ppermute | solution.py:311
  120.7 0.7 copy-start.5
  120.7 0.7 copy-start.6
  123.2 13.5 %collective-permute-start.16 = (f32[264,256]{1,0:T(8,128)S(1)}, f32[264,256]{1,0:T(8,128)S(1)}, u32[]{:S(2)}, u32[]{:S(2)}) collective-permute-start(f32[264,256]{1,0:T(8,128)S(1)} %get-tuple-element.72), channel_id=1, source_target_pairs={{0,64},{64,0},{1,65},{65,1},{2,66},{66,2},{3,67},{67,3},{4,68},{68... | collective-permute-start | bytes 811016 | tf_op jit(solution)/shard_map/ppermute | solution.py:311
  137.3 8.4 %collective-permute-start.17 = (bf16[80,256]{1,0:T(8,128)(2,1)S(1)}, bf16[80,256]{1,0:T(8,128)(2,1)S(1)}, u32[]{:S(2)}, u32[]{:S(2)}) collective-permute-start(bf16[80,256]{1,0:T(8,128)(2,1)S(1)} %get-tuple-element.74), channel_id=1, source_target_pairs={{0,128},{128,256},{256,384},{384,0},{1,129},{129,257},{257,385},{3... | collective-permute-start | bytes 122888 | tf_op jit(solution)/shard_map/ppermute | solution.py:315
  139.2 6.5 %collective-permute-start.18 = (bf16[80,256]{1,0:T(8,128)(2,1)S(1)}, bf16[80,256]{1,0:T(8,128)(2,1)S(1)}, u32[]{:S(2)}, u32[]{:S(2)}) collective-permute-start(bf16[80,256]{1,0:T(8,128)(2,1)S(1)} %get-tuple-element.75), channel_id=1, source_target_pairs={{0,256},{128,384},{256,0},{384,128},{1,257},{129,385},{257,1},{385... | collective-permute-start | bytes 122888 | tf_op jit(solution)/shard_map/ppermute | solution.py:315
  143.5 4.7 %collective-permute-start.19 = (bf16[80,256]{1,0:T(8,128)(2,1)S(1)}, bf16[80,256]{1,0:T(8,128)(2,1)S(1)}, u32[]{:S(2)}, u32[]{:S(2)}) collective-permute-start(bf16[80,256]{1,0:T(8,128)(2,1)S(1)} %get-tuple-element.76), channel_id=1, source_target_pairs={{0,384},{128,0},{256,128},{384,256},{1,385},{129,1},{257,129},{385... | collective-permute-start | bytes 122888 | tf_op jit(solution)/shard_map/ppermute | solution.py:315
  148.3 15.9 %collective-permute-start.20 = (bf16[208,256]{1,0:T(8,128)(2,1)S(1)}, bf16[208,256]{1,0:T(8,128)(2,1)S(1)}, u32[]{:S(2)}, u32[]{:S(2)}) collective-permute-start(bf16[208,256]{1,0:T(8,128)(2,1)S(1)} %shard_map.149.own), channel_id=1, source_target_pairs={{0,4},{1,5},{2,6},{3,7},{4,0},{5,1},{6,2},{7,3},{8,12},{9,13},{10,... | collective-permute-start | bytes 319496 | tf_op jit(solution)/shard_map/ppermute | solution.py:311
  164.2 11.6 %collective-permute-start.21 = (bf16[336,256]{1,0:T(8,128)(2,1)S(1)}, bf16[336,256]{1,0:T(8,128)(2,1)S(1)}, u32[]{:S(2)}, u32[]{:S(2)}) collective-permute-start(bf16[336,256]{1,0:T(8,128)(2,1)S(1)} %shard_map.150.own), channel_id=1, source_target_pairs={{0,2},{1,3},{2,0},{3,1},{4,6},{5,7},{6,4},{7,5},{8,10},{9,11},{10,... | collective-permute-start | bytes 516104 | tf_op jit(solution)/shard_map/ppermute | solution.py:311
  175.9 12.2 %collective-permute-start.25 = (bf16[672,256]{1,0:T(8,128)(2,1)S(1)}, bf16[672,256]{1,0:T(8,128)(2,1)S(1)}, u32[]{:S(2)}, u32[]{:S(2)}) collective-permute-start(bf16[672,256]{1,0:T(8,128)(2,1)S(1)} %shard_map.151.refs_0_), channel_id=1, source_target_pairs={{0,8},{8,16},{16,24},{24,32},{32,40},{40,48},{48,56},{56,0},{1,9},... | collective-permute-start | bytes 1032200 | tf_op jit(solution)/shard_map/ppermute | solution.py:315
  177.8 12.2 %collective-permute-start.22 = (bf16[672,256]{1,0:T(8,128)(2,1)S(1)}, bf16[672,256]{1,0:T(8,128)(2,1)S(1)}, u32[]{:S(2)}, u32[]{:S(2)}) collective-permute-start(bf16[672,256]{1,0:T(8,128)(2,1)S(1)} %shard_map.151.refs_0_), channel_id=1, source_target_pairs={{0,56},{8,0},{16,8},{24,16},{32,24},{40,32},{48,40},{56,48},{1,57}... | collective-permute-start | bytes 1032200 | tf_op jit(solution)/shard_map/ppermute | solution.py:315
  188.1 11.3 %collective-permute-start.26 = (bf16[672,256]{1,0:T(8,128)(2,1)S(1)}, bf16[672,256]{1,0:T(8,128)(2,1)S(1)}, u32[]{:S(2)}, u32[]{:S(2)}) collective-permute-start(bf16[672,256]{1,0:T(8,128)(2,1)S(1)} %collective-permute-done.25.refs_7_), channel_id=1, source_target_pairs={{0,8},{8,16},{16,24},{24,32},{32,40},{40,48},{48,56},{56,0},{1,9},... | collective-permute-start | bytes 1032200 | tf_op jit(solution)/shard_map/ppermute | solution.py:315
  190.1 11.3 %collective-permute-start.23 = (bf16[672,256]{1,0:T(8,128)(2,1)S(1)}, bf16[672,256]{1,0:T(8,128)(2,1)S(1)}, u32[]{:S(2)}, u32[]{:S(2)}) collective-permute-start(bf16[672,256]{1,0:T(8,128)(2,1)S(1)} %collective-permute-done.22.refs_1_), channel_id=1, source_target_pairs={{0,56},{8,0},{16,8},{24,16},{32,24},{40,32},{48,40},{56,48},{1,57}... | collective-permute-start | bytes 1032200 | tf_op jit(solution)/shard_map/ppermute | solution.py:315
  199.4 10.4 %collective-permute-start.27 = (bf16[672,256]{1,0:T(8,128)(2,1)S(1)}, bf16[672,256]{1,0:T(8,128)(2,1)S(1)}, u32[]{:S(2)}, u32[]{:S(2)}) collective-permute-start(bf16[672,256]{1,0:T(8,128)(2,1)S(1)} %collective-permute-done.26.refs_6_), channel_id=1, source_target_pairs={{0,8},{8,16},{16,24},{24,32},{32,40},{40,48},{48,56},{56,0},{1,9},... | collective-permute-start | bytes 1032200 | tf_op jit(solution)/shard_map/ppermute | solution.py:315
  201.4 10.4 %collective-permute-start.24 = (bf16[672,256]{1,0:T(8,128)(2,1)S(1)}, bf16[672,256]{1,0:T(8,128)(2,1)S(1)}, u32[]{:S(2)}, u32[]{:S(2)}) collective-permute-start(bf16[672,256]{1,0:T(8,128)(2,1)S(1)} %collective-permute-done.23.refs_2_), channel_id=1, source_target_pairs={{0,56},{8,0},{16,8},{24,16},{32,24},{40,32},{48,40},{56,48},{1,57}... | collective-permute-start | bytes 1032200 | tf_op jit(solution)/shard_map/ppermute | solution.py:315
  209.8 9.2 %collective-permute-start.28 = (bf16[672,256]{1,0:T(8,128)(2,1)S(1)}, bf16[672,256]{1,0:T(8,128)(2,1)S(1)}, u32[]{:S(2)}, u32[]{:S(2)}) collective-permute-start(bf16[672,256]{1,0:T(8,128)(2,1)S(1)} %collective-permute-done.27.refs_5_), channel_id=1, source_target_pairs={{0,8},{8,16},{16,24},{24,32},{32,40},{40,48},{48,56},{56,0},{1,9},... | collective-permute-start | bytes 1032200 | tf_op jit(solution)/shard_map/ppermute | solution.py:315
  221.0 15.5 %collective-permute-start.29 = (bf16[1440,256]{1,0:T(8,128)(2,1)S(1)}, bf16[1440,256]{1,0:T(8,128)(2,1)S(1)}, u32[]{:S(2)}, u32[]{:S(2)}) collective-permute-start(bf16[1440,256]{1,0:T(8,128)(2,1)S(1)} %shard_map.152.own), channel_id=1, source_target_pairs={{0,1},{1,0},{2,3},{3,2},{4,5},{5,4},{6,7},{7,6},{8,9},{9,8},{10,11... | collective-permute-start | bytes 2211848 | tf_op jit(solution)/shard_map/ppermute | solution.py:311
  240.5 20.1 %collective-permute-start.30 = (bf16[1024,256]{1,0:T(8,128)(2,1)S(1)}, bf16[1024,256]{1,0:T(8,128)(2,1)S(1)}, u32[]{:S(2)}, u32[]{:S(2)}) collective-permute-start(bf16[1024,256]{1,0:T(8,128)(2,1)S(1)} %get-tuple-element.78), channel_id=1, source_target_pairs={{0,64},{64,0},{1,65},{65,1},{2,66},{66,2},{3,67},{67,3},{4,68},{68... | collective-permute-start | bytes 1572872 | tf_op jit(solution)/shard_map/ppermute | solution.py:311
  247.1 13.5 %collective-permute-start.31 = (bf16[80,256]{1,0:T(8,128)(2,1)S(1)}, bf16[80,256]{1,0:T(8,128)(2,1)S(1)}, u32[]{:S(2)}, u32[]{:S(2)}) collective-permute-start(bf16[80,256]{1,0:T(8,128)(2,1)S(1)} %shard_map.154.piece_in), channel_id=1, source_target_pairs={{0,512},{512,0},{1,513},{513,1},{2,514},{514,2},{3,515},{515,3},{4... | collective-permute-start | bytes 122888 | tf_op jit(solution)/shard_map/ppermute | solution.py:311
  260.7 9.4 %collective-permute-start.32 = (bf16[336,256]{1,0:T(8,128)(2,1)S(1)}, bf16[336,256]{1,0:T(8,128)(2,1)S(1)}, u32[]{:S(2)}, u32[]{:S(2)}) collective-permute-start(bf16[336,256]{1,0:T(8,128)(2,1)S(1)} %get-tuple-element.81), channel_id=1, source_target_pairs={{0,128},{128,256},{256,384},{384,0},{1,129},{129,257},{257,385},{3... | collective-permute-start | bytes 516104 | tf_op jit(solution)/shard_map/ppermute | solution.py:315
  263.3 9.7 %collective-permute-start.33 = (bf16[336,256]{1,0:T(8,128)(2,1)S(1)}, bf16[336,256]{1,0:T(8,128)(2,1)S(1)}, u32[]{:S(2)}, u32[]{:S(2)}) collective-permute-start(bf16[336,256]{1,0:T(8,128)(2,1)S(1)} %get-tuple-element.82), channel_id=1, source_target_pairs={{0,256},{128,384},{256,0},{384,128},{1,257},{129,385},{257,1},{385... | collective-permute-start | bytes 516104 | tf_op jit(solution)/shard_map/ppermute | solution.py:315
  267.8 7.1 %collective-permute-start.34 = (bf16[336,256]{1,0:T(8,128)(2,1)S(1)}, bf16[336,256]{1,0:T(8,128)(2,1)S(1)}, u32[]{:S(2)}, u32[]{:S(2)}) collective-permute-start(bf16[336,256]{1,0:T(8,128)(2,1)S(1)} %get-tuple-element.83), channel_id=1, source_target_pairs={{0,384},{128,0},{256,128},{384,256},{1,385},{129,1},{257,129},{385... | collective-permute-start | bytes 516104 | tf_op jit(solution)/shard_map/ppermute | solution.py:315
  275.5 16.2 %collective-permute-start.35 = (bf16[128,256]{1,0:T(8,128)(2,1)S(1)}, bf16[128,256]{1,0:T(8,128)(2,1)S(1)}, u32[]{:S(2)}, u32[]{:S(2)}) collective-permute-start(bf16[128,256]{1,0:T(8,128)(2,1)S(1)} %get-tuple-element.85), channel_id=1, source_target_pairs={{0,512},{512,0},{1,513},{513,1},{2,514},{514,2},{3,515},{515,3},{4... | collective-permute-start | bytes 196616 | tf_op jit(solution)/shard_map/ppermute | solution.py:311
  287.6 5.2 %collective-permute-start.36 = (bf16[272,256]{1,0:T(8,128)(2,1)S(1)}, bf16[272,256]{1,0:T(8,128)(2,1)S(1)}, u32[]{:S(2)}, u32[]{:S(2)}) collective-permute-start(bf16[272,256]{1,0:T(8,128)(2,1)S(1)} %get-tuple-element.86), channel_id=1, source_target_pairs={{0,64},{64,0},{1,65},{65,1},{2,66},{66,2},{3,67},{67,3},{4,68},{68... | collective-permute-start | bytes 417800 | tf_op jit(solution)/shard_map/ppermute | solution.py:311

commit v4 on v3

--- a/solution.py
+++ b/solution.py
@@ -16,6 +16,7 @@
 CHUNK = QUAD * TILE + CNT
 VMEM = pl.BlockSpec(memory_space=pltpu.VMEM)
 SMEM = pl.BlockSpec(memory_space=pltpu.SMEM)
+AFTER = pl.BlockSpec(memory_space=pl.ANY)
 PIECE = 80
 
 
@@ -161,35 +162,27 @@
     scaled[...] = (back / degree).astype(BF)
 
 
-def weight_kernel(place, features, aggregate, grad_pre, w_self, keep, send, self_back):
+def weight_kernel(size, features, aggregate, grad_pre, w_self, cuts, self_back):
     g = grad_pre[...]
     contract = (((0,), (0,)), ((), ()))
     first = lax.dot_general(features[...], g, contract, preferred_element_type=F32)
     second = lax.dot_general(aggregate[...], g, contract, preferred_element_type=F32)
-    bias = jnp.broadcast_to(jnp.sum(g.astype(F32), axis=0, keepdims=True), (8, HID))
-    mine = place[0] == 0
-    keep[0:HID, :] = jnp.where(mine, first, second)
-    send[0:HID, :] = jnp.where(mine, second, first)
-    keep[HID:, :] = bias
-    send[HID:, :] = bias
+    bias = jnp.broadcast_to(jnp.sum(g.astype(F32), axis=0, keepdims=True), (PIECE - 64, HID))
+    rows = HID // size
+    for i in range(size):
+        for j, terms in enumerate((first, second)):
+            at = (i * 2 + j) * PIECE
+            cuts[at : at + rows, :] = terms[i * rows : (i + 1) * rows].astype(BF)
+            cuts[at + rows : at + PIECE, :] = bias[0 : PIECE - rows].astype(BF)
     self_back[...] = lax.dot_general(
         g, w_self[...], (((1,), (1,)), ((), ())), preferred_element_type=F32
     )
 
 
-def weight_cut_kernel(size, place, keep_in, recv, *outs):
-    rows = HID // size
-    bias = keep_in[HID:, :] + recv[HID:, :]
-    for d, ref in enumerate(outs):
-        at = pl.multiple_of(lax.rem(place[1] + d, size) * rows, 8)
-        block = keep_in[pl.ds(at, rows), :] + recv[pl.ds(at, rows), :]
-        ref[...] = jnp.concatenate([block, bias, jnp.zeros_like(bias)], axis=0).astype(ref.dtype)
-
-
-def pack_kernel(scaled, *refs):
-    cuts, out = refs[:-1], refs[-1]
+def pack_kernel(scaled, cuts, out):
     out[0:TILE, :] = scaled[...]
-    out[TILE:, :] = sum(c[...].astype(F32) for c in cuts).astype(BF)
+    pieces = [cuts[i : i + PIECE, :].astype(F32) for i in range(0, cuts.shape[0], PIECE)]
+    out[TILE:, :] = sum(pieces).astype(BF)
 
 
 def two_terms(value):
@@ -209,13 +202,12 @@
     out[2 * n :, :] = two_terms(total) if n == 2 * TILE else total.astype(BF)
 
 
-def piece_kernel(own, recv, out):
-    n = own.shape[0] - 2 * PIECE
-    out[...] = (one_value(own[n:, :]) + one_value(recv[n:, :])).astype(BF)
+def twin_kernel(own, recv, out):
+    out[...] = two_terms(own[...].astype(F32) + recv[...].astype(F32))
 
 
 def pick_kernel(slots, chunks, idx, place, *refs):
-    blocks, msg, held = refs[:chunks], refs[chunks], refs[chunks + 1]
+    blocks, (msg, piece, held) = refs[:chunks], refs[chunks:]
     for s in range(slots):
         for o in range(chunks):
 
@@ -230,10 +222,10 @@
 
     for o in range(chunks):
         held[lax.rem(place[2] + o, chunks)] = one_value(blocks[o][QUAD * TILE :, :])
-    msg[slots * TILE :, :] = two_terms(sum(held[o] for o in range(chunks)))
-
-
-def back_kernel(slots, chunks, src, idx, live, tiles, recv, *refs):
+    piece[...] = sum(held[o] for o in range(chunks)).astype(BF)
+
+
+def back_kernel(slots, chunks, src, idx, live, tiles, recv, after, *refs):
     blocks, (keep, send, acc, got) = refs[:chunks], refs[chunks:]
     acc[...] = jnp.zeros_like(acc)
     for s in range(slots):
@@ -262,8 +254,8 @@
     send[...] = acc[half:, :].astype(BF)
 
 
-def back_cut_kernel(keep_in, recv, piece_in, far_piece, keep, piece, *sends):
-    piece[...] = (piece_in[...].astype(F32) + far_piece[...].astype(F32)).astype(BF)
+def back_cut_kernel(keep_in, recv, twin, other_twin, keep, piece, *sends):
+    piece[...] = (one_value(twin[...]) + one_value(other_twin[...])).astype(BF)
     rows = keep.shape[0]
     for d, ref in enumerate((keep,) + sends):
         at = d * rows
@@ -287,6 +279,15 @@
         @pl.when(at == 0)
         def _():
             whole[HID:, :] = block[rows:, :]
+
+
+def last_kernel(place, self_back, near, far, whole, across, grads, first, second, bias):
+    grads[...] = (self_back[...] + near[...] + far[...].astype(F32)).astype(BF)
+    mine, other = whole[...].astype(F32), across[...].astype(F32)
+    own = place[0] == 0
+    first[...] = jnp.where(own, mine[0:HID], other[0:HID])
+    second[...] = jnp.where(own, other[0:HID], mine[0:HID])
+    bias[...] = jnp.where(own, mine[HID : HID + 1], other[HID : HID + 1])
 
 
 def body(
@@ -409,31 +410,19 @@
         flops=6 * TILE * HID * HID,
     )
 
-    wide = ((HID + 8, HID), F32)
-    w_keep, w_send, self_back = call(
-        weight_kernel,
-        [wide, wide, ((TILE, HID), F32)],
-        [SMEM] + [VMEM] * 4,
-        where,
+    cuts, self_back = call(
+        functools.partial(weight_kernel, nx),
+        [((nx * nk * PIECE, HID), BF), ((TILE, HID), F32)],
+        [VMEM] * 4,
         features,
         aggregate,
         grad_pre,
         w_self,
         flops=6 * TILE * HID * HID,
     )
-    cuts = call(
-        functools.partial(weight_cut_kernel, nx),
-        [((PIECE, HID), F32)] + [((PIECE, HID), BF)] * (nx - 1),
-        [SMEM, VMEM, VMEM],
-        where,
-        w_keep,
-        flip(w_send, "k", 1),
-    )
-    cuts = [cuts[0]] + [shift(cuts[d], "x", d) for d in range(1, nx)]
-
-    (packed,) = call(
-        pack_kernel, [((TILE + PIECE, HID), BF)], [VMEM] * (nx + 1), scaled, *cuts
-    )
+    cuts = lax.all_to_all(cuts, ("x", "k"), split_axis=0, concat_axis=0, tiled=True)
+
+    (packed,) = call(pack_kernel, [((TILE + PIECE, HID), BF)], [VMEM] * 2, scaled, cuts)
     for bit, rows in ((4, 2 * TILE + PIECE), (2, 4 * TILE + 2 * PIECE)):
         (packed,) = call(
             join_kernel,
@@ -450,9 +439,9 @@
         if step <= downs:
             down = shift(down, "y", -1)
             blocks[step] = down
-    (msg,) = call(
+    msg, piece = call(
         functools.partial(pick_kernel, slots, ny),
-        [((slots * TILE + 2 * PIECE, HID), BF)],
+        [((slots * TILE, HID), BF), ((PIECE, HID), BF)],
         [SMEM, SMEM] + [VMEM] * ny,
         other_idx,
         where,
@@ -460,19 +449,20 @@
         scratch=[pltpu.VMEM((ny, PIECE, HID), F32)],
     )
     got = flip(msg, "l", 1)
-    (piece,) = call(piece_kernel, [((PIECE, HID), BF)], [VMEM] * 2, msg, got)
     far_piece = flip(piece, "h", 1) if nh > 1 else jnp.zeros_like(piece)
+    (twin,) = call(twin_kernel, [((2 * PIECE, HID), BF)], [VMEM] * 2, piece, far_piece)
 
     half = sources // 2 * TILE
     keep, send = call(
         functools.partial(back_kernel, slots, ny),
         [((half, HID), F32), ((half, HID), BF)],
-        [SMEM, SMEM, SMEM, VMEM, VMEM] + [VMEM] * ny,
+        [SMEM, SMEM, SMEM, VMEM, VMEM, AFTER] + [VMEM] * ny,
         src,
         own_idx,
         live,
         tiles,
         got,
+        twin,
         *blocks,
         scratch=[pltpu.VMEM((sources * TILE, HID), F32), pltpu.VMEM((TILE, HID), BF)],
         flops=tile_flops,
@@ -484,8 +474,8 @@
         [VMEM] * 4,
         keep,
         flip(send, "k", 1),
-        piece,
-        far_piece,
+        twin,
+        flip(twin, "l", 1),
     )
     whole, *last = call(
         functools.partial(back_gather_kernel, nx),
@@ -496,14 +486,19 @@
         piece,
         *[shift(sends[d - 1], "x", d) for d in range(1, nx)],
     )
-    back = self_back + last[0]
-    if nh > 1:
-        back = back + flip(last[1], "h", 1).astype(F32)
-    grad_features = back.astype(BF)
-    across = flip(whole, "k", 1)
-    first = jnp.where(k == 0, whole, across).astype(F32)
-    second = jnp.where(k == 0, across, whole)[:HID].astype(F32)
-    return hidden, grad_features, first[:HID], second, first[HID]
+    far = flip(last[1], "h", 1) if nh > 1 else jnp.zeros((TILE, HID), BF)
+    grad_features, grad_w_self, grad_w_neigh, grad_bias = call(
+        last_kernel,
+        [node, ((HID, HID), F32), ((HID, HID), F32), ((1, HID), F32)],
+        [SMEM] + [VMEM] * 5,
+        where,
+        self_back,
+        last[0],
+        far,
+        whole,
+        flip(whole, "k", 1),
+    )
+    return hidden, grad_features, grad_w_self, grad_w_neigh, grad_bias.reshape(HID)
 
 
 def on_mesh(mesh):

time: 296 us -> 294 us (level)
  starting transfers between devices: 172 us -> 139 us
  blocking collectives: 0 us -> 18.1 us
  waiting for transfers between devices: 104 us -> 119 us
    ppermute x14, starting transfers between devices: 102 us -> 78 us  [flip(): return lax.ppermute(value, axis, [(i, i ^ bit) for i in range(n)])]
    all_to_all x0 -> x1, blocking collectives: none -> 18.1 us  [body(): lax.all_to_all(cuts, ('x', 'k'), split_axis=0, concat_axis=0, tiled=True)]
    ppermute x14, waiting for transfers between devices: 56.8 us -> 71.9 us  [flip(): return lax.ppermute(value, axis, [(i, i ^ bit) for i in range(n)])]
    ppermute x23 -> x20, starting transfers between devices: 69.9 us -> 61.2 us  [shift(): return lax.ppermute(value, axis, [(i, (i + by) % n) for i in range(n)])]
    ppermute x23 -> x20, waiting for transfers between devices: 47.2 us -> 46.9 us  [shift(): return lax.ppermute(value, axis, [(i, (i + by) % n) for i in range(n)])]
  transfers between devices with their start and end apart: 37 -> 34, of which waited for: 24 -> 22; matrix products, arithmetic and copies ran while one was open for 1% -> 0% of each run, Pallas kernels for 0% -> 0%
where the time goes in v4:
time: 294 us; the launch traced here: 293 us
  starting transfers between devices  139 us (47%)
  waiting for transfers between devices  119 us (40%)
  blocking collectives  18.1 us (6%)
  Pallas kernels  13.3 us (5%)
    ppermute x14, starting transfers between devices, flip(): return lax.ppermute(value, axis, [(i, i ^ bit) for i in range(n)])  78 us
    ppermute x14, waiting for transfers between devices, flip(): return lax.ppermute(value, axis, [(i, i ^ bit) for i in range(n)])  71.9 us
    ppermute x20, starting transfers between devices, shift(): return lax.ppermute(value, axis, [(i, (i + by) % n) for i in range(n)])  61.2 us
    ppermute x20, waiting for transfers between devices, shift(): return lax.ppermute(value, axis, [(i, (i + by) % n) for i in range(n)])  46.9 us
    all_to_all x1, blocking collectives, body(): lax.all_to_all(cuts, ('x', 'k'), split_axis=0, concat_axis=0, tiled=True)  18.1 us
    pallas_call x20, Pallas kernels, call(): pl.pallas_call(kernel, out_shape=shapes, in_specs=in_specs, out_specs=[VM...  13.3 us
  transfers between devices with their start and end apart: 34, of which 22 were waited for; matrix products, arithmetic and copies ran while one was open for 0% of the time, Pallas kernels for 0%

profile of v4, /device:TPU:1, one launch (start us, length us, event | category | flops | bytes accessed | tf_op | source)
XLA Modules:
  0.0 292.9 jit_solution(16911970726389009263)
XLA Ops:
  0.6 19.9 %collective-permute-start.1 = (bf16[128,256]{1,0:T(8,128)(2,1)}, bf16[128,256]{1,0:T(8,128)(2,1)S(1)}, u32[]{:S(2)}, u32[]{:S(2)}) collective-permute-start(bf16[128,256]{1,0:T(8,128)(2,1)} %features.3), channel_id=1, source_target_pairs={{0,512},{512,0},{1,513},{513,1},{2,514},{514,2},{3,515},{515,3},{4... | collective-permute-start | bytes 196616 | tf_op jit(solution)/shard_map/ppermute | solution.py:312
  20.6 0.9 constant_dynamic-update-slice_fusion.6
  21.4 1.2 collective-permute-done.1
  22.6 4.4 %collective-permute-start.2 = (bf16[256,256]{1,0:T(8,128)(2,1)S(1)}, bf16[256,256]{1,0:T(8,128)(2,1)S(1)}, u32[]{:S(2)}, u32[]{:S(2)}) collective-permute-start(bf16[256,256]{1,0:T(8,128)(2,1)S(1)} %get-tuple-element.97), channel_id=1, source_target_pairs={{0,384},{128,0},{256,128},{384,256},{1,385},{129,1},{257,129},{385... | collective-permute-start | bytes 393224 | tf_op jit(solution)/shard_map/ppermute | solution.py:316
  27.0 2.4 collective-permute-start.3
  29.4 2.5 collective-permute-start.4
  32.0 2.2 collective-permute-done.3
  34.2 2.1 collective-permute-done.4
  36.4 9.0 %collective-permute-start.5 = (bf16[1024,256]{1,0:T(8,128)(2,1)S(1)}, bf16[1024,256]{1,0:T(8,128)(2,1)S(1)}, u32[]{:S(2)}, u32[]{:S(2)}) collective-permute-start(bf16[1024,256]{1,0:T(8,128)(2,1)S(1)} %get-tuple-element.89), channel_id=1, source_target_pairs={{0,64},{64,0},{1,65},{65,1},{2,66},{66,2},{3,67},{67,3},{4,68},{68... | collective-permute-start | bytes 1572872 | tf_op jit(solution)/shard_map/ppermute | solution.py:312
  46.0 0.8 collective-permute-done.5
  46.9 1.0 shard_map.137
  47.9 1.9 collective-permute-start.6
  49.9 3.4 %collective-permute-start = (s32[8,128]{1,0:T(8,128)S(1)}, s32[8,128]{1,0:T(8,128)S(1)}, u32[]{:S(2)}, u32[]{:S(2)}) collective-permute-start(s32[8,128]{1,0:T(8,128)S(1)} %scatter.4), channel_id=1, source_target_pairs={{0,1},{1,0},{2,3},{3,2},{4,5},{5,4},{6,7},{7,6},{8,9},{9,8},{10,11... | collective-permute-start | bytes 12296 | tf_op jit(solution)/shard_map/ppermute | solution.py:312
  53.3 12.7 %collective-permute-done = s32[8,128]{1,0:T(8,128)S(1)} collective-permute-done((s32[8,128]{1,0:T(8,128)S(1)}, s32[8,128]{1,0:T(8,128)S(1)}, u32[]{:S(2)}, u32[]{:S(2)}) %collective-permute-start) | collective-permute-done | bytes 4128 | tf_op jit(solution)/shard_map/ppermute | solution.py:312
  66.1 2.3 shard_map.138
  68.3 1.9 collective-permute-start.7
  70.3 4.6 %collective-permute-start.11 = (bf16[528,256]{1,0:T(8,128)(2,1)S(1)}, bf16[528,256]{1,0:T(8,128)(2,1)S(1)}, u32[]{:S(2)}, u32[]{:S(2)}) collective-permute-start(bf16[528,256]{1,0:T(8,128)(2,1)S(1)} %get-tuple-element.60), channel_id=1, source_target_pairs={{0,56},{8,0},{16,8},{24,16},{32,24},{40,32},{48,40},{56,48},{1,57}... | collective-permute-start | bytes 811016 | tf_op jit(solution)/shard_map/ppermute | solution.py:316
  74.9 4.0 %collective-permute-done.7.recv = bf16[528,256]{1,0:T(8,128)(2,1)S(1)} collective-permute-done((bf16[528,256]{1,0:T(8,128)(2,1)S(1)}, bf16[528,256]{1,0:T(8,128)(2,1)S(1)}, u32[]{:S(2)}, u32[]{:S(2)}) %collective-permute-start.7) | collective-permute-done | bytes 270368 | tf_op jit(solution)/shard_map/ppermute | solution.py:316
  79.0 1.9 collective-permute-start.8
  81.0 4.6 %collective-permute-start.12 = (bf16[528,256]{1,0:T(8,128)(2,1)S(1)}, bf16[528,256]{1,0:T(8,128)(2,1)S(1)}, u32[]{:S(2)}, u32[]{:S(2)}) collective-permute-start(bf16[528,256]{1,0:T(8,128)(2,1)S(1)} %shard_map.142), channel_id=1, source_target_pairs={{0,56},{8,0},{16,8},{24,16},{32,24},{40,32},{48,40},{56,48},{1,57}... | collective-permute-start | bytes 811016 | tf_op jit(solution)/shard_map/ppermute | solution.py:316
  85.6 3.0 %collective-permute-done.8.recv = bf16[528,256]{1,0:T(8,128)(2,1)S(1)} collective-permute-done((bf16[528,256]{1,0:T(8,128)(2,1)S(1)}, bf16[528,256]{1,0:T(8,128)(2,1)S(1)}, u32[]{:S(2)}, u32[]{:S(2)}) %collective-permute-start.8) | collective-permute-done | bytes 270368 | tf_op jit(solution)/shard_map/ppermute | solution.py:316
  88.7 1.9 collective-permute-start.9
  90.7 4.6 %collective-permute-start.13 = (bf16[528,256]{1,0:T(8,128)(2,1)S(1)}, bf16[528,256]{1,0:T(8,128)(2,1)S(1)}, u32[]{:S(2)}, u32[]{:S(2)}) collective-permute-start(bf16[528,256]{1,0:T(8,128)(2,1)S(1)} %shard_map.143), channel_id=1, source_target_pairs={{0,56},{8,0},{16,8},{24,16},{32,24},{40,32},{48,40},{56,48},{1,57}... | collective-permute-start | bytes 811016 | tf_op jit(solution)/shard_map/ppermute | solution.py:316
  95.3 1.8 collective-permute-done.9.recv
  97.1 1.9 collective-permute-start.10
  99.1 6.5 %collective-permute-done.10.refs_1_ = bf16[528,256]{1,0:T(8,128)(2,1)S(1)} collective-permute-done((bf16[528,256]{1,0:T(8,128)(2,1)S(1)}, bf16[528,256]{1,0:T(8,128)(2,1)S(1)}, u32[]{:S(2)}, u32[]{:S(2)}) %collective-permute-start.10) | collective-permute-done | bytes 270368 | tf_op jit(solution)/shard_map/ppermute | solution.py:316
  105.7 2.0 collective-permute-start.14
  107.7 5.7 %collective-permute-done.14.recv = bf16[272,256]{1,0:T(8,128)(2,1)S(1)} collective-permute-done((bf16[272,256]{1,0:T(8,128)(2,1)S(1)}, bf16[272,256]{1,0:T(8,128)(2,1)S(1)}, u32[]{:S(2)}, u32[]{:S(2)}) %collective-permute-start.14) | collective-permute-done | bytes 139296 | tf_op jit(solution)/shard_map/ppermute | solution.py:312
  113.4 4.8 %collective-permute-start.15 = (bf16[144,256]{1,0:T(8,128)(2,1)S(1)}, bf16[144,256]{1,0:T(8,128)(2,1)S(1)}, u32[]{:S(2)}, u32[]{:S(2)}) collective-permute-start(bf16[144,256]{1,0:T(8,128)(2,1)S(1)} %get-tuple-element.66), channel_id=1, source_target_pairs={{0,4},{1,5},{2,6},{3,7},{4,0},{5,1},{6,2},{7,3},{8,12},{9,13},{10,... | collective-permute-start | bytes 221192 | tf_op jit(solution)/shard_map/ppermute | solution.py:312
  118.1 4.9 %collective-permute-done.15.recv = bf16[144,256]{1,0:T(8,128)(2,1)S(1)} collective-permute-done((bf16[144,256]{1,0:T(8,128)(2,1)S(1)}, bf16[144,256]{1,0:T(8,128)(2,1)S(1)}, u32[]{:S(2)}, u32[]{:S(2)}) %collective-permute-start.15) | collective-permute-done | bytes 73760 | tf_op jit(solution)/shard_map/ppermute | solution.py:312
  123.7 1.0 shard_map.146
  125.0 18.1 %all_to_all.11 = bf16[8,80,256]{2,1,0:T(8,128)(2,1)S(1)} all-to-all(bf16[8,80,256]{2,1,0:T(8,128)(2,1)S(1)} %bitcast.53), channel_id=1, replica_groups=mesh['h'=2,'x'=4,'k'=2,'y'=8,'l'=8] {'x','k'}, dimensions={0} | all-to-all | bytes 655360 | tf_op jit(solution)/shard_map/all_to_all | solution.py:423
  143.2 4.3 %collective-permute-start.16 = (bf16[208,256]{1,0:T(8,128)(2,1)S(1)}, bf16[208,256]{1,0:T(8,128)(2,1)S(1)}, u32[]{:S(2)}, u32[]{:S(2)}) collective-permute-start(bf16[208,256]{1,0:T(8,128)(2,1)S(1)} %shard_map.148.own), channel_id=1, source_target_pairs={{0,4},{1,5},{2,6},{3,7},{4,0},{5,1},{6,2},{7,3},{8,12},{9,13},{10,... | collective-permute-start | bytes 319496 | tf_op jit(solution)/shard_map/ppermute | solution.py:312
  147.5 12.6 %collective-permute-done.16.recv = bf16[208,256]{1,0:T(8,128)(2,1)S(1)} collective-permute-done((bf16[208,256]{1,0:T(8,128)(2,1)S(1)}, bf16[208,256]{1,0:T(8,128)(2,1)S(1)}, u32[]{:S(2)}, u32[]{:S(2)}) %collective-permute-start.16) | collective-permute-done | bytes 106528 | tf_op jit(solution)/shard_map/ppermute | solution.py:312
  160.1 1.9 collective-permute-start.17
  162.0 8.4 %collective-permute-done.17.recv = bf16[336,256]{1,0:T(8,128)(2,1)S(1)} collective-permute-done((bf16[336,256]{1,0:T(8,128)(2,1)S(1)}, bf16[336,256]{1,0:T(8,128)(2,1)S(1)}, u32[]{:S(2)}, u32[]{:S(2)}) %collective-permute-start.17) | collective-permute-done | bytes 172064 | tf_op jit(solution)/shard_map/ppermute | solution.py:312
  170.5 1.9 collective-permute-start.21
  172.4 4.6 %collective-permute-start.18 = (bf16[672,256]{1,0:T(8,128)(2,1)S(1)}, bf16[672,256]{1,0:T(8,128)(2,1)S(1)}, u32[]{:S(2)}, u32[]{:S(2)}) collective-permute-start(bf16[672,256]{1,0:T(8,128)(2,1)S(1)} %shard_map.150.refs_0_), channel_id=1, source_target_pairs={{0,56},{8,0},{16,8},{24,16},{32,24},{40,32},{48,40},{56,48},{1,57}... | collective-permute-start | bytes 1032200 | tf_op jit(solution)/shard_map/ppermute | solution.py:316
  177.0 5.7 %collective-permute-done.21.refs_7_ = bf16[672,256]{1,0:T(8,128)(2,1)S(1)} collective-permute-done((bf16[672,256]{1,0:T(8,128)(2,1)S(1)}, bf16[672,256]{1,0:T(8,128)(2,1)S(1)}, u32[]{:S(2)}, u32[]{:S(2)}) %collective-permute-start.21) | collective-permute-done | bytes 344096 | tf_op jit(solution)/shard_map/ppermute | solution.py:316
  182.7 1.9 collective-permute-start.22
  184.6 4.6 %collective-permute-start.19 = (bf16[672,256]{1,0:T(8,128)(2,1)S(1)}, bf16[672,256]{1,0:T(8,128)(2,1)S(1)}, u32[]{:S(2)}, u32[]{:S(2)}) collective-permute-start(bf16[672,256]{1,0:T(8,128)(2,1)S(1)} %collective-permute-done.18.refs_1_), channel_id=1, source_target_pairs={{0,56},{8,0},{16,8},{24,16},{32,24},{40,32},{48,40},{56,48},{1,57}... | collective-permute-start | bytes 1032200 | tf_op jit(solution)/shard_map/ppermute | solution.py:316
  189.2 4.8 %collective-permute-done.22.refs_6_ = bf16[672,256]{1,0:T(8,128)(2,1)S(1)} collective-permute-done((bf16[672,256]{1,0:T(8,128)(2,1)S(1)}, bf16[672,256]{1,0:T(8,128)(2,1)S(1)}, u32[]{:S(2)}, u32[]{:S(2)}) %collective-permute-start.22) | collective-permute-done | bytes 344096 | tf_op jit(solution)/shard_map/ppermute | solution.py:316
  194.0 1.9 collective-permute-start.23
  196.0 4.6 %collective-permute-start.20 = (bf16[672,256]{1,0:T(8,128)(2,1)S(1)}, bf16[672,256]{1,0:T(8,128)(2,1)S(1)}, u32[]{:S(2)}, u32[]{:S(2)}) collective-permute-start(bf16[672,256]{1,0:T(8,128)(2,1)S(1)} %collective-permute-done.19.refs_2_), channel_id=1, source_target_pairs={{0,56},{8,0},{16,8},{24,16},{32,24},{40,32},{48,40},{56,48},{1,57}... | collective-permute-start | bytes 1032200 | tf_op jit(solution)/shard_map/ppermute | solution.py:316
  200.5 3.9 %collective-permute-done.23.refs_5_ = bf16[672,256]{1,0:T(8,128)(2,1)S(1)} collective-permute-done((bf16[672,256]{1,0:T(8,128)(2,1)S(1)}, bf16[672,256]{1,0:T(8,128)(2,1)S(1)}, u32[]{:S(2)}, u32[]{:S(2)}) %collective-permute-start.23) | collective-permute-done | bytes 344096 | tf_op jit(solution)/shard_map/ppermute | solution.py:316
  204.4 1.9 collective-permute-start.24
  206.4 7.2 %collective-permute-done.24.refs_4_ = bf16[672,256]{1,0:T(8,128)(2,1)S(1)} collective-permute-done((bf16[672,256]{1,0:T(8,128)(2,1)S(1)}, bf16[672,256]{1,0:T(8,128)(2,1)S(1)}, u32[]{:S(2)}, u32[]{:S(2)}) %collective-permute-start.24) | collective-permute-done | bytes 344096 | tf_op jit(solution)/shard_map/ppermute | solution.py:316
  213.6 1.9 shard_map.151
  215.6 1.9 collective-permute-start.25
  217.5 11.5 %collective-permute-start.26 = (bf16[80,256]{1,0:T(8,128)(2,1)S(1)}, bf16[80,256]{1,0:T(8,128)(2,1)S(1)}, u32[]{:S(2)}, u32[]{:S(2)}) collective-permute-start(bf16[80,256]{1,0:T(8,128)(2,1)S(1)} %get-tuple-element.74.own), channel_id=1, source_target_pairs={{0,512},{512,0},{1,513},{513,1},{2,514},{514,2},{3,515},{515,3},{4... | collective-permute-start | bytes 122888 | tf_op jit(solution)/shard_map/ppermute | solution.py:312
  229.0 10.2 %collective-permute-done.26.recv = bf16[80,256]{1,0:T(8,128)(2,1)S(1)} collective-permute-done((bf16[80,256]{1,0:T(8,128)(2,1)S(1)}, bf16[80,256]{1,0:T(8,128)(2,1)S(1)}, u32[]{:S(2)}, u32[]{:S(2)}) %collective-permute-start.26) | collective-permute-done | bytes 40992 | tf_op jit(solution)/shard_map/ppermute | solution.py:312
  239.2 4.0 %shard_map.153 = (f32[1024,256]{1,0:T(8,128)S(1)}, bf16[1024,256]{1,0:T(8,128)(2,1)S(1)}) custom-call(s32[10]{0:T(128)S(1)} %xor_add_fusion.src, s32[10]{0:T(128)S(1)} %and_select_fusion.6.idx, s32[10]{0:T(128)S(1)} %compare_convert_fusion.1.live, bf16[10,128,128]{2,1,0:T(8,128)(2,1)S(1)} %get-tuple-element.53.tiles, ...), custom_call_target="tpu_custom_call" | custom-call | flops 83886080 | bytes 5390456 | tf_op jit(solution)/shard_map/pallas_call | solution.py:27
  243.3 8.3 %collective-permute-start.27 = (bf16[1024,256]{1,0:T(8,128)(2,1)S(1)}, bf16[1024,256]{1,0:T(8,128)(2,1)S(1)}, u32[]{:S(2)}, u32[]{:S(2)}) collective-permute-start(bf16[1024,256]{1,0:T(8,128)(2,1)S(1)} %get-tuple-element.76), channel_id=1, source_target_pairs={{0,64},{64,0},{1,65},{65,1},{2,66},{66,2},{3,67},{67,3},{4,68},{68... | collective-permute-start | bytes 1572872 | tf_op jit(solution)/shard_map/ppermute | solution.py:312
  251.6 3.1 %collective-permute-start.28 = (bf16[160,256]{1,0:T(8,128)(2,1)S(1)}, bf16[160,256]{1,0:T(8,128)(2,1)S(1)}, u32[]{:S(2)}, u32[]{:S(2)}) collective-permute-start(bf16[160,256]{1,0:T(8,128)(2,1)S(1)} %shard_map.152.after.twin), channel_id=1, source_target_pairs={{0,1},{1,0},{2,3},{3,2},{4,5},{5,4},{6,7},{7,6},{8,9},{9,8},{10,11... | collective-permute-start | bytes 245768 | tf_op jit(solution)/shard_map/ppermute | solution.py:312
  254.7 2.8 collective-permute-done.28.other_twin
  257.7 2.9 collective-permute-start.29
  260.6 3.7 %collective-permute-start.30 = (bf16[336,256]{1,0:T(8,128)(2,1)S(1)}, bf16[336,256]{1,0:T(8,128)(2,1)S(1)}, u32[]{:S(2)}, u32[]{:S(2)}) collective-permute-start(bf16[336,256]{1,0:T(8,128)(2,1)S(1)} %get-tuple-element.80), channel_id=1, source_target_pairs={{0,256},{128,384},{256,0},{384,128},{1,257},{129,385},{257,1},{385... | collective-permute-start | bytes 516104 | tf_op jit(solution)/shard_map/ppermute | solution.py:316
  264.3 2.6 collective-permute-start.31
  266.8 3.1 %collective-permute-done.30.refs_1_ = bf16[336,256]{1,0:T(8,128)(2,1)S(1)} collective-permute-done((bf16[336,256]{1,0:T(8,128)(2,1)S(1)}, bf16[336,256]{1,0:T(8,128)(2,1)S(1)}, u32[]{:S(2)}, u32[]{:S(2)}) %collective-permute-start.30) | collective-permute-done | bytes 172064 | tf_op jit(solution)/shard_map/ppermute | solution.py:316
  269.9 2.5 collective-permute-done.31.refs_2_
  273.0 3.3 %collective-permute-start.33 = (bf16[272,256]{1,0:T(8,128)(2,1)S(1)}, bf16[272,256]{1,0:T(8,128)(2,1)S(1)}, u32[]{:S(2)}, u32[]{:S(2)}) collective-permute-start(bf16[272,256]{1,0:T(8,128)(2,1)S(1)} %get-tuple-element.84.whole), channel_id=1, source_target_pairs={{0,64},{64,0},{1,65},{65,1},{2,66},{66,2},{3,67},{67,3},{4,68},{68... | collective-permute-start | bytes 417800 | tf_op jit(solution)/shard_map/ppermute | solution.py:312
  276.4 2.6 collective-permute-start.32
  279.0 12.6 %collective-permute-done.32.far = bf16[128,256]{1,0:T(8,128)(2,1)S(1)} collective-permute-done((bf16[128,256]{1,0:T(8,128)(2,1)S(1)}, bf16[128,256]{1,0:T(8,128)(2,1)S(1)}, u32[]{:S(2)}, u32[]{:S(2)}) %collective-permute-start.32) | collective-permute-done | bytes 65568 | tf_op jit(solution)/shard_map/ppermute | solution.py:312
  291.5 1.4 shard_map.156
  (56 shorter events, 2.6 us)
Async XLA Ops:
  0.6 21.9 %collective-permute-start.1 = (bf16[128,256]{1,0:T(8,128)(2,1)}, bf16[128,256]{1,0:T(8,128)(2,1)S(1)}, u32[]{:S(2)}, u32[]{:S(2)}) collective-permute-start(bf16[128,256]{1,0:T(8,128)(2,1)} %features.3), channel_id=1, source_target_pairs={{0,512},{512,0},{1,513},{513,1},{2,514},{514,2},{3,515},{515,3},{4... | collective-permute-start | bytes 196616 | tf_op jit(solution)/shard_map/ppermute | solution.py:312
  22.6 9.4 %collective-permute-start.2 = (bf16[256,256]{1,0:T(8,128)(2,1)S(1)}, bf16[256,256]{1,0:T(8,128)(2,1)S(1)}, u32[]{:S(2)}, u32[]{:S(2)}) collective-permute-start(bf16[256,256]{1,0:T(8,128)(2,1)S(1)} %get-tuple-element.97), channel_id=1, source_target_pairs={{0,384},{128,0},{256,128},{384,256},{1,385},{129,1},{257,129},{385... | collective-permute-start | bytes 393224 | tf_op jit(solution)/shard_map/ppermute | solution.py:316
  27.0 7.2 %collective-permute-start.3 = (bf16[256,256]{1,0:T(8,128)(2,1)S(1)}, bf16[256,256]{1,0:T(8,128)(2,1)S(1)}, u32[]{:S(2)}, u32[]{:S(2)}) collective-permute-start(bf16[256,256]{1,0:T(8,128)(2,1)S(1)} %get-tuple-element.97), channel_id=1, source_target_pairs={{0,256},{128,384},{256,0},{384,128},{1,257},{129,385},{257,1},{385... | collective-permute-start | bytes 393224 | tf_op jit(solution)/shard_map/ppermute | solution.py:316
  29.4 6.9 %collective-permute-start.4 = (bf16[256,256]{1,0:T(8,128)(2,1)S(1)}, bf16[256,256]{1,0:T(8,128)(2,1)S(1)}, u32[]{:S(2)}, u32[]{:S(2)}) collective-permute-start(bf16[256,256]{1,0:T(8,128)(2,1)S(1)} %get-tuple-element.97), channel_id=1, source_target_pairs={{0,128},{128,256},{256,384},{384,0},{1,129},{129,257},{257,385},{3... | collective-permute-start | bytes 393224 | tf_op jit(solution)/shard_map/ppermute | solution.py:316
  34.2 11.8 %copy-start.7 = (s32[1,1,10]{2,1,0:T(1,128)S(1)}, s32[1,1,10]{2,1,0:T(1,128)}, u32[]{:S(2)}) copy-start(s32[1,1,10]{2,1,0:T(1,128)} %param.15) | copy-start | bytes 124
  36.3 10.5 %copy-start = (s32[1,1,10,128,128]{4,3,2,1,0:T(8,128)S(1)}, s32[1,1,10,128,128]{4,3,2,1,0:T(8,128)}, u32[]{:S(2)}) copy-start(s32[1,1,10,128,128]{4,3,2,1,0:T(8,128)} %param.13) | copy-start | bytes 1966084
  36.4 10.5 %collective-permute-start.5 = (bf16[1024,256]{1,0:T(8,128)(2,1)S(1)}, bf16[1024,256]{1,0:T(8,128)(2,1)S(1)}, u32[]{:S(2)}, u32[]{:S(2)}) collective-permute-start(bf16[1024,256]{1,0:T(8,128)(2,1)S(1)} %get-tuple-element.89), channel_id=1, source_target_pairs={{0,64},{64,0},{1,65},{65,1},{2,66},{66,2},{3,67},{67,3},{4,68},{68... | collective-permute-start | bytes 1572872 | tf_op jit(solution)/shard_map/ppermute | solution.py:312
  47.9 1.9 copy-start.8
  47.9 18.1 %collective-permute-start.6 = (bf16[1296,256]{1,0:T(8,128)(2,1)S(1)}, bf16[1296,256]{1,0:T(8,128)(2,1)S(1)}, u32[]{:S(2)}, u32[]{:S(2)}) collective-permute-start(bf16[1296,256]{1,0:T(8,128)(2,1)S(1)} %get-tuple-element.54), channel_id=1, source_target_pairs={{0,1},{1,0},{2,3},{3,2},{4,5},{5,4},{6,7},{7,6},{8,9},{9,8},{10,11... | collective-permute-start | bytes 1990664 | tf_op jit(solution)/shard_map/ppermute | solution.py:312
  49.9 16.1 %collective-permute-start = (s32[8,128]{1,0:T(8,128)S(1)}, s32[8,128]{1,0:T(8,128)S(1)}, u32[]{:S(2)}, u32[]{:S(2)}) collective-permute-start(s32[8,128]{1,0:T(8,128)S(1)} %scatter.4), channel_id=1, source_target_pairs={{0,1},{1,0},{2,3},{3,2},{4,5},{5,4},{6,7},{7,6},{8,9},{9,8},{10,11... | collective-permute-start | bytes 12296 | tf_op jit(solution)/shard_map/ppermute | solution.py:312
  68.3 10.5 %collective-permute-start.7 = (bf16[528,256]{1,0:T(8,128)(2,1)S(1)}, bf16[528,256]{1,0:T(8,128)(2,1)S(1)}, u32[]{:S(2)}, u32[]{:S(2)}) collective-permute-start(bf16[528,256]{1,0:T(8,128)(2,1)S(1)} %get-tuple-element.56), channel_id=1, source_target_pairs={{0,8},{8,16},{16,24},{24,32},{32,40},{40,48},{48,56},{56,0},{1,9},... | collective-permute-start | bytes 811016 | tf_op jit(solution)/shard_map/ppermute | solution.py:316
  70.3 10.6 %collective-permute-start.11 = (bf16[528,256]{1,0:T(8,128)(2,1)S(1)}, bf16[528,256]{1,0:T(8,128)(2,1)S(1)}, u32[]{:S(2)}, u32[]{:S(2)}) collective-permute-start(bf16[528,256]{1,0:T(8,128)(2,1)S(1)} %get-tuple-element.60), channel_id=1, source_target_pairs={{0,56},{8,0},{16,8},{24,16},{32,24},{40,32},{48,40},{56,48},{1,57}... | collective-permute-start | bytes 811016 | tf_op jit(solution)/shard_map/ppermute | solution.py:316
  79.0 9.6 %collective-permute-start.8 = (bf16[528,256]{1,0:T(8,128)(2,1)S(1)}, bf16[528,256]{1,0:T(8,128)(2,1)S(1)}, u32[]{:S(2)}, u32[]{:S(2)}) collective-permute-start(bf16[528,256]{1,0:T(8,128)(2,1)S(1)} %shard_map.139), channel_id=1, source_target_pairs={{0,8},{8,16},{16,24},{24,32},{32,40},{40,48},{48,56},{56,0},{1,9},... | collective-permute-start | bytes 811016 | tf_op jit(solution)/shard_map/ppermute | solution.py:316
  81.0 9.6 %collective-permute-start.12 = (bf16[528,256]{1,0:T(8,128)(2,1)S(1)}, bf16[528,256]{1,0:T(8,128)(2,1)S(1)}, u32[]{:S(2)}, u32[]{:S(2)}) collective-permute-start(bf16[528,256]{1,0:T(8,128)(2,1)S(1)} %shard_map.142), channel_id=1, source_target_pairs={{0,56},{8,0},{16,8},{24,16},{32,24},{40,32},{48,40},{56,48},{1,57}... | collective-permute-start | bytes 811016 | tf_op jit(solution)/shard_map/ppermute | solution.py:316
  88.7 8.4 %collective-permute-start.9 = (bf16[528,256]{1,0:T(8,128)(2,1)S(1)}, bf16[528,256]{1,0:T(8,128)(2,1)S(1)}, u32[]{:S(2)}, u32[]{:S(2)}) collective-permute-start(bf16[528,256]{1,0:T(8,128)(2,1)S(1)} %shard_map.140), channel_id=1, source_target_pairs={{0,8},{8,16},{16,24},{24,32},{32,40},{40,48},{48,56},{56,0},{1,9},... | collective-permute-start | bytes 811016 | tf_op jit(solution)/shard_map/ppermute | solution.py:316
  90.7 8.4 %collective-permute-start.13 = (bf16[528,256]{1,0:T(8,128)(2,1)S(1)}, bf16[528,256]{1,0:T(8,128)(2,1)S(1)}, u32[]{:S(2)}, u32[]{:S(2)}) collective-permute-start(bf16[528,256]{1,0:T(8,128)(2,1)S(1)} %shard_map.143), channel_id=1, source_target_pairs={{0,56},{8,0},{16,8},{24,16},{32,24},{40,32},{48,40},{56,48},{1,57}... | collective-permute-start | bytes 811016 | tf_op jit(solution)/shard_map/ppermute | solution.py:316
  97.1 8.4 %collective-permute-start.10 = (bf16[528,256]{1,0:T(8,128)(2,1)S(1)}, bf16[528,256]{1,0:T(8,128)(2,1)S(1)}, u32[]{:S(2)}, u32[]{:S(2)}) collective-permute-start(bf16[528,256]{1,0:T(8,128)(2,1)S(1)} %shard_map.141), channel_id=1, source_target_pairs={{0,8},{8,16},{16,24},{24,32},{32,40},{40,48},{48,56},{56,0},{1,9},... | collective-permute-start | bytes 811016 | tf_op jit(solution)/shard_map/ppermute | solution.py:316
  105.7 7.7 %collective-permute-start.14 = (bf16[272,256]{1,0:T(8,128)(2,1)S(1)}, bf16[272,256]{1,0:T(8,128)(2,1)S(1)}, u32[]{:S(2)}, u32[]{:S(2)}) collective-permute-start(bf16[272,256]{1,0:T(8,128)(2,1)S(1)} %get-tuple-element.64), channel_id=1, source_target_pairs={{0,2},{1,3},{2,0},{3,1},{4,6},{5,7},{6,4},{7,5},{8,10},{9,11},{10,... | collective-permute-start | bytes 417800 | tf_op jit(solution)/shard_map/ppermute | solution.py:312
  113.3 9.7 %copy-start.1 = (bf16[128,256]{1,0:T(8,128)(2,1)S(1)}, bf16[128,256]{1,0:T(8,128)(2,1)}, u32[]{:S(2)}) copy-start(bf16[128,256]{1,0:T(8,128)(2,1)} %features.3) | copy-start | bytes 196612
  113.3 9.7 %copy-start.2 = (bf16[256,256]{1,0:T(8,128)(2,1)S(1)}, bf16[256,256]{1,0:T(8,128)(2,1)}, u32[]{:S(2)}) copy-start(bf16[256,256]{1,0:T(8,128)(2,1)} %w_self.3) | copy-start | bytes 393220
  113.3 9.7 %copy-start.3 = (bf16[256,256]{1,0:T(8,128)(2,1)S(1)}, bf16[256,256]{1,0:T(8,128)(2,1)}, u32[]{:S(2)}) copy-start(bf16[256,256]{1,0:T(8,128)(2,1)} %w_neigh.1) | copy-start | bytes 393220
  113.3 9.7 %copy-start.4 = (bf16[128,256]{1,0:T(8,128)(2,1)S(1)}, bf16[128,256]{1,0:T(8,128)(2,1)}, u32[]{:S(2)}) copy-start(bf16[128,256]{1,0:T(8,128)(2,1)} %grad_out.1) | copy-start | bytes 196612
  113.4 9.7 %collective-permute-start.15 = (bf16[144,256]{1,0:T(8,128)(2,1)S(1)}, bf16[144,256]{1,0:T(8,128)(2,1)S(1)}, u32[]{:S(2)}, u32[]{:S(2)}) collective-permute-start(bf16[144,256]{1,0:T(8,128)(2,1)S(1)} %get-tuple-element.66), channel_id=1, source_target_pairs={{0,4},{1,5},{2,6},{3,7},{4,0},{5,1},{6,2},{7,3},{8,12},{9,13},{10,... | collective-permute-start | bytes 221192 | tf_op jit(solution)/shard_map/ppermute | solution.py:312
  123.0 0.7 copy-start.5
  123.0 0.7 copy-start.6
  143.2 16.9 %collective-permute-start.16 = (bf16[208,256]{1,0:T(8,128)(2,1)S(1)}, bf16[208,256]{1,0:T(8,128)(2,1)S(1)}, u32[]{:S(2)}, u32[]{:S(2)}) collective-permute-start(bf16[208,256]{1,0:T(8,128)(2,1)S(1)} %shard_map.148.own), channel_id=1, source_target_pairs={{0,4},{1,5},{2,6},{3,7},{4,0},{5,1},{6,2},{7,3},{8,12},{9,13},{10,... | collective-permute-start | bytes 319496 | tf_op jit(solution)/shard_map/ppermute | solution.py:312
  160.1 10.4 %collective-permute-start.17 = (bf16[336,256]{1,0:T(8,128)(2,1)S(1)}, bf16[336,256]{1,0:T(8,128)(2,1)S(1)}, u32[]{:S(2)}, u32[]{:S(2)}) collective-permute-start(bf16[336,256]{1,0:T(8,128)(2,1)S(1)} %shard_map.149.own), channel_id=1, source_target_pairs={{0,2},{1,3},{2,0},{3,1},{4,6},{5,7},{6,4},{7,5},{8,10},{9,11},{10,... | collective-permute-start | bytes 516104 | tf_op jit(solution)/shard_map/ppermute | solution.py:312
  170.5 12.2 %collective-permute-start.21 = (bf16[672,256]{1,0:T(8,128)(2,1)S(1)}, bf16[672,256]{1,0:T(8,128)(2,1)S(1)}, u32[]{:S(2)}, u32[]{:S(2)}) collective-permute-start(bf16[672,256]{1,0:T(8,128)(2,1)S(1)} %shard_map.150.refs_0_), channel_id=1, source_target_pairs={{0,8},{8,16},{16,24},{24,32},{32,40},{40,48},{48,56},{56,0},{1,9},... | collective-permute-start | bytes 1032200 | tf_op jit(solution)/shard_map/ppermute | solution.py:316
  172.4 12.2 %collective-permute-start.18 = (bf16[672,256]{1,0:T(8,128)(2,1)S(1)}, bf16[672,256]{1,0:T(8,128)(2,1)S(1)}, u32[]{:S(2)}, u32[]{:S(2)}) collective-permute-start(bf16[672,256]{1,0:T(8,128)(2,1)S(1)} %shard_map.150.refs_0_), channel_id=1, source_target_pairs={{0,56},{8,0},{16,8},{24,16},{32,24},{40,32},{48,40},{56,48},{1,57}... | collective-permute-start | bytes 1032200 | tf_op jit(solution)/shard_map/ppermute | solution.py:316
  182.7 11.3 %collective-permute-start.22 = (bf16[672,256]{1,0:T(8,128)(2,1)S(1)}, bf16[672,256]{1,0:T(8,128)(2,1)S(1)}, u32[]{:S(2)}, u32[]{:S(2)}) collective-permute-start(bf16[672,256]{1,0:T(8,128)(2,1)S(1)} %collective-permute-done.21.refs_7_), channel_id=1, source_target_pairs={{0,8},{8,16},{16,24},{24,32},{32,40},{40,48},{48,56},{56,0},{1,9},... | collective-permute-start | bytes 1032200 | tf_op jit(solution)/shard_map/ppermute | solution.py:316
  184.6 11.3 %collective-permute-start.19 = (bf16[672,256]{1,0:T(8,128)(2,1)S(1)}, bf16[672,256]{1,0:T(8,128)(2,1)S(1)}, u32[]{:S(2)}, u32[]{:S(2)}) collective-permute-start(bf16[672,256]{1,0:T(8,128)(2,1)S(1)} %collective-permute-done.18.refs_1_), channel_id=1, source_target_pairs={{0,56},{8,0},{16,8},{24,16},{32,24},{40,32},{48,40},{56,48},{1,57}... | collective-permute-start | bytes 1032200 | tf_op jit(solution)/shard_map/ppermute | solution.py:316
  194.0 10.4 %collective-permute-start.23 = (bf16[672,256]{1,0:T(8,128)(2,1)S(1)}, bf16[672,256]{1,0:T(8,128)(2,1)S(1)}, u32[]{:S(2)}, u32[]{:S(2)}) collective-permute-start(bf16[672,256]{1,0:T(8,128)(2,1)S(1)} %collective-permute-done.22.refs_6_), channel_id=1, source_target_pairs={{0,8},{8,16},{16,24},{24,32},{32,40},{40,48},{48,56},{56,0},{1,9},... | collective-permute-start | bytes 1032200 | tf_op jit(solution)/shard_map/ppermute | solution.py:316
  196.0 10.5 %collective-permute-start.20 = (bf16[672,256]{1,0:T(8,128)(2,1)S(1)}, bf16[672,256]{1,0:T(8,128)(2,1)S(1)}, u32[]{:S(2)}, u32[]{:S(2)}) collective-permute-start(bf16[672,256]{1,0:T(8,128)(2,1)S(1)} %collective-permute-done.19.refs_2_), channel_id=1, source_target_pairs={{0,56},{8,0},{16,8},{24,16},{32,24},{40,32},{48,40},{56,48},{1,57}... | collective-permute-start | bytes 1032200 | tf_op jit(solution)/shard_map/ppermute | solution.py:316
  204.4 9.2 %collective-permute-start.24 = (bf16[672,256]{1,0:T(8,128)(2,1)S(1)}, bf16[672,256]{1,0:T(8,128)(2,1)S(1)}, u32[]{:S(2)}, u32[]{:S(2)}) collective-permute-start(bf16[672,256]{1,0:T(8,128)(2,1)S(1)} %collective-permute-done.23.refs_5_), channel_id=1, source_target_pairs={{0,8},{8,16},{16,24},{24,32},{32,40},{40,48},{48,56},{56,0},{1,9},... | collective-permute-start | bytes 1032200 | tf_op jit(solution)/shard_map/ppermute | solution.py:316
  215.6 23.7 %collective-permute-start.25 = (bf16[1280,256]{1,0:T(8,128)(2,1)S(1)}, bf16[1280,256]{1,0:T(8,128)(2,1)S(1)}, u32[]{:S(2)}, u32[]{:S(2)}) collective-permute-start(bf16[1280,256]{1,0:T(8,128)(2,1)S(1)} %get-tuple-element.73), channel_id=1, source_target_pairs={{0,1},{1,0},{2,3},{3,2},{4,5},{5,4},{6,7},{7,6},{8,9},{9,8},{10,11... | collective-permute-start | bytes 1966088 | tf_op jit(solution)/shard_map/ppermute | solution.py:312
  217.5 21.7 %collective-permute-start.26 = (bf16[80,256]{1,0:T(8,128)(2,1)S(1)}, bf16[80,256]{1,0:T(8,128)(2,1)S(1)}, u32[]{:S(2)}, u32[]{:S(2)}) collective-permute-start(bf16[80,256]{1,0:T(8,128)(2,1)S(1)} %get-tuple-element.74.own), channel_id=1, source_target_pairs={{0,512},{512,0},{1,513},{513,1},{2,514},{514,2},{3,515},{515,3},{4... | collective-permute-start | bytes 122888 | tf_op jit(solution)/shard_map/ppermute | solution.py:312
  243.3 14.3 %collective-permute-start.27 = (bf16[1024,256]{1,0:T(8,128)(2,1)S(1)}, bf16[1024,256]{1,0:T(8,128)(2,1)S(1)}, u32[]{:S(2)}, u32[]{:S(2)}) collective-permute-start(bf16[1024,256]{1,0:T(8,128)(2,1)S(1)} %get-tuple-element.76), channel_id=1, source_target_pairs={{0,64},{64,0},{1,65},{65,1},{2,66},{66,2},{3,67},{67,3},{4,68},{68... | collective-permute-start | bytes 1572872 | tf_op jit(solution)/shard_map/ppermute | solution.py:312
  251.6 6.0 %collective-permute-start.28 = (bf16[160,256]{1,0:T(8,128)(2,1)S(1)}, bf16[160,256]{1,0:T(8,128)(2,1)S(1)}, u32[]{:S(2)}, u32[]{:S(2)}) collective-permute-start(bf16[160,256]{1,0:T(8,128)(2,1)S(1)} %shard_map.152.after.twin), channel_id=1, source_target_pairs={{0,1},{1,0},{2,3},{3,2},{4,5},{5,4},{6,7},{7,6},{8,9},{9,8},{10,11... | collective-permute-start | bytes 245768 | tf_op jit(solution)/shard_map/ppermute | solution.py:312
  257.7 9.1 %collective-permute-start.29 = (bf16[336,256]{1,0:T(8,128)(2,1)S(1)}, bf16[336,256]{1,0:T(8,128)(2,1)S(1)}, u32[]{:S(2)}, u32[]{:S(2)}) collective-permute-start(bf16[336,256]{1,0:T(8,128)(2,1)S(1)} %get-tuple-element.79), channel_id=1, source_target_pairs={{0,128},{128,256},{256,384},{384,0},{1,129},{129,257},{257,385},{3... | collective-permute-start | bytes 516104 | tf_op jit(solution)/shard_map/ppermute | solution.py:316
  260.6 9.3 %collective-permute-start.30 = (bf16[336,256]{1,0:T(8,128)(2,1)S(1)}, bf16[336,256]{1,0:T(8,128)(2,1)S(1)}, u32[]{:S(2)}, u32[]{:S(2)}) collective-permute-start(bf16[336,256]{1,0:T(8,128)(2,1)S(1)} %get-tuple-element.80), channel_id=1, source_target_pairs={{0,256},{128,384},{256,0},{384,128},{1,257},{129,385},{257,1},{385... | collective-permute-start | bytes 516104 | tf_op jit(solution)/shard_map/ppermute | solution.py:316
  264.3 8.1 %collective-permute-start.31 = (bf16[336,256]{1,0:T(8,128)(2,1)S(1)}, bf16[336,256]{1,0:T(8,128)(2,1)S(1)}, u32[]{:S(2)}, u32[]{:S(2)}) collective-permute-start(bf16[336,256]{1,0:T(8,128)(2,1)S(1)} %get-tuple-element.81), channel_id=1, source_target_pairs={{0,384},{128,0},{256,128},{384,256},{1,385},{129,1},{257,129},{385... | collective-permute-start | bytes 516104 | tf_op jit(solution)/shard_map/ppermute | solution.py:316
  273.0 18.5 %collective-permute-start.33 = (bf16[272,256]{1,0:T(8,128)(2,1)S(1)}, bf16[272,256]{1,0:T(8,128)(2,1)S(1)}, u32[]{:S(2)}, u32[]{:S(2)}) collective-permute-start(bf16[272,256]{1,0:T(8,128)(2,1)S(1)} %get-tuple-element.84.whole), channel_id=1, source_target_pairs={{0,64},{64,0},{1,65},{65,1},{2,66},{66,2},{3,67},{67,3},{4,68},{68... | collective-permute-start | bytes 417800 | tf_op jit(solution)/shard_map/ppermute | solution.py:312
  276.4 15.2 %collective-permute-start.32 = (bf16[128,256]{1,0:T(8,128)(2,1)S(1)}, bf16[128,256]{1,0:T(8,128)(2,1)S(1)}, u32[]{:S(2)}, u32[]{:S(2)}) collective-permute-start(bf16[128,256]{1,0:T(8,128)(2,1)S(1)} %get-tuple-element.83), channel_id=1, source_target_pairs={{0,512},{512,0},{1,513},{513,1},{2,514},{514,2},{3,515},{515,3},{4... | collective-permute-start | bytes 196616 | tf_op jit(solution)/shard_map/ppermute | solution.py:312

commit v5 on v4

--- a/solution.py
+++ b/solution.py
@@ -16,7 +16,6 @@
 CHUNK = QUAD * TILE + CNT
 VMEM = pl.BlockSpec(memory_space=pltpu.VMEM)
 SMEM = pl.BlockSpec(memory_space=pltpu.SMEM)
-AFTER = pl.BlockSpec(memory_space=pl.ANY)
 PIECE = 80
 
 
@@ -179,12 +178,6 @@
     )
 
 
-def pack_kernel(scaled, cuts, out):
-    out[0:TILE, :] = scaled[...]
-    pieces = [cuts[i : i + PIECE, :].astype(F32) for i in range(0, cuts.shape[0], PIECE)]
-    out[TILE:, :] = sum(pieces).astype(BF)
-
-
 def two_terms(value):
     hi = value.astype(BF)
     return jnp.concatenate([hi, (value - hi.astype(F32)).astype(BF)], axis=0)
@@ -194,20 +187,27 @@
     return terms[0:PIECE].astype(F32) + terms[PIECE:].astype(F32)
 
 
-def join_kernel(own, recv, out):
-    n = own.shape[0] - PIECE
+def pair_kernel(own, recv, cuts, out):
+    out[0:TILE, :] = own[...]
+    out[TILE : 2 * TILE, :] = recv[...]
+    pieces = [cuts[i : i + PIECE, :].astype(F32) for i in range(0, cuts.shape[0], PIECE)]
+    out[2 * TILE :, :] = sum(pieces).astype(BF)
+
+
+def quad_kernel(own, recv, out):
+    n = 2 * TILE
     out[0:n, :] = own[0:n, :]
     out[n : 2 * n, :] = recv[0:n, :]
-    total = own[n:, :].astype(F32) + recv[n:, :].astype(F32)
-    out[2 * n :, :] = two_terms(total) if n == 2 * TILE else total.astype(BF)
-
-
-def twin_kernel(own, recv, out):
-    out[...] = two_terms(own[...].astype(F32) + recv[...].astype(F32))
+    out[2 * n :, :] = two_terms(own[n:, :].astype(F32) + recv[n:, :].astype(F32))
+
+
+def piece_kernel(own, recv, out):
+    n = own.shape[0] - 2 * PIECE
+    out[...] = (one_value(own[n:, :]) + one_value(recv[n:, :])).astype(BF)
 
 
 def pick_kernel(slots, chunks, idx, place, *refs):
-    blocks, (msg, piece, held) = refs[:chunks], refs[chunks:]
+    blocks, (msg, held) = refs[:chunks], refs[chunks:]
     for s in range(slots):
         for o in range(chunks):
 
@@ -221,11 +221,11 @@
             msg[s * TILE : (s + 1) * TILE, :] = jnp.zeros((TILE, HID), BF)
 
     for o in range(chunks):
-        held[lax.rem(place[2] + o, chunks)] = one_value(blocks[o][QUAD * TILE :, :])
-    piece[...] = sum(held[o] for o in range(chunks)).astype(BF)
-
-
-def back_kernel(slots, chunks, src, idx, live, tiles, recv, after, *refs):
+        held[lax.rem(place[0] + o, chunks)] = one_value(blocks[o][QUAD * TILE :, :])
+    msg[slots * TILE :, :] = two_terms(sum(held[o] for o in range(chunks)))
+
+
+def back_kernel(slots, chunks, src, idx, live, tiles, recv, *refs):
     blocks, (keep, send, acc, got) = refs[:chunks], refs[chunks:]
     acc[...] = jnp.zeros_like(acc)
     for s in range(slots):
@@ -254,40 +254,37 @@
     send[...] = acc[half:, :].astype(BF)
 
 
-def back_cut_kernel(keep_in, recv, twin, other_twin, keep, piece, *sends):
-    piece[...] = (one_value(twin[...]) + one_value(other_twin[...])).astype(BF)
+def back_cut_kernel(keep_in, recv, piece_in, other, keep, piece, *sends):
+    piece[...] = (piece_in[...].astype(F32) + other[...].astype(F32)).astype(BF)
     rows = keep.shape[0]
     for d, ref in enumerate((keep,) + sends):
         at = d * rows
         got = keep_in[at : at + rows, :] + recv[at : at + rows, :].astype(F32)
-        ref[0:rows, :] = got.astype(ref.dtype)
-        if d:
-            ref[rows:, :] = piece[...]
-
-
-def back_gather_kernel(size, place, near, piece, *refs):
-    recvs, (whole, *outs) = refs[: size - 1], refs[size - 1 :]
-    rows, n = HID // size, near.shape[0]
-    for d, ref in enumerate(outs):
-        at = slice(d * TILE, (d + 1) * TILE)
-        ref[...] = (near[at, :] + sum(r[at, :].astype(F32) for r in recvs)).astype(ref.dtype)
-    for d in range(size):
-        at = lax.rem(place[1] + size - d, size)
-        block = piece[...] if d == 0 else recvs[d - 1][n:, :]
-        whole[pl.ds(pl.multiple_of(at * rows, 16), rows), :] = block[0:rows, :]
-
-        @pl.when(at == 0)
-        def _():
-            whole[HID:, :] = block[rows:, :]
-
-
-def last_kernel(place, self_back, near, far, whole, across, grads, first, second, bias):
-    grads[...] = (self_back[...] + near[...] + far[...].astype(F32)).astype(BF)
-    mine, other = whole[...].astype(F32), across[...].astype(F32)
-    own = place[0] == 0
-    first[...] = jnp.where(own, mine[0:HID], other[0:HID])
-    second[...] = jnp.where(own, other[0:HID], mine[0:HID])
-    bias[...] = jnp.where(own, mine[HID : HID + 1], other[HID : HID + 1])
+        ref[...] = got.astype(ref.dtype)
+
+
+def back_gather_kernel(size, near, piece, *refs):
+    recvs, (keep, send) = refs[: size - 1], refs[size - 1 :]
+    total = near[...] + sum(r[...].astype(F32) for r in recvs)
+    keep[...] = total[0:TILE]
+    send[0:TILE, :] = total[total.shape[0] - TILE :].astype(BF)
+    send[TILE:, :] = piece[...]
+
+
+def copies_kernel(own, far, out):
+    total = (own[TILE:, :].astype(F32) + far[TILE:, :].astype(F32)).astype(BF)
+    for i in range(0, out.shape[0], PIECE):
+        out[i : i + PIECE, :] = total
+
+
+def last_kernel(size, self_back, near, far, pieces, grads, first, second, bias):
+    grads[...] = (self_back[...] + near[...] + far[0:TILE, :].astype(F32)).astype(BF)
+    rows = HID // size
+    for i in range(size):
+        for j, ref in enumerate((first, second)):
+            at = (i * 2 + j) * PIECE
+            ref[i * rows : (i + 1) * rows, :] = pieces[at : at + rows, :].astype(F32)
+    bias[...] = pieces[rows : rows + 8, :].astype(F32)[0:1]
 
 
 def body(
@@ -332,7 +329,7 @@
     meta = jnp.zeros((8, TILE), jnp.int32).at[0, :slots].set(dest)
     other = flip(meta, "l", 1)[0, :slots]
     own_idx, other_idx = place(dest), place(other)
-    where = jnp.stack([k, x, y]).astype(jnp.int32)
+    where = y.astype(jnp.int32)[None]
 
     panel = features
     if nh > 1:
@@ -422,15 +419,21 @@
     )
     cuts = lax.all_to_all(cuts, ("x", "k"), split_axis=0, concat_axis=0, tiled=True)
 
-    (packed,) = call(pack_kernel, [((TILE + PIECE, HID), BF)], [VMEM] * 2, scaled, cuts)
-    for bit, rows in ((4, 2 * TILE + PIECE), (2, 4 * TILE + 2 * PIECE)):
-        (packed,) = call(
-            join_kernel,
-            [((rows, HID), BF)],
-            [VMEM] * 2,
-            packed,
-            flip(packed, "l", bit),
-        )
+    (packed,) = call(
+        pair_kernel,
+        [((2 * TILE + PIECE, HID), BF)],
+        [VMEM] * 3,
+        scaled,
+        flip(scaled, "l", 4),
+        cuts,
+    )
+    (packed,) = call(
+        quad_kernel,
+        [((4 * TILE + 2 * PIECE, HID), BF)],
+        [VMEM] * 2,
+        packed,
+        flip(packed, "l", 2),
+    )
     blocks = [packed] * ny
     up = down = packed
     for step in range(1, ups + 1):
@@ -439,9 +442,9 @@
         if step <= downs:
             down = shift(down, "y", -1)
             blocks[step] = down
-    msg, piece = call(
+    (msg,) = call(
         functools.partial(pick_kernel, slots, ny),
-        [((slots * TILE, HID), BF), ((PIECE, HID), BF)],
+        [((slots * TILE + 2 * PIECE, HID), BF)],
         [SMEM, SMEM] + [VMEM] * ny,
         other_idx,
         where,
@@ -449,20 +452,18 @@
         scratch=[pltpu.VMEM((ny, PIECE, HID), F32)],
     )
     got = flip(msg, "l", 1)
-    far_piece = flip(piece, "h", 1) if nh > 1 else jnp.zeros_like(piece)
-    (twin,) = call(twin_kernel, [((2 * PIECE, HID), BF)], [VMEM] * 2, piece, far_piece)
+    (piece,) = call(piece_kernel, [((PIECE, HID), BF)], [VMEM] * 2, msg, got)
 
     half = sources // 2 * TILE
     keep, send = call(
         functools.partial(back_kernel, slots, ny),
         [((half, HID), F32), ((half, HID), BF)],
-        [SMEM, SMEM, SMEM, VMEM, VMEM, AFTER] + [VMEM] * ny,
+        [SMEM, SMEM, SMEM, VMEM, VMEM] + [VMEM] * ny,
         src,
         own_idx,
         live,
         tiles,
         got,
-        twin,
         *blocks,
         scratch=[pltpu.VMEM((sources * TILE, HID), F32), pltpu.VMEM((TILE, HID), BF)],
         flops=tile_flops,
@@ -470,33 +471,32 @@
     group = nh * TILE
     near, piece, *sends = call(
         back_cut_kernel,
-        [((group, HID), F32), ((PIECE, HID), BF)] + [((group + PIECE, HID), BF)] * (nx - 1),
+        [((group, HID), F32), ((PIECE, HID), BF)] + [((group, HID), BF)] * (nx - 1),
         [VMEM] * 4,
         keep,
         flip(send, "k", 1),
-        twin,
-        flip(twin, "l", 1),
-    )
-    whole, *last = call(
+        piece,
+        flip(piece, "l", 4),
+    )
+    near, send = call(
         functools.partial(back_gather_kernel, nx),
-        [((HID + 16, HID), BF), ((TILE, HID), F32)] + [node] * (nh - 1),
-        [SMEM] + [VMEM] * (nx + 1),
-        where,
+        [((TILE, HID), F32), ((TILE + PIECE, HID), BF)],
+        [VMEM] * (nx + 1),
         near,
         piece,
         *[shift(sends[d - 1], "x", d) for d in range(1, nx)],
     )
-    far = flip(last[1], "h", 1) if nh > 1 else jnp.zeros((TILE, HID), BF)
+    far = flip(send, "h", 1) if nh > 1 else jnp.zeros_like(send)
+    (copies,) = call(copies_kernel, [((nx * nk * PIECE, HID), BF)], [VMEM] * 2, send, far)
+    pieces = lax.all_to_all(copies, ("x", "k"), split_axis=0, concat_axis=0, tiled=True)
     grad_features, grad_w_self, grad_w_neigh, grad_bias = call(
-        last_kernel,
+        functools.partial(last_kernel, nx),
         [node, ((HID, HID), F32), ((HID, HID), F32), ((1, HID), F32)],
-        [SMEM] + [VMEM] * 5,
-        where,
+        [VMEM] * 4,
         self_back,
-        last[0],
+        near,
         far,
-        whole,
-        flip(whole, "k", 1),
+        pieces,
     )
     return hidden, grad_features, grad_w_self, grad_w_neigh, grad_bias.reshape(HID)
 

time: 294 us -> 289 us (0.983)
  waiting for transfers between devices: 119 us -> 101 us
  starting transfers between devices: 139 us -> 155 us
    ppermute x14 -> x12, waiting for transfers between devices: 71.9 us -> 58.2 us  [flip(): return lax.ppermute(value, axis, [(i, i ^ bit) for i in range(n)])]
    all_to_all x0 -> x1, starting transfers between devices: none -> 12.9 us  [body(): lax.all_to_all(cuts, ('x', 'k'), split_axis=0, concat_axis=0, tiled=True)]
    ppermute x20, waiting for transfers between devices: 46.9 us -> 42.4 us  [shift(): return lax.ppermute(value, axis, [(i, (i + by) % n) for i in range(n)])]
    ppermute x14 -> x12, starting transfers between devices: 78 us -> 79.4 us  [flip(): return lax.ppermute(value, axis, [(i, i ^ bit) for i in range(n)])]
  transfers between devices with their start and end apart: 34 -> 33, of which waited for: 22 -> 23; matrix products, arithmetic and copies ran while one was open for 0% -> 0% of each run, Pallas kernels for 0% -> 0%
where the time goes in v5:
time: 289 us; the launch traced here: 288 us
  starting transfers between devices  155 us (54%)
  waiting for transfers between devices  101 us (35%)
  blocking collectives  15.8 us (5%)
  Pallas kernels  12.2 us (4%)
    ppermute x12, starting transfers between devices, flip(): return lax.ppermute(value, axis, [(i, i ^ bit) for i in range(n)])  79.4 us
    ppermute x20, starting transfers between devices, shift(): return lax.ppermute(value, axis, [(i, (i + by) % n) for i in range(n)])  63.1 us
    ppermute x12, waiting for transfers between devices, flip(): return lax.ppermute(value, axis, [(i, i ^ bit) for i in range(n)])  58.2 us
    ppermute x20, waiting for transfers between devices, shift(): return lax.ppermute(value, axis, [(i, (i + by) % n) for i in range(n)])  42.4 us
    all_to_all x1, blocking collectives, body(): lax.all_to_all(copies, ('x', 'k'), split_axis=0, concat_axis=0, tiled=True)  15.8 us
    all_to_all x1, starting transfers between devices, body(): lax.all_to_all(cuts, ('x', 'k'), split_axis=0, concat_axis=0, tiled=True)  12.9 us
    pallas_call x20, Pallas kernels, call(): pl.pallas_call(kernel, out_shape=shapes, in_specs=in_specs, out_specs=[VM...  12.2 us
  transfers between devices with their start and end apart: 33, of which 23 were waited for; matrix products, arithmetic and copies ran while one was open for 0% of the time, Pallas kernels for 0%

profile of v5, /device:TPU:1, one launch (start us, length us, event | category | flops | bytes accessed | tf_op | source)
XLA Modules:
  0.0 287.5 jit_solution(6930189265747554075)
XLA Ops:
  0.6 19.9 %collective-permute-start.1 = (bf16[128,256]{1,0:T(8,128)(2,1)}, bf16[128,256]{1,0:T(8,128)(2,1)S(1)}, u32[]{:S(2)}, u32[]{:S(2)}) collective-permute-start(bf16[128,256]{1,0:T(8,128)(2,1)} %features.3), channel_id=1, source_target_pairs={{0,512},{512,0},{1,513},{513,1},{2,514},{514,2},{3,515},{515,3},{4... | collective-permute-start | bytes 196616 | tf_op jit(solution)/shard_map/ppermute | solution.py:309
  20.6 0.9 constant_dynamic-update-slice_fusion.6
  21.4 1.2 collective-permute-done.1
  22.6 4.4 %collective-permute-start.2 = (bf16[256,256]{1,0:T(8,128)(2,1)S(1)}, bf16[256,256]{1,0:T(8,128)(2,1)S(1)}, u32[]{:S(2)}, u32[]{:S(2)}) collective-permute-start(bf16[256,256]{1,0:T(8,128)(2,1)S(1)} %get-tuple-element.91), channel_id=1, source_target_pairs={{0,384},{128,0},{256,128},{384,256},{1,385},{129,1},{257,129},{385... | collective-permute-start | bytes 393224 | tf_op jit(solution)/shard_map/ppermute | solution.py:313
  27.0 2.4 collective-permute-start.3
  29.4 2.5 collective-permute-start.4
  32.0 2.2 collective-permute-done.3
  34.2 2.1 collective-permute-done.4
  36.4 9.0 %collective-permute-start.5 = (bf16[1024,256]{1,0:T(8,128)(2,1)S(1)}, bf16[1024,256]{1,0:T(8,128)(2,1)S(1)}, u32[]{:S(2)}, u32[]{:S(2)}) collective-permute-start(bf16[1024,256]{1,0:T(8,128)(2,1)S(1)} %get-tuple-element.83), channel_id=1, source_target_pairs={{0,64},{64,0},{1,65},{65,1},{2,66},{66,2},{3,67},{67,3},{4,68},{68... | collective-permute-start | bytes 1572872 | tf_op jit(solution)/shard_map/ppermute | solution.py:309
  46.0 0.8 collective-permute-done.5
  46.9 1.0 shard_map.137
  47.9 1.9 collective-permute-start.6
  49.9 3.4 %collective-permute-start = (s32[8,128]{1,0:T(8,128)S(1)}, s32[8,128]{1,0:T(8,128)S(1)}, u32[]{:S(2)}, u32[]{:S(2)}) collective-permute-start(s32[8,128]{1,0:T(8,128)S(1)} %scatter.4), channel_id=1, source_target_pairs={{0,1},{1,0},{2,3},{3,2},{4,5},{5,4},{6,7},{7,6},{8,9},{9,8},{10,11... | collective-permute-start | bytes 12296 | tf_op jit(solution)/shard_map/ppermute | solution.py:309
  53.3 12.7 %collective-permute-done = s32[8,128]{1,0:T(8,128)S(1)} collective-permute-done((s32[8,128]{1,0:T(8,128)S(1)}, s32[8,128]{1,0:T(8,128)S(1)}, u32[]{:S(2)}, u32[]{:S(2)}) %collective-permute-start) | collective-permute-done | bytes 4128 | tf_op jit(solution)/shard_map/ppermute | solution.py:309
  66.1 1.9 shard_map.138
  68.0 1.9 collective-permute-start.7
  69.9 4.6 %collective-permute-start.11 = (bf16[528,256]{1,0:T(8,128)(2,1)S(1)}, bf16[528,256]{1,0:T(8,128)(2,1)S(1)}, u32[]{:S(2)}, u32[]{:S(2)}) collective-permute-start(bf16[528,256]{1,0:T(8,128)(2,1)S(1)} %get-tuple-element.57), channel_id=1, source_target_pairs={{0,56},{8,0},{16,8},{24,16},{32,24},{40,32},{48,40},{56,48},{1,57}... | collective-permute-start | bytes 811016 | tf_op jit(solution)/shard_map/ppermute | solution.py:313
  74.5 3.4 %collective-permute-done.7.recv = bf16[528,256]{1,0:T(8,128)(2,1)S(1)} collective-permute-done((bf16[528,256]{1,0:T(8,128)(2,1)S(1)}, bf16[528,256]{1,0:T(8,128)(2,1)S(1)}, u32[]{:S(2)}, u32[]{:S(2)}) %collective-permute-start.7) | collective-permute-done | bytes 270368 | tf_op jit(solution)/shard_map/ppermute | solution.py:313
  78.0 1.9 collective-permute-start.8
  80.0 4.6 %collective-permute-start.12 = (bf16[528,256]{1,0:T(8,128)(2,1)S(1)}, bf16[528,256]{1,0:T(8,128)(2,1)S(1)}, u32[]{:S(2)}, u32[]{:S(2)}) collective-permute-start(bf16[528,256]{1,0:T(8,128)(2,1)S(1)} %shard_map.142), channel_id=1, source_target_pairs={{0,56},{8,0},{16,8},{24,16},{32,24},{40,32},{48,40},{56,48},{1,57}... | collective-permute-start | bytes 811016 | tf_op jit(solution)/shard_map/ppermute | solution.py:313
  84.6 2.4 collective-permute-done.8.recv
  87.0 1.9 collective-permute-start.9
  89.0 4.6 %collective-permute-start.13 = (bf16[528,256]{1,0:T(8,128)(2,1)S(1)}, bf16[528,256]{1,0:T(8,128)(2,1)S(1)}, u32[]{:S(2)}, u32[]{:S(2)}) collective-permute-start(bf16[528,256]{1,0:T(8,128)(2,1)S(1)} %shard_map.143), channel_id=1, source_target_pairs={{0,56},{8,0},{16,8},{24,16},{32,24},{40,32},{48,40},{56,48},{1,57}... | collective-permute-start | bytes 811016 | tf_op jit(solution)/shard_map/ppermute | solution.py:313
  93.6 1.8 collective-permute-done.9.recv
  95.5 1.9 collective-permute-start.10
  97.4 6.5 %collective-permute-done.10.refs_1_ = bf16[528,256]{1,0:T(8,128)(2,1)S(1)} collective-permute-done((bf16[528,256]{1,0:T(8,128)(2,1)S(1)}, bf16[528,256]{1,0:T(8,128)(2,1)S(1)}, u32[]{:S(2)}, u32[]{:S(2)}) %collective-permute-start.10) | collective-permute-done | bytes 270368 | tf_op jit(solution)/shard_map/ppermute | solution.py:313
  104.0 4.1 %collective-permute-start.14 = (bf16[272,256]{1,0:T(8,128)(2,1)S(1)}, bf16[272,256]{1,0:T(8,128)(2,1)S(1)}, u32[]{:S(2)}, u32[]{:S(2)}) collective-permute-start(bf16[272,256]{1,0:T(8,128)(2,1)S(1)} %get-tuple-element.61), channel_id=1, source_target_pairs={{0,2},{1,3},{2,0},{3,1},{4,6},{5,7},{6,4},{7,5},{8,10},{9,11},{10,... | collective-permute-start | bytes 417800 | tf_op jit(solution)/shard_map/ppermute | solution.py:309
  108.0 4.1 %collective-permute-done.14.recv = bf16[272,256]{1,0:T(8,128)(2,1)S(1)} collective-permute-done((bf16[272,256]{1,0:T(8,128)(2,1)S(1)}, bf16[272,256]{1,0:T(8,128)(2,1)S(1)}, u32[]{:S(2)}, u32[]{:S(2)}) %collective-permute-start.14) | collective-permute-done | bytes 139296 | tf_op jit(solution)/shard_map/ppermute | solution.py:309
  112.2 7.7 %collective-permute-start.15 = (bf16[144,256]{1,0:T(8,128)(2,1)S(1)}, bf16[144,256]{1,0:T(8,128)(2,1)S(1)}, u32[]{:S(2)}, u32[]{:S(2)}) collective-permute-start(bf16[144,256]{1,0:T(8,128)(2,1)S(1)} %get-tuple-element.63), channel_id=1, source_target_pairs={{0,4},{1,5},{2,6},{3,7},{4,0},{5,1},{6,2},{7,3},{8,12},{9,13},{10,... | collective-permute-start | bytes 221192 | tf_op jit(solution)/shard_map/ppermute | solution.py:309
  120.0 1.8 collective-permute-done.15.recv
  121.8 0.6 copy-done.5
  122.5 1.0 shard_map.146
  123.4 1.0 shard_map.147
  124.4 12.9 %all-to-all-start = ((bf16[8,80,256]{2,1,0:T(8,128)(2,1)}), bf16[8,80,256]{2,1,0:T(8,128)(2,1)S(1)}, u32[]{:S(2)}, u32[]{:S(2)}) async-start(bf16[8,80,256]{2,1,0:T(8,128)(2,1)} %bitcast.9), calls=%async_computation | async-start | bytes 655360 | tf_op jit(solution)/shard_map/all_to_all | solution.py:420
  137.3 6.0 %collective-permute-start.16 = (bf16[128,256]{1,0:T(8,128)(2,1)S(1)}, bf16[128,256]{1,0:T(8,128)(2,1)S(1)}, u32[]{:S(2)}, u32[]{:S(2)}) collective-permute-start(bf16[128,256]{1,0:T(8,128)(2,1)S(1)} %get-tuple-element.68.own), channel_id=1, source_target_pairs={{0,4},{1,5},{2,6},{3,7},{4,0},{5,1},{6,2},{7,3},{8,12},{9,13},{10,... | collective-permute-start | bytes 196616 | tf_op jit(solution)/shard_map/ppermute | solution.py:309
  143.3 5.3 %collective-permute-done.16.recv = bf16[128,256]{1,0:T(8,128)(2,1)S(1)} collective-permute-done((bf16[128,256]{1,0:T(8,128)(2,1)S(1)}, bf16[128,256]{1,0:T(8,128)(2,1)S(1)}, u32[]{:S(2)}, u32[]{:S(2)}) %collective-permute-start.16) | collective-permute-done | bytes 65568 | tf_op jit(solution)/shard_map/ppermute | solution.py:309
  148.7 1.9 collective-permute-start.17
  150.6 9.0 %collective-permute-done.17.recv = bf16[336,256]{1,0:T(8,128)(2,1)S(1)} collective-permute-done((bf16[336,256]{1,0:T(8,128)(2,1)S(1)}, bf16[336,256]{1,0:T(8,128)(2,1)S(1)}, u32[]{:S(2)}, u32[]{:S(2)}) %collective-permute-start.17) | collective-permute-done | bytes 172064 | tf_op jit(solution)/shard_map/ppermute | solution.py:309
  159.7 1.9 collective-permute-start.21
  161.6 4.6 %collective-permute-start.18 = (bf16[672,256]{1,0:T(8,128)(2,1)S(1)}, bf16[672,256]{1,0:T(8,128)(2,1)S(1)}, u32[]{:S(2)}, u32[]{:S(2)}) collective-permute-start(bf16[672,256]{1,0:T(8,128)(2,1)S(1)} %shard_map.149.refs_0_), channel_id=1, source_target_pairs={{0,56},{8,0},{16,8},{24,16},{32,24},{40,32},{48,40},{56,48},{1,57}... | collective-permute-start | bytes 1032200 | tf_op jit(solution)/shard_map/ppermute | solution.py:313
  166.2 5.7 %collective-permute-done.21.refs_7_ = bf16[672,256]{1,0:T(8,128)(2,1)S(1)} collective-permute-done((bf16[672,256]{1,0:T(8,128)(2,1)S(1)}, bf16[672,256]{1,0:T(8,128)(2,1)S(1)}, u32[]{:S(2)}, u32[]{:S(2)}) %collective-permute-start.21) | collective-permute-done | bytes 344096 | tf_op jit(solution)/shard_map/ppermute | solution.py:313
  171.9 1.9 collective-permute-start.22
  173.8 4.6 %collective-permute-start.19 = (bf16[672,256]{1,0:T(8,128)(2,1)S(1)}, bf16[672,256]{1,0:T(8,128)(2,1)S(1)}, u32[]{:S(2)}, u32[]{:S(2)}) collective-permute-start(bf16[672,256]{1,0:T(8,128)(2,1)S(1)} %collective-permute-done.18.refs_1_), channel_id=1, source_target_pairs={{0,56},{8,0},{16,8},{24,16},{32,24},{40,32},{48,40},{56,48},{1,57}... | collective-permute-start | bytes 1032200 | tf_op jit(solution)/shard_map/ppermute | solution.py:313
  178.4 4.8 %collective-permute-done.22.refs_6_ = bf16[672,256]{1,0:T(8,128)(2,1)S(1)} collective-permute-done((bf16[672,256]{1,0:T(8,128)(2,1)S(1)}, bf16[672,256]{1,0:T(8,128)(2,1)S(1)}, u32[]{:S(2)}, u32[]{:S(2)}) %collective-permute-start.22) | collective-permute-done | bytes 344096 | tf_op jit(solution)/shard_map/ppermute | solution.py:313
  183.2 1.9 collective-permute-start.23
  185.2 4.6 %collective-permute-start.20 = (bf16[672,256]{1,0:T(8,128)(2,1)S(1)}, bf16[672,256]{1,0:T(8,128)(2,1)S(1)}, u32[]{:S(2)}, u32[]{:S(2)}) collective-permute-start(bf16[672,256]{1,0:T(8,128)(2,1)S(1)} %collective-permute-done.19.refs_2_), channel_id=1, source_target_pairs={{0,56},{8,0},{16,8},{24,16},{32,24},{40,32},{48,40},{56,48},{1,57}... | collective-permute-start | bytes 1032200 | tf_op jit(solution)/shard_map/ppermute | solution.py:313
  189.7 3.9 %collective-permute-done.23.refs_5_ = bf16[672,256]{1,0:T(8,128)(2,1)S(1)} collective-permute-done((bf16[672,256]{1,0:T(8,128)(2,1)S(1)}, bf16[672,256]{1,0:T(8,128)(2,1)S(1)}, u32[]{:S(2)}, u32[]{:S(2)}) %collective-permute-start.23) | collective-permute-done | bytes 344096 | tf_op jit(solution)/shard_map/ppermute | solution.py:313
  193.6 1.9 collective-permute-start.24
  195.7 7.1 %collective-permute-done.24.refs_4_ = bf16[672,256]{1,0:T(8,128)(2,1)S(1)} collective-permute-done((bf16[672,256]{1,0:T(8,128)(2,1)S(1)}, bf16[672,256]{1,0:T(8,128)(2,1)S(1)}, u32[]{:S(2)}, u32[]{:S(2)}) %collective-permute-start.24) | collective-permute-done | bytes 344096 | tf_op jit(solution)/shard_map/ppermute | solution.py:313
  202.8 1.9 shard_map.150.own
  204.8 1.9 collective-permute-start.25
  206.7 13.6 %collective-permute-done.25.recv = bf16[1440,256]{1,0:T(8,128)(2,1)S(1)} collective-permute-done((bf16[1440,256]{1,0:T(8,128)(2,1)S(1)}, bf16[1440,256]{1,0:T(8,128)(2,1)S(1)}, u32[]{:S(2)}, u32[]{:S(2)}) %collective-permute-start.25) | collective-permute-done | bytes 737312 | tf_op jit(solution)/shard_map/ppermute | solution.py:309
  220.3 3.7 %shard_map.151 = (f32[1024,256]{1,0:T(8,128)S(1)}, bf16[1024,256]{1,0:T(8,128)(2,1)S(1)}) custom-call(s32[10]{0:T(128)S(1)} %xor_add_fusion.src, s32[10]{0:T(128)S(1)} %and_select_fusion.6.idx, s32[10]{0:T(128)S(1)} %compare_convert_fusion.1.live, bf16[10,128,128]{2,1,0:T(8,128)(2,1)S(1)} %get-tuple-element.50.tiles, ...), custom_call_target="tpu_custom_call" | custom-call | flops 83886080 | bytes 5390456 | tf_op jit(solution)/shard_map/pallas_call | solution.py:26
  224.0 6.9 %collective-permute-start.26 = (bf16[1024,256]{1,0:T(8,128)(2,1)S(1)}, bf16[1024,256]{1,0:T(8,128)(2,1)S(1)}, u32[]{:S(2)}, u32[]{:S(2)}) collective-permute-start(bf16[1024,256]{1,0:T(8,128)(2,1)S(1)} %get-tuple-element.71), channel_id=1, source_target_pairs={{0,64},{64,0},{1,65},{65,1},{2,66},{66,2},{3,67},{67,3},{4,68},{68... | collective-permute-start | bytes 1572872 | tf_op jit(solution)/shard_map/ppermute | solution.py:309
  230.9 5.5 %collective-permute-start.27 = (bf16[80,256]{1,0:T(8,128)(2,1)S(1)}, bf16[80,256]{1,0:T(8,128)(2,1)S(1)}, u32[]{:S(2)}, u32[]{:S(2)}) collective-permute-start(bf16[80,256]{1,0:T(8,128)(2,1)S(1)} %shard_map.152.piece_in), channel_id=1, source_target_pairs={{0,4},{1,5},{2,6},{3,7},{4,0},{5,1},{6,2},{7,3},{8,12},{9,13},{10,... | collective-permute-start | bytes 122888 | tf_op jit(solution)/shard_map/ppermute | solution.py:309
  236.4 6.3 %collective-permute-done.27.other = bf16[80,256]{1,0:T(8,128)(2,1)S(1)} collective-permute-done((bf16[80,256]{1,0:T(8,128)(2,1)S(1)}, bf16[80,256]{1,0:T(8,128)(2,1)S(1)}, u32[]{:S(2)}, u32[]{:S(2)}) %collective-permute-start.27) | collective-permute-done | bytes 40992 | tf_op jit(solution)/shard_map/ppermute | solution.py:309
  242.9 3.5 %collective-permute-start.28 = (bf16[256,256]{1,0:T(8,128)(2,1)S(1)}, bf16[256,256]{1,0:T(8,128)(2,1)S(1)}, u32[]{:S(2)}, u32[]{:S(2)}) collective-permute-start(bf16[256,256]{1,0:T(8,128)(2,1)S(1)} %get-tuple-element.74), channel_id=1, source_target_pairs={{0,128},{128,256},{256,384},{384,0},{1,129},{129,257},{257,385},{3... | collective-permute-start | bytes 393224 | tf_op jit(solution)/shard_map/ppermute | solution.py:313
  246.5 4.1 %collective-permute-start.29 = (bf16[256,256]{1,0:T(8,128)(2,1)S(1)}, bf16[256,256]{1,0:T(8,128)(2,1)S(1)}, u32[]{:S(2)}, u32[]{:S(2)}) collective-permute-start(bf16[256,256]{1,0:T(8,128)(2,1)S(1)} %get-tuple-element.75), channel_id=1, source_target_pairs={{0,256},{128,384},{256,0},{384,128},{1,257},{129,385},{257,1},{385... | collective-permute-start | bytes 393224 | tf_op jit(solution)/shard_map/ppermute | solution.py:313
  250.6 3.4 %collective-permute-start.30 = (bf16[256,256]{1,0:T(8,128)(2,1)S(1)}, bf16[256,256]{1,0:T(8,128)(2,1)S(1)}, u32[]{:S(2)}, u32[]{:S(2)}) collective-permute-start(bf16[256,256]{1,0:T(8,128)(2,1)S(1)} %get-tuple-element.76), channel_id=1, source_target_pairs={{0,384},{128,0},{256,128},{384,256},{1,385},{129,1},{257,129},{385... | collective-permute-start | bytes 393224 | tf_op jit(solution)/shard_map/ppermute | solution.py:313
  254.5 1.8 collective-permute-done.30.refs_2_
  256.4 11.2 %collective-permute-start.31 = (bf16[208,256]{1,0:T(8,128)(2,1)S(1)}, bf16[208,256]{1,0:T(8,128)(2,1)S(1)}, u32[]{:S(2)}, u32[]{:S(2)}) collective-permute-start(bf16[208,256]{1,0:T(8,128)(2,1)S(1)} %get-tuple-element.78.own), channel_id=1, source_target_pairs={{0,512},{512,0},{1,513},{513,1},{2,514},{514,2},{3,515},{515,3},{4... | collective-permute-start | bytes 319496 | tf_op jit(solution)/shard_map/ppermute | solution.py:309
  267.6 3.3 %collective-permute-done.31.far = bf16[208,256]{1,0:T(8,128)(2,1)S(1)} collective-permute-done((bf16[208,256]{1,0:T(8,128)(2,1)S(1)}, bf16[208,256]{1,0:T(8,128)(2,1)S(1)}, u32[]{:S(2)}, u32[]{:S(2)}) %collective-permute-start.31) | collective-permute-done | bytes 106528 | tf_op jit(solution)/shard_map/ppermute | solution.py:309
  270.9 15.8 %all_to_all.22 = bf16[8,80,256]{2,1,0:T(8,128)(2,1)S(1)} all-to-all(bf16[8,80,256]{2,1,0:T(8,128)(2,1)S(1)} %bitcast.53), channel_id=1, replica_groups=mesh['h'=2,'x'=4,'k'=2,'y'=8,'l'=8] {'x','k'}, dimensions={0} | all-to-all | bytes 655360 | tf_op jit(solution)/shard_map/all_to_all | solution.py:491
  286.7 0.8 shard_map.156
  (53 shorter events, 1.7 us)
Async XLA Ops:
  0.6 21.9 %collective-permute-start.1 = (bf16[128,256]{1,0:T(8,128)(2,1)}, bf16[128,256]{1,0:T(8,128)(2,1)S(1)}, u32[]{:S(2)}, u32[]{:S(2)}) collective-permute-start(bf16[128,256]{1,0:T(8,128)(2,1)} %features.3), channel_id=1, source_target_pairs={{0,512},{512,0},{1,513},{513,1},{2,514},{514,2},{3,515},{515,3},{4... | collective-permute-start | bytes 196616 | tf_op jit(solution)/shard_map/ppermute | solution.py:309
  22.6 9.4 %collective-permute-start.2 = (bf16[256,256]{1,0:T(8,128)(2,1)S(1)}, bf16[256,256]{1,0:T(8,128)(2,1)S(1)}, u32[]{:S(2)}, u32[]{:S(2)}) collective-permute-start(bf16[256,256]{1,0:T(8,128)(2,1)S(1)} %get-tuple-element.91), channel_id=1, source_target_pairs={{0,384},{128,0},{256,128},{384,256},{1,385},{129,1},{257,129},{385... | collective-permute-start | bytes 393224 | tf_op jit(solution)/shard_map/ppermute | solution.py:313
  27.0 7.2 %collective-permute-start.3 = (bf16[256,256]{1,0:T(8,128)(2,1)S(1)}, bf16[256,256]{1,0:T(8,128)(2,1)S(1)}, u32[]{:S(2)}, u32[]{:S(2)}) collective-permute-start(bf16[256,256]{1,0:T(8,128)(2,1)S(1)} %get-tuple-element.91), channel_id=1, source_target_pairs={{0,256},{128,384},{256,0},{384,128},{1,257},{129,385},{257,1},{385... | collective-permute-start | bytes 393224 | tf_op jit(solution)/shard_map/ppermute | solution.py:313
  29.4 6.9 %collective-permute-start.4 = (bf16[256,256]{1,0:T(8,128)(2,1)S(1)}, bf16[256,256]{1,0:T(8,128)(2,1)S(1)}, u32[]{:S(2)}, u32[]{:S(2)}) collective-permute-start(bf16[256,256]{1,0:T(8,128)(2,1)S(1)} %get-tuple-element.91), channel_id=1, source_target_pairs={{0,128},{128,256},{256,384},{384,0},{1,129},{129,257},{257,385},{3... | collective-permute-start | bytes 393224 | tf_op jit(solution)/shard_map/ppermute | solution.py:313
  34.2 11.8 %copy-start.7 = (s32[1,1,10]{2,1,0:T(1,128)S(1)}, s32[1,1,10]{2,1,0:T(1,128)}, u32[]{:S(2)}) copy-start(s32[1,1,10]{2,1,0:T(1,128)} %param.15) | copy-start | bytes 124
  36.3 10.5 %copy-start = (s32[1,1,10,128,128]{4,3,2,1,0:T(8,128)S(1)}, s32[1,1,10,128,128]{4,3,2,1,0:T(8,128)}, u32[]{:S(2)}) copy-start(s32[1,1,10,128,128]{4,3,2,1,0:T(8,128)} %param.13) | copy-start | bytes 1966084
  36.4 10.5 %collective-permute-start.5 = (bf16[1024,256]{1,0:T(8,128)(2,1)S(1)}, bf16[1024,256]{1,0:T(8,128)(2,1)S(1)}, u32[]{:S(2)}, u32[]{:S(2)}) collective-permute-start(bf16[1024,256]{1,0:T(8,128)(2,1)S(1)} %get-tuple-element.83), channel_id=1, source_target_pairs={{0,64},{64,0},{1,65},{65,1},{2,66},{66,2},{3,67},{67,3},{4,68},{68... | collective-permute-start | bytes 1572872 | tf_op jit(solution)/shard_map/ppermute | solution.py:309
  47.9 1.9 copy-start.8
  47.9 18.1 %collective-permute-start.6 = (bf16[1296,256]{1,0:T(8,128)(2,1)S(1)}, bf16[1296,256]{1,0:T(8,128)(2,1)S(1)}, u32[]{:S(2)}, u32[]{:S(2)}) collective-permute-start(bf16[1296,256]{1,0:T(8,128)(2,1)S(1)} %get-tuple-element.51), channel_id=1, source_target_pairs={{0,1},{1,0},{2,3},{3,2},{4,5},{5,4},{6,7},{7,6},{8,9},{9,8},{10,11... | collective-permute-start | bytes 1990664 | tf_op jit(solution)/shard_map/ppermute | solution.py:309
  49.9 16.1 %collective-permute-start = (s32[8,128]{1,0:T(8,128)S(1)}, s32[8,128]{1,0:T(8,128)S(1)}, u32[]{:S(2)}, u32[]{:S(2)}) collective-permute-start(s32[8,128]{1,0:T(8,128)S(1)} %scatter.4), channel_id=1, source_target_pairs={{0,1},{1,0},{2,3},{3,2},{4,5},{5,4},{6,7},{7,6},{8,9},{9,8},{10,11... | collective-permute-start | bytes 12296 | tf_op jit(solution)/shard_map/ppermute | solution.py:309
  68.0 9.9 %collective-permute-start.7 = (bf16[528,256]{1,0:T(8,128)(2,1)S(1)}, bf16[528,256]{1,0:T(8,128)(2,1)S(1)}, u32[]{:S(2)}, u32[]{:S(2)}) collective-permute-start(bf16[528,256]{1,0:T(8,128)(2,1)S(1)} %get-tuple-element.53), channel_id=1, source_target_pairs={{0,8},{8,16},{16,24},{24,32},{32,40},{40,48},{48,56},{56,0},{1,9},... | collective-permute-start | bytes 811016 | tf_op jit(solution)/shard_map/ppermute | solution.py:313
  69.9 10.0 %collective-permute-start.11 = (bf16[528,256]{1,0:T(8,128)(2,1)S(1)}, bf16[528,256]{1,0:T(8,128)(2,1)S(1)}, u32[]{:S(2)}, u32[]{:S(2)}) collective-permute-start(bf16[528,256]{1,0:T(8,128)(2,1)S(1)} %get-tuple-element.57), channel_id=1, source_target_pairs={{0,56},{8,0},{16,8},{24,16},{32,24},{40,32},{48,40},{56,48},{1,57}... | collective-permute-start | bytes 811016 | tf_op jit(solution)/shard_map/ppermute | solution.py:313
  78.0 9.0 %collective-permute-start.8 = (bf16[528,256]{1,0:T(8,128)(2,1)S(1)}, bf16[528,256]{1,0:T(8,128)(2,1)S(1)}, u32[]{:S(2)}, u32[]{:S(2)}) collective-permute-start(bf16[528,256]{1,0:T(8,128)(2,1)S(1)} %shard_map.139), channel_id=1, source_target_pairs={{0,8},{8,16},{16,24},{24,32},{32,40},{40,48},{48,56},{56,0},{1,9},... | collective-permute-start | bytes 811016 | tf_op jit(solution)/shard_map/ppermute | solution.py:313
  80.0 8.9 %collective-permute-start.12 = (bf16[528,256]{1,0:T(8,128)(2,1)S(1)}, bf16[528,256]{1,0:T(8,128)(2,1)S(1)}, u32[]{:S(2)}, u32[]{:S(2)}) collective-permute-start(bf16[528,256]{1,0:T(8,128)(2,1)S(1)} %shard_map.142), channel_id=1, source_target_pairs={{0,56},{8,0},{16,8},{24,16},{32,24},{40,32},{48,40},{56,48},{1,57}... | collective-permute-start | bytes 811016 | tf_op jit(solution)/shard_map/ppermute | solution.py:313
  87.0 8.4 %collective-permute-start.9 = (bf16[528,256]{1,0:T(8,128)(2,1)S(1)}, bf16[528,256]{1,0:T(8,128)(2,1)S(1)}, u32[]{:S(2)}, u32[]{:S(2)}) collective-permute-start(bf16[528,256]{1,0:T(8,128)(2,1)S(1)} %shard_map.140), channel_id=1, source_target_pairs={{0,8},{8,16},{16,24},{24,32},{32,40},{40,48},{48,56},{56,0},{1,9},... | collective-permute-start | bytes 811016 | tf_op jit(solution)/shard_map/ppermute | solution.py:313
  89.0 8.4 %collective-permute-start.13 = (bf16[528,256]{1,0:T(8,128)(2,1)S(1)}, bf16[528,256]{1,0:T(8,128)(2,1)S(1)}, u32[]{:S(2)}, u32[]{:S(2)}) collective-permute-start(bf16[528,256]{1,0:T(8,128)(2,1)S(1)} %shard_map.143), channel_id=1, source_target_pairs={{0,56},{8,0},{16,8},{24,16},{32,24},{40,32},{48,40},{56,48},{1,57}... | collective-permute-start | bytes 811016 | tf_op jit(solution)/shard_map/ppermute | solution.py:313
  95.5 8.4 %collective-permute-start.10 = (bf16[528,256]{1,0:T(8,128)(2,1)S(1)}, bf16[528,256]{1,0:T(8,128)(2,1)S(1)}, u32[]{:S(2)}, u32[]{:S(2)}) collective-permute-start(bf16[528,256]{1,0:T(8,128)(2,1)S(1)} %shard_map.141), channel_id=1, source_target_pairs={{0,8},{8,16},{16,24},{24,32},{32,40},{40,48},{48,56},{56,0},{1,9},... | collective-permute-start | bytes 811016 | tf_op jit(solution)/shard_map/ppermute | solution.py:313
  104.0 8.2 %collective-permute-start.14 = (bf16[272,256]{1,0:T(8,128)(2,1)S(1)}, bf16[272,256]{1,0:T(8,128)(2,1)S(1)}, u32[]{:S(2)}, u32[]{:S(2)}) collective-permute-start(bf16[272,256]{1,0:T(8,128)(2,1)S(1)} %get-tuple-element.61), channel_id=1, source_target_pairs={{0,2},{1,3},{2,0},{3,1},{4,6},{5,7},{6,4},{7,5},{8,10},{9,11},{10,... | collective-permute-start | bytes 417800 | tf_op jit(solution)/shard_map/ppermute | solution.py:309
  112.2 9.6 %copy-start.1 = (bf16[128,256]{1,0:T(8,128)(2,1)S(1)}, bf16[128,256]{1,0:T(8,128)(2,1)}, u32[]{:S(2)}) copy-start(bf16[128,256]{1,0:T(8,128)(2,1)} %features.3) | copy-start | bytes 196612
  112.2 9.6 %copy-start.2 = (bf16[256,256]{1,0:T(8,128)(2,1)S(1)}, bf16[256,256]{1,0:T(8,128)(2,1)}, u32[]{:S(2)}) copy-start(bf16[256,256]{1,0:T(8,128)(2,1)} %w_self.3) | copy-start | bytes 393220
  112.2 9.6 %copy-start.3 = (bf16[256,256]{1,0:T(8,128)(2,1)S(1)}, bf16[256,256]{1,0:T(8,128)(2,1)}, u32[]{:S(2)}) copy-start(bf16[256,256]{1,0:T(8,128)(2,1)} %w_neigh.1) | copy-start | bytes 393220
  112.2 9.6 %copy-start.4 = (bf16[128,256]{1,0:T(8,128)(2,1)S(1)}, bf16[128,256]{1,0:T(8,128)(2,1)}, u32[]{:S(2)}) copy-start(bf16[128,256]{1,0:T(8,128)(2,1)} %grad_out.1) | copy-start | bytes 196612
  112.2 9.6 %collective-permute-start.15 = (bf16[144,256]{1,0:T(8,128)(2,1)S(1)}, bf16[144,256]{1,0:T(8,128)(2,1)S(1)}, u32[]{:S(2)}, u32[]{:S(2)}) collective-permute-start(bf16[144,256]{1,0:T(8,128)(2,1)S(1)} %get-tuple-element.63), channel_id=1, source_target_pairs={{0,4},{1,5},{2,6},{3,7},{4,0},{5,1},{6,2},{7,3},{8,12},{9,13},{10,... | collective-permute-start | bytes 221192 | tf_op jit(solution)/shard_map/ppermute | solution.py:309
  121.8 0.7 copy-start.5
  121.8 0.7 copy-start.6
  124.4 24.2 %all-to-all-start = ((bf16[8,80,256]{2,1,0:T(8,128)(2,1)}), bf16[8,80,256]{2,1,0:T(8,128)(2,1)S(1)}, u32[]{:S(2)}, u32[]{:S(2)}) async-start(bf16[8,80,256]{2,1,0:T(8,128)(2,1)} %bitcast.9), calls=%async_computation | async-start | bytes 655360 | tf_op jit(solution)/shard_map/all_to_all | solution.py:420
  137.3 11.3 %collective-permute-start.16 = (bf16[128,256]{1,0:T(8,128)(2,1)S(1)}, bf16[128,256]{1,0:T(8,128)(2,1)S(1)}, u32[]{:S(2)}, u32[]{:S(2)}) collective-permute-start(bf16[128,256]{1,0:T(8,128)(2,1)S(1)} %get-tuple-element.68.own), channel_id=1, source_target_pairs={{0,4},{1,5},{2,6},{3,7},{4,0},{5,1},{6,2},{7,3},{8,12},{9,13},{10,... | collective-permute-start | bytes 196616 | tf_op jit(solution)/shard_map/ppermute | solution.py:309
  148.7 11.0 %collective-permute-start.17 = (bf16[336,256]{1,0:T(8,128)(2,1)S(1)}, bf16[336,256]{1,0:T(8,128)(2,1)S(1)}, u32[]{:S(2)}, u32[]{:S(2)}) collective-permute-start(bf16[336,256]{1,0:T(8,128)(2,1)S(1)} %shard_map.148.own), channel_id=1, source_target_pairs={{0,2},{1,3},{2,0},{3,1},{4,6},{5,7},{6,4},{7,5},{8,10},{9,11},{10,... | collective-permute-start | bytes 516104 | tf_op jit(solution)/shard_map/ppermute | solution.py:309
  159.7 12.2 %collective-permute-start.21 = (bf16[672,256]{1,0:T(8,128)(2,1)S(1)}, bf16[672,256]{1,0:T(8,128)(2,1)S(1)}, u32[]{:S(2)}, u32[]{:S(2)}) collective-permute-start(bf16[672,256]{1,0:T(8,128)(2,1)S(1)} %shard_map.149.refs_0_), channel_id=1, source_target_pairs={{0,8},{8,16},{16,24},{24,32},{32,40},{40,48},{48,56},{56,0},{1,9},... | collective-permute-start | bytes 1032200 | tf_op jit(solution)/shard_map/ppermute | solution.py:313
  161.6 12.2 %collective-permute-start.18 = (bf16[672,256]{1,0:T(8,128)(2,1)S(1)}, bf16[672,256]{1,0:T(8,128)(2,1)S(1)}, u32[]{:S(2)}, u32[]{:S(2)}) collective-permute-start(bf16[672,256]{1,0:T(8,128)(2,1)S(1)} %shard_map.149.refs_0_), channel_id=1, source_target_pairs={{0,56},{8,0},{16,8},{24,16},{32,24},{40,32},{48,40},{56,48},{1,57}... | collective-permute-start | bytes 1032200 | tf_op jit(solution)/shard_map/ppermute | solution.py:313
  171.9 11.3 %collective-permute-start.22 = (bf16[672,256]{1,0:T(8,128)(2,1)S(1)}, bf16[672,256]{1,0:T(8,128)(2,1)S(1)}, u32[]{:S(2)}, u32[]{:S(2)}) collective-permute-start(bf16[672,256]{1,0:T(8,128)(2,1)S(1)} %collective-permute-done.21.refs_7_), channel_id=1, source_target_pairs={{0,8},{8,16},{16,24},{24,32},{32,40},{40,48},{48,56},{56,0},{1,9},... | collective-permute-start | bytes 1032200 | tf_op jit(solution)/shard_map/ppermute | solution.py:313
  173.8 11.3 %collective-permute-start.19 = (bf16[672,256]{1,0:T(8,128)(2,1)S(1)}, bf16[672,256]{1,0:T(8,128)(2,1)S(1)}, u32[]{:S(2)}, u32[]{:S(2)}) collective-permute-start(bf16[672,256]{1,0:T(8,128)(2,1)S(1)} %collective-permute-done.18.refs_1_), channel_id=1, source_target_pairs={{0,56},{8,0},{16,8},{24,16},{32,24},{40,32},{48,40},{56,48},{1,57}... | collective-permute-start | bytes 1032200 | tf_op jit(solution)/shard_map/ppermute | solution.py:313
  183.2 10.4 %collective-permute-start.23 = (bf16[672,256]{1,0:T(8,128)(2,1)S(1)}, bf16[672,256]{1,0:T(8,128)(2,1)S(1)}, u32[]{:S(2)}, u32[]{:S(2)}) collective-permute-start(bf16[672,256]{1,0:T(8,128)(2,1)S(1)} %collective-permute-done.22.refs_6_), channel_id=1, source_target_pairs={{0,8},{8,16},{16,24},{24,32},{32,40},{40,48},{48,56},{56,0},{1,9},... | collective-permute-start | bytes 1032200 | tf_op jit(solution)/shard_map/ppermute | solution.py:313
  185.2 10.5 %collective-permute-start.20 = (bf16[672,256]{1,0:T(8,128)(2,1)S(1)}, bf16[672,256]{1,0:T(8,128)(2,1)S(1)}, u32[]{:S(2)}, u32[]{:S(2)}) collective-permute-start(bf16[672,256]{1,0:T(8,128)(2,1)S(1)} %collective-permute-done.19.refs_2_), channel_id=1, source_target_pairs={{0,56},{8,0},{16,8},{24,16},{32,24},{40,32},{48,40},{56,48},{1,57}... | collective-permute-start | bytes 1032200 | tf_op jit(solution)/shard_map/ppermute | solution.py:313
  193.6 9.2 %collective-permute-start.24 = (bf16[672,256]{1,0:T(8,128)(2,1)S(1)}, bf16[672,256]{1,0:T(8,128)(2,1)S(1)}, u32[]{:S(2)}, u32[]{:S(2)}) collective-permute-start(bf16[672,256]{1,0:T(8,128)(2,1)S(1)} %collective-permute-done.23.refs_5_), channel_id=1, source_target_pairs={{0,8},{8,16},{16,24},{24,32},{32,40},{40,48},{48,56},{56,0},{1,9},... | collective-permute-start | bytes 1032200 | tf_op jit(solution)/shard_map/ppermute | solution.py:313
  204.8 15.5 %collective-permute-start.25 = (bf16[1440,256]{1,0:T(8,128)(2,1)S(1)}, bf16[1440,256]{1,0:T(8,128)(2,1)S(1)}, u32[]{:S(2)}, u32[]{:S(2)}) collective-permute-start(bf16[1440,256]{1,0:T(8,128)(2,1)S(1)} %shard_map.150.own), channel_id=1, source_target_pairs={{0,1},{1,0},{2,3},{3,2},{4,5},{5,4},{6,7},{7,6},{8,9},{9,8},{10,11... | collective-permute-start | bytes 2211848 | tf_op jit(solution)/shard_map/ppermute | solution.py:309
  224.0 18.8 %collective-permute-start.26 = (bf16[1024,256]{1,0:T(8,128)(2,1)S(1)}, bf16[1024,256]{1,0:T(8,128)(2,1)S(1)}, u32[]{:S(2)}, u32[]{:S(2)}) collective-permute-start(bf16[1024,256]{1,0:T(8,128)(2,1)S(1)} %get-tuple-element.71), channel_id=1, source_target_pairs={{0,64},{64,0},{1,65},{65,1},{2,66},{66,2},{3,67},{67,3},{4,68},{68... | collective-permute-start | bytes 1572872 | tf_op jit(solution)/shard_map/ppermute | solution.py:309
  230.9 11.9 %collective-permute-start.27 = (bf16[80,256]{1,0:T(8,128)(2,1)S(1)}, bf16[80,256]{1,0:T(8,128)(2,1)S(1)}, u32[]{:S(2)}, u32[]{:S(2)}) collective-permute-start(bf16[80,256]{1,0:T(8,128)(2,1)S(1)} %shard_map.152.piece_in), channel_id=1, source_target_pairs={{0,4},{1,5},{2,6},{3,7},{4,0},{5,1},{6,2},{7,3},{8,12},{9,13},{10,... | collective-permute-start | bytes 122888 | tf_op jit(solution)/shard_map/ppermute | solution.py:309
  242.9 11.1 %collective-permute-start.28 = (bf16[256,256]{1,0:T(8,128)(2,1)S(1)}, bf16[256,256]{1,0:T(8,128)(2,1)S(1)}, u32[]{:S(2)}, u32[]{:S(2)}) collective-permute-start(bf16[256,256]{1,0:T(8,128)(2,1)S(1)} %get-tuple-element.74), channel_id=1, source_target_pairs={{0,128},{128,256},{256,384},{384,0},{1,129},{129,257},{257,385},{3... | collective-permute-start | bytes 393224 | tf_op jit(solution)/shard_map/ppermute | solution.py:313
  246.5 8.0 %collective-permute-start.29 = (bf16[256,256]{1,0:T(8,128)(2,1)S(1)}, bf16[256,256]{1,0:T(8,128)(2,1)S(1)}, u32[]{:S(2)}, u32[]{:S(2)}) collective-permute-start(bf16[256,256]{1,0:T(8,128)(2,1)S(1)} %get-tuple-element.75), channel_id=1, source_target_pairs={{0,256},{128,384},{256,0},{384,128},{1,257},{129,385},{257,1},{385... | collective-permute-start | bytes 393224 | tf_op jit(solution)/shard_map/ppermute | solution.py:313
  250.6 5.7 %collective-permute-start.30 = (bf16[256,256]{1,0:T(8,128)(2,1)S(1)}, bf16[256,256]{1,0:T(8,128)(2,1)S(1)}, u32[]{:S(2)}, u32[]{:S(2)}) collective-permute-start(bf16[256,256]{1,0:T(8,128)(2,1)S(1)} %get-tuple-element.76), channel_id=1, source_target_pairs={{0,384},{128,0},{256,128},{384,256},{1,385},{129,1},{257,129},{385... | collective-permute-start | bytes 393224 | tf_op jit(solution)/shard_map/ppermute | solution.py:313
  256.4 14.5 %collective-permute-start.31 = (bf16[208,256]{1,0:T(8,128)(2,1)S(1)}, bf16[208,256]{1,0:T(8,128)(2,1)S(1)}, u32[]{:S(2)}, u32[]{:S(2)}) collective-permute-start(bf16[208,256]{1,0:T(8,128)(2,1)S(1)} %get-tuple-element.78.own), channel_id=1, source_target_pairs={{0,512},{512,0},{1,513},{513,1},{2,514},{514,2},{3,515},{515,3},{4... | collective-permute-start | bytes 319496 | tf_op jit(solution)/shard_map/ppermute | solution.py:309

commit v6 on v4

--- a/solution.py
+++ b/solution.py
@@ -179,35 +179,27 @@
     )
 
 
-def pack_kernel(scaled, cuts, out):
-    out[0:TILE, :] = scaled[...]
+def pair_kernel(own, recv, cuts, out):
+    out[0:TILE, :] = own[...]
+    out[TILE : 2 * TILE, :] = recv[...]
     pieces = [cuts[i : i + PIECE, :].astype(F32) for i in range(0, cuts.shape[0], PIECE)]
-    out[TILE:, :] = sum(pieces).astype(BF)
-
-
-def two_terms(value):
-    hi = value.astype(BF)
-    return jnp.concatenate([hi, (value - hi.astype(F32)).astype(BF)], axis=0)
-
-
-def one_value(terms):
-    return terms[0:PIECE].astype(F32) + terms[PIECE:].astype(F32)
-
-
-def join_kernel(own, recv, out):
-    n = own.shape[0] - PIECE
+    out[2 * TILE :, :] = sum(pieces).astype(BF)
+
+
+def quad_kernel(own, recv, out, piece):
+    n = 2 * TILE
     out[0:n, :] = own[0:n, :]
-    out[n : 2 * n, :] = recv[0:n, :]
-    total = own[n:, :].astype(F32) + recv[n:, :].astype(F32)
-    out[2 * n :, :] = two_terms(total) if n == 2 * TILE else total.astype(BF)
-
-
-def twin_kernel(own, recv, out):
-    out[...] = two_terms(own[...].astype(F32) + recv[...].astype(F32))
-
-
-def pick_kernel(slots, chunks, idx, place, *refs):
-    blocks, (msg, piece, held) = refs[:chunks], refs[chunks:]
+    out[n:, :] = recv[0:n, :]
+    piece[...] = (own[n:, :].astype(F32) + recv[n:, :].astype(F32)).astype(BF)
+
+
+def pass_kernel(block, own, other, out, total):
+    out[...] = block[...]
+    total[...] = (own[...].astype(F32) + other[...].astype(F32)).astype(total.dtype)
+
+
+def pick_kernel(slots, chunks, idx, *refs):
+    blocks, msg = refs[:chunks], refs[chunks]
     for s in range(slots):
         for o in range(chunks):
 
@@ -219,10 +211,6 @@
         @pl.when(idx[s] < 0)
         def _():
             msg[s * TILE : (s + 1) * TILE, :] = jnp.zeros((TILE, HID), BF)
-
-    for o in range(chunks):
-        held[lax.rem(place[2] + o, chunks)] = one_value(blocks[o][QUAD * TILE :, :])
-    piece[...] = sum(held[o] for o in range(chunks)).astype(BF)
 
 
 def back_kernel(slots, chunks, src, idx, live, tiles, recv, after, *refs):
@@ -254,8 +242,8 @@
     send[...] = acc[half:, :].astype(BF)
 
 
-def back_cut_kernel(keep_in, recv, twin, other_twin, keep, piece, *sends):
-    piece[...] = (one_value(twin[...]) + one_value(other_twin[...])).astype(BF)
+def back_cut_kernel(keep_in, recv, piece_in, far_piece, keep, piece, *sends):
+    piece[...] = (piece_in[...].astype(F32) + far_piece[...].astype(F32)).astype(BF)
     rows = keep.shape[0]
     for d, ref in enumerate((keep,) + sends):
         at = d * rows
@@ -332,7 +320,7 @@
     meta = jnp.zeros((8, TILE), jnp.int32).at[0, :slots].set(dest)
     other = flip(meta, "l", 1)[0, :slots]
     own_idx, other_idx = place(dest), place(other)
-    where = jnp.stack([k, x, y]).astype(jnp.int32)
+    where = jnp.stack([k, x]).astype(jnp.int32)
 
     panel = features
     if nh > 1:
@@ -422,35 +410,57 @@
     )
     cuts = lax.all_to_all(cuts, ("x", "k"), split_axis=0, concat_axis=0, tiled=True)
 
-    (packed,) = call(pack_kernel, [((TILE + PIECE, HID), BF)], [VMEM] * 2, scaled, cuts)
-    for bit, rows in ((4, 2 * TILE + PIECE), (2, 4 * TILE + 2 * PIECE)):
-        (packed,) = call(
-            join_kernel,
-            [((rows, HID), BF)],
-            [VMEM] * 2,
-            packed,
-            flip(packed, "l", bit),
-        )
+    (packed,) = call(
+        pair_kernel,
+        [((2 * TILE + PIECE, HID), BF)],
+        [VMEM] * 3,
+        scaled,
+        flip(scaled, "l", 4),
+        cuts,
+    )
+    packed, total = call(
+        quad_kernel,
+        [((4 * TILE, HID), BF), ((PIECE, HID), BF)],
+        [VMEM] * 2,
+        packed,
+        flip(packed, "l", 2),
+    )
+
+    def partner(axis, bit):
+        there = bit < lax.axis_size(axis)
+        return flip(total, axis, bit) if there else jnp.zeros_like(total)
+
+    sums = [("h", 1, F32), ("l", 4, F32), ("l", 1, F32)]
     blocks = [packed] * ny
     up = down = packed
     for step in range(1, ups + 1):
         up = shift(up, "y", 1)
-        blocks[(-step) % ny] = up
         if step <= downs:
             down = shift(down, "y", -1)
             blocks[step] = down
-    msg, piece = call(
+        if step < ups and sums:
+            axis, bit, kind = sums.pop(0)
+            up, total = call(
+                pass_kernel,
+                [((4 * TILE, HID), BF), ((PIECE, HID), kind)],
+                [VMEM] * 3,
+                up,
+                total,
+                partner(axis, bit),
+            )
+        blocks[(-step) % ny] = up
+    for axis, bit, kind in sums:
+        total = (total.astype(F32) + partner(axis, bit).astype(F32)).astype(kind)
+    (msg,) = call(
         functools.partial(pick_kernel, slots, ny),
-        [((slots * TILE, HID), BF), ((PIECE, HID), BF)],
-        [SMEM, SMEM] + [VMEM] * ny,
+        [((slots * TILE, HID), BF)],
+        [SMEM] + [VMEM] * ny,
         other_idx,
-        where,
         *blocks,
-        scratch=[pltpu.VMEM((ny, PIECE, HID), F32)],
     )
     got = flip(msg, "l", 1)
-    far_piece = flip(piece, "h", 1) if nh > 1 else jnp.zeros_like(piece)
-    (twin,) = call(twin_kernel, [((2 * PIECE, HID), BF)], [VMEM] * 2, piece, far_piece)
+    total = total + partner("y", 1)
+    total = total + partner("y", 2)
 
     half = sources // 2 * TILE
     keep, send = call(
@@ -462,7 +472,7 @@
         live,
         tiles,
         got,
-        twin,
+        total,
         *blocks,
         scratch=[pltpu.VMEM((sources * TILE, HID), F32), pltpu.VMEM((TILE, HID), BF)],
         flops=tile_flops,
@@ -474,8 +484,8 @@
         [VMEM] * 4,
         keep,
         flip(send, "k", 1),
-        twin,
-        flip(twin, "l", 1),
+        total,
+        partner("y", 4),
     )
     whole, *last = call(
         functools.partial(back_gather_kernel, nx),

time: 294 us -> 291 us (0.990)
  starting transfers between devices: 139 us -> 184 us
  waiting for transfers between devices: 119 us -> 87.1 us
  blocking collectives: 18.1 us -> 0 us
    ppermute x14 -> x18, starting transfers between devices: 78 us -> 106 us  [flip(): return lax.ppermute(value, axis, [(i, i ^ bit) for i in range(n)])]
    all_to_all x1 -> x0, blocking collectives: 18.1 us -> none  [body(): lax.all_to_all(cuts, ('x', 'k'), split_axis=0, concat_axis=0, tiled=True)]
    ppermute x14 -> x18, waiting for transfers between devices: 71.9 us -> 55.7 us  [flip(): return lax.ppermute(value, axis, [(i, i ^ bit) for i in range(n)])]
    ppermute x20, waiting for transfers between devices: 46.9 us -> 31.5 us  [shift(): return lax.ppermute(value, axis, [(i, (i + by) % n) for i in range(n)])]
    all_to_all x0 -> x1, starting transfers between devices: none -> 13.8 us  [body(): lax.all_to_all(cuts, ('x', 'k'), split_axis=0, concat_axis=0, tiled=True)]
    ppermute x20, starting transfers between devices: 61.2 us -> 64.4 us  [shift(): return lax.ppermute(value, axis, [(i, (i + by) % n) for i in range(n)])]
    pallas_call x20 -> x21, Pallas kernels: 13.3 us -> 13.5 us  [call(): pl.pallas_call(kernel, out_shape=shapes, in_specs=in_specs, out_specs=[VM...]
  transfers between devices with their start and end apart: 34 -> 39, of which waited for: 22 -> 24; matrix products, arithmetic and copies ran while one was open for 0% -> 0% of each run, Pallas kernels for 0% -> 0%
where the time goes in v6:
time: 291 us; the launch traced here: 289 us
  starting transfers between devices  184 us (63%)
  waiting for transfers between devices  87.1 us (30%)
  Pallas kernels  13.5 us (5%)
    ppermute x18, starting transfers between devices, flip(): return lax.ppermute(value, axis, [(i, i ^ bit) for i in range(n)])  106 us
    ppermute x20, starting transfers between devices, shift(): return lax.ppermute(value, axis, [(i, (i + by) % n) for i in range(n)])  64.4 us
    ppermute x18, waiting for transfers between devices, flip(): return lax.ppermute(value, axis, [(i, i ^ bit) for i in range(n)])  55.7 us
    ppermute x20, waiting for transfers between devices, shift(): return lax.ppermute(value, axis, [(i, (i + by) % n) for i in range(n)])  31.5 us
    all_to_all x1, starting transfers between devices, body(): lax.all_to_all(cuts, ('x', 'k'), split_axis=0, concat_axis=0, tiled=True)  13.8 us
    pallas_call x21, Pallas kernels, call(): pl.pallas_call(kernel, out_shape=shapes, in_specs=in_specs, out_specs=[VM...  13.5 us
  transfers between devices with their start and end apart: 39, of which 24 were waited for; matrix products, arithmetic and copies ran while one was open for 0% of the time, Pallas kernels for 0%

profile of v6, /device:TPU:1, one launch (start us, length us, event | category | flops | bytes accessed | tf_op | source)
XLA Modules:
  0.0 288.5 jit_solution(164149407581659661)
XLA Ops:
  0.6 19.9 %collective-permute-start.1 = (bf16[128,256]{1,0:T(8,128)(2,1)}, bf16[128,256]{1,0:T(8,128)(2,1)S(1)}, u32[]{:S(2)}, u32[]{:S(2)}) collective-permute-start(bf16[128,256]{1,0:T(8,128)(2,1)} %features.3), channel_id=1, source_target_pairs={{0,512},{512,0},{1,513},{513,1},{2,514},{514,2},{3,515},{515,3},{4... | collective-permute-start | bytes 196616 | tf_op jit(solution)/shard_map/ppermute | solution.py:300
  22.6 4.4 %collective-permute-start.2 = (bf16[256,256]{1,0:T(8,128)(2,1)S(1)}, bf16[256,256]{1,0:T(8,128)(2,1)S(1)}, u32[]{:S(2)}, u32[]{:S(2)}) collective-permute-start(bf16[256,256]{1,0:T(8,128)(2,1)S(1)} %get-tuple-element.109), channel_id=1, source_target_pairs={{0,384},{128,0},{256,128},{384,256},{1,385},{129,1},{257,129},{385... | collective-permute-start | bytes 393224 | tf_op jit(solution)/shard_map/ppermute | solution.py:304
  27.0 2.4 collective-permute-start.3
  29.4 2.5 collective-permute-start.4
  32.0 2.2 collective-permute-done.3
  34.2 2.1 collective-permute-done.4
  36.4 9.0 %collective-permute-start.5 = (bf16[1024,256]{1,0:T(8,128)(2,1)S(1)}, bf16[1024,256]{1,0:T(8,128)(2,1)S(1)}, u32[]{:S(2)}, u32[]{:S(2)}) collective-permute-start(bf16[1024,256]{1,0:T(8,128)(2,1)S(1)} %get-tuple-element.101), channel_id=1, source_target_pairs={{0,64},{64,0},{1,65},{65,1},{2,66},{66,2},{3,67},{67,3},{4,68},{68... | collective-permute-start | bytes 1572872 | tf_op jit(solution)/shard_map/ppermute | solution.py:300
  47.9 1.9 collective-permute-start.6
  49.9 3.4 %collective-permute-start = (s32[8,128]{1,0:T(8,128)S(1)}, s32[8,128]{1,0:T(8,128)S(1)}, u32[]{:S(2)}, u32[]{:S(2)}) collective-permute-start(s32[8,128]{1,0:T(8,128)S(1)} %scatter.4), channel_id=1, source_target_pairs={{0,1},{1,0},{2,3},{3,2},{4,5},{5,4},{6,7},{7,6},{8,9},{9,8},{10,11... | collective-permute-start | bytes 12296 | tf_op jit(solution)/shard_map/ppermute | solution.py:300
  53.3 12.7 %collective-permute-done = s32[8,128]{1,0:T(8,128)S(1)} collective-permute-done((s32[8,128]{1,0:T(8,128)S(1)}, s32[8,128]{1,0:T(8,128)S(1)}, u32[]{:S(2)}, u32[]{:S(2)}) %collective-permute-start) | collective-permute-done | bytes 4128 | tf_op jit(solution)/shard_map/ppermute | solution.py:300
  66.1 1.8 shard_map.138
  67.9 2.1 collective-permute-start.7
  70.0 4.4 %collective-permute-start.11 = (bf16[528,256]{1,0:T(8,128)(2,1)S(1)}, bf16[528,256]{1,0:T(8,128)(2,1)S(1)}, u32[]{:S(2)}, u32[]{:S(2)}) collective-permute-start(bf16[528,256]{1,0:T(8,128)(2,1)S(1)} %get-tuple-element.66), channel_id=1, source_target_pairs={{0,56},{8,0},{16,8},{24,16},{32,24},{40,32},{48,40},{56,48},{1,57}... | collective-permute-start | bytes 811016 | tf_op jit(solution)/shard_map/ppermute | solution.py:304
  74.4 3.4 %collective-permute-done.7.recv = bf16[528,256]{1,0:T(8,128)(2,1)S(1)} collective-permute-done((bf16[528,256]{1,0:T(8,128)(2,1)S(1)}, bf16[528,256]{1,0:T(8,128)(2,1)S(1)}, u32[]{:S(2)}, u32[]{:S(2)}) %collective-permute-start.7) | collective-permute-done | bytes 270368 | tf_op jit(solution)/shard_map/ppermute | solution.py:304
  77.9 1.9 collective-permute-start.8
  79.9 4.6 %collective-permute-start.12 = (bf16[528,256]{1,0:T(8,128)(2,1)S(1)}, bf16[528,256]{1,0:T(8,128)(2,1)S(1)}, u32[]{:S(2)}, u32[]{:S(2)}) collective-permute-start(bf16[528,256]{1,0:T(8,128)(2,1)S(1)} %shard_map.142), channel_id=1, source_target_pairs={{0,56},{8,0},{16,8},{24,16},{32,24},{40,32},{48,40},{56,48},{1,57}... | collective-permute-start | bytes 811016 | tf_op jit(solution)/shard_map/ppermute | solution.py:304
  84.5 2.4 collective-permute-done.8.recv
  87.0 1.9 collective-permute-start.9
  89.0 4.6 %collective-permute-start.13 = (bf16[528,256]{1,0:T(8,128)(2,1)S(1)}, bf16[528,256]{1,0:T(8,128)(2,1)S(1)}, u32[]{:S(2)}, u32[]{:S(2)}) collective-permute-start(bf16[528,256]{1,0:T(8,128)(2,1)S(1)} %shard_map.143), channel_id=1, source_target_pairs={{0,56},{8,0},{16,8},{24,16},{32,24},{40,32},{48,40},{56,48},{1,57}... | collective-permute-start | bytes 811016 | tf_op jit(solution)/shard_map/ppermute | solution.py:304
  93.6 1.8 collective-permute-done.9.recv
  95.5 1.9 collective-permute-start.10
  97.4 6.5 %collective-permute-done.10.refs_1_ = bf16[528,256]{1,0:T(8,128)(2,1)S(1)} collective-permute-done((bf16[528,256]{1,0:T(8,128)(2,1)S(1)}, bf16[528,256]{1,0:T(8,128)(2,1)S(1)}, u32[]{:S(2)}, u32[]{:S(2)}) %collective-permute-start.10) | collective-permute-done | bytes 270368 | tf_op jit(solution)/shard_map/ppermute | solution.py:304
  104.0 3.7 %collective-permute-start.14 = (bf16[272,256]{1,0:T(8,128)(2,1)S(1)}, bf16[272,256]{1,0:T(8,128)(2,1)S(1)}, u32[]{:S(2)}, u32[]{:S(2)}) collective-permute-start(bf16[272,256]{1,0:T(8,128)(2,1)S(1)} %get-tuple-element.70), channel_id=1, source_target_pairs={{0,2},{1,3},{2,0},{3,1},{4,6},{5,7},{6,4},{7,5},{8,10},{9,11},{10,... | collective-permute-start | bytes 417800 | tf_op jit(solution)/shard_map/ppermute | solution.py:300
  107.7 3.0 %collective-permute-done.14.recv = bf16[272,256]{1,0:T(8,128)(2,1)S(1)} collective-permute-done((bf16[272,256]{1,0:T(8,128)(2,1)S(1)}, bf16[272,256]{1,0:T(8,128)(2,1)S(1)}, u32[]{:S(2)}, u32[]{:S(2)}) %collective-permute-start.14) | collective-permute-done | bytes 139296 | tf_op jit(solution)/shard_map/ppermute | solution.py:300
  110.7 7.6 %collective-permute-start.15 = (bf16[144,256]{1,0:T(8,128)(2,1)S(1)}, bf16[144,256]{1,0:T(8,128)(2,1)S(1)}, u32[]{:S(2)}, u32[]{:S(2)}) collective-permute-start(bf16[144,256]{1,0:T(8,128)(2,1)S(1)} %get-tuple-element.72), channel_id=1, source_target_pairs={{0,4},{1,5},{2,6},{3,7},{4,0},{5,1},{6,2},{7,3},{8,12},{9,13},{10,... | collective-permute-start | bytes 221192 | tf_op jit(solution)/shard_map/ppermute | solution.py:300
  118.3 1.7 collective-permute-done.15.recv
  122.7 13.8 %all-to-all-start = ((bf16[8,80,256]{2,1,0:T(8,128)(2,1)}), bf16[8,80,256]{2,1,0:T(8,128)(2,1)S(1)}, u32[]{:S(2)}, u32[]{:S(2)}) async-start(bf16[8,80,256]{2,1,0:T(8,128)(2,1)} %bitcast.10), calls=%async_computation | async-start | bytes 655360 | tf_op jit(solution)/shard_map/all_to_all | solution.py:411
  136.5 6.0 %collective-permute-start.16 = (bf16[128,256]{1,0:T(8,128)(2,1)S(1)}, bf16[128,256]{1,0:T(8,128)(2,1)S(1)}, u32[]{:S(2)}, u32[]{:S(2)}) collective-permute-start(bf16[128,256]{1,0:T(8,128)(2,1)S(1)} %get-tuple-element.77.own), channel_id=1, source_target_pairs={{0,4},{1,5},{2,6},{3,7},{4,0},{5,1},{6,2},{7,3},{8,12},{9,13},{10,... | collective-permute-start | bytes 196616 | tf_op jit(solution)/shard_map/ppermute | solution.py:300
  142.5 7.3 %collective-permute-done.16.recv = bf16[128,256]{1,0:T(8,128)(2,1)S(1)} collective-permute-done((bf16[128,256]{1,0:T(8,128)(2,1)S(1)}, bf16[128,256]{1,0:T(8,128)(2,1)S(1)}, u32[]{:S(2)}, u32[]{:S(2)}) %collective-permute-start.16) | collective-permute-done | bytes 65568 | tf_op jit(solution)/shard_map/ppermute | solution.py:300
  149.9 1.9 collective-permute-start.17
  151.8 9.2 %collective-permute-done.17.recv = bf16[336,256]{1,0:T(8,128)(2,1)S(1)} collective-permute-done((bf16[336,256]{1,0:T(8,128)(2,1)S(1)}, bf16[336,256]{1,0:T(8,128)(2,1)S(1)}, u32[]{:S(2)}, u32[]{:S(2)}) %collective-permute-start.17) | collective-permute-done | bytes 172064 | tf_op jit(solution)/shard_map/ppermute | solution.py:300
  161.1 1.9 collective-permute-start.21
  163.0 12.4 %collective-permute-start.22 = (bf16[80,256]{1,0:T(8,128)(2,1)S(1)}, bf16[80,256]{1,0:T(8,128)(2,1)S(1)}, u32[]{:S(2)}, u32[]{:S(2)}) collective-permute-start(bf16[80,256]{1,0:T(8,128)(2,1)S(1)} %get-tuple-element.80.own), channel_id=1, source_target_pairs={{0,512},{512,0},{1,513},{513,1},{2,514},{514,2},{3,515},{515,3},{4... | collective-permute-start | bytes 122888 | tf_op jit(solution)/shard_map/ppermute | solution.py:300
  175.4 4.6 %collective-permute-start.18 = (bf16[512,256]{1,0:T(8,128)(2,1)S(1)}, bf16[512,256]{1,0:T(8,128)(2,1)S(1)}, u32[]{:S(2)}, u32[]{:S(2)}) collective-permute-start(bf16[512,256]{1,0:T(8,128)(2,1)S(1)} %get-tuple-element.79.refs_0_), channel_id=1, source_target_pairs={{0,56},{8,0},{16,8},{24,16},{32,24},{40,32},{48,40},{56,48},{1,57}... | collective-permute-start | bytes 786440 | tf_op jit(solution)/shard_map/ppermute | solution.py:304
  180.1 1.9 collective-permute-start.23
  182.0 4.7 %collective-permute-start.24 = (f32[80,256]{1,0:T(8,128)S(1)}, f32[80,256]{1,0:T(8,128)S(1)}, u32[]{:S(2)}, u32[]{:S(2)}) collective-permute-start(f32[80,256]{1,0:T(8,128)S(1)} %get-tuple-element.82.own), channel_id=1, source_target_pairs={{0,4},{1,5},{2,6},{3,7},{4,0},{5,1},{6,2},{7,3},{8,12},{9,13},{10,... | collective-permute-start | bytes 245768 | tf_op jit(solution)/shard_map/ppermute | solution.py:300
  186.7 4.6 %collective-permute-start.19 = (bf16[512,256]{1,0:T(8,128)(2,1)S(1)}, bf16[512,256]{1,0:T(8,128)(2,1)S(1)}, u32[]{:S(2)}, u32[]{:S(2)}) collective-permute-start(bf16[512,256]{1,0:T(8,128)(2,1)S(1)} %collective-permute-done.18.refs_1_), channel_id=1, source_target_pairs={{0,56},{8,0},{16,8},{24,16},{32,24},{40,32},{48,40},{56,48},{1,57}... | collective-permute-start | bytes 786440 | tf_op jit(solution)/shard_map/ppermute | solution.py:304
  191.3 4.0 %collective-permute-done.24.other = f32[80,256]{1,0:T(8,128)S(1)} collective-permute-done((f32[80,256]{1,0:T(8,128)S(1)}, f32[80,256]{1,0:T(8,128)S(1)}, u32[]{:S(2)}, u32[]{:S(2)}) %collective-permute-start.24) | collective-permute-done | bytes 81952 | tf_op jit(solution)/shard_map/ppermute | solution.py:300
  195.3 1.9 collective-permute-start.25
  197.2 1.9 collective-permute-start.26
  199.1 4.6 %collective-permute-start.20 = (bf16[512,256]{1,0:T(8,128)(2,1)S(1)}, bf16[512,256]{1,0:T(8,128)(2,1)S(1)}, u32[]{:S(2)}, u32[]{:S(2)}) collective-permute-start(bf16[512,256]{1,0:T(8,128)(2,1)S(1)} %collective-permute-done.19.refs_2_), channel_id=1, source_target_pairs={{0,56},{8,0},{16,8},{24,16},{32,24},{40,32},{48,40},{56,48},{1,57}... | collective-permute-start | bytes 786440 | tf_op jit(solution)/shard_map/ppermute | solution.py:304
  203.7 1.5 collective-permute-done.25.block
  205.3 2.2 collective-permute-start.27
  207.5 1.9 collective-permute-done.20.refs_3_
  209.4 5.0 %collective-permute-done.27.refs_4_ = bf16[512,256]{1,0:T(8,128)(2,1)S(1)} collective-permute-done((bf16[512,256]{1,0:T(8,128)(2,1)S(1)}, bf16[512,256]{1,0:T(8,128)(2,1)S(1)}, u32[]{:S(2)}, u32[]{:S(2)}) %collective-permute-start.27) | collective-permute-done | bytes 262176 | tf_op jit(solution)/shard_map/ppermute | solution.py:304
  214.3 1.9 shard_map.153
  216.2 1.9 collective-permute-start.28
  218.1 1.9 collective-permute-start.29
  220.1 3.3 %collective-permute-done.29 = f32[80,256]{1,0:T(8,128)S(1)} collective-permute-done((f32[80,256]{1,0:T(8,128)S(1)}, f32[80,256]{1,0:T(8,128)S(1)}, u32[]{:S(2)}, u32[]{:S(2)}) %collective-permute-start.29) | collective-permute-done | bytes 81952 | tf_op jit(solution)/shard_map/ppermute | solution.py:300
  223.3 4.3 %collective-permute-start.30 = (f32[80,256]{1,0:T(8,128)S(1)}, f32[80,256]{1,0:T(8,128)S(1)}, u32[]{:S(2)}, u32[]{:S(2)}) collective-permute-start(f32[80,256]{1,0:T(8,128)S(1)} %add.67), channel_id=1, source_target_pairs={{0,16},{8,24},{16,0},{24,8},{32,48},{40,56},{48,32},{56,40},{1,17}... | collective-permute-start | bytes 245768 | tf_op jit(solution)/shard_map/ppermute | solution.py:300
  227.7 1.8 collective-permute-done.30
  229.5 2.0 collective-permute-done.28.recv
  231.6 4.0 %shard_map.154 = (f32[1024,256]{1,0:T(8,128)S(1)}, bf16[1024,256]{1,0:T(8,128)(2,1)S(1)}) custom-call(s32[10]{0:T(128)S(1)} %xor_add_fusion.src, s32[10]{0:T(128)S(1)} %and_select_fusion.6.idx, s32[10]{0:T(128)S(1)} %compare_convert_fusion.1.live, bf16[10,128,128]{2,1,0:T(8,128)(2,1)S(1)} %get-tuple-element.59.tiles, ...), custom_call_target="tpu_custom_call" | custom-call | flops 83886080 | bytes 4735096 | tf_op jit(solution)/shard_map/pallas_call | solution.py:27
  235.6 5.6 %collective-permute-start.31 = (bf16[1024,256]{1,0:T(8,128)(2,1)S(1)}, bf16[1024,256]{1,0:T(8,128)(2,1)S(1)}, u32[]{:S(2)}, u32[]{:S(2)}) collective-permute-start(bf16[1024,256]{1,0:T(8,128)(2,1)S(1)} %get-tuple-element.88), channel_id=1, source_target_pairs={{0,64},{64,0},{1,65},{65,1},{2,66},{66,2},{3,67},{67,3},{4,68},{68... | collective-permute-start | bytes 1572872 | tf_op jit(solution)/shard_map/ppermute | solution.py:300
  241.2 7.4 %collective-permute-start.32 = (f32[80,256]{1,0:T(8,128)S(1)}, f32[80,256]{1,0:T(8,128)S(1)}, u32[]{:S(2)}, u32[]{:S(2)}) collective-permute-start(f32[80,256]{1,0:T(8,128)S(1)} %add.68.after.piece_in), channel_id=1, source_target_pairs={{0,32},{8,40},{16,48},{24,56},{32,0},{40,8},{48,16},{56,24},{1,33}... | collective-permute-start | bytes 245768 | tf_op jit(solution)/shard_map/ppermute | solution.py:300
  248.6 2.7 collective-permute-done.32.far_piece
  251.5 5.7 %collective-permute-start.33 = (bf16[336,256]{1,0:T(8,128)(2,1)S(1)}, bf16[336,256]{1,0:T(8,128)(2,1)S(1)}, u32[]{:S(2)}, u32[]{:S(2)}) collective-permute-start(bf16[336,256]{1,0:T(8,128)(2,1)S(1)} %get-tuple-element.91), channel_id=1, source_target_pairs={{0,128},{128,256},{256,384},{384,0},{1,129},{129,257},{257,385},{3... | collective-permute-start | bytes 516104 | tf_op jit(solution)/shard_map/ppermute | solution.py:304
  257.2 4.4 %collective-permute-start.34 = (bf16[336,256]{1,0:T(8,128)(2,1)S(1)}, bf16[336,256]{1,0:T(8,128)(2,1)S(1)}, u32[]{:S(2)}, u32[]{:S(2)}) collective-permute-start(bf16[336,256]{1,0:T(8,128)(2,1)S(1)} %get-tuple-element.92), channel_id=1, source_target_pairs={{0,256},{128,384},{256,0},{384,128},{1,257},{129,385},{257,1},{385... | collective-permute-start | bytes 516104 | tf_op jit(solution)/shard_map/ppermute | solution.py:304
  261.6 1.9 collective-permute-start.35
  263.6 3.6 %collective-permute-done.34.refs_1_ = bf16[336,256]{1,0:T(8,128)(2,1)S(1)} collective-permute-done((bf16[336,256]{1,0:T(8,128)(2,1)S(1)}, bf16[336,256]{1,0:T(8,128)(2,1)S(1)}, u32[]{:S(2)}, u32[]{:S(2)}) %collective-permute-start.34) | collective-permute-done | bytes 172064 | tf_op jit(solution)/shard_map/ppermute | solution.py:304
  268.8 4.0 %collective-permute-start.37 = (bf16[272,256]{1,0:T(8,128)(2,1)S(1)}, bf16[272,256]{1,0:T(8,128)(2,1)S(1)}, u32[]{:S(2)}, u32[]{:S(2)}) collective-permute-start(bf16[272,256]{1,0:T(8,128)(2,1)S(1)} %get-tuple-element.96.whole), channel_id=1, source_target_pairs={{0,64},{64,0},{1,65},{65,1},{2,66},{66,2},{3,67},{67,3},{4,68},{68... | collective-permute-start | bytes 417800 | tf_op jit(solution)/shard_map/ppermute | solution.py:300
  272.8 8.4 %collective-permute-start.36 = (bf16[128,256]{1,0:T(8,128)(2,1)S(1)}, bf16[128,256]{1,0:T(8,128)(2,1)S(1)}, u32[]{:S(2)}, u32[]{:S(2)}) collective-permute-start(bf16[128,256]{1,0:T(8,128)(2,1)S(1)} %get-tuple-element.95), channel_id=1, source_target_pairs={{0,512},{512,0},{1,513},{513,1},{2,514},{514,2},{3,515},{515,3},{4... | collective-permute-start | bytes 196616 | tf_op jit(solution)/shard_map/ppermute | solution.py:300
  281.2 5.9 %collective-permute-done.36.far = bf16[128,256]{1,0:T(8,128)(2,1)S(1)} collective-permute-done((bf16[128,256]{1,0:T(8,128)(2,1)S(1)}, bf16[128,256]{1,0:T(8,128)(2,1)S(1)}, u32[]{:S(2)}, u32[]{:S(2)}) %collective-permute-start.36) | collective-permute-done | bytes 65568 | tf_op jit(solution)/shard_map/ppermute | solution.py:300
  287.1 1.4 shard_map.157
  (68 shorter events, 9.2 us)
Async XLA Ops:
  0.6 21.9 %collective-permute-start.1 = (bf16[128,256]{1,0:T(8,128)(2,1)}, bf16[128,256]{1,0:T(8,128)(2,1)S(1)}, u32[]{:S(2)}, u32[]{:S(2)}) collective-permute-start(bf16[128,256]{1,0:T(8,128)(2,1)} %features.3), channel_id=1, source_target_pairs={{0,512},{512,0},{1,513},{513,1},{2,514},{514,2},{3,515},{515,3},{4... | collective-permute-start | bytes 196616 | tf_op jit(solution)/shard_map/ppermute | solution.py:300
  22.6 9.4 %collective-permute-start.2 = (bf16[256,256]{1,0:T(8,128)(2,1)S(1)}, bf16[256,256]{1,0:T(8,128)(2,1)S(1)}, u32[]{:S(2)}, u32[]{:S(2)}) collective-permute-start(bf16[256,256]{1,0:T(8,128)(2,1)S(1)} %get-tuple-element.109), channel_id=1, source_target_pairs={{0,384},{128,0},{256,128},{384,256},{1,385},{129,1},{257,129},{385... | collective-permute-start | bytes 393224 | tf_op jit(solution)/shard_map/ppermute | solution.py:304
  27.0 7.2 %collective-permute-start.3 = (bf16[256,256]{1,0:T(8,128)(2,1)S(1)}, bf16[256,256]{1,0:T(8,128)(2,1)S(1)}, u32[]{:S(2)}, u32[]{:S(2)}) collective-permute-start(bf16[256,256]{1,0:T(8,128)(2,1)S(1)} %get-tuple-element.109), channel_id=1, source_target_pairs={{0,256},{128,384},{256,0},{384,128},{1,257},{129,385},{257,1},{385... | collective-permute-start | bytes 393224 | tf_op jit(solution)/shard_map/ppermute | solution.py:304
  29.4 6.9 %collective-permute-start.4 = (bf16[256,256]{1,0:T(8,128)(2,1)S(1)}, bf16[256,256]{1,0:T(8,128)(2,1)S(1)}, u32[]{:S(2)}, u32[]{:S(2)}) collective-permute-start(bf16[256,256]{1,0:T(8,128)(2,1)S(1)} %get-tuple-element.109), channel_id=1, source_target_pairs={{0,128},{128,256},{256,384},{384,0},{1,129},{129,257},{257,385},{3... | collective-permute-start | bytes 393224 | tf_op jit(solution)/shard_map/ppermute | solution.py:304
  34.2 11.8 %copy-start.7 = (s32[1,1,10]{2,1,0:T(1,128)S(1)}, s32[1,1,10]{2,1,0:T(1,128)}, u32[]{:S(2)}) copy-start(s32[1,1,10]{2,1,0:T(1,128)} %param.15) | copy-start | bytes 124
  36.3 10.5 %copy-start = (s32[1,1,10,128,128]{4,3,2,1,0:T(8,128)S(1)}, s32[1,1,10,128,128]{4,3,2,1,0:T(8,128)}, u32[]{:S(2)}) copy-start(s32[1,1,10,128,128]{4,3,2,1,0:T(8,128)} %param.13) | copy-start | bytes 1966084
  36.4 10.5 %collective-permute-start.5 = (bf16[1024,256]{1,0:T(8,128)(2,1)S(1)}, bf16[1024,256]{1,0:T(8,128)(2,1)S(1)}, u32[]{:S(2)}, u32[]{:S(2)}) collective-permute-start(bf16[1024,256]{1,0:T(8,128)(2,1)S(1)} %get-tuple-element.101), channel_id=1, source_target_pairs={{0,64},{64,0},{1,65},{65,1},{2,66},{66,2},{3,67},{67,3},{4,68},{68... | collective-permute-start | bytes 1572872 | tf_op jit(solution)/shard_map/ppermute | solution.py:300
  47.9 1.9 copy-start.8
  47.9 18.1 %collective-permute-start.6 = (bf16[1296,256]{1,0:T(8,128)(2,1)S(1)}, bf16[1296,256]{1,0:T(8,128)(2,1)S(1)}, u32[]{:S(2)}, u32[]{:S(2)}) collective-permute-start(bf16[1296,256]{1,0:T(8,128)(2,1)S(1)} %get-tuple-element.60), channel_id=1, source_target_pairs={{0,1},{1,0},{2,3},{3,2},{4,5},{5,4},{6,7},{7,6},{8,9},{9,8},{10,11... | collective-permute-start | bytes 1990664 | tf_op jit(solution)/shard_map/ppermute | solution.py:300
  49.9 16.1 %collective-permute-start = (s32[8,128]{1,0:T(8,128)S(1)}, s32[8,128]{1,0:T(8,128)S(1)}, u32[]{:S(2)}, u32[]{:S(2)}) collective-permute-start(s32[8,128]{1,0:T(8,128)S(1)} %scatter.4), channel_id=1, source_target_pairs={{0,1},{1,0},{2,3},{3,2},{4,5},{5,4},{6,7},{7,6},{8,9},{9,8},{10,11... | collective-permute-start | bytes 12296 | tf_op jit(solution)/shard_map/ppermute | solution.py:300
  67.9 9.9 %collective-permute-start.7 = (bf16[528,256]{1,0:T(8,128)(2,1)S(1)}, bf16[528,256]{1,0:T(8,128)(2,1)S(1)}, u32[]{:S(2)}, u32[]{:S(2)}) collective-permute-start(bf16[528,256]{1,0:T(8,128)(2,1)S(1)} %get-tuple-element.62), channel_id=1, source_target_pairs={{0,8},{8,16},{16,24},{24,32},{32,40},{40,48},{48,56},{56,0},{1,9},... | collective-permute-start | bytes 811016 | tf_op jit(solution)/shard_map/ppermute | solution.py:304
  70.0 9.8 %collective-permute-start.11 = (bf16[528,256]{1,0:T(8,128)(2,1)S(1)}, bf16[528,256]{1,0:T(8,128)(2,1)S(1)}, u32[]{:S(2)}, u32[]{:S(2)}) collective-permute-start(bf16[528,256]{1,0:T(8,128)(2,1)S(1)} %get-tuple-element.66), channel_id=1, source_target_pairs={{0,56},{8,0},{16,8},{24,16},{32,24},{40,32},{48,40},{56,48},{1,57}... | collective-permute-start | bytes 811016 | tf_op jit(solution)/shard_map/ppermute | solution.py:304
  77.9 9.0 %collective-permute-start.8 = (bf16[528,256]{1,0:T(8,128)(2,1)S(1)}, bf16[528,256]{1,0:T(8,128)(2,1)S(1)}, u32[]{:S(2)}, u32[]{:S(2)}) collective-permute-start(bf16[528,256]{1,0:T(8,128)(2,1)S(1)} %shard_map.139), channel_id=1, source_target_pairs={{0,8},{8,16},{16,24},{24,32},{32,40},{40,48},{48,56},{56,0},{1,9},... | collective-permute-start | bytes 811016 | tf_op jit(solution)/shard_map/ppermute | solution.py:304
  79.9 9.0 %collective-permute-start.12 = (bf16[528,256]{1,0:T(8,128)(2,1)S(1)}, bf16[528,256]{1,0:T(8,128)(2,1)S(1)}, u32[]{:S(2)}, u32[]{:S(2)}) collective-permute-start(bf16[528,256]{1,0:T(8,128)(2,1)S(1)} %shard_map.142), channel_id=1, source_target_pairs={{0,56},{8,0},{16,8},{24,16},{32,24},{40,32},{48,40},{56,48},{1,57}... | collective-permute-start | bytes 811016 | tf_op jit(solution)/shard_map/ppermute | solution.py:304
  87.0 8.4 %collective-permute-start.9 = (bf16[528,256]{1,0:T(8,128)(2,1)S(1)}, bf16[528,256]{1,0:T(8,128)(2,1)S(1)}, u32[]{:S(2)}, u32[]{:S(2)}) collective-permute-start(bf16[528,256]{1,0:T(8,128)(2,1)S(1)} %shard_map.140), channel_id=1, source_target_pairs={{0,8},{8,16},{16,24},{24,32},{32,40},{40,48},{48,56},{56,0},{1,9},... | collective-permute-start | bytes 811016 | tf_op jit(solution)/shard_map/ppermute | solution.py:304
  89.0 8.4 %collective-permute-start.13 = (bf16[528,256]{1,0:T(8,128)(2,1)S(1)}, bf16[528,256]{1,0:T(8,128)(2,1)S(1)}, u32[]{:S(2)}, u32[]{:S(2)}) collective-permute-start(bf16[528,256]{1,0:T(8,128)(2,1)S(1)} %shard_map.143), channel_id=1, source_target_pairs={{0,56},{8,0},{16,8},{24,16},{32,24},{40,32},{48,40},{56,48},{1,57}... | collective-permute-start | bytes 811016 | tf_op jit(solution)/shard_map/ppermute | solution.py:304
  95.5 8.4 %collective-permute-start.10 = (bf16[528,256]{1,0:T(8,128)(2,1)S(1)}, bf16[528,256]{1,0:T(8,128)(2,1)S(1)}, u32[]{:S(2)}, u32[]{:S(2)}) collective-permute-start(bf16[528,256]{1,0:T(8,128)(2,1)S(1)} %shard_map.141), channel_id=1, source_target_pairs={{0,8},{8,16},{16,24},{24,32},{32,40},{40,48},{48,56},{56,0},{1,9},... | collective-permute-start | bytes 811016 | tf_op jit(solution)/shard_map/ppermute | solution.py:304
  104.0 6.7 %collective-permute-start.14 = (bf16[272,256]{1,0:T(8,128)(2,1)S(1)}, bf16[272,256]{1,0:T(8,128)(2,1)S(1)}, u32[]{:S(2)}, u32[]{:S(2)}) collective-permute-start(bf16[272,256]{1,0:T(8,128)(2,1)S(1)} %get-tuple-element.70), channel_id=1, source_target_pairs={{0,2},{1,3},{2,0},{3,1},{4,6},{5,7},{6,4},{7,5},{8,10},{9,11},{10,... | collective-permute-start | bytes 417800 | tf_op jit(solution)/shard_map/ppermute | solution.py:300
  110.7 9.4 %copy-start.1 = (bf16[128,256]{1,0:T(8,128)(2,1)S(1)}, bf16[128,256]{1,0:T(8,128)(2,1)}, u32[]{:S(2)}) copy-start(bf16[128,256]{1,0:T(8,128)(2,1)} %features.3) | copy-start | bytes 196612
  110.7 9.4 %copy-start.2 = (bf16[256,256]{1,0:T(8,128)(2,1)S(1)}, bf16[256,256]{1,0:T(8,128)(2,1)}, u32[]{:S(2)}) copy-start(bf16[256,256]{1,0:T(8,128)(2,1)} %w_self.3) | copy-start | bytes 393220
  110.7 9.4 %copy-start.3 = (bf16[256,256]{1,0:T(8,128)(2,1)S(1)}, bf16[256,256]{1,0:T(8,128)(2,1)}, u32[]{:S(2)}) copy-start(bf16[256,256]{1,0:T(8,128)(2,1)} %w_neigh.1) | copy-start | bytes 393220
  110.7 9.4 %copy-start.4 = (bf16[128,256]{1,0:T(8,128)(2,1)S(1)}, bf16[128,256]{1,0:T(8,128)(2,1)}, u32[]{:S(2)}) copy-start(bf16[128,256]{1,0:T(8,128)(2,1)} %grad_out.1) | copy-start | bytes 196612
  110.7 9.3 %collective-permute-start.15 = (bf16[144,256]{1,0:T(8,128)(2,1)S(1)}, bf16[144,256]{1,0:T(8,128)(2,1)S(1)}, u32[]{:S(2)}, u32[]{:S(2)}) collective-permute-start(bf16[144,256]{1,0:T(8,128)(2,1)S(1)} %get-tuple-element.72), channel_id=1, source_target_pairs={{0,4},{1,5},{2,6},{3,7},{4,0},{5,1},{6,2},{7,3},{8,12},{9,13},{10,... | collective-permute-start | bytes 221192 | tf_op jit(solution)/shard_map/ppermute | solution.py:300
  120.1 0.7 copy-start.5
  120.1 0.7 copy-start.6
  122.7 27.2 %all-to-all-start = ((bf16[8,80,256]{2,1,0:T(8,128)(2,1)}), bf16[8,80,256]{2,1,0:T(8,128)(2,1)S(1)}, u32[]{:S(2)}, u32[]{:S(2)}) async-start(bf16[8,80,256]{2,1,0:T(8,128)(2,1)} %bitcast.10), calls=%async_computation | async-start | bytes 655360 | tf_op jit(solution)/shard_map/all_to_all | solution.py:411
  136.5 13.4 %collective-permute-start.16 = (bf16[128,256]{1,0:T(8,128)(2,1)S(1)}, bf16[128,256]{1,0:T(8,128)(2,1)S(1)}, u32[]{:S(2)}, u32[]{:S(2)}) collective-permute-start(bf16[128,256]{1,0:T(8,128)(2,1)S(1)} %get-tuple-element.77.own), channel_id=1, source_target_pairs={{0,4},{1,5},{2,6},{3,7},{4,0},{5,1},{6,2},{7,3},{8,12},{9,13},{10,... | collective-permute-start | bytes 196616 | tf_op jit(solution)/shard_map/ppermute | solution.py:300
  149.9 11.1 %collective-permute-start.17 = (bf16[336,256]{1,0:T(8,128)(2,1)S(1)}, bf16[336,256]{1,0:T(8,128)(2,1)S(1)}, u32[]{:S(2)}, u32[]{:S(2)}) collective-permute-start(bf16[336,256]{1,0:T(8,128)(2,1)S(1)} %shard_map.148.own), channel_id=1, source_target_pairs={{0,2},{1,3},{2,0},{3,1},{4,6},{5,7},{6,4},{7,5},{8,10},{9,11},{10,... | collective-permute-start | bytes 516104 | tf_op jit(solution)/shard_map/ppermute | solution.py:300
  161.1 19.0 %collective-permute-start.21 = (bf16[512,256]{1,0:T(8,128)(2,1)S(1)}, bf16[512,256]{1,0:T(8,128)(2,1)S(1)}, u32[]{:S(2)}, u32[]{:S(2)}) collective-permute-start(bf16[512,256]{1,0:T(8,128)(2,1)S(1)} %get-tuple-element.79.refs_0_), channel_id=1, source_target_pairs={{0,8},{8,16},{16,24},{24,32},{32,40},{40,48},{48,56},{56,0},{1,9},... | collective-permute-start | bytes 786440 | tf_op jit(solution)/shard_map/ppermute | solution.py:304
  163.0 17.0 %collective-permute-start.22 = (bf16[80,256]{1,0:T(8,128)(2,1)S(1)}, bf16[80,256]{1,0:T(8,128)(2,1)S(1)}, u32[]{:S(2)}, u32[]{:S(2)}) collective-permute-start(bf16[80,256]{1,0:T(8,128)(2,1)S(1)} %get-tuple-element.80.own), channel_id=1, source_target_pairs={{0,512},{512,0},{1,513},{513,1},{2,514},{514,2},{3,515},{515,3},{4... | collective-permute-start | bytes 122888 | tf_op jit(solution)/shard_map/ppermute | solution.py:300
  175.4 11.3 %collective-permute-start.18 = (bf16[512,256]{1,0:T(8,128)(2,1)S(1)}, bf16[512,256]{1,0:T(8,128)(2,1)S(1)}, u32[]{:S(2)}, u32[]{:S(2)}) collective-permute-start(bf16[512,256]{1,0:T(8,128)(2,1)S(1)} %get-tuple-element.79.refs_0_), channel_id=1, source_target_pairs={{0,56},{8,0},{16,8},{24,16},{32,24},{40,32},{48,40},{56,48},{1,57}... | collective-permute-start | bytes 786440 | tf_op jit(solution)/shard_map/ppermute | solution.py:304
  180.1 15.2 %collective-permute-start.23 = (bf16[512,256]{1,0:T(8,128)(2,1)S(1)}, bf16[512,256]{1,0:T(8,128)(2,1)S(1)}, u32[]{:S(2)}, u32[]{:S(2)}) collective-permute-start(bf16[512,256]{1,0:T(8,128)(2,1)S(1)} %get-tuple-element.81.refs_7_), channel_id=1, source_target_pairs={{0,8},{8,16},{16,24},{24,32},{32,40},{40,48},{48,56},{56,0},{1,9},... | collective-permute-start | bytes 786440 | tf_op jit(solution)/shard_map/ppermute | solution.py:304
  182.0 13.2 %collective-permute-start.24 = (f32[80,256]{1,0:T(8,128)S(1)}, f32[80,256]{1,0:T(8,128)S(1)}, u32[]{:S(2)}, u32[]{:S(2)}) collective-permute-start(f32[80,256]{1,0:T(8,128)S(1)} %get-tuple-element.82.own), channel_id=1, source_target_pairs={{0,4},{1,5},{2,6},{3,7},{4,0},{5,1},{6,2},{7,3},{8,12},{9,13},{10,... | collective-permute-start | bytes 245768 | tf_op jit(solution)/shard_map/ppermute | solution.py:300
  186.7 12.4 %collective-permute-start.19 = (bf16[512,256]{1,0:T(8,128)(2,1)S(1)}, bf16[512,256]{1,0:T(8,128)(2,1)S(1)}, u32[]{:S(2)}, u32[]{:S(2)}) collective-permute-start(bf16[512,256]{1,0:T(8,128)(2,1)S(1)} %collective-permute-done.18.refs_1_), channel_id=1, source_target_pairs={{0,56},{8,0},{16,8},{24,16},{32,24},{40,32},{48,40},{56,48},{1,57}... | collective-permute-start | bytes 786440 | tf_op jit(solution)/shard_map/ppermute | solution.py:304
  195.3 10.0 %collective-permute-start.25 = (bf16[512,256]{1,0:T(8,128)(2,1)S(1)}, bf16[512,256]{1,0:T(8,128)(2,1)S(1)}, u32[]{:S(2)}, u32[]{:S(2)}) collective-permute-start(bf16[512,256]{1,0:T(8,128)(2,1)S(1)} %get-tuple-element.83.refs_6_), channel_id=1, source_target_pairs={{0,8},{8,16},{16,24},{24,32},{32,40},{40,48},{48,56},{56,0},{1,9},... | collective-permute-start | bytes 786440 | tf_op jit(solution)/shard_map/ppermute | solution.py:304
  197.2 6.5 %collective-permute-start.26 = (f32[80,256]{1,0:T(8,128)S(1)}, f32[80,256]{1,0:T(8,128)S(1)}, u32[]{:S(2)}, u32[]{:S(2)}) collective-permute-start(f32[80,256]{1,0:T(8,128)S(1)} %get-tuple-element.84.own), channel_id=1, source_target_pairs={{0,1},{1,0},{2,3},{3,2},{4,5},{5,4},{6,7},{7,6},{8,9},{9,8},{10,11... | collective-permute-start | bytes 245768 | tf_op jit(solution)/shard_map/ppermute | solution.py:300
  199.1 10.2 %collective-permute-start.20 = (bf16[512,256]{1,0:T(8,128)(2,1)S(1)}, bf16[512,256]{1,0:T(8,128)(2,1)S(1)}, u32[]{:S(2)}, u32[]{:S(2)}) collective-permute-start(bf16[512,256]{1,0:T(8,128)(2,1)S(1)} %collective-permute-done.19.refs_2_), channel_id=1, source_target_pairs={{0,56},{8,0},{16,8},{24,16},{32,24},{40,32},{48,40},{56,48},{1,57}... | collective-permute-start | bytes 786440 | tf_op jit(solution)/shard_map/ppermute | solution.py:304
  205.3 9.1 %collective-permute-start.27 = (bf16[512,256]{1,0:T(8,128)(2,1)S(1)}, bf16[512,256]{1,0:T(8,128)(2,1)S(1)}, u32[]{:S(2)}, u32[]{:S(2)}) collective-permute-start(bf16[512,256]{1,0:T(8,128)(2,1)S(1)} %get-tuple-element.85.refs_5_), channel_id=1, source_target_pairs={{0,8},{8,16},{16,24},{24,32},{32,40},{40,48},{48,56},{56,0},{1,9},... | collective-permute-start | bytes 786440 | tf_op jit(solution)/shard_map/ppermute | solution.py:304
  216.2 15.4 %collective-permute-start.28 = (bf16[1280,256]{1,0:T(8,128)(2,1)S(1)}, bf16[1280,256]{1,0:T(8,128)(2,1)S(1)}, u32[]{:S(2)}, u32[]{:S(2)}) collective-permute-start(bf16[1280,256]{1,0:T(8,128)(2,1)S(1)} %shard_map.153), channel_id=1, source_target_pairs={{0,1},{1,0},{2,3},{3,2},{4,5},{5,4},{6,7},{7,6},{8,9},{9,8},{10,11... | collective-permute-start | bytes 1966088 | tf_op jit(solution)/shard_map/ppermute | solution.py:300
  218.1 5.2 %collective-permute-start.29 = (f32[80,256]{1,0:T(8,128)S(1)}, f32[80,256]{1,0:T(8,128)S(1)}, u32[]{:S(2)}, u32[]{:S(2)}) collective-permute-start(f32[80,256]{1,0:T(8,128)S(1)} %get-tuple-element.86), channel_id=1, source_target_pairs={{0,8},{8,0},{16,24},{24,16},{32,40},{40,32},{48,56},{56,48},{1,9},... | collective-permute-start | bytes 245768 | tf_op jit(solution)/shard_map/ppermute | solution.py:300
  223.3 6.2 %collective-permute-start.30 = (f32[80,256]{1,0:T(8,128)S(1)}, f32[80,256]{1,0:T(8,128)S(1)}, u32[]{:S(2)}, u32[]{:S(2)}) collective-permute-start(f32[80,256]{1,0:T(8,128)S(1)} %add.67), channel_id=1, source_target_pairs={{0,16},{8,24},{16,0},{24,8},{32,48},{40,56},{48,32},{56,40},{1,17}... | collective-permute-start | bytes 245768 | tf_op jit(solution)/shard_map/ppermute | solution.py:300
  235.6 15.8 %collective-permute-start.31 = (bf16[1024,256]{1,0:T(8,128)(2,1)S(1)}, bf16[1024,256]{1,0:T(8,128)(2,1)S(1)}, u32[]{:S(2)}, u32[]{:S(2)}) collective-permute-start(bf16[1024,256]{1,0:T(8,128)(2,1)S(1)} %get-tuple-element.88), channel_id=1, source_target_pairs={{0,64},{64,0},{1,65},{65,1},{2,66},{66,2},{3,67},{67,3},{4,68},{68... | collective-permute-start | bytes 1572872 | tf_op jit(solution)/shard_map/ppermute | solution.py:300
  241.2 10.1 %collective-permute-start.32 = (f32[80,256]{1,0:T(8,128)S(1)}, f32[80,256]{1,0:T(8,128)S(1)}, u32[]{:S(2)}, u32[]{:S(2)}) collective-permute-start(f32[80,256]{1,0:T(8,128)S(1)} %add.68.after.piece_in), channel_id=1, source_target_pairs={{0,32},{8,40},{16,48},{24,56},{32,0},{40,8},{48,16},{56,24},{1,33}... | collective-permute-start | bytes 245768 | tf_op jit(solution)/shard_map/ppermute | solution.py:300
  251.5 12.1 %collective-permute-start.33 = (bf16[336,256]{1,0:T(8,128)(2,1)S(1)}, bf16[336,256]{1,0:T(8,128)(2,1)S(1)}, u32[]{:S(2)}, u32[]{:S(2)}) collective-permute-start(bf16[336,256]{1,0:T(8,128)(2,1)S(1)} %get-tuple-element.91), channel_id=1, source_target_pairs={{0,128},{128,256},{256,384},{384,0},{1,129},{129,257},{257,385},{3... | collective-permute-start | bytes 516104 | tf_op jit(solution)/shard_map/ppermute | solution.py:304
  257.2 10.0 %collective-permute-start.34 = (bf16[336,256]{1,0:T(8,128)(2,1)S(1)}, bf16[336,256]{1,0:T(8,128)(2,1)S(1)}, u32[]{:S(2)}, u32[]{:S(2)}) collective-permute-start(bf16[336,256]{1,0:T(8,128)(2,1)S(1)} %get-tuple-element.92), channel_id=1, source_target_pairs={{0,256},{128,384},{256,0},{384,128},{1,257},{129,385},{257,1},{385... | collective-permute-start | bytes 516104 | tf_op jit(solution)/shard_map/ppermute | solution.py:304
  261.6 6.6 %collective-permute-start.35 = (bf16[336,256]{1,0:T(8,128)(2,1)S(1)}, bf16[336,256]{1,0:T(8,128)(2,1)S(1)}, u32[]{:S(2)}, u32[]{:S(2)}) collective-permute-start(bf16[336,256]{1,0:T(8,128)(2,1)S(1)} %get-tuple-element.93), channel_id=1, source_target_pairs={{0,384},{128,0},{256,128},{384,256},{1,385},{129,1},{257,129},{385... | collective-permute-start | bytes 516104 | tf_op jit(solution)/shard_map/ppermute | solution.py:304
  268.8 18.3 %collective-permute-start.37 = (bf16[272,256]{1,0:T(8,128)(2,1)S(1)}, bf16[272,256]{1,0:T(8,128)(2,1)S(1)}, u32[]{:S(2)}, u32[]{:S(2)}) collective-permute-start(bf16[272,256]{1,0:T(8,128)(2,1)S(1)} %get-tuple-element.96.whole), channel_id=1, source_target_pairs={{0,64},{64,0},{1,65},{65,1},{2,66},{66,2},{3,67},{67,3},{4,68},{68... | collective-permute-start | bytes 417800 | tf_op jit(solution)/shard_map/ppermute | solution.py:300
  272.8 14.3 %collective-permute-start.36 = (bf16[128,256]{1,0:T(8,128)(2,1)S(1)}, bf16[128,256]{1,0:T(8,128)(2,1)S(1)}, u32[]{:S(2)}, u32[]{:S(2)}) collective-permute-start(bf16[128,256]{1,0:T(8,128)(2,1)S(1)} %get-tuple-element.95), channel_id=1, source_target_pairs={{0,512},{512,0},{1,513},{513,1},{2,514},{514,2},{3,515},{515,3},{4... | collective-permute-start | bytes 196616 | tf_op jit(solution)/shard_map/ppermute | solution.py:300

commit v7 on v6

--- a/solution.py
+++ b/solution.py
@@ -430,7 +430,7 @@
         there = bit < lax.axis_size(axis)
         return flip(total, axis, bit) if there else jnp.zeros_like(total)
 
-    sums = [("h", 1, F32), ("l", 4, F32), ("l", 1, F32)]
+    sums = [("l", 4, F32), ("l", 1, F32), ("y", 1, F32)]
     blocks = [packed] * ny
     up = down = packed
     for step in range(1, ups + 1):
@@ -459,8 +459,8 @@
         *blocks,
     )
     got = flip(msg, "l", 1)
-    total = total + partner("y", 1)
     total = total + partner("y", 2)
+    total = (total + partner("y", 4)).astype(BF)
 
     half = sources // 2 * TILE
     keep, send = call(
@@ -485,7 +485,7 @@
         keep,
         flip(send, "k", 1),
         total,
-        partner("y", 4),
+        partner("h", 1),
     )
     whole, *last = call(
         functools.partial(back_gather_kernel, nx),

time: 291 us -> 286 us (0.983)
  waiting for transfers between devices: 87.1 us -> 77.4 us
  starting transfers between devices: 184 us -> 189 us
    ppermute x18, starting transfers between devices: 106 us -> 116 us  [flip(): return lax.ppermute(value, axis, [(i, i ^ bit) for i in range(n)])]
    ppermute x18, waiting for transfers between devices: 55.7 us -> 50.4 us  [flip(): return lax.ppermute(value, axis, [(i, i ^ bit) for i in range(n)])]
    ppermute x20, waiting for transfers between devices: 31.5 us -> 27 us  [shift(): return lax.ppermute(value, axis, [(i, (i + by) % n) for i in range(n)])]
    all_to_all x1, starting transfers between devices: 13.8 us -> 10.8 us  [body(): lax.all_to_all(cuts, ('x', 'k'), split_axis=0, concat_axis=0, tiled=True)]
  transfers between devices with their start and end apart: 39 -> 39, of which waited for: 24 -> 21; matrix products, arithmetic and copies ran while one was open for 0% -> 0% of each run, Pallas kernels for 0% -> 0%
where the time goes in v7:
time: 286 us; the launch traced here: 283 us
  starting transfers between devices  189 us (66%)
  waiting for transfers between devices  77.4 us (27%)
  Pallas kernels  13.4 us (5%)
    ppermute x18, starting transfers between devices, flip(): return lax.ppermute(value, axis, [(i, i ^ bit) for i in range(n)])  116 us
    ppermute x20, starting transfers between devices, shift(): return lax.ppermute(value, axis, [(i, (i + by) % n) for i in range(n)])  62.1 us
    ppermute x18, waiting for transfers between devices, flip(): return lax.ppermute(value, axis, [(i, i ^ bit) for i in range(n)])  50.4 us
    ppermute x20, waiting for transfers between devices, shift(): return lax.ppermute(value, axis, [(i, (i + by) % n) for i in range(n)])  27 us
    pallas_call x21, Pallas kernels, call(): pl.pallas_call(kernel, out_shape=shapes, in_specs=in_specs, out_specs=[VM...  13.4 us
    all_to_all x1, starting transfers between devices, body(): lax.all_to_all(cuts, ('x', 'k'), split_axis=0, concat_axis=0, tiled=True)  10.8 us
  transfers between devices with their start and end apart: 39, of which 21 were waited for; matrix products, arithmetic and copies ran while one was open for 0% of the time, Pallas kernels for 0%

profile of v7, /device:TPU:1, one launch (start us, length us, event | category | flops | bytes accessed | tf_op | source)
XLA Modules:
  0.0 283.0 jit_solution(18132563042625055884)
XLA Ops:
  0.6 19.9 %collective-permute-start.1 = (bf16[128,256]{1,0:T(8,128)(2,1)}, bf16[128,256]{1,0:T(8,128)(2,1)S(1)}, u32[]{:S(2)}, u32[]{:S(2)}) collective-permute-start(bf16[128,256]{1,0:T(8,128)(2,1)} %features.3), channel_id=1, source_target_pairs={{0,512},{512,0},{1,513},{513,1},{2,514},{514,2},{3,515},{515,3},{4... | collective-permute-start | bytes 196616 | tf_op jit(solution)/shard_map/ppermute | solution.py:300
  21.4 1.2 collective-permute-done.1
  22.6 4.4 %collective-permute-start.2 = (bf16[256,256]{1,0:T(8,128)(2,1)S(1)}, bf16[256,256]{1,0:T(8,128)(2,1)S(1)}, u32[]{:S(2)}, u32[]{:S(2)}) collective-permute-start(bf16[256,256]{1,0:T(8,128)(2,1)S(1)} %get-tuple-element.109), channel_id=1, source_target_pairs={{0,384},{128,0},{256,128},{384,256},{1,385},{129,1},{257,129},{385... | collective-permute-start | bytes 393224 | tf_op jit(solution)/shard_map/ppermute | solution.py:304
  27.0 2.4 collective-permute-start.3
  29.4 2.5 collective-permute-start.4
  32.0 2.2 collective-permute-done.3
  34.2 2.1 collective-permute-done.4
  36.4 9.0 %collective-permute-start.5 = (bf16[1024,256]{1,0:T(8,128)(2,1)S(1)}, bf16[1024,256]{1,0:T(8,128)(2,1)S(1)}, u32[]{:S(2)}, u32[]{:S(2)}) collective-permute-start(bf16[1024,256]{1,0:T(8,128)(2,1)S(1)} %get-tuple-element.101), channel_id=1, source_target_pairs={{0,64},{64,0},{1,65},{65,1},{2,66},{66,2},{3,67},{67,3},{4,68},{68... | collective-permute-start | bytes 1572872 | tf_op jit(solution)/shard_map/ppermute | solution.py:300
  46.9 1.0 shard_map.137
  47.9 1.9 collective-permute-start.6
  49.9 3.4 %collective-permute-start = (s32[8,128]{1,0:T(8,128)S(1)}, s32[8,128]{1,0:T(8,128)S(1)}, u32[]{:S(2)}, u32[]{:S(2)}) collective-permute-start(s32[8,128]{1,0:T(8,128)S(1)} %scatter.4), channel_id=1, source_target_pairs={{0,1},{1,0},{2,3},{3,2},{4,5},{5,4},{6,7},{7,6},{8,9},{9,8},{10,11... | collective-permute-start | bytes 12296 | tf_op jit(solution)/shard_map/ppermute | solution.py:300
  53.3 12.7 %collective-permute-done = s32[8,128]{1,0:T(8,128)S(1)} collective-permute-done((s32[8,128]{1,0:T(8,128)S(1)}, s32[8,128]{1,0:T(8,128)S(1)}, u32[]{:S(2)}, u32[]{:S(2)}) %collective-permute-start) | collective-permute-done | bytes 4128 | tf_op jit(solution)/shard_map/ppermute | solution.py:300
  66.1 1.8 shard_map.138
  67.8 2.1 collective-permute-start.7
  70.0 4.4 %collective-permute-start.11 = (bf16[528,256]{1,0:T(8,128)(2,1)S(1)}, bf16[528,256]{1,0:T(8,128)(2,1)S(1)}, u32[]{:S(2)}, u32[]{:S(2)}) collective-permute-start(bf16[528,256]{1,0:T(8,128)(2,1)S(1)} %get-tuple-element.66), channel_id=1, source_target_pairs={{0,56},{8,0},{16,8},{24,16},{32,24},{40,32},{48,40},{56,48},{1,57}... | collective-permute-start | bytes 811016 | tf_op jit(solution)/shard_map/ppermute | solution.py:304
  74.3 3.2 %collective-permute-done.7.recv = bf16[528,256]{1,0:T(8,128)(2,1)S(1)} collective-permute-done((bf16[528,256]{1,0:T(8,128)(2,1)S(1)}, bf16[528,256]{1,0:T(8,128)(2,1)S(1)}, u32[]{:S(2)}, u32[]{:S(2)}) %collective-permute-start.7) | collective-permute-done | bytes 270368 | tf_op jit(solution)/shard_map/ppermute | solution.py:304
  77.6 1.9 collective-permute-start.8
  79.6 4.6 %collective-permute-start.12 = (bf16[528,256]{1,0:T(8,128)(2,1)S(1)}, bf16[528,256]{1,0:T(8,128)(2,1)S(1)}, u32[]{:S(2)}, u32[]{:S(2)}) collective-permute-start(bf16[528,256]{1,0:T(8,128)(2,1)S(1)} %shard_map.142), channel_id=1, source_target_pairs={{0,56},{8,0},{16,8},{24,16},{32,24},{40,32},{48,40},{56,48},{1,57}... | collective-permute-start | bytes 811016 | tf_op jit(solution)/shard_map/ppermute | solution.py:304
  84.2 2.2 collective-permute-done.8.recv
  86.4 1.9 collective-permute-start.9
  88.4 4.6 %collective-permute-start.13 = (bf16[528,256]{1,0:T(8,128)(2,1)S(1)}, bf16[528,256]{1,0:T(8,128)(2,1)S(1)}, u32[]{:S(2)}, u32[]{:S(2)}) collective-permute-start(bf16[528,256]{1,0:T(8,128)(2,1)S(1)} %shard_map.143), channel_id=1, source_target_pairs={{0,56},{8,0},{16,8},{24,16},{32,24},{40,32},{48,40},{56,48},{1,57}... | collective-permute-start | bytes 811016 | tf_op jit(solution)/shard_map/ppermute | solution.py:304
  93.0 1.8 collective-permute-done.9.recv
  94.9 1.9 collective-permute-start.10
  96.8 6.5 %collective-permute-done.10.refs_1_ = bf16[528,256]{1,0:T(8,128)(2,1)S(1)} collective-permute-done((bf16[528,256]{1,0:T(8,128)(2,1)S(1)}, bf16[528,256]{1,0:T(8,128)(2,1)S(1)}, u32[]{:S(2)}, u32[]{:S(2)}) %collective-permute-start.10) | collective-permute-done | bytes 270368 | tf_op jit(solution)/shard_map/ppermute | solution.py:304
  103.4 3.6 %collective-permute-start.14 = (bf16[272,256]{1,0:T(8,128)(2,1)S(1)}, bf16[272,256]{1,0:T(8,128)(2,1)S(1)}, u32[]{:S(2)}, u32[]{:S(2)}) collective-permute-start(bf16[272,256]{1,0:T(8,128)(2,1)S(1)} %get-tuple-element.70), channel_id=1, source_target_pairs={{0,2},{1,3},{2,0},{3,1},{4,6},{5,7},{6,4},{7,5},{8,10},{9,11},{10,... | collective-permute-start | bytes 417800 | tf_op jit(solution)/shard_map/ppermute | solution.py:300
  107.0 3.1 %collective-permute-done.14.recv = bf16[272,256]{1,0:T(8,128)(2,1)S(1)} collective-permute-done((bf16[272,256]{1,0:T(8,128)(2,1)S(1)}, bf16[272,256]{1,0:T(8,128)(2,1)S(1)}, u32[]{:S(2)}, u32[]{:S(2)}) %collective-permute-start.14) | collective-permute-done | bytes 139296 | tf_op jit(solution)/shard_map/ppermute | solution.py:300
  110.1 10.2 %collective-permute-start.15 = (bf16[144,256]{1,0:T(8,128)(2,1)S(1)}, bf16[144,256]{1,0:T(8,128)(2,1)S(1)}, u32[]{:S(2)}, u32[]{:S(2)}) collective-permute-start(bf16[144,256]{1,0:T(8,128)(2,1)S(1)} %get-tuple-element.72), channel_id=1, source_target_pairs={{0,4},{1,5},{2,6},{3,7},{4,0},{5,1},{6,2},{7,3},{8,12},{9,13},{10,... | collective-permute-start | bytes 221192 | tf_op jit(solution)/shard_map/ppermute | solution.py:300
  120.4 2.7 collective-permute-done.15.recv
  123.8 1.0 shard_map.146
  125.7 10.8 %all-to-all-start = ((bf16[8,80,256]{2,1,0:T(8,128)(2,1)}), bf16[8,80,256]{2,1,0:T(8,128)(2,1)S(1)}, u32[]{:S(2)}, u32[]{:S(2)}) async-start(bf16[8,80,256]{2,1,0:T(8,128)(2,1)} %bitcast.10), calls=%async_computation | async-start | bytes 655360 | tf_op jit(solution)/shard_map/all_to_all | solution.py:411
  136.5 6.5 %collective-permute-start.16 = (bf16[128,256]{1,0:T(8,128)(2,1)S(1)}, bf16[128,256]{1,0:T(8,128)(2,1)S(1)}, u32[]{:S(2)}, u32[]{:S(2)}) collective-permute-start(bf16[128,256]{1,0:T(8,128)(2,1)S(1)} %get-tuple-element.77.own), channel_id=1, source_target_pairs={{0,4},{1,5},{2,6},{3,7},{4,0},{5,1},{6,2},{7,3},{8,12},{9,13},{10,... | collective-permute-start | bytes 196616 | tf_op jit(solution)/shard_map/ppermute | solution.py:300
  143.0 6.2 %collective-permute-done.16.recv = bf16[128,256]{1,0:T(8,128)(2,1)S(1)} collective-permute-done((bf16[128,256]{1,0:T(8,128)(2,1)S(1)}, bf16[128,256]{1,0:T(8,128)(2,1)S(1)}, u32[]{:S(2)}, u32[]{:S(2)}) %collective-permute-start.16) | collective-permute-done | bytes 65568 | tf_op jit(solution)/shard_map/ppermute | solution.py:300
  149.2 1.9 collective-permute-start.17
  151.2 9.9 %collective-permute-done.17.recv = bf16[336,256]{1,0:T(8,128)(2,1)S(1)} collective-permute-done((bf16[336,256]{1,0:T(8,128)(2,1)S(1)}, bf16[336,256]{1,0:T(8,128)(2,1)S(1)}, u32[]{:S(2)}, u32[]{:S(2)}) %collective-permute-start.17) | collective-permute-done | bytes 172064 | tf_op jit(solution)/shard_map/ppermute | solution.py:300
  161.1 1.9 collective-permute-start.21
  163.0 5.4 %collective-permute-start.22 = (bf16[80,256]{1,0:T(8,128)(2,1)S(1)}, bf16[80,256]{1,0:T(8,128)(2,1)S(1)}, u32[]{:S(2)}, u32[]{:S(2)}) collective-permute-start(bf16[80,256]{1,0:T(8,128)(2,1)S(1)} %get-tuple-element.80.own), channel_id=1, source_target_pairs={{0,4},{1,5},{2,6},{3,7},{4,0},{5,1},{6,2},{7,3},{8,12},{9,13},{10,... | collective-permute-start | bytes 122888 | tf_op jit(solution)/shard_map/ppermute | solution.py:300
  168.4 4.6 %collective-permute-start.18 = (bf16[512,256]{1,0:T(8,128)(2,1)S(1)}, bf16[512,256]{1,0:T(8,128)(2,1)S(1)}, u32[]{:S(2)}, u32[]{:S(2)}) collective-permute-start(bf16[512,256]{1,0:T(8,128)(2,1)S(1)} %get-tuple-element.79.refs_0_), channel_id=1, source_target_pairs={{0,56},{8,0},{16,8},{24,16},{32,24},{40,32},{48,40},{56,48},{1,57}... | collective-permute-start | bytes 786440 | tf_op jit(solution)/shard_map/ppermute | solution.py:304
  173.0 1.9 collective-permute-start.23
  174.9 2.9 %collective-permute-start.24 = (f32[80,256]{1,0:T(8,128)S(1)}, f32[80,256]{1,0:T(8,128)S(1)}, u32[]{:S(2)}, u32[]{:S(2)}) collective-permute-start(f32[80,256]{1,0:T(8,128)S(1)} %get-tuple-element.82.own), channel_id=1, source_target_pairs={{0,1},{1,0},{2,3},{3,2},{4,5},{5,4},{6,7},{7,6},{8,9},{9,8},{10,11... | collective-permute-start | bytes 245768 | tf_op jit(solution)/shard_map/ppermute | solution.py:300
  177.9 4.6 %collective-permute-start.19 = (bf16[512,256]{1,0:T(8,128)(2,1)S(1)}, bf16[512,256]{1,0:T(8,128)(2,1)S(1)}, u32[]{:S(2)}, u32[]{:S(2)}) collective-permute-start(bf16[512,256]{1,0:T(8,128)(2,1)S(1)} %collective-permute-done.18.refs_1_), channel_id=1, source_target_pairs={{0,56},{8,0},{16,8},{24,16},{32,24},{40,32},{48,40},{56,48},{1,57}... | collective-permute-start | bytes 786440 | tf_op jit(solution)/shard_map/ppermute | solution.py:304
  182.5 1.9 collective-permute-start.25
  184.4 4.2 %collective-permute-start.26 = (f32[80,256]{1,0:T(8,128)S(1)}, f32[80,256]{1,0:T(8,128)S(1)}, u32[]{:S(2)}, u32[]{:S(2)}) collective-permute-start(f32[80,256]{1,0:T(8,128)S(1)} %get-tuple-element.84.own), channel_id=1, source_target_pairs={{0,8},{8,0},{16,24},{24,16},{32,40},{40,32},{48,56},{56,48},{1,9},... | collective-permute-start | bytes 245768 | tf_op jit(solution)/shard_map/ppermute | solution.py:300
  188.6 2.6 collective-permute-start.20
  191.4 3.7 %collective-permute-start.27 = (bf16[512,256]{1,0:T(8,128)(2,1)S(1)}, bf16[512,256]{1,0:T(8,128)(2,1)S(1)}, u32[]{:S(2)}, u32[]{:S(2)}) collective-permute-start(bf16[512,256]{1,0:T(8,128)(2,1)S(1)} %get-tuple-element.85.refs_5_), channel_id=1, source_target_pairs={{0,8},{8,16},{16,24},{24,32},{32,40},{40,48},{48,56},{56,0},{1,9},... | collective-permute-start | bytes 786440 | tf_op jit(solution)/shard_map/ppermute | solution.py:304
  195.9 3.8 %collective-permute-done.27.refs_4_ = bf16[512,256]{1,0:T(8,128)(2,1)S(1)} collective-permute-done((bf16[512,256]{1,0:T(8,128)(2,1)S(1)}, bf16[512,256]{1,0:T(8,128)(2,1)S(1)}, u32[]{:S(2)}, u32[]{:S(2)}) %collective-permute-start.27) | collective-permute-done | bytes 262176 | tf_op jit(solution)/shard_map/ppermute | solution.py:304
  199.7 1.8 shard_map.153
  201.5 3.4 %collective-permute-start.28 = (bf16[1280,256]{1,0:T(8,128)(2,1)S(1)}, bf16[1280,256]{1,0:T(8,128)(2,1)S(1)}, u32[]{:S(2)}, u32[]{:S(2)}) collective-permute-start(bf16[1280,256]{1,0:T(8,128)(2,1)S(1)} %shard_map.153), channel_id=1, source_target_pairs={{0,1},{1,0},{2,3},{3,2},{4,5},{5,4},{6,7},{7,6},{8,9},{9,8},{10,11... | collective-permute-start | bytes 1966088 | tf_op jit(solution)/shard_map/ppermute | solution.py:300
  204.9 2.6 collective-permute-start.29
  207.5 4.3 %collective-permute-done.29 = f32[80,256]{1,0:T(8,128)S(1)} collective-permute-done((f32[80,256]{1,0:T(8,128)S(1)}, f32[80,256]{1,0:T(8,128)S(1)}, u32[]{:S(2)}, u32[]{:S(2)}) %collective-permute-start.29) | collective-permute-done | bytes 81952 | tf_op jit(solution)/shard_map/ppermute | solution.py:300
  211.9 4.9 %collective-permute-start.30 = (f32[80,256]{1,0:T(8,128)S(1)}, f32[80,256]{1,0:T(8,128)S(1)}, u32[]{:S(2)}, u32[]{:S(2)}) collective-permute-start(f32[80,256]{1,0:T(8,128)S(1)} %add.67), channel_id=1, source_target_pairs={{0,32},{8,40},{16,48},{24,56},{32,0},{40,8},{48,16},{56,24},{1,33}... | collective-permute-start | bytes 245768 | tf_op jit(solution)/shard_map/ppermute | solution.py:300
  216.8 5.1 %collective-permute-done.30 = f32[80,256]{1,0:T(8,128)S(1)} collective-permute-done((f32[80,256]{1,0:T(8,128)S(1)}, f32[80,256]{1,0:T(8,128)S(1)}, u32[]{:S(2)}, u32[]{:S(2)}) %collective-permute-start.30) | collective-permute-done | bytes 81952 | tf_op jit(solution)/shard_map/ppermute | solution.py:300
  221.9 4.0 %shard_map.154 = (f32[1024,256]{1,0:T(8,128)S(1)}, bf16[1024,256]{1,0:T(8,128)(2,1)S(1)}) custom-call(s32[10]{0:T(128)S(1)} %xor_add_fusion.src, s32[10]{0:T(128)S(1)} %and_select_fusion.6.idx, s32[10]{0:T(128)S(1)} %compare_convert_fusion.1.live, bf16[10,128,128]{2,1,0:T(8,128)(2,1)S(1)} %get-tuple-element.59.tiles, ...), custom_call_target="tpu_custom_call" | custom-call | flops 83886080 | bytes 4694136 | tf_op jit(solution)/shard_map/pallas_call | solution.py:27
  225.9 6.7 %collective-permute-start.31 = (bf16[1024,256]{1,0:T(8,128)(2,1)S(1)}, bf16[1024,256]{1,0:T(8,128)(2,1)S(1)}, u32[]{:S(2)}, u32[]{:S(2)}) collective-permute-start(bf16[1024,256]{1,0:T(8,128)(2,1)S(1)} %get-tuple-element.88), channel_id=1, source_target_pairs={{0,64},{64,0},{1,65},{65,1},{2,66},{66,2},{3,67},{67,3},{4,68},{68... | collective-permute-start | bytes 1572872 | tf_op jit(solution)/shard_map/ppermute | solution.py:300
  232.6 12.6 %collective-permute-start.32 = (bf16[80,256]{1,0:T(8,128)(2,1)S(1)}, bf16[80,256]{1,0:T(8,128)(2,1)S(1)}, u32[]{:S(2)}, u32[]{:S(2)}) collective-permute-start(bf16[80,256]{1,0:T(8,128)(2,1)S(1)} %add_convert_fusion.after.piece_in), channel_id=1, source_target_pairs={{0,512},{512,0},{1,513},{513,1},{2,514},{514,2},{3,515},{515,3},{4... | collective-permute-start | bytes 122888 | tf_op jit(solution)/shard_map/ppermute | solution.py:300
  245.2 1.9 collective-permute-done.32.far_piece
  247.3 2.9 %collective-permute-start.33 = (bf16[336,256]{1,0:T(8,128)(2,1)S(1)}, bf16[336,256]{1,0:T(8,128)(2,1)S(1)}, u32[]{:S(2)}, u32[]{:S(2)}) collective-permute-start(bf16[336,256]{1,0:T(8,128)(2,1)S(1)} %get-tuple-element.91), channel_id=1, source_target_pairs={{0,128},{128,256},{256,384},{384,0},{1,129},{129,257},{257,385},{3... | collective-permute-start | bytes 516104 | tf_op jit(solution)/shard_map/ppermute | solution.py:304
  250.2 4.1 %collective-permute-start.34 = (bf16[336,256]{1,0:T(8,128)(2,1)S(1)}, bf16[336,256]{1,0:T(8,128)(2,1)S(1)}, u32[]{:S(2)}, u32[]{:S(2)}) collective-permute-start(bf16[336,256]{1,0:T(8,128)(2,1)S(1)} %get-tuple-element.92), channel_id=1, source_target_pairs={{0,256},{128,384},{256,0},{384,128},{1,257},{129,385},{257,1},{385... | collective-permute-start | bytes 516104 | tf_op jit(solution)/shard_map/ppermute | solution.py:304
  254.3 3.1 %collective-permute-start.35 = (bf16[336,256]{1,0:T(8,128)(2,1)S(1)}, bf16[336,256]{1,0:T(8,128)(2,1)S(1)}, u32[]{:S(2)}, u32[]{:S(2)}) collective-permute-start(bf16[336,256]{1,0:T(8,128)(2,1)S(1)} %get-tuple-element.93), channel_id=1, source_target_pairs={{0,384},{128,0},{256,128},{384,256},{1,385},{129,1},{257,129},{385... | collective-permute-start | bytes 516104 | tf_op jit(solution)/shard_map/ppermute | solution.py:304
  257.4 2.6 collective-permute-done.34.refs_1_
  260.0 1.8 collective-permute-done.35.refs_2_
  262.5 3.8 %collective-permute-start.37 = (bf16[272,256]{1,0:T(8,128)(2,1)S(1)}, bf16[272,256]{1,0:T(8,128)(2,1)S(1)}, u32[]{:S(2)}, u32[]{:S(2)}) collective-permute-start(bf16[272,256]{1,0:T(8,128)(2,1)S(1)} %get-tuple-element.96.whole), channel_id=1, source_target_pairs={{0,64},{64,0},{1,65},{65,1},{2,66},{66,2},{3,67},{67,3},{4,68},{68... | collective-permute-start | bytes 417800 | tf_op jit(solution)/shard_map/ppermute | solution.py:300
  266.3 12.9 %collective-permute-start.36 = (bf16[128,256]{1,0:T(8,128)(2,1)S(1)}, bf16[128,256]{1,0:T(8,128)(2,1)S(1)}, u32[]{:S(2)}, u32[]{:S(2)}) collective-permute-start(bf16[128,256]{1,0:T(8,128)(2,1)S(1)} %get-tuple-element.95), channel_id=1, source_target_pairs={{0,512},{512,0},{1,513},{513,1},{2,514},{514,2},{3,515},{515,3},{4... | collective-permute-start | bytes 196616 | tf_op jit(solution)/shard_map/ppermute | solution.py:300
  279.2 2.4 collective-permute-done.36.far
  281.6 1.4 shard_map.157
  (68 shorter events, 5.9 us)
Async XLA Ops:
  0.6 21.9 %collective-permute-start.1 = (bf16[128,256]{1,0:T(8,128)(2,1)}, bf16[128,256]{1,0:T(8,128)(2,1)S(1)}, u32[]{:S(2)}, u32[]{:S(2)}) collective-permute-start(bf16[128,256]{1,0:T(8,128)(2,1)} %features.3), channel_id=1, source_target_pairs={{0,512},{512,0},{1,513},{513,1},{2,514},{514,2},{3,515},{515,3},{4... | collective-permute-start | bytes 196616 | tf_op jit(solution)/shard_map/ppermute | solution.py:300
  22.6 9.4 %collective-permute-start.2 = (bf16[256,256]{1,0:T(8,128)(2,1)S(1)}, bf16[256,256]{1,0:T(8,128)(2,1)S(1)}, u32[]{:S(2)}, u32[]{:S(2)}) collective-permute-start(bf16[256,256]{1,0:T(8,128)(2,1)S(1)} %get-tuple-element.109), channel_id=1, source_target_pairs={{0,384},{128,0},{256,128},{384,256},{1,385},{129,1},{257,129},{385... | collective-permute-start | bytes 393224 | tf_op jit(solution)/shard_map/ppermute | solution.py:304
  27.0 7.2 %collective-permute-start.3 = (bf16[256,256]{1,0:T(8,128)(2,1)S(1)}, bf16[256,256]{1,0:T(8,128)(2,1)S(1)}, u32[]{:S(2)}, u32[]{:S(2)}) collective-permute-start(bf16[256,256]{1,0:T(8,128)(2,1)S(1)} %get-tuple-element.109), channel_id=1, source_target_pairs={{0,256},{128,384},{256,0},{384,128},{1,257},{129,385},{257,1},{385... | collective-permute-start | bytes 393224 | tf_op jit(solution)/shard_map/ppermute | solution.py:304
  29.4 6.9 %collective-permute-start.4 = (bf16[256,256]{1,0:T(8,128)(2,1)S(1)}, bf16[256,256]{1,0:T(8,128)(2,1)S(1)}, u32[]{:S(2)}, u32[]{:S(2)}) collective-permute-start(bf16[256,256]{1,0:T(8,128)(2,1)S(1)} %get-tuple-element.109), channel_id=1, source_target_pairs={{0,128},{128,256},{256,384},{384,0},{1,129},{129,257},{257,385},{3... | collective-permute-start | bytes 393224 | tf_op jit(solution)/shard_map/ppermute | solution.py:304
  34.2 11.8 %copy-start.7 = (s32[1,1,10]{2,1,0:T(1,128)S(1)}, s32[1,1,10]{2,1,0:T(1,128)}, u32[]{:S(2)}) copy-start(s32[1,1,10]{2,1,0:T(1,128)} %param.15) | copy-start | bytes 124
  36.3 10.5 %copy-start = (s32[1,1,10,128,128]{4,3,2,1,0:T(8,128)S(1)}, s32[1,1,10,128,128]{4,3,2,1,0:T(8,128)}, u32[]{:S(2)}) copy-start(s32[1,1,10,128,128]{4,3,2,1,0:T(8,128)} %param.13) | copy-start | bytes 1966084
  36.4 10.5 %collective-permute-start.5 = (bf16[1024,256]{1,0:T(8,128)(2,1)S(1)}, bf16[1024,256]{1,0:T(8,128)(2,1)S(1)}, u32[]{:S(2)}, u32[]{:S(2)}) collective-permute-start(bf16[1024,256]{1,0:T(8,128)(2,1)S(1)} %get-tuple-element.101), channel_id=1, source_target_pairs={{0,64},{64,0},{1,65},{65,1},{2,66},{66,2},{3,67},{67,3},{4,68},{68... | collective-permute-start | bytes 1572872 | tf_op jit(solution)/shard_map/ppermute | solution.py:300
  47.9 1.9 copy-start.8
  47.9 18.1 %collective-permute-start.6 = (bf16[1296,256]{1,0:T(8,128)(2,1)S(1)}, bf16[1296,256]{1,0:T(8,128)(2,1)S(1)}, u32[]{:S(2)}, u32[]{:S(2)}) collective-permute-start(bf16[1296,256]{1,0:T(8,128)(2,1)S(1)} %get-tuple-element.60), channel_id=1, source_target_pairs={{0,1},{1,0},{2,3},{3,2},{4,5},{5,4},{6,7},{7,6},{8,9},{9,8},{10,11... | collective-permute-start | bytes 1990664 | tf_op jit(solution)/shard_map/ppermute | solution.py:300
  49.9 16.1 %collective-permute-start = (s32[8,128]{1,0:T(8,128)S(1)}, s32[8,128]{1,0:T(8,128)S(1)}, u32[]{:S(2)}, u32[]{:S(2)}) collective-permute-start(s32[8,128]{1,0:T(8,128)S(1)} %scatter.4), channel_id=1, source_target_pairs={{0,1},{1,0},{2,3},{3,2},{4,5},{5,4},{6,7},{7,6},{8,9},{9,8},{10,11... | collective-permute-start | bytes 12296 | tf_op jit(solution)/shard_map/ppermute | solution.py:300
  67.8 9.7 %collective-permute-start.7 = (bf16[528,256]{1,0:T(8,128)(2,1)S(1)}, bf16[528,256]{1,0:T(8,128)(2,1)S(1)}, u32[]{:S(2)}, u32[]{:S(2)}) collective-permute-start(bf16[528,256]{1,0:T(8,128)(2,1)S(1)} %get-tuple-element.62), channel_id=1, source_target_pairs={{0,8},{8,16},{16,24},{24,32},{32,40},{40,48},{48,56},{56,0},{1,9},... | collective-permute-start | bytes 811016 | tf_op jit(solution)/shard_map/ppermute | solution.py:304
  70.0 9.5 %collective-permute-start.11 = (bf16[528,256]{1,0:T(8,128)(2,1)S(1)}, bf16[528,256]{1,0:T(8,128)(2,1)S(1)}, u32[]{:S(2)}, u32[]{:S(2)}) collective-permute-start(bf16[528,256]{1,0:T(8,128)(2,1)S(1)} %get-tuple-element.66), channel_id=1, source_target_pairs={{0,56},{8,0},{16,8},{24,16},{32,24},{40,32},{48,40},{56,48},{1,57}... | collective-permute-start | bytes 811016 | tf_op jit(solution)/shard_map/ppermute | solution.py:304
  77.6 8.7 %collective-permute-start.8 = (bf16[528,256]{1,0:T(8,128)(2,1)S(1)}, bf16[528,256]{1,0:T(8,128)(2,1)S(1)}, u32[]{:S(2)}, u32[]{:S(2)}) collective-permute-start(bf16[528,256]{1,0:T(8,128)(2,1)S(1)} %shard_map.139), channel_id=1, source_target_pairs={{0,8},{8,16},{16,24},{24,32},{32,40},{40,48},{48,56},{56,0},{1,9},... | collective-permute-start | bytes 811016 | tf_op jit(solution)/shard_map/ppermute | solution.py:304
  79.6 8.7 %collective-permute-start.12 = (bf16[528,256]{1,0:T(8,128)(2,1)S(1)}, bf16[528,256]{1,0:T(8,128)(2,1)S(1)}, u32[]{:S(2)}, u32[]{:S(2)}) collective-permute-start(bf16[528,256]{1,0:T(8,128)(2,1)S(1)} %shard_map.142), channel_id=1, source_target_pairs={{0,56},{8,0},{16,8},{24,16},{32,24},{40,32},{48,40},{56,48},{1,57}... | collective-permute-start | bytes 811016 | tf_op jit(solution)/shard_map/ppermute | solution.py:304
  86.4 8.4 %collective-permute-start.9 = (bf16[528,256]{1,0:T(8,128)(2,1)S(1)}, bf16[528,256]{1,0:T(8,128)(2,1)S(1)}, u32[]{:S(2)}, u32[]{:S(2)}) collective-permute-start(bf16[528,256]{1,0:T(8,128)(2,1)S(1)} %shard_map.140), channel_id=1, source_target_pairs={{0,8},{8,16},{16,24},{24,32},{32,40},{40,48},{48,56},{56,0},{1,9},... | collective-permute-start | bytes 811016 | tf_op jit(solution)/shard_map/ppermute | solution.py:304
  88.4 8.4 %collective-permute-start.13 = (bf16[528,256]{1,0:T(8,128)(2,1)S(1)}, bf16[528,256]{1,0:T(8,128)(2,1)S(1)}, u32[]{:S(2)}, u32[]{:S(2)}) collective-permute-start(bf16[528,256]{1,0:T(8,128)(2,1)S(1)} %shard_map.143), channel_id=1, source_target_pairs={{0,56},{8,0},{16,8},{24,16},{32,24},{40,32},{48,40},{56,48},{1,57}... | collective-permute-start | bytes 811016 | tf_op jit(solution)/shard_map/ppermute | solution.py:304
  94.9 8.4 %collective-permute-start.10 = (bf16[528,256]{1,0:T(8,128)(2,1)S(1)}, bf16[528,256]{1,0:T(8,128)(2,1)S(1)}, u32[]{:S(2)}, u32[]{:S(2)}) collective-permute-start(bf16[528,256]{1,0:T(8,128)(2,1)S(1)} %shard_map.141), channel_id=1, source_target_pairs={{0,8},{8,16},{16,24},{24,32},{32,40},{40,48},{48,56},{56,0},{1,9},... | collective-permute-start | bytes 811016 | tf_op jit(solution)/shard_map/ppermute | solution.py:304
  103.4 6.7 %collective-permute-start.14 = (bf16[272,256]{1,0:T(8,128)(2,1)S(1)}, bf16[272,256]{1,0:T(8,128)(2,1)S(1)}, u32[]{:S(2)}, u32[]{:S(2)}) collective-permute-start(bf16[272,256]{1,0:T(8,128)(2,1)S(1)} %get-tuple-element.70), channel_id=1, source_target_pairs={{0,2},{1,3},{2,0},{3,1},{4,6},{5,7},{6,4},{7,5},{8,10},{9,11},{10,... | collective-permute-start | bytes 417800 | tf_op jit(solution)/shard_map/ppermute | solution.py:300
  110.1 13.0 %copy-start.1 = (bf16[128,256]{1,0:T(8,128)(2,1)S(1)}, bf16[128,256]{1,0:T(8,128)(2,1)}, u32[]{:S(2)}) copy-start(bf16[128,256]{1,0:T(8,128)(2,1)} %features.3) | copy-start | bytes 196612
  110.1 13.0 %copy-start.2 = (bf16[256,256]{1,0:T(8,128)(2,1)S(1)}, bf16[256,256]{1,0:T(8,128)(2,1)}, u32[]{:S(2)}) copy-start(bf16[256,256]{1,0:T(8,128)(2,1)} %w_self.3) | copy-start | bytes 393220
  110.1 13.0 %copy-start.3 = (bf16[256,256]{1,0:T(8,128)(2,1)S(1)}, bf16[256,256]{1,0:T(8,128)(2,1)}, u32[]{:S(2)}) copy-start(bf16[256,256]{1,0:T(8,128)(2,1)} %w_neigh.1) | copy-start | bytes 393220
  110.1 13.0 %copy-start.4 = (bf16[128,256]{1,0:T(8,128)(2,1)S(1)}, bf16[128,256]{1,0:T(8,128)(2,1)}, u32[]{:S(2)}) copy-start(bf16[128,256]{1,0:T(8,128)(2,1)} %grad_out.1) | copy-start | bytes 196612
  110.1 13.0 %collective-permute-start.15 = (bf16[144,256]{1,0:T(8,128)(2,1)S(1)}, bf16[144,256]{1,0:T(8,128)(2,1)S(1)}, u32[]{:S(2)}, u32[]{:S(2)}) collective-permute-start(bf16[144,256]{1,0:T(8,128)(2,1)S(1)} %get-tuple-element.72), channel_id=1, source_target_pairs={{0,4},{1,5},{2,6},{3,7},{4,0},{5,1},{6,2},{7,3},{8,12},{9,13},{10,... | collective-permute-start | bytes 221192 | tf_op jit(solution)/shard_map/ppermute | solution.py:300
  123.1 0.7 copy-start.5
  123.1 0.7 copy-start.6
  125.7 23.4 %all-to-all-start = ((bf16[8,80,256]{2,1,0:T(8,128)(2,1)}), bf16[8,80,256]{2,1,0:T(8,128)(2,1)S(1)}, u32[]{:S(2)}, u32[]{:S(2)}) async-start(bf16[8,80,256]{2,1,0:T(8,128)(2,1)} %bitcast.10), calls=%async_computation | async-start | bytes 655360 | tf_op jit(solution)/shard_map/all_to_all | solution.py:411
  136.5 12.7 %collective-permute-start.16 = (bf16[128,256]{1,0:T(8,128)(2,1)S(1)}, bf16[128,256]{1,0:T(8,128)(2,1)S(1)}, u32[]{:S(2)}, u32[]{:S(2)}) collective-permute-start(bf16[128,256]{1,0:T(8,128)(2,1)S(1)} %get-tuple-element.77.own), channel_id=1, source_target_pairs={{0,4},{1,5},{2,6},{3,7},{4,0},{5,1},{6,2},{7,3},{8,12},{9,13},{10,... | collective-permute-start | bytes 196616 | tf_op jit(solution)/shard_map/ppermute | solution.py:300
  149.2 11.8 %collective-permute-start.17 = (bf16[336,256]{1,0:T(8,128)(2,1)S(1)}, bf16[336,256]{1,0:T(8,128)(2,1)S(1)}, u32[]{:S(2)}, u32[]{:S(2)}) collective-permute-start(bf16[336,256]{1,0:T(8,128)(2,1)S(1)} %shard_map.148.own), channel_id=1, source_target_pairs={{0,2},{1,3},{2,0},{3,1},{4,6},{5,7},{6,4},{7,5},{8,10},{9,11},{10,... | collective-permute-start | bytes 516104 | tf_op jit(solution)/shard_map/ppermute | solution.py:300
  161.1 11.9 %collective-permute-start.21 = (bf16[512,256]{1,0:T(8,128)(2,1)S(1)}, bf16[512,256]{1,0:T(8,128)(2,1)S(1)}, u32[]{:S(2)}, u32[]{:S(2)}) collective-permute-start(bf16[512,256]{1,0:T(8,128)(2,1)S(1)} %get-tuple-element.79.refs_0_), channel_id=1, source_target_pairs={{0,8},{8,16},{16,24},{24,32},{32,40},{40,48},{48,56},{56,0},{1,9},... | collective-permute-start | bytes 786440 | tf_op jit(solution)/shard_map/ppermute | solution.py:304
  163.0 9.9 %collective-permute-start.22 = (bf16[80,256]{1,0:T(8,128)(2,1)S(1)}, bf16[80,256]{1,0:T(8,128)(2,1)S(1)}, u32[]{:S(2)}, u32[]{:S(2)}) collective-permute-start(bf16[80,256]{1,0:T(8,128)(2,1)S(1)} %get-tuple-element.80.own), channel_id=1, source_target_pairs={{0,4},{1,5},{2,6},{3,7},{4,0},{5,1},{6,2},{7,3},{8,12},{9,13},{10,... | collective-permute-start | bytes 122888 | tf_op jit(solution)/shard_map/ppermute | solution.py:300
  168.4 9.5 %collective-permute-start.18 = (bf16[512,256]{1,0:T(8,128)(2,1)S(1)}, bf16[512,256]{1,0:T(8,128)(2,1)S(1)}, u32[]{:S(2)}, u32[]{:S(2)}) collective-permute-start(bf16[512,256]{1,0:T(8,128)(2,1)S(1)} %get-tuple-element.79.refs_0_), channel_id=1, source_target_pairs={{0,56},{8,0},{16,8},{24,16},{32,24},{40,32},{48,40},{56,48},{1,57}... | collective-permute-start | bytes 786440 | tf_op jit(solution)/shard_map/ppermute | solution.py:304
  173.0 9.4 %collective-permute-start.23 = (bf16[512,256]{1,0:T(8,128)(2,1)S(1)}, bf16[512,256]{1,0:T(8,128)(2,1)S(1)}, u32[]{:S(2)}, u32[]{:S(2)}) collective-permute-start(bf16[512,256]{1,0:T(8,128)(2,1)S(1)} %get-tuple-element.81.refs_7_), channel_id=1, source_target_pairs={{0,8},{8,16},{16,24},{24,32},{32,40},{40,48},{48,56},{56,0},{1,9},... | collective-permute-start | bytes 786440 | tf_op jit(solution)/shard_map/ppermute | solution.py:304
  174.9 7.5 %collective-permute-start.24 = (f32[80,256]{1,0:T(8,128)S(1)}, f32[80,256]{1,0:T(8,128)S(1)}, u32[]{:S(2)}, u32[]{:S(2)}) collective-permute-start(f32[80,256]{1,0:T(8,128)S(1)} %get-tuple-element.82.own), channel_id=1, source_target_pairs={{0,1},{1,0},{2,3},{3,2},{4,5},{5,4},{6,7},{7,6},{8,9},{9,8},{10,11... | collective-permute-start | bytes 245768 | tf_op jit(solution)/shard_map/ppermute | solution.py:300
  177.9 10.8 %collective-permute-start.19 = (bf16[512,256]{1,0:T(8,128)(2,1)S(1)}, bf16[512,256]{1,0:T(8,128)(2,1)S(1)}, u32[]{:S(2)}, u32[]{:S(2)}) collective-permute-start(bf16[512,256]{1,0:T(8,128)(2,1)S(1)} %collective-permute-done.18.refs_1_), channel_id=1, source_target_pairs={{0,56},{8,0},{16,8},{24,16},{32,24},{40,32},{48,40},{56,48},{1,57}... | collective-permute-start | bytes 786440 | tf_op jit(solution)/shard_map/ppermute | solution.py:304
  182.5 8.8 %collective-permute-start.25 = (bf16[512,256]{1,0:T(8,128)(2,1)S(1)}, bf16[512,256]{1,0:T(8,128)(2,1)S(1)}, u32[]{:S(2)}, u32[]{:S(2)}) collective-permute-start(bf16[512,256]{1,0:T(8,128)(2,1)S(1)} %get-tuple-element.83.refs_6_), channel_id=1, source_target_pairs={{0,8},{8,16},{16,24},{24,32},{32,40},{40,48},{48,56},{56,0},{1,9},... | collective-permute-start | bytes 786440 | tf_op jit(solution)/shard_map/ppermute | solution.py:304
  184.4 6.9 %collective-permute-start.26 = (f32[80,256]{1,0:T(8,128)S(1)}, f32[80,256]{1,0:T(8,128)S(1)}, u32[]{:S(2)}, u32[]{:S(2)}) collective-permute-start(f32[80,256]{1,0:T(8,128)S(1)} %get-tuple-element.84.own), channel_id=1, source_target_pairs={{0,8},{8,0},{16,24},{24,16},{32,40},{40,32},{48,56},{56,48},{1,9},... | collective-permute-start | bytes 245768 | tf_op jit(solution)/shard_map/ppermute | solution.py:300
  188.6 7.2 %collective-permute-start.20 = (bf16[512,256]{1,0:T(8,128)(2,1)S(1)}, bf16[512,256]{1,0:T(8,128)(2,1)S(1)}, u32[]{:S(2)}, u32[]{:S(2)}) collective-permute-start(bf16[512,256]{1,0:T(8,128)(2,1)S(1)} %collective-permute-done.19.refs_2_), channel_id=1, source_target_pairs={{0,56},{8,0},{16,8},{24,16},{32,24},{40,32},{48,40},{56,48},{1,57}... | collective-permute-start | bytes 786440 | tf_op jit(solution)/shard_map/ppermute | solution.py:304
  191.4 8.3 %collective-permute-start.27 = (bf16[512,256]{1,0:T(8,128)(2,1)S(1)}, bf16[512,256]{1,0:T(8,128)(2,1)S(1)}, u32[]{:S(2)}, u32[]{:S(2)}) collective-permute-start(bf16[512,256]{1,0:T(8,128)(2,1)S(1)} %get-tuple-element.85.refs_5_), channel_id=1, source_target_pairs={{0,8},{8,16},{16,24},{24,32},{32,40},{40,48},{48,56},{56,0},{1,9},... | collective-permute-start | bytes 786440 | tf_op jit(solution)/shard_map/ppermute | solution.py:304
  201.5 20.3 %collective-permute-start.28 = (bf16[1280,256]{1,0:T(8,128)(2,1)S(1)}, bf16[1280,256]{1,0:T(8,128)(2,1)S(1)}, u32[]{:S(2)}, u32[]{:S(2)}) collective-permute-start(bf16[1280,256]{1,0:T(8,128)(2,1)S(1)} %shard_map.153), channel_id=1, source_target_pairs={{0,1},{1,0},{2,3},{3,2},{4,5},{5,4},{6,7},{7,6},{8,9},{9,8},{10,11... | collective-permute-start | bytes 1966088 | tf_op jit(solution)/shard_map/ppermute | solution.py:300
  204.9 7.0 %collective-permute-start.29 = (f32[80,256]{1,0:T(8,128)S(1)}, f32[80,256]{1,0:T(8,128)S(1)}, u32[]{:S(2)}, u32[]{:S(2)}) collective-permute-start(f32[80,256]{1,0:T(8,128)S(1)} %get-tuple-element.86), channel_id=1, source_target_pairs={{0,16},{8,24},{16,0},{24,8},{32,48},{40,56},{48,32},{56,40},{1,17}... | collective-permute-start | bytes 245768 | tf_op jit(solution)/shard_map/ppermute | solution.py:300
  211.9 10.0 %collective-permute-start.30 = (f32[80,256]{1,0:T(8,128)S(1)}, f32[80,256]{1,0:T(8,128)S(1)}, u32[]{:S(2)}, u32[]{:S(2)}) collective-permute-start(f32[80,256]{1,0:T(8,128)S(1)} %add.67), channel_id=1, source_target_pairs={{0,32},{8,40},{16,48},{24,56},{32,0},{40,8},{48,16},{56,24},{1,33}... | collective-permute-start | bytes 245768 | tf_op jit(solution)/shard_map/ppermute | solution.py:300
  225.9 21.2 %collective-permute-start.31 = (bf16[1024,256]{1,0:T(8,128)(2,1)S(1)}, bf16[1024,256]{1,0:T(8,128)(2,1)S(1)}, u32[]{:S(2)}, u32[]{:S(2)}) collective-permute-start(bf16[1024,256]{1,0:T(8,128)(2,1)S(1)} %get-tuple-element.88), channel_id=1, source_target_pairs={{0,64},{64,0},{1,65},{65,1},{2,66},{66,2},{3,67},{67,3},{4,68},{68... | collective-permute-start | bytes 1572872 | tf_op jit(solution)/shard_map/ppermute | solution.py:300
  232.6 14.5 %collective-permute-start.32 = (bf16[80,256]{1,0:T(8,128)(2,1)S(1)}, bf16[80,256]{1,0:T(8,128)(2,1)S(1)}, u32[]{:S(2)}, u32[]{:S(2)}) collective-permute-start(bf16[80,256]{1,0:T(8,128)(2,1)S(1)} %add_convert_fusion.after.piece_in), channel_id=1, source_target_pairs={{0,512},{512,0},{1,513},{513,1},{2,514},{514,2},{3,515},{515,3},{4... | collective-permute-start | bytes 122888 | tf_op jit(solution)/shard_map/ppermute | solution.py:300
  247.3 10.2 %collective-permute-start.33 = (bf16[336,256]{1,0:T(8,128)(2,1)S(1)}, bf16[336,256]{1,0:T(8,128)(2,1)S(1)}, u32[]{:S(2)}, u32[]{:S(2)}) collective-permute-start(bf16[336,256]{1,0:T(8,128)(2,1)S(1)} %get-tuple-element.91), channel_id=1, source_target_pairs={{0,128},{128,256},{256,384},{384,0},{1,129},{129,257},{257,385},{3... | collective-permute-start | bytes 516104 | tf_op jit(solution)/shard_map/ppermute | solution.py:304
  250.2 9.8 %collective-permute-start.34 = (bf16[336,256]{1,0:T(8,128)(2,1)S(1)}, bf16[336,256]{1,0:T(8,128)(2,1)S(1)}, u32[]{:S(2)}, u32[]{:S(2)}) collective-permute-start(bf16[336,256]{1,0:T(8,128)(2,1)S(1)} %get-tuple-element.92), channel_id=1, source_target_pairs={{0,256},{128,384},{256,0},{384,128},{1,257},{129,385},{257,1},{385... | collective-permute-start | bytes 516104 | tf_op jit(solution)/shard_map/ppermute | solution.py:304
  254.3 7.6 %collective-permute-start.35 = (bf16[336,256]{1,0:T(8,128)(2,1)S(1)}, bf16[336,256]{1,0:T(8,128)(2,1)S(1)}, u32[]{:S(2)}, u32[]{:S(2)}) collective-permute-start(bf16[336,256]{1,0:T(8,128)(2,1)S(1)} %get-tuple-element.93), channel_id=1, source_target_pairs={{0,384},{128,0},{256,128},{384,256},{1,385},{129,1},{257,129},{385... | collective-permute-start | bytes 516104 | tf_op jit(solution)/shard_map/ppermute | solution.py:304
  262.5 19.1 %collective-permute-start.37 = (bf16[272,256]{1,0:T(8,128)(2,1)S(1)}, bf16[272,256]{1,0:T(8,128)(2,1)S(1)}, u32[]{:S(2)}, u32[]{:S(2)}) collective-permute-start(bf16[272,256]{1,0:T(8,128)(2,1)S(1)} %get-tuple-element.96.whole), channel_id=1, source_target_pairs={{0,64},{64,0},{1,65},{65,1},{2,66},{66,2},{3,67},{67,3},{4,68},{68... | collective-permute-start | bytes 417800 | tf_op jit(solution)/shard_map/ppermute | solution.py:300
  266.3 15.3 %collective-permute-start.36 = (bf16[128,256]{1,0:T(8,128)(2,1)S(1)}, bf16[128,256]{1,0:T(8,128)(2,1)S(1)}, u32[]{:S(2)}, u32[]{:S(2)}) collective-permute-start(bf16[128,256]{1,0:T(8,128)(2,1)S(1)} %get-tuple-element.95), channel_id=1, source_target_pairs={{0,512},{512,0},{1,513},{513,1},{2,514},{514,2},{3,515},{515,3},{4... | collective-permute-start | bytes 196616 | tf_op jit(solution)/shard_map/ppermute | solution.py:300
